TPU v7x, 32 devices: a whole 2x2x4 slice. The times are simulated.
32 devices in a mesh: dp: 8 (over z, x), tensor: 4 (over y, core).
Axes of the slice: x: 2, y: 2, z: 4, core: 2. Of those that a mesh axis runs over, the one named last changes fastest.
Arguments:
- hidden_in: bfloat16 [8192, 2048], P('dp'), may hold values from -6 to 6
- out_cotangent: bfloat16 [8192, 2048], P('dp'), may hold values from -6 to 6
- episode_lengths: int32 [8, 8], P('dp'), may hold values from 1 to 512, 1024 in all within a row
- self_generated: int32 [8192], P('dp'), may hold values 0 or 1
- loss_numerator: int32 [8192], P('dp'), may hold values from 1 to 8
- attend_weights: float32 [2048, 3, 2048], P('dp', None, 'tensor'), may hold values from -0.125 to 0.125
- attend_first: float32 [2048, 3, 2048], P('dp', None, 'tensor'), may hold values from -512 to 512
- attend_second: float32 [2048, 3, 2048], P('dp', None, 'tensor'), may hold values from 4096 to 65536
- attend_average: float32 [2048, 3, 2048], P('dp', None, 'tensor'), may hold values from -0.125 to 0.125
- combine_weights: float32 [2048, 2048], P('tensor', 'dp'), may hold values from -1 to 1
- combine_first: float32 [2048, 2048], P('tensor', 'dp'), may hold values from -80 to 80
- combine_second: float32 [2048, 2048], P('tensor', 'dp'), may hold values from 96 to 1600
- combine_average: float32 [2048, 2048], P('tensor', 'dp'), may hold values from -1 to 1
- expand_weights: float32 [2048, 8192], P('dp', 'tensor'), may hold values from -0.125 to 0.125
- expand_first: float32 [2048, 8192], P('dp', 'tensor'), may hold values from -128 to 128
- expand_second: float32 [2048, 8192], P('dp', 'tensor'), may hold values from 245.76 to 4096
- expand_average: float32 [2048, 8192], P('dp', 'tensor'), may hold values from -0.125 to 0.125
- shrink_weights: float32 [8192, 2048], P('tensor', 'dp'), may hold values from -0.0625 to 0.0625
- shrink_first: float32 [8192, 2048], P('tensor', 'dp'), may hold values from -256 to 256
- shrink_second: float32 [8192, 2048], P('tensor', 'dp'), may hold values from 983.04 to 16384
- shrink_average: float32 [8192, 2048], P('tensor', 'dp'), may hold values from -0.0625 to 0.0625
- layernorm_params: float32 [4, 2048], P(None, 'dp'), may hold values from -1 to 1.3, as said below
- layernorm_first: float32 [4, 2048], P(None, 'dp'), may hold values from -384 to 384
- layernorm_second: float32 [4, 2048], P(None, 'dp'), may hold values from 2048 to 32768
- layernorm_average: float32 [4, 2048], P(None, 'dp'), may hold values from -1 to 1.3, as said below
Outputs:
- layer_output: bfloat16 [8192, 2048], P('dp')
- input_gradient: float32 [8192, 2048], P('dp')
- attend_master: float32 [2048, 3, 2048], P('dp', None, 'tensor')
- attend_moment: float32 [2048, 3, 2048], P('dp', None, 'tensor')
- attend_square: float32 [2048, 3, 2048], P('dp', None, 'tensor')
- attend_smooth: float32 [2048, 3, 2048], P('dp', None, 'tensor')
- attend_copy: bfloat16 [2048, 3, 2048], P('dp', None, 'tensor')
- combine_master: float32 [2048, 2048], P('tensor', 'dp')
- combine_moment: float32 [2048, 2048], P('tensor', 'dp')
- combine_square: float32 [2048, 2048], P('tensor', 'dp')
- combine_smooth: float32 [2048, 2048], P('tensor', 'dp')
- combine_copy: bfloat16 [2048, 2048], P('tensor', 'dp')
- expand_master: float32 [2048, 8192], P('dp', 'tensor')
- expand_moment: float32 [2048, 8192], P('dp', 'tensor')
- expand_square: float32 [2048, 8192], P('dp', 'tensor')
- expand_smooth: float32 [2048, 8192], P('dp', 'tensor')
- expand_copy: bfloat16 [2048, 8192], P('dp', 'tensor')
- shrink_master: float32 [8192, 2048], P('tensor', 'dp')
- shrink_moment: float32 [8192, 2048], P('tensor', 'dp')
- shrink_square: float32 [8192, 2048], P('tensor', 'dp')
- shrink_smooth: float32 [8192, 2048], P('tensor', 'dp')
- shrink_copy: bfloat16 [8192, 2048], P('tensor', 'dp')
- layernorm_master: float32 [4, 2048], P(None, 'dp')
- layernorm_moment: float32 [4, 2048], P(None, 'dp')
- layernorm_square: float32 [4, 2048], P(None, 'dp')
- layernorm_smooth: float32 [4, 2048], P(None, 'dp')
- layernorm_copy: bfloat16 [4, 2048], P(None, 'dp')
Inputs may be any that keep to these rules, and one draw needn't show every extreme that they name: `layernorm_params`: gains about one, biases of either sign. `layernorm_average`: gains about one, biases of either sign.
All inputs are finite; a program needn't handle non-finite values. No bound on the sum of `self_generated` on one device may be relied on, other than what follows from the above.
Results may differ from a plain program's by a relative error of at most 0.012.
The roundings to bfloat16 on the way count: a program that leaves them out, or rounds other values in their place, can miss the bound.
Values may be sent and summed in bfloat16 or wider, within the bound.
No kernel may reach another device: no remote copies, remote signals or barrier semaphores. Data moves between devices by JAX's collectives and lax.ppermute only.
A program may use at most 320 MiB of HBM per device.

v0:
```python
import jax
import jax.numpy as jnp
from jax import lax
from jax.sharding import PartitionSpec as P

HEAD_DIM = 128
STEP = 10


beta_first = 0.5
beta_second = 0.5
average_decay = 0.5
adam_epsilon = 1e-08
weight_decay = 0.1
matrix_rate = 0.02
norm_rate = 0.2
norm_epsilon = 1e-05


def layer_norm(values, gain_row, shift_row):
    center = values - jnp.mean(values, axis=-1, keepdims=True)
    spread = jnp.mean(center * center, axis=-1, keepdims=True)
    return center * lax.rsqrt(spread + norm_epsilon) * gain_row + shift_row


def segment_ids(lengths_row, row_length):
    bounds = jnp.cumsum(lengths_row)
    places = jnp.arange(row_length, dtype=jnp.int32)
    return jnp.sum((places[:, None] >= bounds[None, :]).astype(jnp.int32), axis=1)


def allowed_mask(segment, first_row, block_rows):
    row_length = segment.shape[0]
    query_places = first_row + jnp.arange(block_rows, dtype=jnp.int32)
    key_places = jnp.arange(row_length, dtype=jnp.int32)
    query_segment = segment[first_row : first_row + block_rows]
    return (query_segment[:, None] == segment[None, :]) & (
        key_places[None, :] <= query_places[:, None]
    )


def attend_row(packed):
    queries, keys_row, values_row, segment = packed
    row_length = queries.shape[0]
    block_rows = min(512, row_length)
    score_scale = HEAD_DIM ** (-0.5)
    out_parts = []
    logsum_parts = []
    for first_row in range(0, row_length, block_rows):
        query_block = queries[first_row : first_row + block_rows]
        allowed = allowed_mask(segment, first_row, block_rows)
        scores = (
            jnp.einsum("qhd,khd->hqk", query_block, keys_row, preferred_element_type=jnp.float32)
            * score_scale
        )
        masked = jnp.where(allowed[None], scores, -1e30)
        row_top = jnp.max(masked, axis=-1, keepdims=True)
        exponent = jnp.exp(masked - row_top)
        row_total = jnp.sum(exponent, axis=-1, keepdims=True)
        softmax_low = (exponent / row_total).astype(jnp.bfloat16)
        out_parts.append(
            jnp.einsum("hqk,khd->qhd", softmax_low, values_row, preferred_element_type=jnp.float32)
        )
        logsum_parts.append((row_top + jnp.log(row_total))[..., 0])
    return (jnp.concatenate(out_parts, axis=0), jnp.concatenate(logsum_parts, axis=1))


def attend_row_back(packed):
    queries, keys_row, values_row, segment, logsum, grad_row = packed
    row_length = queries.shape[0]
    block_rows = min(512, row_length)
    score_scale = HEAD_DIM ** (-0.5)
    keys_grad = jnp.zeros(keys_row.shape, jnp.float32)
    values_grad = jnp.zeros(values_row.shape, jnp.float32)
    query_parts = []
    for first_row in range(0, row_length, block_rows):
        query_block = queries[first_row : first_row + block_rows]
        grad_block = grad_row[first_row : first_row + block_rows]
        allowed = allowed_mask(segment, first_row, block_rows)
        scores = (
            jnp.einsum("qhd,khd->hqk", query_block, keys_row, preferred_element_type=jnp.float32)
            * score_scale
        )
        masked = jnp.where(allowed[None], scores, -1e30)
        softmax_full = jnp.exp(masked - logsum[:, first_row : first_row + block_rows, None])
        softmax_low = softmax_full.astype(jnp.bfloat16)
        values_grad = values_grad + jnp.einsum(
            "hqk,qhd->khd", softmax_low, grad_block, preferred_element_type=jnp.float32
        )
        prob_grad = jnp.einsum(
            "qhd,khd->hqk", grad_block, values_row, preferred_element_type=jnp.float32
        )
        row_delta = jnp.sum(prob_grad * softmax_full, axis=-1, keepdims=True)
        score_grad = (softmax_full * (prob_grad - row_delta)).astype(jnp.bfloat16)
        query_parts.append(
            jnp.einsum("hqk,khd->qhd", score_grad, keys_row, preferred_element_type=jnp.float32)
            * score_scale
        )
        keys_grad = (
            keys_grad
            + jnp.einsum(
                "hqk,qhd->khd", score_grad, query_block, preferred_element_type=jnp.float32
            )
            * score_scale
        )
    stacked = jnp.stack([jnp.concatenate(query_parts, axis=0), keys_grad, values_grad], axis=1)
    return stacked.astype(jnp.bfloat16)


def adam_update(master, moment, square, gradient, rate_value, decay_value):
    moment_new = beta_first * moment + (1.0 - beta_first) * gradient
    square_new = beta_second * square + (1.0 - beta_second) * gradient * gradient
    fix_first = 1.0 - beta_first**STEP
    fix_second = 1.0 - beta_second**STEP
    direction = moment_new / fix_first / (jnp.sqrt(square_new / fix_second) + adam_epsilon)
    master_new = master - rate_value * (direction + decay_value * master)
    return (master_new, moment_new, square_new)


def shards(
    hidden_in,
    out_cotangent,
    episode_lengths,
    self_generated,
    loss_numerator,
    attend_weights,
    attend_first,
    attend_second,
    attend_average,
    combine_weights,
    combine_first,
    combine_second,
    combine_average,
    expand_weights,
    expand_first,
    expand_second,
    expand_average,
    shrink_weights,
    shrink_first,
    shrink_second,
    shrink_average,
    layernorm_params,
    layernorm_first,
    layernorm_second,
    layernorm_average,
):
    local_tokens = hidden_in.shape[0]
    row_count = episode_lengths.shape[0]
    row_length = local_tokens // row_count
    attend_low = attend_weights.astype(jnp.bfloat16)
    combine_low = combine_weights.astype(jnp.bfloat16)
    expand_low = expand_weights.astype(jnp.bfloat16)
    shrink_low = shrink_weights.astype(jnp.bfloat16)
    norm_low = layernorm_params.astype(jnp.bfloat16)
    attend_full, combine_full, expand_full, shrink_full, norm_full = (
        lax.all_gather(attend_low, "dp", axis=0, tiled=True),
        lax.all_gather(combine_low, "dp", axis=1, tiled=True),
        lax.all_gather(expand_low, "dp", axis=0, tiled=True),
        lax.all_gather(shrink_low, "dp", axis=1, tiled=True),
        lax.all_gather(norm_low, "dp", axis=1, tiled=True),
    )
    norm_values = norm_full.astype(jnp.float32)
    hidden = hidden_in.astype(jnp.float32)
    normed_one, pull_one = jax.vjp(layer_norm, hidden, norm_values[0], norm_values[1])
    normed_low = normed_one.astype(jnp.bfloat16)
    projected = jnp.einsum(
        "nd,dke->nke", normed_low, attend_full, preferred_element_type=jnp.float32
    ).astype(jnp.bfloat16)
    local_width = projected.shape[2]
    head_count = local_width // HEAD_DIM
    shaped = projected.reshape(row_count, row_length, 3, head_count, HEAD_DIM)
    segments = jax.vmap(lambda lengths_row: segment_ids(lengths_row, row_length))(episode_lengths)
    queries_all = shaped[:, :, 0]
    keys_all = shaped[:, :, 1]
    values_all = shaped[:, :, 2]
    mixed_heads, logsum = lax.map(attend_row, (queries_all, keys_all, values_all, segments))
    mixed_low = mixed_heads.reshape(local_tokens, local_width).astype(jnp.bfloat16)
    attended = lax.psum(
        jnp.dot(mixed_low, combine_full, preferred_element_type=jnp.float32), "tensor"
    )
    residual = hidden + attended
    normed_two, pull_two = jax.vjp(layer_norm, residual, norm_values[2], norm_values[3])
    normed_two_low = normed_two.astype(jnp.bfloat16)
    expanded = jnp.dot(normed_two_low, expand_full, preferred_element_type=jnp.float32)
    activated, pull_gelu = jax.vjp(jax.nn.gelu, expanded)
    activated_low = activated.astype(jnp.bfloat16)
    branch = lax.psum(
        jnp.dot(activated_low, shrink_full, preferred_element_type=jnp.float32), "tensor"
    )
    layer_output = (residual + branch).astype(jnp.bfloat16)
    factor = loss_numerator.astype(jnp.float32) / (4.0 * (1.0 + self_generated.astype(jnp.float32)))
    out_grad = factor[:, None] * out_cotangent.astype(jnp.float32)
    attend_back, combine_back, expand_back, shrink_back = (
        lax.all_gather(attend_low, "dp", axis=0, tiled=True),
        lax.all_gather(combine_low, "dp", axis=1, tiled=True),
        lax.all_gather(expand_low, "dp", axis=0, tiled=True),
        lax.all_gather(shrink_low, "dp", axis=1, tiled=True),
    )
    branch_grad_low = out_grad.astype(jnp.bfloat16)
    shrink_grad = jnp.einsum(
        "nf,nd->fd", activated_low, branch_grad_low, preferred_element_type=jnp.float32
    )
    activated_grad = jnp.einsum(
        "nd,fd->nf", branch_grad_low, shrink_back, preferred_element_type=jnp.float32
    )
    expanded_grad_low = pull_gelu(activated_grad)[0].astype(jnp.bfloat16)
    expand_grad = jnp.einsum(
        "nd,nf->df", normed_two_low, expanded_grad_low, preferred_element_type=jnp.float32
    )
    normed_two_grad = lax.psum(
        jnp.einsum("nf,df->nd", expanded_grad_low, expand_back, preferred_element_type=jnp.float32),
        "tensor",
    )
    residual_from_norm, gain_two_grad, shift_two_grad = pull_two(normed_two_grad)
    residual_grad = out_grad + residual_from_norm
    attended_grad_low = residual_grad.astype(jnp.bfloat16)
    combine_grad = jnp.einsum(
        "ne,nd->ed", mixed_low, attended_grad_low, preferred_element_type=jnp.float32
    )
    mixed_grad = jnp.einsum(
        "nd,ed->ne", attended_grad_low, combine_back, preferred_element_type=jnp.float32
    ).astype(jnp.bfloat16)
    mixed_grad_rows = mixed_grad.reshape(row_count, row_length, head_count, HEAD_DIM)
    projected_grad = lax.map(
        attend_row_back, (queries_all, keys_all, values_all, segments, logsum, mixed_grad_rows)
    )
    projected_grad = projected_grad.reshape(local_tokens, 3, local_width)
    attend_grad = jnp.einsum(
        "nd,nke->dke", normed_low, projected_grad, preferred_element_type=jnp.float32
    )
    normed_one_grad = lax.psum(
        jnp.einsum("nke,dke->nd", projected_grad, attend_back, preferred_element_type=jnp.float32),
        "tensor",
    )
    hidden_from_norm, gain_one_grad, shift_one_grad = pull_one(normed_one_grad)
    input_gradient = residual_grad + hidden_from_norm
    norm_grad = jnp.stack([gain_one_grad, shift_one_grad, gain_two_grad, shift_two_grad])
    attend_sum, combine_sum, expand_sum, shrink_sum, norm_sum = (
        lax.psum_scatter(attend_grad, "dp", scatter_dimension=0, tiled=True),
        lax.psum_scatter(combine_grad, "dp", scatter_dimension=1, tiled=True),
        lax.psum_scatter(expand_grad, "dp", scatter_dimension=0, tiled=True),
        lax.psum_scatter(shrink_grad, "dp", scatter_dimension=1, tiled=True),
        lax.psum_scatter(norm_grad, "dp", scatter_dimension=1, tiled=True),
    )
    kinds = (
        (
            attend_weights,
            attend_first,
            attend_second,
            attend_average,
            attend_sum,
            matrix_rate,
            weight_decay,
        ),
        (
            combine_weights,
            combine_first,
            combine_second,
            combine_average,
            combine_sum,
            matrix_rate,
            weight_decay,
        ),
        (
            expand_weights,
            expand_first,
            expand_second,
            expand_average,
            expand_sum,
            matrix_rate,
            weight_decay,
        ),
        (
            shrink_weights,
            shrink_first,
            shrink_second,
            shrink_average,
            shrink_sum,
            matrix_rate,
            weight_decay,
        ),
        (
            layernorm_params,
            layernorm_first,
            layernorm_second,
            layernorm_average,
            norm_sum,
            norm_rate,
            0.0,
        ),
    )
    results = [layer_output, input_gradient]
    for master, moment, square, average, gradient, rate_value, decay_value in kinds:
        master_new, moment_new, square_new = adam_update(
            master, moment, square, gradient, rate_value, decay_value
        )
        smooth_new = average_decay * average + (1.0 - average_decay) * master_new
        results.extend(
            [master_new, moment_new, square_new, smooth_new, master_new.astype(jnp.bfloat16)]
        )
    return tuple(results)


def solution(mesh):
    placed = (
        P("dp", None),
        P("dp", None),
        P("dp", None),
        P("dp"),
        P("dp"),
        P("dp", None, "tensor"),
        P("dp", None, "tensor"),
        P("dp", None, "tensor"),
        P("dp", None, "tensor"),
        P("tensor", "dp"),
        P("tensor", "dp"),
        P("tensor", "dp"),
        P("tensor", "dp"),
        P("dp", "tensor"),
        P("dp", "tensor"),
        P("dp", "tensor"),
        P("dp", "tensor"),
        P("tensor", "dp"),
        P("tensor", "dp"),
        P("tensor", "dp"),
        P("tensor", "dp"),
        P(None, "dp"),
        P(None, "dp"),
        P(None, "dp"),
        P(None, "dp"),
    )
    return jax.shard_map(
        shards,
        mesh=mesh,
        in_specs=placed,
        out_specs=(
            P("dp", None),
            P("dp", None),
            P("dp", None, "tensor"),
            P("dp", None, "tensor"),
            P("dp", None, "tensor"),
            P("dp", None, "tensor"),
            P("dp", None, "tensor"),
            P("tensor", "dp"),
            P("tensor", "dp"),
            P("tensor", "dp"),
            P("tensor", "dp"),
            P("tensor", "dp"),
            P("dp", "tensor"),
            P("dp", "tensor"),
            P("dp", "tensor"),
            P("dp", "tensor"),
            P("dp", "tensor"),
            P("tensor", "dp"),
            P("tensor", "dp"),
            P("tensor", "dp"),
            P("tensor", "dp"),
            P("tensor", "dp"),
            P(None, "dp"),
            P(None, "dp"),
            P(None, "dp"),
            P(None, "dp"),
            P(None, "dp"),
        ),
        check_vma=False,
    )
```

profile of v0, /device:TPU:0, one launch (start us, length us, event | category | flops | bytes accessed | tf_op | source)
XLA Modules:
  0.0 2105.7 jit_solution(13383608278149614679)
XLA Ops:
  12.4 28.2 %all_gather.19 = bf16[4,2048]{1,0:T(4,128)(2,1)S(1)} all-gather(bf16[4,256]{1,0:T(4,128)(2,1)S(1)} %convert_element_type.115), channel_id=1, replica_groups=mesh['dp'=8,'tensor'=4] {'dp'}, dimensions={1}, use_global_device_ids=true | all-gather | bytes 18432 | tf_op jit(solution)/shard_map/all_gather | solution.py:160
  49.8 63.7 %all-gather.5.cloned.1.call-done = bf16[2048,3,512]{0,2,1:T(8,128)(2,1)} async-done(((bf16[256,3,512]{0,2,1:T(8,128)(2,1)}), bf16[2048,3,512]{0,2,1:T(8,128)(2,1)}) %all-gather.5.cloned.1.call-update) | async-done | bytes 6291472 | tf_op jit(solution)/shard_map/all_gather | solution.py:156
  113.5 11.2 convolution_convert_fusion
  138.3 27.1 %all-gather.7.cloned.1.call-done = bf16[512,2048]{1,0:T(8,128)(2,1)} async-done(((bf16[512,256]{1,0:T(8,128)(2,1)}), bf16[512,2048]{1,0:T(8,128)(2,1)}) %all-gather.7.cloned.1.call-update) | async-done | bytes 2097168 | tf_op jit(solution)/shard_map/all_gather | solution.py:157
  176.0 148.3 %all-reduce.5.cloned.1.call-done = f32[1024,2048]{1,0:T(8,128)} async-done(((f32[1024,2048]{1,0:T(8,128)}), f32[1024,2048]{1,0:T(8,128)}) %all-reduce.5.cloned.1.call-update) | async-done | bytes 8388624 | tf_op jit(solution)/shard_map/psum | solution.py:178
  334.2 117.8 %all-gather.9.cloned.1.call-done = bf16[2048,2048]{1,0:T(8,128)(2,1)} async-done(((bf16[256,2048]{1,0:T(8,128)(2,1)}), bf16[2048,2048]{1,0:T(8,128)(2,1)}) %all-gather.9.cloned.1.call-update) | async-done | bytes 8388624 | tf_op jit(solution)/shard_map/all_gather | solution.py:158
  451.9 14.0 fusion.69
  469.3 13.8 fusion.37
  483.5 280.5 %reduce-scatter.14.cloned.1.call-done = f32[2048,256]{1,0:T(8,128)} async-done(((f32[2048,2048]{1,0:T(8,128)}), f32[2048,256]{1,0:T(8,128)}) %reduce-scatter.14.cloned.1.call-update) | async-done | bytes 2097168 | tf_op jit(solution)/shard_map/reduce_scatter | solution.py:242
  772.6 124.6 %all-gather.11.cloned.1.call-done = bf16[2048,2048]{1,0:T(8,128)(2,1)} async-done(((bf16[2048,256]{1,0:T(8,128)(2,1)}), bf16[2048,2048]{1,0:T(8,128)(2,1)}) %all-gather.11.cloned.1.call-update) | async-done | bytes 8388624 | tf_op jit(solution)/shard_map/all_gather | solution.py:159
  897.2 18.0 fusion.15
  917.3 13.3 fusion.88
  930.9 17.1 fusion.66
  947.9 133.9 %all-reduce.7.cloned.1.call-done = f32[1024,2048]{1,0:T(8,128)} async-done(((f32[1024,2048]{1,0:T(8,128)}), f32[1024,2048]{1,0:T(8,128)}) %all-reduce.7.cloned.1.call-update) | async-done | bytes 8388624 | tf_op jit(solution)/shard_map/psum | solution.py:210
  1133.2 11.1 convolution_bitcast_fusion
  1152.1 281.4 %all-reduce.9.cloned.1.call-done = (f32[1024,2048]{1,0:T(8,128)}, f32[1024,2048]{1,0:T(8,128)}) async-done(((f32[1024,2048]{1,0:T(8,128)}, f32[1024,2048]{1,0:T(8,128)}), (f32[1024,2048]{1,0:T(8,128)}, f32[1024,2048]{1,0:T(8,128)})) %all-reduce.9.cloned.1.call-update) | async-done | bytes 16777232 | tf_op jit(solution)/shard_map/psum | solution.py:187
  1447.4 13.4 fusion.50
  1461.4 16.8 fusion.68
  1483.0 43.0 %reduce-scatter.10.cloned.1.call-done = f32[512,256]{1,0:T(8,128)} async-done(((f32[512,2048]{1,0:T(8,128)}), f32[512,256]{1,0:T(8,128)}) %reduce-scatter.10.cloned.1.call-update) | async-done | bytes 524304 | tf_op jit(solution)/shard_map/reduce_scatter | solution.py:240
  1530.8 9.4 add_convert_fusion
  1540.3 11.6 add_add_fusion.2
  1551.9 41.2 %reduce-scatter.16.cloned.1.call-done = f32[256,4]{1,0:T(8,128)} async-done(((f32[2048,4]{1,0:T(8,128)}), f32[256,4]{1,0:T(8,128)}) %reduce-scatter.16.cloned.1.call-update) | async-done | bytes 4112
  1595.3 208.7 %reduce-scatter.8.cloned.1.call-done = f32[256,3,512]{2,0,1:T(8,128)} async-done(((f32[2048,3,512]{2,0,1:T(8,128)}), f32[256,3,512]{2,0,1:T(8,128)}) %reduce-scatter.8.cloned.1.call-update) | async-done | bytes 1572880 | tf_op jit(solution)/shard_map/reduce_scatter | solution.py:239
  1812.4 277.6 %reduce-scatter.12.cloned.1.call-done = f32[256,2048]{1,0:T(8,128)} async-done(((f32[2048,2048]{1,0:T(8,128)}), f32[256,2048]{1,0:T(8,128)}) %reduce-scatter.12.cloned.1.call-update) | async-done | bytes 2097168 | tf_op jit(solution)/shard_map/reduce_scatter | solution.py:241
  (200 shorter events, 165.1 us)
Async XLA Ops:
  7.2 106.3 %all-gather.5.cloned.1.call-start = ((), (), s32[]{:S(2)}) async-start(), calls=%async_computation.5 | async-start | bytes 7077888 | tf_op jit(solution)/shard_map/all_gather | solution.py:156
  9.8 155.6 %all-gather.7.cloned.1.call-start = ((), (), s32[]{:S(2)}) async-start(), calls=%async_computation.6 | async-start | bytes 2359296 | tf_op jit(solution)/shard_map/all_gather | solution.py:157
  11.7 312.6 %all-reduce.5.cloned.1.call-start = ((), (), s32[]{:S(2)}) async-start(), calls=%async_computation.7 | async-start | bytes 16777216 | tf_op jit(solution)/shard_map/psum | solution.py:178
  40.7 84.0 %copy-start.26 = (f32[1,2048]{1,0:T(1,128)}, f32[1,2048]{1,0:T(1,128)S(1)}, u32[]{:S(2)}) copy-start(f32[1,2048]{1,0:T(1,128)S(1)} %get-tuple-element.109) | copy-start | bytes 24580
  40.7 84.0 %copy-start.38 = (f32[1,2048]{1,0:T(1,128)}, f32[1,2048]{1,0:T(1,128)S(1)}, u32[]{:S(2)}) copy-start(f32[1,2048]{1,0:T(1,128)S(1)} %get-tuple-element.110) | copy-start | bytes 24580
  40.7 411.2 %copy-start.36 = (f32[1,2048]{1,0:T(1,128)}, f32[1,2048]{1,0:T(1,128)S(1)}, u32[]{:S(2)}) copy-start(f32[1,2048]{1,0:T(1,128)S(1)} %get-tuple-element.108) | copy-start | bytes 24580
  43.6 81.1 %copy-start.28 = (f32[1024]{0:T(1024)}, f32[1024]{0:T(1024)S(1)}, u32[]{:S(2)}) copy-start(f32[1024]{0:T(1024)S(1)} %broadcast_multiply_fusion.1) | copy-start | bytes 12292
  47.0 77.7 %copy-start.30 = (f32[1024]{0:T(1024)}, f32[1024]{0:T(1024)S(1)}, u32[]{:S(2)}) copy-start(f32[1024]{0:T(1024)S(1)} %fusion.62) | copy-start | bytes 12292
  124.7 985.1 %copy-start.10 = (bf16[1024,3,512]{0,2,1:T(8,128)(2,1)}, bf16[1024,3,512]{0,2,1:T(8,128)(2,1)S(1)}, u32[]{:S(2)}) copy-start(bf16[1024,3,512]{0,2,1:T(8,128)(2,1)S(1)} %convolution_convert_fusion) | copy-start | bytes 9437188
  173.1 278.8 %all-gather.9.cloned.1.call-start = ((), (), s32[]{:S(2)}) async-start(), calls=%async_computation.8 | async-start | bytes 9437184 | tf_op jit(solution)/shard_map/all_gather | solution.py:158
  175.9 588.1 %reduce-scatter.14.cloned.1.call-start = ((), (), s32[]{:S(2)}) async-start(), calls=%async_computation.14 | async-start | bytes 18874368 | tf_op jit(solution)/shard_map/reduce_scatter | solution.py:242
  483.1 414.1 %all-gather.11.cloned.1.call-start = ((), (), s32[]{:S(2)}) async-start(), calls=%async_computation.9 | async-start | bytes 9437184 | tf_op jit(solution)/shard_map/all_gather | solution.py:159
  772.6 309.3 %all-reduce.7.cloned.1.call-start = ((), (), s32[]{:S(2)}) async-start(), calls=%async_computation.10 | async-start | bytes 16777216 | tf_op jit(solution)/shard_map/psum | solution.py:210
  930.6 502.9 %all-reduce.9.cloned.1.call-start = ((), (), s32[]{:S(2)}) async-start(), calls=%async_computation.16 | async-start | bytes 33554432 | tf_op jit(solution)/shard_map/psum | solution.py:187
  1144.3 289.2 %copy-start.27 = (f32[1,2048]{1,0:T(1,128)S(1)}, f32[1,2048]{1,0:T(1,128)}, u32[]{:S(2)}) copy-start(f32[1,2048]{1,0:T(1,128)} %copy-done.26) | copy-start | bytes 24580
  1144.3 289.2 %copy-start.29 = (f32[1024]{0:T(1024)S(1)}, f32[1024]{0:T(1024)}, u32[]{:S(2)}) copy-start(f32[1024]{0:T(1024)} %copy-done.28) | copy-start | bytes 12292
  1144.3 381.7 %reduce-scatter.10.cloned.1.call-start = ((), (), s32[]{:S(2)}) async-start(), calls=%async_computation.12 | async-start | bytes 4718592 | tf_op jit(solution)/shard_map/reduce_scatter | solution.py:240
  1152.0 287.6 %copy-start.33 = (f32[1024]{0:T(1024)S(1)}, f32[1024]{0:T(1024)}, u32[]{:S(2)}) copy-start(f32[1024]{0:T(1024)} %copy-done.32) | copy-start | bytes 12292
  1152.0 287.7 %copy-start.31 = (f32[1024]{0:T(1024)S(1)}, f32[1024]{0:T(1024)}, u32[]{:S(2)}) copy-start(f32[1024]{0:T(1024)} %copy-done.30) | copy-start | bytes 12292
  1152.0 441.1 %reduce-scatter.16.cloned.1.call-start = ((), (), s32[]{:S(2)}) async-start(), calls=%async_computation.15 | async-start | bytes 1179648
  1447.3 356.7 %reduce-scatter.8.cloned.1.call-start = ((), (), s32[]{:S(2)}) async-start(), calls=%async_computation.11 | async-start | bytes 14155776 | tf_op jit(solution)/shard_map/reduce_scatter | solution.py:239
  1460.8 629.2 %reduce-scatter.12.cloned.1.call-start = ((), (), s32[]{:S(2)}) async-start(), calls=%async_computation.13 | async-start | bytes 18874368 | tf_op jit(solution)/shard_map/reduce_scatter | solution.py:241
  1551.9 538.1 %copy-start.14 = (f32[256,2048]{1,0:T(8,128)S(1)}, f32[256,2048]{1,0:T(8,128)}, u32[]{:S(2)}) copy-start(f32[256,2048]{1,0:T(8,128)} %param.38) | copy-start | bytes 6291460
  1594.7 501.9 %copy-start.34 = (f32[4,256]{1,0:T(4,128)}, f32[4,256]{1,0:T(4,128)S(1)}, u32[]{:S(2)}) copy-start(f32[4,256]{1,0:T(4,128)S(1)} %get-tuple-element.81) | copy-start | bytes 12292
  (41 other events, 488.8 us)
Sparse Core Ops, SparseCore 0:
  10.7 102.7 all-gather.4
  116.1 49.2 all-gather.6
  173.3 151.0 all-reduce.4
  326.9 124.9 all-gather.8
  483.2 280.8 reduce-scatter.13
  772.7 124.4 all-gather.10
  930.7 151.0 all-reduce.6
  1144.4 288.9 all-reduce.8
  1437.6 88.4 reduce-scatter.9
  1529.9 63.1 reduce-scatter.15
  1597.2 206.7 reduce-scatter.7
  1808.1 281.8 reduce-scatter.11
where the time goes:
time: 2110 us
  waiting for transfers between devices  1750 us (83%)
  matrix products  171 us (8%)
  other arithmetic  114 us (5%)
  local copies, waits for them, and re-layouts  28.6 us (1%)
  blocking collectives  28.2 us (1%)
    psum x1, waiting for transfers between devices, shards(): lax.psum(jnp.dot(activated_low, shrink_full, preferred_element_type=jnp.f...  281 us
    reduce_scatter x1, waiting for transfers between devices, shards(): lax.psum_scatter(shrink_grad, 'dp', scatter_dimension=1, tiled=True)  281 us
    reduce_scatter x1, waiting for transfers between devices, shards(): lax.psum_scatter(expand_grad, 'dp', scatter_dimension=0, tiled=True)  278 us
    reduce_scatter x1, waiting for transfers between devices, shards(): lax.psum_scatter(attend_grad, 'dp', scatter_dimension=0, tiled=True)  209 us
    psum x1, waiting for transfers between devices, shards(): lax.psum(jnp.dot(mixed_low, combine_full, preferred_element_type=jnp.floa...  148 us
    psum x1, waiting for transfers between devices, shards(): lax.psum(jnp.einsum('nf,df->nd', expanded_grad_low, expand_back, preferre...  134 us
    all_gather x1, waiting for transfers between devices, shards(): lax.all_gather(shrink_low, 'dp', axis=1, tiled=True)  125 us
    all_gather x1, waiting for transfers between devices, shards(): lax.all_gather(expand_low, 'dp', axis=0, tiled=True)  118 us
  transfers between devices with their start and end apart: 12, of which 12 were waited for; matrix products, arithmetic and copies ran while one was open for 7% of the time, Pallas kernels for 0%

commit v1 on v0

--- a/solution.py
+++ b/solution.py
@@ -24,7 +24,9 @@
 
 
 def segment_ids(lengths_row, row_length):
-    bounds = jnp.cumsum(lengths_row)
+    order = jnp.arange(lengths_row.shape[0], dtype=jnp.int32)
+    earlier = order[None, :] <= order[:, None]
+    bounds = jnp.sum(jnp.where(earlier, lengths_row[None, :], 0), axis=1)
     places = jnp.arange(row_length, dtype=jnp.int32)
     return jnp.sum((places[:, None] >= bounds[None, :]).astype(jnp.int32), axis=1)
 
@@ -176,8 +178,8 @@
     mixed_heads, logsum = lax.map(attend_row, (queries_all, keys_all, values_all, segments))
     mixed_low = mixed_heads.reshape(local_tokens, local_width).astype(jnp.bfloat16)
     attended = lax.psum(
-        jnp.dot(mixed_low, combine_full, preferred_element_type=jnp.float32), "tensor"
-    )
+        jnp.dot(mixed_low, combine_full, preferred_element_type=jnp.float32).astype(jnp.bfloat16), "tensor"
+    ).astype(jnp.float32)
     residual = hidden + attended
     normed_two, pull_two = jax.vjp(layer_norm, residual, norm_values[2], norm_values[3])
     normed_two_low = normed_two.astype(jnp.bfloat16)
@@ -185,8 +187,8 @@
     activated, pull_gelu = jax.vjp(jax.nn.gelu, expanded)
     activated_low = activated.astype(jnp.bfloat16)
     branch = lax.psum(
-        jnp.dot(activated_low, shrink_full, preferred_element_type=jnp.float32), "tensor"
-    )
+        jnp.dot(activated_low, shrink_full, preferred_element_type=jnp.float32).astype(jnp.bfloat16), "tensor"
+    ).astype(jnp.float32)
     layer_output = (residual + branch).astype(jnp.bfloat16)
     factor = loss_numerator.astype(jnp.float32) / (4.0 * (1.0 + self_generated.astype(jnp.float32)))
     out_grad = factor[:, None] * out_cotangent.astype(jnp.float32)
@@ -208,9 +210,9 @@
         "nd,nf->df", normed_two_low, expanded_grad_low, preferred_element_type=jnp.float32
     )
     normed_two_grad = lax.psum(
-        jnp.einsum("nf,df->nd", expanded_grad_low, expand_back, preferred_element_type=jnp.float32),
+        jnp.einsum("nf,df->nd", expanded_grad_low, expand_back, preferred_element_type=jnp.float32).astype(jnp.bfloat16),
         "tensor",
-    )
+    ).astype(jnp.float32)
     residual_from_norm, gain_two_grad, shift_two_grad = pull_two(normed_two_grad)
     residual_grad = out_grad + residual_from_norm
     attended_grad_low = residual_grad.astype(jnp.bfloat16)
@@ -229,17 +231,17 @@
         "nd,nke->dke", normed_low, projected_grad, preferred_element_type=jnp.float32
     )
     normed_one_grad = lax.psum(
-        jnp.einsum("nke,dke->nd", projected_grad, attend_back, preferred_element_type=jnp.float32),
+        jnp.einsum("nke,dke->nd", projected_grad, attend_back, preferred_element_type=jnp.float32).astype(jnp.bfloat16),
         "tensor",
-    )
+    ).astype(jnp.float32)
     hidden_from_norm, gain_one_grad, shift_one_grad = pull_one(normed_one_grad)
     input_gradient = residual_grad + hidden_from_norm
     norm_grad = jnp.stack([gain_one_grad, shift_one_grad, gain_two_grad, shift_two_grad])
     attend_sum, combine_sum, expand_sum, shrink_sum, norm_sum = (
-        lax.psum_scatter(attend_grad, "dp", scatter_dimension=0, tiled=True),
-        lax.psum_scatter(combine_grad, "dp", scatter_dimension=1, tiled=True),
-        lax.psum_scatter(expand_grad, "dp", scatter_dimension=0, tiled=True),
-        lax.psum_scatter(shrink_grad, "dp", scatter_dimension=1, tiled=True),
+        lax.psum_scatter(attend_grad.astype(jnp.bfloat16), "dp", scatter_dimension=0, tiled=True),
+        lax.psum_scatter(combine_grad.astype(jnp.bfloat16), "dp", scatter_dimension=1, tiled=True),
+        lax.psum_scatter(expand_grad.astype(jnp.bfloat16), "dp", scatter_dimension=0, tiled=True),
+        lax.psum_scatter(shrink_grad.astype(jnp.bfloat16), "dp", scatter_dimension=1, tiled=True),
         lax.psum_scatter(norm_grad, "dp", scatter_dimension=1, tiled=True),
     )
     kinds = (
@@ -291,6 +293,7 @@
     )
     results = [layer_output, input_gradient]
     for master, moment, square, average, gradient, rate_value, decay_value in kinds:
+        gradient = gradient.astype(jnp.float32)
         master_new, moment_new, square_new = adam_update(
             master, moment, square, gradient, rate_value, decay_value
         )

time: 2110 us -> 1460 us (0.69)
  waiting for transfers between devices: 1750 us -> 1100 us
    reduce_scatter x4, waiting for transfers between devices: 810 us -> 438 us  [the longest x1 148 us: shards(): lax.psum_scatter(shrink_grad.astype(jnp.bfloat16), 'dp', scatter_dimensio...]
    psum x1, waiting for transfers between devices: 281 us -> 146 us  [shards(): lax.psum(jnp.dot(activated_low, shrink_full, preferred_element_type=jnp.f...]
    psum x1, waiting for transfers between devices: 148 us -> 81 us  [shards(): lax.psum(jnp.dot(mixed_low, combine_full, preferred_element_type=jnp.floa...]
    psum x1, waiting for transfers between devices: 134 us -> 67.2 us  [shards(): lax.psum(jnp.einsum('nf,df->nd', expanded_grad_low, expand_back, preferre...]
  transfers between devices with their start and end apart: 12 -> 12, of which waited for: 12 -> 12; matrix products, arithmetic and copies ran while one was open for 7% -> 10% of each run, Pallas kernels for 0% -> 0%
where the time goes in v1:
time: 1460 us
  waiting for transfers between devices  1100 us (75%)
  matrix products  176 us (12%)
  other arithmetic  107 us (7%)
  blocking collectives  28.3 us (2%)
  local copies, waits for them, and re-layouts  25 us (2%)
  between operations  15.2 us (1%)
    reduce_scatter x1, waiting for transfers between devices, shards(): lax.psum_scatter(shrink_grad.astype(jnp.bfloat16), 'dp', scatter_dimensio...  148 us
    psum x1, waiting for transfers between devices, shards(): lax.psum(jnp.dot(activated_low, shrink_full, preferred_element_type=jnp.f...  146 us
    reduce_scatter x1, waiting for transfers between devices, shards(): lax.psum_scatter(expand_grad.astype(jnp.bfloat16), 'dp', scatter_dimensio...  144 us
    all_gather x1, waiting for transfers between devices, shards(): lax.all_gather(shrink_low, 'dp', axis=1, tiled=True)  124 us
    all_gather x1, waiting for transfers between devices, shards(): lax.all_gather(expand_low, 'dp', axis=0, tiled=True)  120 us
    reduce_scatter x1, waiting for transfers between devices, shards(): lax.psum_scatter(attend_grad.astype(jnp.bfloat16), 'dp', scatter_dimensio...  119 us
    psum x1, waiting for transfers between devices, shards(): lax.psum(jnp.dot(mixed_low, combine_full, preferred_element_type=jnp.floa...  81 us
    psum x1, waiting for transfers between devices, shards(): lax.psum(jnp.einsum('nf,df->nd', expanded_grad_low, expand_back, preferre...  67.2 us
  transfers between devices with their start and end apart: 12, of which 12 were waited for; matrix products, arithmetic and copies ran while one was open for 10% of the time, Pallas kernels for 0%

profile of v1, /device:TPU:0, one launch (start us, length us, event | category | flops | bytes accessed | tf_op | source)
XLA Modules:
  0.0 1455.5 jit_solution(4528785793352716169)
XLA Ops:
  12.6 28.3 %all_gather.19 = bf16[4,2048]{1,0:T(4,128)(2,1)S(1)} all-gather(bf16[4,256]{1,0:T(4,128)(2,1)S(1)} %convert_element_type.163), channel_id=1, replica_groups=mesh['dp'=8,'tensor'=4] {'dp'}, dimensions={1}, use_global_device_ids=true | all-gather | bytes 18432 | tf_op jit(solution)/shard_map/all_gather | solution.py:162
  48.3 65.2 %all-gather.5.cloned.1.call-done = bf16[2048,3,512]{0,2,1:T(8,128)(2,1)} async-done(((bf16[256,3,512]{0,2,1:T(8,128)(2,1)}), bf16[2048,3,512]{0,2,1:T(8,128)(2,1)}) %all-gather.5.cloned.1.call-update) | async-done | bytes 6291472 | tf_op jit(solution)/shard_map/all_gather | solution.py:158
  113.5 11.2 convolution_convert_fusion.7
  134.6 13.4 fusion.56
  149.1 16.3 %all-gather.7.cloned.1.call-done = bf16[512,2048]{1,0:T(8,128)(2,1)} async-done(((bf16[512,256]{1,0:T(8,128)(2,1)}), bf16[512,2048]{1,0:T(8,128)(2,1)}) %all-gather.7.cloned.1.call-update) | async-done | bytes 2097168 | tf_op jit(solution)/shard_map/all_gather | solution.py:159
  174.6 81.0 %all-reduce.5.cloned.1.call-done = bf16[1024,2048]{1,0:T(8,128)(2,1)} async-done(((bf16[1024,2048]{1,0:T(8,128)(2,1)}), bf16[1024,2048]{1,0:T(8,128)(2,1)}) %all-reduce.5.cloned.1.call-update) | async-done | bytes 4194320 | tf_op jit(solution)/shard_map/psum | solution.py:180
  263.7 119.8 %all-gather.9.cloned.1.call-done = bf16[2048,2048]{1,0:T(8,128)(2,1)} async-done(((bf16[256,2048]{1,0:T(8,128)(2,1)}), bf16[2048,2048]{1,0:T(8,128)(2,1)}) %all-gather.9.cloned.1.call-update) | async-done | bytes 8388624 | tf_op jit(solution)/shard_map/all_gather | solution.py:160
  383.4 14.0 fusion.71
  400.7 13.2 convolution_convert_fusion
  414.1 147.7 %reduce-scatter.14.cloned.1.call-done = bf16[2048,256]{1,0:T(8,128)(2,1)} async-done(((bf16[2048,2048]{1,0:T(8,128)(2,1)}), bf16[2048,256]{1,0:T(8,128)(2,1)}) %reduce-scatter.14.cloned.1.call-update) | async-done | bytes 1048592 | tf_op jit(solution)/shard_map/reduce_scatter | solution.py:244
  569.8 124.5 %all-gather.11.cloned.1.call-done = bf16[2048,2048]{1,0:T(8,128)(2,1)} async-done(((bf16[2048,256]{1,0:T(8,128)(2,1)}), bf16[2048,2048]{1,0:T(8,128)(2,1)}) %all-gather.11.cloned.1.call-update) | async-done | bytes 8388624 | tf_op jit(solution)/shard_map/all_gather | solution.py:161
  694.3 18.4 %fusion.17 = bf16[1024,2048]{1,0:T(8,128)(2,1)S(1)} fusion(f32[1024,2048]{1,0:T(8,128)} %copy-done.52, bf16[2048,2048]{1,0:T(8,128)(2,1)} %all-gather.11.cloned.1.call-done, bf16[1024,2048]{1,0:T(8,128)(2,1)} %param.26, f32[1024]{0:T(1024)S(1)} %multiply_divide_fusion), kind=kOutput, calls=%fused_computation.30 | convolution fusion | flops 8638169088 | bytes 25169920 | tf_op jit(solution)/shard_map/nd,fd->nf/dot_general | solution.py:205
  714.7 12.6 convolution_convert_fusion.3
  727.4 16.6 %convolution_convert_fusion.4 = bf16[1024,2048]{1,0:T(8,128)(2,1)} fusion(bf16[2048,2048]{1,0:T(8,128)(2,1)} %all-gather.11.cloned.1.call-done, f32[1024,2048]{1,0:T(8,128)} %copy-done.52), kind=kOutput, calls=%fused_computation.75 | convolution fusion | flops 8610906112 | bytes 20971520 | tf_op jit(solution)/shard_map/dot_general | solution.py:190
  744.0 67.2 %all-reduce.7.cloned.1.call-done = bf16[1024,2048]{1,0:T(8,128)(2,1)} async-done(((bf16[1024,2048]{1,0:T(8,128)(2,1)}), bf16[1024,2048]{1,0:T(8,128)(2,1)}) %all-reduce.7.cloned.1.call-update) | async-done | bytes 4194320 | tf_op jit(solution)/shard_map/psum | solution.py:212
  863.1 11.2 bitcast_convert_fusion
  881.4 146.4 %all-reduce.9.cloned.1.call-done = (bf16[1024,2048]{1,0:T(8,128)(2,1)}, bf16[1024,2048]{1,0:T(8,128)(2,1)}) async-done(((bf16[1024,2048]{1,0:T(8,128)(2,1)}, bf16[1024,2048]{1,0:T(8,128)(2,1)}), (bf16[1024,2048]{1,0:T(8,128)(2,1)}, bf16[1024,2048]{1,0:T(8,128)(2,1)})) %all-reduce.9.cloned.1.call-update) | async-done | bytes 8388624 | tf_op jit(solution)/shard_map/psum | solution.py:189
  1039.7 12.4 convolution_convert_fusion.2
  1052.8 15.6 %convolution_convert_fusion.1 = bf16[2048,2048]{1,0:T(8,128)(2,1)} fusion(bf16[1024,2048]{1,0:T(8,128)(2,1)} %copy-done.53, bf16[1024,2048]{1,0:T(8,128)(2,1)} %all-reduce.5.cloned.1.call-done, bf16[1024,2048]{1,0:T(8,128)(2,1)} %param.25, f32[2048]{0:T(1024)S(1)} %bitcast.142, f32[2048]{0:T(1024)S(1)} %bitcast.133, f32[1024]{0:T(1024)S(1)} %fusion.68, ...), kind=kOutput, calls=%fused_computation.57 | convolution fusion | flops 8610906112 | bytes 20996096 | tf_op jit(solution)/shard_map/nd,nf->df/dot_general | solution.py:209
  1073.2 27.7 %reduce-scatter.10.cloned.1.call-done = bf16[512,256]{1,0:T(8,128)(2,1)} async-done(((bf16[512,2048]{1,0:T(8,128)(2,1)}), bf16[512,256]{1,0:T(8,128)(2,1)}) %reduce-scatter.10.cloned.1.call-update) | async-done | bytes 262160 | tf_op jit(solution)/shard_map/reduce_scatter | solution.py:242
  1105.8 16.4 %add_add_fusion.2 = (f32[1024,2048]{1,0:T(8,128)}, bf16[1024,2048]{1,0:T(8,128)(2,1)}) fusion(bf16[1024,2048]{1,0:T(8,128)(2,1)S(1)} %copy-done.4, bf16[1024,2048]{1,0:T(8,128)(2,1)} %get-tuple-element.79, f32[1024,2048]{1,0:T(8,128)} %copy-done.9, bf16[1024,2048]{1,0:T(8,128)(2,1)} %param.26, f32[1024]{0:T(1024)S(1)} %negate_multiply_fusion, ...), kind=kLoop, calls=%fused_computation.36 | loop fusion | flops 39845888 | bytes 41975808 | tf_op jit(solution)/shard_map/add | solution.py:238
  1122.2 45.5 %reduce-scatter.16.cloned.1.call-done = f32[256,4]{1,0:T(8,128)} async-done(((f32[2048,4]{1,0:T(8,128)}), f32[256,4]{1,0:T(8,128)}) %reduce-scatter.16.cloned.1.call-update) | async-done | bytes 4112
  1169.9 118.8 %reduce-scatter.8.cloned.1.call-done = bf16[256,3,512]{2,0,1:T(8,128)(2,1)} async-done(((bf16[2048,3,512]{2,0,1:T(8,128)(2,1)}), bf16[256,3,512]{2,0,1:T(8,128)(2,1)}) %reduce-scatter.8.cloned.1.call-update) | async-done | bytes 786448 | tf_op jit(solution)/shard_map/reduce_scatter | solution.py:241
  1296.7 143.6 %reduce-scatter.12.cloned.1.call-done = bf16[256,2048]{1,0:T(8,128)(2,1)} async-done(((bf16[2048,2048]{1,0:T(8,128)(2,1)}), bf16[256,2048]{1,0:T(8,128)(2,1)}) %reduce-scatter.12.cloned.1.call-update) | async-done | bytes 1048592 | tf_op jit(solution)/shard_map/reduce_scatter | solution.py:243
  (209 shorter events, 153.6 us)
Async XLA Ops:
  7.2 106.3 %all-gather.5.cloned.1.call-start = ((), (), s32[]{:S(2)}) async-start(), calls=%async_computation.5 | async-start | bytes 7077888 | tf_op jit(solution)/shard_map/all_gather | solution.py:158
  9.8 155.5 %all-gather.7.cloned.1.call-start = ((), (), s32[]{:S(2)}) async-start(), calls=%async_computation.6 | async-start | bytes 2359296 | tf_op jit(solution)/shard_map/all_gather | solution.py:159
  11.7 243.9 %all-reduce.5.cloned.1.call-start = ((), (), s32[]{:S(2)}) async-start(), calls=%async_computation.7 | async-start | bytes 8388608 | tf_op jit(solution)/shard_map/psum | solution.py:180
  40.9 83.7 %copy-start.31 = (f32[1,2048]{1,0:T(1,128)}, f32[1,2048]{1,0:T(1,128)S(1)}, u32[]{:S(2)}) copy-start(f32[1,2048]{1,0:T(1,128)S(1)} %get-tuple-element.109) | copy-start | bytes 24580
  40.9 83.7 %copy-start.43 = (f32[1,2048]{1,0:T(1,128)}, f32[1,2048]{1,0:T(1,128)S(1)}, u32[]{:S(2)}) copy-start(f32[1,2048]{1,0:T(1,128)S(1)} %get-tuple-element.110) | copy-start | bytes 24580
  41.0 342.5 %copy-start.41 = (f32[1,2048]{1,0:T(1,128)}, f32[1,2048]{1,0:T(1,128)S(1)}, u32[]{:S(2)}) copy-start(f32[1,2048]{1,0:T(1,128)S(1)} %get-tuple-element.108) | copy-start | bytes 24580
  43.8 80.8 %copy-start.33 = (f32[1024]{0:T(1024)}, f32[1024]{0:T(1024)S(1)}, u32[]{:S(2)}) copy-start(f32[1024]{0:T(1024)S(1)} %broadcast_multiply_fusion.1) | copy-start | bytes 12292
  45.1 79.6 %copy-start.35 = (f32[1024]{0:T(1024)}, f32[1024]{0:T(1024)S(1)}, u32[]{:S(2)}) copy-start(f32[1024]{0:T(1024)S(1)} %fusion.67) | copy-start | bytes 12292
  124.7 714.3 %copy-start.14 = (bf16[1024,3,512]{0,2,1:T(8,128)(2,1)}, bf16[1024,3,512]{0,2,1:T(8,128)(2,1)S(1)}, u32[]{:S(2)}) copy-start(bf16[1024,3,512]{0,2,1:T(8,128)(2,1)S(1)} %convolution_convert_fusion.7) | copy-start | bytes 9437188
  171.7 211.7 %all-gather.9.cloned.1.call-start = ((), (), s32[]{:S(2)}) async-start(), calls=%async_computation.8 | async-start | bytes 9437184 | tf_op jit(solution)/shard_map/all_gather | solution.py:160
  174.5 387.2 %reduce-scatter.14.cloned.1.call-start = ((), (), s32[]{:S(2)}) async-start(), calls=%async_computation.14 | async-start | bytes 9437184 | tf_op jit(solution)/shard_map/reduce_scatter | solution.py:244
  414.0 280.3 %all-gather.11.cloned.1.call-start = ((), (), s32[]{:S(2)}) async-start(), calls=%async_computation.9 | async-start | bytes 9437184 | tf_op jit(solution)/shard_map/all_gather | solution.py:161
  569.8 241.4 %all-reduce.7.cloned.1.call-start = ((), (), s32[]{:S(2)}) async-start(), calls=%async_computation.10 | async-start | bytes 8388608 | tf_op jit(solution)/shard_map/psum | solution.py:212
  727.3 300.5 %all-reduce.9.cloned.1.call-start = ((), (), s32[]{:S(2)}) async-start(), calls=%async_computation.16 | async-start | bytes 16777216 | tf_op jit(solution)/shard_map/psum | solution.py:189
  874.3 153.5 %copy-start.32 = (f32[1,2048]{1,0:T(1,128)S(1)}, f32[1,2048]{1,0:T(1,128)}, u32[]{:S(2)}) copy-start(f32[1,2048]{1,0:T(1,128)} %copy-done.31) | copy-start | bytes 24580
  874.3 153.5 %copy-start.34 = (f32[1024]{0:T(1024)S(1)}, f32[1024]{0:T(1024)}, u32[]{:S(2)}) copy-start(f32[1024]{0:T(1024)} %copy-done.33) | copy-start | bytes 12292
  874.4 226.6 %reduce-scatter.10.cloned.1.call-start = ((), (), s32[]{:S(2)}) async-start(), calls=%async_computation.12 | async-start | bytes 2359296 | tf_op jit(solution)/shard_map/reduce_scatter | solution.py:242
  881.4 152.0 %copy-start.38 = (f32[1024]{0:T(1024)S(1)}, f32[1024]{0:T(1024)}, u32[]{:S(2)}) copy-start(f32[1024]{0:T(1024)} %copy-done.37) | copy-start | bytes 12292
  881.4 152.0 %copy-start.36 = (f32[1024]{0:T(1024)S(1)}, f32[1024]{0:T(1024)}, u32[]{:S(2)}) copy-start(f32[1024]{0:T(1024)} %copy-done.35) | copy-start | bytes 12292
  881.4 286.3 %reduce-scatter.16.cloned.1.call-start = ((), (), s32[]{:S(2)}) async-start(), calls=%async_computation.15 | async-start | bytes 1179648
  1039.6 249.0 %reduce-scatter.8.cloned.1.call-start = ((), (), s32[]{:S(2)}) async-start(), calls=%async_computation.11 | async-start | bytes 7077888 | tf_op jit(solution)/shard_map/reduce_scatter | solution.py:241
  1052.1 388.2 %reduce-scatter.12.cloned.1.call-start = ((), (), s32[]{:S(2)}) async-start(), calls=%async_computation.13 | async-start | bytes 9437184 | tf_op jit(solution)/shard_map/reduce_scatter | solution.py:243
  1169.3 127.5 %copy-start.39 = (f32[4,256]{1,0:T(4,128)}, f32[4,256]{1,0:T(4,128)S(1)}, u32[]{:S(2)}) copy-start(f32[4,256]{1,0:T(4,128)S(1)} %get-tuple-element.81) | copy-start | bytes 12292
  1169.9 270.5 %copy-start.19 = (f32[256,2048]{1,0:T(8,128)S(1)}, f32[256,2048]{1,0:T(8,128)}, u32[]{:S(2)}) copy-start(f32[256,2048]{1,0:T(8,128)} %param.38) | copy-start | bytes 6291460
  (46 other events, 555.9 us)
Sparse Core Ops, SparseCore 0:
  10.7 102.7 all-gather.4
  116.1 49.2 all-gather.6
  171.9 83.6 all-reduce.4
  258.3 125.0 all-gather.8
  414.1 147.5 reduce-scatter.13
  569.9 124.3 all-gather.10
  727.5 83.6 all-reduce.6
  874.4 153.3 all-reduce.8
  1032.4 68.5 reduce-scatter.9
  1105.1 62.4 reduce-scatter.15
  1171.3 117.3 reduce-scatter.7
  1292.1 148.1 reduce-scatter.11

commit v2 on v1

--- a/solution.py
+++ b/solution.py
@@ -1,3 +1,6 @@
+import functools
+import math
+
 import jax
 import jax.numpy as jnp
 from jax import lax
@@ -15,12 +18,32 @@
 matrix_rate = 0.02
 norm_rate = 0.2
 norm_epsilon = 1e-05
-
-
-def layer_norm(values, gain_row, shift_row):
+low_type = jnp.bfloat16
+wide = jnp.float32
+
+
+def norm_parts(values):
     center = values - jnp.mean(values, axis=-1, keepdims=True)
     spread = jnp.mean(center * center, axis=-1, keepdims=True)
-    return center * lax.rsqrt(spread + norm_epsilon) * gain_row + shift_row
+    inverse = lax.rsqrt(spread + norm_epsilon)
+    return center * inverse, inverse
+
+
+def norm_back(grad, scaled, inverse, gain_row):
+    inner = grad * gain_row
+    mean_inner = jnp.mean(inner, axis=-1, keepdims=True)
+    mean_scaled = jnp.mean(inner * scaled, axis=-1, keepdims=True)
+    result = inverse * (inner - mean_inner - scaled * mean_scaled)
+    return result, jnp.sum(grad * scaled, axis=0), jnp.sum(grad, axis=0)
+
+
+def gelu_parts(v):
+    scale = math.sqrt(2.0 / math.pi)
+    bend = jnp.tanh(scale * (v + 0.044715 * (v * v * v)))
+    slope = 0.5 * (1.0 + bend) + 0.5 * v * (1.0 - bend * bend) * scale * (
+        1.0 + 3.0 * 0.044715 * (v * v)
+    )
+    return 0.5 * v * (1.0 + bend), slope
 
 
 def segment_ids(lengths_row, row_length):
@@ -109,6 +132,148 @@
     return stacked.astype(jnp.bfloat16)
 
 
+def after(value, *earlier):
+    return lax.optimization_barrier((value,) + earlier)[0]
+
+
+class Links:
+    def __init__(self, mesh):
+        self.count = mesh.shape["dp"]
+        self.outer = 4 if self.count % 4 == 0 else 1
+        self.inner = self.count // self.outer
+        self.group = mesh.shape["tensor"]
+        self.cores = 2 if self.group % 2 == 0 else 1
+        self.chips = self.group // self.cores
+
+    def place(self):
+        index = lax.axis_index("dp")
+        self.out_at, self.in_at = index // self.inner, index % self.inner
+        index = lax.axis_index("tensor")
+        self.chip_at, self.core_at = index // self.cores, index % self.cores
+
+    def shift(self, value, over_outer, over_inner):
+        pairs = []
+        for a in range(self.outer):
+            for b in range(self.inner):
+                to = (a + over_outer) % self.outer * self.inner + (b + over_inner) % self.inner
+                pairs.append((a * self.inner + b, to))
+        return lax.ppermute(value, "dp", pairs)
+
+    def turn(self, value, over_chips, over_cores):
+        pairs = []
+        for a in range(self.chips):
+            for b in range(self.cores):
+                to = (a + over_chips) % self.chips * self.cores + (b + over_cores) % self.cores
+                pairs.append((a * self.cores + b, to))
+        return lax.ppermute(value, "tensor", pairs)
+
+    def outer_order(self):
+        return sorted(range(1, self.outer), key=lambda k: min(k, self.outer - k))
+
+    def gather(self, shard, gate):
+        rows = shard.shape[0]
+        full = jnp.zeros((rows * self.count,) + shard.shape[1:], shard.dtype)
+        arrived = {0: shard}
+        if gate:
+            shard = after(shard, *gate)
+        for k in self.outer_order():
+            arrived[k] = self.shift(shard, k, 0)
+        for k, piece in arrived.items():
+            for j in range(self.inner):
+                part = self.shift(piece, 0, j) if j else piece
+                owner = (self.out_at - k) % self.outer * self.inner + (self.in_at - j) % self.inner
+                full = lax.dynamic_update_slice_in_dim(full, part, owner * rows, 0)
+        return full, [arrived[k] for k in self.outer_order()]
+
+    def reduce(self, partial):
+        rows = partial.shape[0] // self.count
+
+        def block(k, j):
+            owner = (self.out_at + k) % self.outer * self.inner + (self.in_at + j) % self.inner
+            return lax.dynamic_slice_in_dim(partial, owner * rows, rows, 0)
+
+        total = None
+        for k in self.outer_order() + [0]:
+            sums = block(k, 0).astype(wide)
+            for j in range(1, self.inner):
+                sums = sums + self.shift(block(k, j), 0, j).astype(wide)
+            if k:
+                sums = self.shift(sums.astype(low_type), k, 0).astype(wide)
+            total = sums if total is None else total + sums
+        return total
+
+    def gather_small(self, shard):
+        columns = shard.shape[1]
+        full = jnp.zeros((shard.shape[0], self.count, columns), shard.dtype)
+        for k in range(self.outer):
+            for j in range(self.inner):
+                part = self.shift(shard, k, j) if k or j else shard
+                owner = (self.out_at - k) % self.outer * self.inner + (self.in_at - j) % self.inner
+                full = lax.dynamic_update_slice_in_dim(full, part[:, None], owner, 1)
+        return full.reshape(shard.shape[0], -1)
+
+    def reduce_small(self, partial):
+        split = partial.reshape(partial.shape[0], self.count, -1)
+        total = None
+        for k in range(self.outer):
+            for j in range(self.inner):
+                owner = (self.out_at + k) % self.outer * self.inner + (self.in_at + j) % self.inner
+                part = lax.dynamic_index_in_dim(split, owner, 1, keepdims=False)
+                part = self.shift(part, k, j) if k or j else part
+                total = part if total is None else total + part
+        for parts, step in ((self.cores, (0, 1)), (self.chips, (1, 0))):
+            moving = total
+            for _ in range(parts - 1):
+                moving = self.turn(moving, *step)
+                total = total + moving
+        return total
+
+    def own_rows(self, value):
+        rows = value.shape[0] // self.group
+        return lax.dynamic_slice_in_dim(
+            value, (self.core_at * self.chips + self.chip_at) * rows, rows, 0
+        )
+
+    def reduce_tensor(self, partial):
+        rows = partial.shape[0] // self.cores
+
+        def half(j):
+            return lax.dynamic_slice_in_dim(
+                partial, (self.core_at + j) % self.cores * rows, rows, 0
+            )
+
+        sums = half(0).astype(wide)
+        for j in range(1, self.cores):
+            sums = sums + self.turn(half(j), 0, j).astype(wide)
+        rows = rows // self.chips
+
+        def quarter(values, j):
+            return lax.dynamic_slice_in_dim(
+                values, (self.chip_at + j) % self.chips * rows, rows, 0
+            )
+
+        total = quarter(sums, 0)
+        low_sums = sums.astype(low_type)
+        for j in range(1, self.chips):
+            total = total + self.turn(quarter(low_sums, j), j, 0).astype(wide)
+        return total
+
+    def gather_tensor(self, own):
+        for parts, at, step in (
+            (self.chips, self.chip_at, (1, 0)),
+            (self.cores, self.core_at, (0, 1)),
+        ):
+            rows = own.shape[0]
+            full = jnp.zeros((parts * rows,) + own.shape[1:], own.dtype)
+            full = lax.dynamic_update_slice_in_dim(full, own, at * rows, 0)
+            moving = own
+            for j in range(1, parts):
+                moving = self.turn(moving, *step)
+                full = lax.dynamic_update_slice_in_dim(full, moving, (at - j) % parts * rows, 0)
+            own = full
+        return own
+
+
 def adam_update(master, moment, square, gradient, rate_value, decay_value):
     moment_new = beta_first * moment + (1.0 - beta_first) * gradient
     square_new = beta_second * square + (1.0 - beta_second) * gradient * gradient
@@ -119,7 +284,12 @@
     return (master_new, moment_new, square_new)
 
 
+def dot_low(spec, left, right):
+    return jnp.einsum(spec, left, right, preferred_element_type=wide).astype(low_type)
+
+
 def shards(
+    links,
     hidden_in,
     out_cotangent,
     episode_lengths,
@@ -146,103 +316,90 @@
     layernorm_second,
     layernorm_average,
 ):
-    local_tokens = hidden_in.shape[0]
+    links.place()
+    local_tokens, width = hidden_in.shape
     row_count = episode_lengths.shape[0]
     row_length = local_tokens // row_count
-    attend_low = attend_weights.astype(jnp.bfloat16)
-    combine_low = combine_weights.astype(jnp.bfloat16)
-    expand_low = expand_weights.astype(jnp.bfloat16)
-    shrink_low = shrink_weights.astype(jnp.bfloat16)
-    norm_low = layernorm_params.astype(jnp.bfloat16)
-    attend_full, combine_full, expand_full, shrink_full, norm_full = (
-        lax.all_gather(attend_low, "dp", axis=0, tiled=True),
-        lax.all_gather(combine_low, "dp", axis=1, tiled=True),
-        lax.all_gather(expand_low, "dp", axis=0, tiled=True),
-        lax.all_gather(shrink_low, "dp", axis=1, tiled=True),
-        lax.all_gather(norm_low, "dp", axis=1, tiled=True),
-    )
-    norm_values = norm_full.astype(jnp.float32)
-    hidden = hidden_in.astype(jnp.float32)
-    normed_one, pull_one = jax.vjp(layer_norm, hidden, norm_values[0], norm_values[1])
-    normed_low = normed_one.astype(jnp.bfloat16)
-    projected = jnp.einsum(
-        "nd,dke->nke", normed_low, attend_full, preferred_element_type=jnp.float32
-    ).astype(jnp.bfloat16)
-    local_width = projected.shape[2]
+    shard_rows, kinds_count, local_width = attend_weights.shape
     head_count = local_width // HEAD_DIM
-    shaped = projected.reshape(row_count, row_length, 3, head_count, HEAD_DIM)
-    segments = jax.vmap(lambda lengths_row: segment_ids(lengths_row, row_length))(episode_lengths)
-    queries_all = shaped[:, :, 0]
-    keys_all = shaped[:, :, 1]
-    values_all = shaped[:, :, 2]
-    mixed_heads, logsum = lax.map(attend_row, (queries_all, keys_all, values_all, segments))
-    mixed_low = mixed_heads.reshape(local_tokens, local_width).astype(jnp.bfloat16)
-    attended = lax.psum(
-        jnp.dot(mixed_low, combine_full, preferred_element_type=jnp.float32).astype(jnp.bfloat16), "tensor"
-    ).astype(jnp.float32)
-    residual = hidden + attended
-    normed_two, pull_two = jax.vjp(layer_norm, residual, norm_values[2], norm_values[3])
-    normed_two_low = normed_two.astype(jnp.bfloat16)
-    expanded = jnp.dot(normed_two_low, expand_full, preferred_element_type=jnp.float32)
-    activated, pull_gelu = jax.vjp(jax.nn.gelu, expanded)
-    activated_low = activated.astype(jnp.bfloat16)
-    branch = lax.psum(
-        jnp.dot(activated_low, shrink_full, preferred_element_type=jnp.float32).astype(jnp.bfloat16), "tensor"
-    ).astype(jnp.float32)
-    layer_output = (residual + branch).astype(jnp.bfloat16)
-    factor = loss_numerator.astype(jnp.float32) / (4.0 * (1.0 + self_generated.astype(jnp.float32)))
-    out_grad = factor[:, None] * out_cotangent.astype(jnp.float32)
-    attend_back, combine_back, expand_back, shrink_back = (
-        lax.all_gather(attend_low, "dp", axis=0, tiled=True),
-        lax.all_gather(combine_low, "dp", axis=1, tiled=True),
-        lax.all_gather(expand_low, "dp", axis=0, tiled=True),
-        lax.all_gather(shrink_low, "dp", axis=1, tiled=True),
-    )
-    branch_grad_low = out_grad.astype(jnp.bfloat16)
-    shrink_grad = jnp.einsum(
-        "nf,nd->fd", activated_low, branch_grad_low, preferred_element_type=jnp.float32
-    )
+
+    norm_values = links.gather_small(layernorm_params.astype(low_type)).astype(wide)
+    attend_low = attend_weights.astype(low_type).reshape(shard_rows, kinds_count * local_width)
+    combine_low = combine_weights.astype(low_type).T
+    expand_low = expand_weights.astype(low_type)
+    shrink_low = shrink_weights.astype(low_type).T
+    attend_full, gate = links.gather(attend_low, ())
+    combine_full, gate_two = links.gather(combine_low, gate[-1:])
+    expand_full, gate_three = links.gather(expand_low, gate_two[:1])
+    shrink_full, _ = links.gather(shrink_low, gate_three[-1:])
+
+    hidden = hidden_in.astype(wide)
+    scaled_one, _ = norm_parts(hidden)
+    normed_low = (scaled_one * norm_values[0] + norm_values[1]).astype(low_type)
+    projected = dot_low("nd,de->ne", normed_low, attend_full)
+    shaped = projected.reshape(row_count, row_length, kinds_count, head_count, HEAD_DIM)
+    rows = [
+        (shaped[r, :, 0], shaped[r, :, 1], shaped[r, :, 2], segment_ids(episode_lengths[r], row_length))
+        for r in range(row_count)
+    ]
+    forward = [attend_row(row) for row in rows]
+    mixed_low = jnp.concatenate(
+        [mixed.reshape(row_length, local_width).astype(low_type) for mixed, _ in forward], axis=0
+    )
+    attended = links.reduce_tensor(dot_low("ne,de->nd", mixed_low, combine_full))
+    hidden_own = links.own_rows(hidden_in).astype(wide)
+    residual = hidden_own + attended
+    scaled_two, inverse_two = norm_parts(residual)
+    normed_two_low = links.gather_tensor(
+        (scaled_two * norm_values[2] + norm_values[3]).astype(low_type)
+    )
+    expanded = jnp.einsum("nd,df->nf", normed_two_low, expand_full, preferred_element_type=wide)
+    activated, slope = gelu_parts(expanded)
+    activated_low = activated.astype(low_type)
+
+    factor = loss_numerator.astype(wide) / (4.0 * (1.0 + self_generated.astype(wide)))
+    branch_grad_low = (factor[:, None] * out_cotangent.astype(wide)).astype(low_type)
+    out_grad_own = links.own_rows(factor)[:, None] * links.own_rows(out_cotangent).astype(wide)
+    shrink_grad = dot_low("nd,nf->df", branch_grad_low, activated_low)
+    shrink_sum = links.reduce(shrink_grad).T
+
     activated_grad = jnp.einsum(
-        "nd,fd->nf", branch_grad_low, shrink_back, preferred_element_type=jnp.float32
-    )
-    expanded_grad_low = pull_gelu(activated_grad)[0].astype(jnp.bfloat16)
-    expand_grad = jnp.einsum(
-        "nd,nf->df", normed_two_low, expanded_grad_low, preferred_element_type=jnp.float32
-    )
-    normed_two_grad = lax.psum(
-        jnp.einsum("nf,df->nd", expanded_grad_low, expand_back, preferred_element_type=jnp.float32).astype(jnp.bfloat16),
-        "tensor",
-    ).astype(jnp.float32)
-    residual_from_norm, gain_two_grad, shift_two_grad = pull_two(normed_two_grad)
-    residual_grad = out_grad + residual_from_norm
-    attended_grad_low = residual_grad.astype(jnp.bfloat16)
-    combine_grad = jnp.einsum(
-        "ne,nd->ed", mixed_low, attended_grad_low, preferred_element_type=jnp.float32
-    )
-    mixed_grad = jnp.einsum(
-        "nd,ed->ne", attended_grad_low, combine_back, preferred_element_type=jnp.float32
-    ).astype(jnp.bfloat16)
+        "nd,df->nf", branch_grad_low, shrink_full, preferred_element_type=wide
+    )
+    expanded_grad_low = (activated_grad * slope).astype(low_type)
+    normed_two_grad = links.reduce_tensor(dot_low("nf,df->nd", expanded_grad_low, expand_full))
+    expand_grad = dot_low("nd,nf->df", normed_two_low, expanded_grad_low)
+    expand_sum = links.reduce(expand_grad)
+    residual_from_norm, gain_two_grad, shift_two_grad = norm_back(
+        normed_two_grad, scaled_two, inverse_two, norm_values[2]
+    )
+    residual_grad = out_grad_own + residual_from_norm
+    attended_grad_low = links.gather_tensor(residual_grad.astype(low_type))
+    mixed_grad = dot_low("nd,de->ne", attended_grad_low, combine_full)
+    combine_grad = dot_low("nd,ne->de", attended_grad_low, mixed_low)
+    combine_sum = links.reduce(combine_grad).T
+    branch = links.reduce_tensor(dot_low("nf,df->nd", activated_low, shrink_full))
+    layer_output = links.gather_tensor((residual + branch).astype(low_type))
     mixed_grad_rows = mixed_grad.reshape(row_count, row_length, head_count, HEAD_DIM)
-    projected_grad = lax.map(
-        attend_row_back, (queries_all, keys_all, values_all, segments, logsum, mixed_grad_rows)
-    )
-    projected_grad = projected_grad.reshape(local_tokens, 3, local_width)
-    attend_grad = jnp.einsum(
-        "nd,nke->dke", normed_low, projected_grad, preferred_element_type=jnp.float32
-    )
-    normed_one_grad = lax.psum(
-        jnp.einsum("nke,dke->nd", projected_grad, attend_back, preferred_element_type=jnp.float32).astype(jnp.bfloat16),
-        "tensor",
-    ).astype(jnp.float32)
-    hidden_from_norm, gain_one_grad, shift_one_grad = pull_one(normed_one_grad)
-    input_gradient = residual_grad + hidden_from_norm
-    norm_grad = jnp.stack([gain_one_grad, shift_one_grad, gain_two_grad, shift_two_grad])
-    attend_sum, combine_sum, expand_sum, shrink_sum, norm_sum = (
-        lax.psum_scatter(attend_grad.astype(jnp.bfloat16), "dp", scatter_dimension=0, tiled=True),
-        lax.psum_scatter(combine_grad.astype(jnp.bfloat16), "dp", scatter_dimension=1, tiled=True),
-        lax.psum_scatter(expand_grad.astype(jnp.bfloat16), "dp", scatter_dimension=0, tiled=True),
-        lax.psum_scatter(shrink_grad.astype(jnp.bfloat16), "dp", scatter_dimension=1, tiled=True),
-        lax.psum_scatter(norm_grad, "dp", scatter_dimension=1, tiled=True),
+    projected_grad = jnp.concatenate(
+        [
+            attend_row_back(row + (kept[1], mixed_grad_rows[r]))
+            for r, (row, kept) in enumerate(zip(rows, forward))
+        ],
+        axis=0,
+    ).reshape(local_tokens, kinds_count * local_width)
+    attend_grad = dot_low("nd,ne->de", normed_low, projected_grad)
+    attend_sum = links.reduce(attend_grad).reshape(attend_weights.shape)
+    normed_one_grad = links.reduce_tensor(dot_low("ne,de->nd", projected_grad, attend_full))
+    scaled_own, inverse_own = norm_parts(hidden_own)
+    hidden_from_norm, gain_one_grad, shift_one_grad = norm_back(
+        normed_one_grad, scaled_own, inverse_own, norm_values[0]
+    )
+    input_gradient = links.gather_tensor((residual_grad + hidden_from_norm).astype(low_type)).astype(
+        wide
+    )
+    norm_sum = links.reduce_small(
+        jnp.stack([gain_one_grad, shift_one_grad, gain_two_grad, shift_two_grad])
     )
     kinds = (
         (
@@ -293,7 +450,6 @@
     )
     results = [layer_output, input_gradient]
     for master, moment, square, average, gradient, rate_value, decay_value in kinds:
-        gradient = gradient.astype(jnp.float32)
         master_new, moment_new, square_new = adam_update(
             master, moment, square, gradient, rate_value, decay_value
         )
@@ -333,7 +489,7 @@
         P(None, "dp"),
     )
     return jax.shard_map(
-        shards,
+        functools.partial(shards, Links(mesh)),
         mesh=mesh,
         in_specs=placed,
         out_specs=(

time: 1460 us -> 1160 us (0.79)
  waiting for transfers between devices: 1100 us -> 468 us
  starting transfers between devices: 0.5 us -> 265 us
  local copies, waits for them, and re-layouts: 25 us -> 174 us
  blocking collectives: 28.3 us -> 0 us
  matrix products: 176 us -> 150 us
    ppermute x0 -> x88, waiting for transfers between devices: none -> 468 us  [the longest x70 433 us: shift(): return lax.ppermute(value, 'dp', pairs)]
    reduce_scatter x4 -> x0, waiting for transfers between devices: 438 us -> none  [the longest x1 148 us: shards(): lax.psum_scatter(shrink_grad.astype(jnp.bfloat16), 'dp', scatter_dimensio...]
    all_gather x4 -> x0, waiting for transfers between devices: 326 us -> none  [the longest x1 124 us: shards(): lax.all_gather(shrink_low, 'dp', axis=1, tiled=True)]
    psum x3 -> x0, waiting for transfers between devices: 295 us -> none  [the longest x1 146 us: shards(): lax.psum(jnp.dot(activated_low, shrink_full, preferred_element_type=jnp.f...]
    ppermute x0 -> x88, starting transfers between devices: none -> 265 us  [the longest x70 254 us: shift(): return lax.ppermute(value, 'dp', pairs)]
    dynamic_update_slice x0 -> x49, local copies, waits for them, and re-layouts: none -> 59.9 us  [the longest x30 39.4 us: gather(): full = lax.dynamic_update_slice_in_dim(full, part, owner * rows, 0)]
    unnamed x13 -> x0, waiting for transfers between devices: 45.7 us -> none
    unnamed x119 -> x212, local copies, waits for them, and re-layouts: 21.7 us -> 58.1 us
  transfers between devices with their start and end apart: 12 -> 88, of which waited for: 12 -> 37; matrix products, arithmetic and copies ran while one was open for 10% -> 25% of each run, Pallas kernels for 0% -> 0%
where the time goes in v2:
time: 1160 us; the launch traced here: 1150 us
  waiting for transfers between devices  468 us (40%)
  starting transfers between devices  265 us (23%)
  local copies, waits for them, and re-layouts  174 us (15%)
  matrix products  150 us (13%)
  other arithmetic  93.8 us (8%)
    ppermute x70, waiting for transfers between devices, shift(): return lax.ppermute(value, 'dp', pairs)  433 us
    ppermute x70, starting transfers between devices, shift(): return lax.ppermute(value, 'dp', pairs)  254 us
    dot_general x10, matrix products, dot_low(): jnp.einsum(spec, left, right, preferred_element_type=wide).astype(low_type)  88.7 us
    unnamed x212, local copies, waits for them, and re-layouts  58.1 us
    dynamic_update_slice x30, local copies, waits for them, and re-layouts, gather(): full = lax.dynamic_update_slice_in_dim(full, part, owner * rows, 0)  39.4 us
    ppermute x18, waiting for transfers between devices, turn(): return lax.ppermute(value, 'tensor', pairs)  34.7 us
  transfers between devices with their start and end apart: 88, of which 37 were waited for; matrix products, arithmetic and copies ran while one was open for 25% of the time, Pallas kernels for 0%

profile of v2, /device:TPU:0, one launch (start us, length us, event | category | flops | bytes accessed | tf_op | source)
XLA Modules:
  0.0 1152.9 jit_solution(176568567804170010)
XLA Ops:
  24.9 35.2 %collective-permute-done.1 = bf16[4,256]{1,0:T(4,128)(2,1)S(1)} collective-permute-done((bf16[4,256]{1,0:T(4,128)(2,1)S(1)}, bf16[4,256]{1,0:T(4,128)(2,1)S(1)}, u32[]{:S(2)}, u32[]{:S(2)}) %collective-permute-start.1) | collective-permute-done | bytes 2080 | tf_op jit(solution)/shard_map/ppermute | solution.py:160
  60.1 15.5 %collective-permute-start.2 = (bf16[4,256]{1,0:T(4,128)(2,1)S(1)}, bf16[4,256]{1,0:T(4,128)(2,1)S(1)}, u32[]{:S(2)}, u32[]{:S(2)}) collective-permute-start(bf16[4,256]{1,0:T(4,128)(2,1)S(1)} %get-tuple-element.160), channel_id=1, source_target_pairs={{0,12},{4,8},{8,20},{12,16},{16,28},{20,24},{24,4},{28,0},{1,13},{... | collective-permute-start | bytes 6152 | tf_op jit(solution)/shard_map/ppermute | solution.py:160
  122.9 15.0 %collective-permute-done.16 = bf16[256,512]{0,1:T(8,128)(2,1)S(1)} collective-permute-done((bf16[256,512]{0,1:T(8,128)(2,1)S(1)}, bf16[256,512]{0,1:T(8,128)(2,1)S(1)}, u32[]{:S(2)}, u32[]{:S(2)}) %collective-permute-start.16) | collective-permute-done | bytes 262176 | tf_op jit(solution)/shard_map/ppermute | solution.py:160
  143.6 28.2 %collective-permute-done.20 = bf16[256,512]{0,1:T(8,128)(2,1)S(1)} collective-permute-done((bf16[256,512]{0,1:T(8,128)(2,1)S(1)}, bf16[256,512]{0,1:T(8,128)(2,1)S(1)}, u32[]{:S(2)}, u32[]{:S(2)}) %collective-permute-start.20) | collective-permute-done | bytes 262176 | tf_op jit(solution)/shard_map/ppermute | solution.py:160
  248.1 30.5 %collective-permute-done.25 = bf16[256,2048]{1,0:T(8,128)(2,1)} collective-permute-done((bf16[256,2048]{1,0:T(8,128)(2,1)S(1)}, bf16[256,2048]{1,0:T(8,128)(2,1)}, u32[]{:S(2)}, u32[]{:S(2)}) %collective-permute-start.25) | collective-permute-done | bytes 1048608 | tf_op jit(solution)/shard_map/ppermute | solution.py:160
  324.1 16.6 %collective-permute-done.27 = bf16[256,2048]{1,0:T(8,128)(2,1)} collective-permute-done((bf16[256,2048]{1,0:T(8,128)(2,1)}, bf16[256,2048]{1,0:T(8,128)(2,1)}, u32[]{:S(2)}, u32[]{:S(2)}) %collective-permute-start.27) | collective-permute-done | bytes 1048608 | tf_op jit(solution)/shard_map/ppermute | solution.py:160
  351.7 25.2 %collective-permute-start.37 = (bf16[256,2048]{0,1:T(8,128)(2,1)}, bf16[256,2048]{0,1:T(8,128)(2,1)}, u32[]{:S(2)}, u32[]{:S(2)}) collective-permute-start(bf16[256,2048]{0,1:T(8,128)(2,1)} %get-tuple-element.32), channel_id=1, source_target_pairs={{0,16},{4,20},{8,24},{12,28},{16,0},{20,4},{24,8},{28,12},{1,17},{... | collective-permute-start | bytes 3145736 | tf_op jit(solution)/shard_map/ppermute | solution.py:160
  397.2 25.6 %collective-permute-done.37 = bf16[256,2048]{0,1:T(8,128)(2,1)} collective-permute-done((bf16[256,2048]{0,1:T(8,128)(2,1)}, bf16[256,2048]{0,1:T(8,128)(2,1)}, u32[]{:S(2)}, u32[]{:S(2)}) %collective-permute-start.37) | collective-permute-done | bytes 1048608 | tf_op jit(solution)/shard_map/ppermute | solution.py:160
  437.2 14.8 %collective-permute-done.38 = bf16[256,2048]{0,1:T(8,128)(2,1)S(1)} collective-permute-done((bf16[256,2048]{0,1:T(8,128)(2,1)}, bf16[256,2048]{0,1:T(8,128)(2,1)S(1)}, u32[]{:S(2)}, u32[]{:S(2)}) %collective-permute-start.38) | collective-permute-done | bytes 1048608 | tf_op jit(solution)/shard_map/ppermute | solution.py:160
  467.8 15.8 %convolution_convert_fusion.1 = bf16[2048,2048]{1,0:T(8,128)(2,1)} fusion(bf16[1024,2048]{1,0:T(8,128)(2,1)S(1)} %copy-done.66, f32[1024]{0:T(1024)S(1)} %multiply_divide_fusion, f32[1024,2048]{1,0:T(8,128)} %fusion.103), kind=kOutput, calls=%fused_computation.34 | convolution fusion | flops 8619294720 | bytes 20975616 | tf_op jit(solution)/shard_map/nd,nf->df/dot_general | solution.py:288
  483.5 19.3 %fusion.14 = bf16[1024,2048]{1,0:T(8,128)(2,1)} fusion(f32[1024,2048]{1,0:T(8,128)} %fusion.103, bf16[2048,2048]{0,1:T(8,128)(2,1)} %constant_dynamic-update-slice_fusion.12, bf16[1024,2048]{1,0:T(8,128)(2,1)} %param.26, f32[1024]{0:T(1024)S(1)} %multiply_divide_fusion), kind=kOutput, calls=%fused_computation.18 | convolution fusion | flops 8633974784 | bytes 25169920 | tf_op jit(solution)/shard_map/nd,df->nf/dot_general | solution.py:366
  542.9 21.3 %collective-permute-done.76 = bf16[256,2048]{1,0:T(8,128)(2,1)S(1)} collective-permute-done((bf16[256,2048]{1,0:T(8,128)(2,1)S(1)}, bf16[256,2048]{1,0:T(8,128)(2,1)S(1)}, u32[]{:S(2)}, u32[]{:S(2)}) %collective-permute-start.76) | collective-permute-done | bytes 1048608 | tf_op jit(solution)/shard_map/ppermute | solution.py:160
  566.3 14.6 %convolution_convert_fusion.6 = bf16[1024,2048]{1,0:T(8,128)(2,1)S(1)} fusion(bf16[2048,2048]{0,1:T(8,128)(2,1)} %constant_dynamic-update-slice_fusion.12, f32[1024,2048]{1,0:T(8,128)} %fusion.103), kind=kOutput, calls=%fused_computation.53 | convolution fusion | flops 8610906112 | bytes 20971520 | tf_op jit(solution)/shard_map/nf,df->nd/dot_general | solution.py:288
  582.5 67.9 %collective-permute-done.74 = bf16[256,2048]{1,0:T(8,128)(2,1)} collective-permute-done((bf16[256,2048]{1,0:T(8,128)(2,1)}, bf16[256,2048]{1,0:T(8,128)(2,1)}, u32[]{:S(2)}, u32[]{:S(2)}) %collective-permute-start.74) | collective-permute-done | bytes 1048608 | tf_op jit(solution)/shard_map/ppermute | solution.py:160
  654.2 21.6 %collective-permute-start.77 = (bf16[256,2048]{1,0:T(8,128)(2,1)S(1)}, bf16[256,2048]{1,0:T(8,128)(2,1)}, u32[]{:S(2)}, u32[]{:S(2)}) collective-permute-start(bf16[256,2048]{1,0:T(8,128)(2,1)S(1)} %get-tuple-element.162), channel_id=1, source_target_pairs={{0,16},{4,20},{8,24},{12,28},{16,0},{20,4},{24,8},{28,12},{1,17},{... | collective-permute-start | bytes 3145736 | tf_op jit(solution)/shard_map/ppermute | solution.py:160
  688.7 34.3 %collective-permute-done.77 = bf16[256,2048]{1,0:T(8,128)(2,1)} collective-permute-done((bf16[256,2048]{1,0:T(8,128)(2,1)S(1)}, bf16[256,2048]{1,0:T(8,128)(2,1)}, u32[]{:S(2)}, u32[]{:S(2)}) %collective-permute-start.77) | collective-permute-done | bytes 1048608 | tf_op jit(solution)/shard_map/ppermute | solution.py:160
  723.0 22.3 %collective-permute-done.75 = bf16[256,2048]{1,0:T(8,128)(2,1)} collective-permute-done((bf16[256,2048]{1,0:T(8,128)(2,1)S(1)}, bf16[256,2048]{1,0:T(8,128)(2,1)}, u32[]{:S(2)}, u32[]{:S(2)}) %collective-permute-start.75) | collective-permute-done | bytes 1048608 | tf_op jit(solution)/shard_map/ppermute | solution.py:160
  762.3 64.9 %collective-permute-start.66 = (bf16[256,2048]{1,0:T(8,128)(2,1)}, bf16[256,2048]{1,0:T(8,128)(2,1)S(1)}, u32[]{:S(2)}, u32[]{:S(2)}) collective-permute-start(bf16[256,2048]{1,0:T(8,128)(2,1)} %get-tuple-element.168), channel_id=1, source_target_pairs={{0,8},{4,12},{8,16},{12,20},{16,24},{20,28},{24,0},{28,4},{1,9},{5... | collective-permute-start | bytes 3145736 | tf_op jit(solution)/shard_map/ppermute | solution.py:160
  840.4 16.4 %collective-permute-done.68 = bf16[256,2048]{1,0:T(8,128)(2,1)} collective-permute-done((bf16[256,2048]{1,0:T(8,128)(2,1)}, bf16[256,2048]{1,0:T(8,128)(2,1)}, u32[]{:S(2)}, u32[]{:S(2)}) %collective-permute-start.68) | collective-permute-done | bytes 1048608 | tf_op jit(solution)/shard_map/ppermute | solution.py:160
  865.3 19.2 %collective-permute-done.40 = bf16[256,2048]{1,0:T(8,128)(2,1)S(1)} collective-permute-done((bf16[256,2048]{1,0:T(8,128)(2,1)S(1)}, bf16[256,2048]{1,0:T(8,128)(2,1)S(1)}, u32[]{:S(2)}, u32[]{:S(2)}) %collective-permute-start.40) | collective-permute-done | bytes 1048608 | tf_op jit(solution)/shard_map/ppermute | solution.py:168
  896.5 14.6 %collective-permute-done.41 = bf16[256,2048]{1,0:T(8,128)(2,1)} collective-permute-done((bf16[256,2048]{1,0:T(8,128)(2,1)}, bf16[256,2048]{1,0:T(8,128)(2,1)}, u32[]{:S(2)}, u32[]{:S(2)}) %collective-permute-start.41) | collective-permute-done | bytes 1048608 | tf_op jit(solution)/shard_map/ppermute | solution.py:168
  985.0 15.2 %collective-permute-done.58 = bf16[256,512]{1,0:T(8,128)(2,1)S(1)} collective-permute-done((bf16[256,512]{1,0:T(8,128)(2,1)S(1)}, bf16[256,512]{1,0:T(8,128)(2,1)S(1)}, u32[]{:S(2)}, u32[]{:S(2)}) %collective-permute-start.58) | collective-permute-done | bytes 262176 | tf_op jit(solution)/shard_map/ppermute | solution.py:160
  1072.2 20.8 %collective-permute-done.56 = bf16[256,1536]{0,1:T(8,128)(2,1)} collective-permute-done((bf16[256,1536]{0,1:T(8,128)(2,1)}, bf16[256,1536]{0,1:T(8,128)(2,1)}, u32[]{:S(2)}, u32[]{:S(2)}) %collective-permute-start.56) | collective-permute-done | bytes 786464 | tf_op jit(solution)/shard_map/ppermute | solution.py:160
  1093.0 16.7 %collective-permute-start.84 = (f32[4,256]{1,0:T(4,128)S(1)}, f32[4,256]{1,0:T(4,128)S(1)}, u32[]{:S(2)}, u32[]{:S(2)}) collective-permute-start(f32[4,256]{1,0:T(4,128)S(1)} %get-tuple-element.198), channel_id=1, source_target_pairs={{0,24},{4,28},{8,0},{12,4},{16,8},{20,12},{24,16},{28,20},{1,25},{... | collective-permute-start | bytes 12296 | tf_op jit(solution)/shard_map/ppermute | solution.py:160
  (543 shorter events, 559.1 us)
Async XLA Ops:
  2.3 109.2 %collective-permute-start.7 = (bf16[256,1536]{0,1:T(8,128)(2,1)S(1)}, bf16[256,1536]{0,1:T(8,128)(2,1)}, u32[]{:S(2)}, u32[]{:S(2)}) collective-permute-start(bf16[256,1536]{0,1:T(8,128)(2,1)S(1)} %bitcast.169), channel_id=1, source_target_pairs={{0,4},{4,0},{8,12},{12,8},{16,20},{20,16},{24,28},{28,24},{1,5},{5... | collective-permute-start | bytes 2359304 | tf_op jit(solution)/shard_map/ppermute | solution.py:160
  5.4 106.2 %collective-permute-start.8 = (bf16[256,1536]{0,1:T(8,128)(2,1)S(1)}, bf16[256,1536]{0,1:T(8,128)(2,1)}, u32[]{:S(2)}, u32[]{:S(2)}) collective-permute-start(bf16[256,1536]{0,1:T(8,128)(2,1)S(1)} %bitcast.170), channel_id=1, source_target_pairs={{0,8},{4,12},{8,16},{12,20},{16,24},{20,28},{24,0},{28,4},{1,9},{5... | collective-permute-start | bytes 2359304 | tf_op jit(solution)/shard_map/ppermute | solution.py:160
  6.9 112.4 %collective-permute-start.10 = (bf16[256,1536]{0,1:T(8,128)(2,1)S(1)}, bf16[256,1536]{0,1:T(8,128)(2,1)}, u32[]{:S(2)}, u32[]{:S(2)}) collective-permute-start(bf16[256,1536]{0,1:T(8,128)(2,1)S(1)} %bitcast.171), channel_id=1, source_target_pairs={{0,24},{4,28},{8,0},{12,4},{16,8},{20,12},{24,16},{28,20},{1,25},{... | collective-permute-start | bytes 2359304 | tf_op jit(solution)/shard_map/ppermute | solution.py:160
  9.2 89.5 %collective-permute-start.12 = (bf16[256,1536]{0,1:T(8,128)(2,1)S(1)}, bf16[256,1536]{0,1:T(8,128)(2,1)}, u32[]{:S(2)}, u32[]{:S(2)}) collective-permute-start(bf16[256,1536]{0,1:T(8,128)(2,1)S(1)} %bitcast.172), channel_id=1, source_target_pairs={{0,16},{4,20},{8,24},{12,28},{16,0},{20,4},{24,8},{28,12},{1,17},{... | collective-permute-start | bytes 2359304 | tf_op jit(solution)/shard_map/ppermute | solution.py:160
  230.3 69.9 %collective-permute-start.32 = (bf16[256,2048]{0,1:T(8,128)(2,1)}, bf16[256,2048]{0,1:T(8,128)(2,1)}, u32[]{:S(2)}, u32[]{:S(2)}) collective-permute-start(bf16[256,2048]{0,1:T(8,128)(2,1)} %get-tuple-element.32), channel_id=1, source_target_pairs={{0,4},{4,0},{8,12},{12,8},{16,20},{20,16},{24,28},{28,24},{1,5},{5... | collective-permute-start | bytes 3145736 | tf_op jit(solution)/shard_map/ppermute | solution.py:160
  236.7 71.3 %collective-permute-start.30 = (bf16[256,2048]{1,0:T(8,128)(2,1)S(1)}, bf16[256,2048]{1,0:T(8,128)(2,1)}, u32[]{:S(2)}, u32[]{:S(2)}) collective-permute-start(bf16[256,2048]{1,0:T(8,128)(2,1)S(1)} %convert_element_type.373), channel_id=1, source_target_pairs={{0,16},{4,20},{8,24},{12,28},{16,0},{20,4},{24,8},{28,12},{1,17},{... | collective-permute-start | bytes 3145736 | tf_op jit(solution)/shard_map/ppermute | solution.py:160
  238.8 73.0 %collective-permute-start.26 = (bf16[256,2048]{1,0:T(8,128)(2,1)S(1)}, bf16[256,2048]{1,0:T(8,128)(2,1)}, u32[]{:S(2)}, u32[]{:S(2)}) collective-permute-start(bf16[256,2048]{1,0:T(8,128)(2,1)S(1)} %convert_element_type.373), channel_id=1, source_target_pairs={{0,8},{4,12},{8,16},{12,20},{16,24},{20,28},{24,0},{28,4},{1,9},{5... | collective-permute-start | bytes 3145736 | tf_op jit(solution)/shard_map/ppermute | solution.py:160
  240.0 75.4 %collective-permute-start.28 = (bf16[256,2048]{1,0:T(8,128)(2,1)S(1)}, bf16[256,2048]{1,0:T(8,128)(2,1)}, u32[]{:S(2)}, u32[]{:S(2)}) collective-permute-start(bf16[256,2048]{1,0:T(8,128)(2,1)S(1)} %convert_element_type.373), channel_id=1, source_target_pairs={{0,24},{4,28},{8,0},{12,4},{16,8},{20,12},{24,16},{28,20},{1,25},{... | collective-permute-start | bytes 3145736 | tf_op jit(solution)/shard_map/ppermute | solution.py:160
  308.0 81.5 %collective-permute-start.35 = (bf16[256,2048]{0,1:T(8,128)(2,1)}, bf16[256,2048]{0,1:T(8,128)(2,1)}, u32[]{:S(2)}, u32[]{:S(2)}) collective-permute-start(bf16[256,2048]{0,1:T(8,128)(2,1)} %get-tuple-element.32), channel_id=1, source_target_pairs={{0,24},{4,28},{8,0},{12,4},{16,8},{20,12},{24,16},{28,20},{1,25},{... | collective-permute-start | bytes 3145736 | tf_op jit(solution)/shard_map/ppermute | solution.py:160
  315.4 74.9 %collective-permute-start.31 = (bf16[256,2048]{1,0:T(8,128)(2,1)}, bf16[256,2048]{1,0:T(8,128)(2,1)}, u32[]{:S(2)}, u32[]{:S(2)}) collective-permute-start(bf16[256,2048]{1,0:T(8,128)(2,1)} %collective-permute-done.30), channel_id=1, source_target_pairs={{0,4},{4,0},{8,12},{12,8},{16,20},{20,16},{24,28},{28,24},{1,5},{5... | collective-permute-start | bytes 3145736 | tf_op jit(solution)/shard_map/ppermute | solution.py:160
  351.7 71.0 %collective-permute-start.37 = (bf16[256,2048]{0,1:T(8,128)(2,1)}, bf16[256,2048]{0,1:T(8,128)(2,1)}, u32[]{:S(2)}, u32[]{:S(2)}) collective-permute-start(bf16[256,2048]{0,1:T(8,128)(2,1)} %get-tuple-element.32), channel_id=1, source_target_pairs={{0,16},{4,20},{8,24},{12,28},{16,0},{20,4},{24,8},{28,12},{1,17},{... | collective-permute-start | bytes 3145736 | tf_op jit(solution)/shard_map/ppermute | solution.py:160
  530.8 145.6 %collective-permute-start.43 = (bf16[512,2048]{1,0:T(8,128)(2,1)S(1)}, bf16[512,2048]{1,0:T(8,128)(2,1)}, u32[]{:S(2)}, u32[]{:S(2)}) collective-permute-start(bf16[512,2048]{1,0:T(8,128)(2,1)S(1)} %constant_dynamic-slice_fusion.25), channel_id=1, source_target_pairs={{0,1},{1,0},{2,3},{3,2},{4,5},{5,4},{6,7},{7,6},{8,9},{9,8},{10,11... | collective-permute-start | bytes 6291464 | tf_op jit(solution)/shard_map/ppermute | solution.py:168
  533.9 119.1 %collective-permute-start.65 = (bf16[256,2048]{1,0:T(8,128)(2,1)}, bf16[256,2048]{1,0:T(8,128)(2,1)}, u32[]{:S(2)}, u32[]{:S(2)}) collective-permute-start(bf16[256,2048]{1,0:T(8,128)(2,1)} %get-tuple-element.171), channel_id=1, source_target_pairs={{0,4},{4,0},{8,12},{12,8},{16,20},{20,16},{24,28},{28,24},{1,5},{5... | collective-permute-start | bytes 3145736 | tf_op jit(solution)/shard_map/ppermute | solution.py:160
  535.1 119.2 %collective-permute-start.69 = (bf16[256,2048]{1,0:T(8,128)(2,1)}, bf16[256,2048]{1,0:T(8,128)(2,1)}, u32[]{:S(2)}, u32[]{:S(2)}) collective-permute-start(bf16[256,2048]{1,0:T(8,128)(2,1)} %get-tuple-element.173), channel_id=1, source_target_pairs={{0,4},{4,0},{8,12},{12,8},{16,20},{20,16},{24,28},{28,24},{1,5},{5... | collective-permute-start | bytes 3145736 | tf_op jit(solution)/shard_map/ppermute | solution.py:160
  541.7 134.1 %collective-permute-start.67 = (bf16[256,2048]{1,0:T(8,128)(2,1)}, bf16[256,2048]{1,0:T(8,128)(2,1)}, u32[]{:S(2)}, u32[]{:S(2)}) collective-permute-start(bf16[256,2048]{1,0:T(8,128)(2,1)} %get-tuple-element.174), channel_id=1, source_target_pairs={{0,4},{4,0},{8,12},{12,8},{16,20},{20,16},{24,28},{28,24},{1,5},{5... | collective-permute-start | bytes 3145736 | tf_op jit(solution)/shard_map/ppermute | solution.py:160
  565.2 85.2 %collective-permute-start.74 = (bf16[256,2048]{1,0:T(8,128)(2,1)}, bf16[256,2048]{1,0:T(8,128)(2,1)}, u32[]{:S(2)}, u32[]{:S(2)}) collective-permute-start(bf16[256,2048]{1,0:T(8,128)(2,1)} %get-tuple-element.167), channel_id=1, source_target_pairs={{0,4},{4,0},{8,12},{12,8},{16,20},{20,16},{24,28},{28,24},{1,5},{5... | collective-permute-start | bytes 3145736 | tf_op jit(solution)/shard_map/ppermute | solution.py:160
  650.4 111.9 %collective-permute-start.39 = (bf16[512,2048]{1,0:T(8,128)(2,1)}, bf16[512,2048]{1,0:T(8,128)(2,1)}, u32[]{:S(2)}, u32[]{:S(2)}) collective-permute-start(bf16[512,2048]{1,0:T(8,128)(2,1)} %constant_dynamic-slice_fusion.26), channel_id=1, source_target_pairs={{0,1},{1,0},{2,3},{3,2},{4,5},{5,4},{6,7},{7,6},{8,9},{9,8},{10,11... | collective-permute-start | bytes 6291464 | tf_op jit(solution)/shard_map/ppermute | solution.py:168
  675.8 69.6 %collective-permute-start.75 = (bf16[256,2048]{1,0:T(8,128)(2,1)S(1)}, bf16[256,2048]{1,0:T(8,128)(2,1)}, u32[]{:S(2)}, u32[]{:S(2)}) collective-permute-start(bf16[256,2048]{1,0:T(8,128)(2,1)S(1)} %get-tuple-element.163), channel_id=1, source_target_pairs={{0,24},{4,28},{8,0},{12,4},{16,8},{20,12},{24,16},{28,20},{1,25},{... | collective-permute-start | bytes 3145736 | tf_op jit(solution)/shard_map/ppermute | solution.py:160
  676.4 69.0 %collective-permute-start.73 = (bf16[256,2048]{1,0:T(8,128)(2,1)S(1)}, bf16[256,2048]{1,0:T(8,128)(2,1)}, u32[]{:S(2)}, u32[]{:S(2)}) collective-permute-start(bf16[256,2048]{1,0:T(8,128)(2,1)S(1)} %get-tuple-element.161), channel_id=1, source_target_pairs={{0,8},{4,12},{8,16},{12,20},{16,24},{20,28},{24,0},{28,4},{1,9},{5... | collective-permute-start | bytes 3145736 | tf_op jit(solution)/shard_map/ppermute | solution.py:160
  688.0 150.8 %collective-permute-start.71 = (bf16[256,2048]{1,0:T(8,128)(2,1)}, bf16[256,2048]{1,0:T(8,128)(2,1)}, u32[]{:S(2)}, u32[]{:S(2)}) collective-permute-start(bf16[256,2048]{1,0:T(8,128)(2,1)} %get-tuple-element.172), channel_id=1, source_target_pairs={{0,4},{4,0},{8,12},{12,8},{16,20},{20,16},{24,28},{28,24},{1,5},{5... | collective-permute-start | bytes 3145736 | tf_op jit(solution)/shard_map/ppermute | solution.py:160
  723.0 117.3 %collective-permute-start.70 = (bf16[256,2048]{1,0:T(8,128)(2,1)}, bf16[256,2048]{1,0:T(8,128)(2,1)}, u32[]{:S(2)}, u32[]{:S(2)}) collective-permute-start(bf16[256,2048]{1,0:T(8,128)(2,1)} %get-tuple-element.169), channel_id=1, source_target_pairs={{0,16},{4,20},{8,24},{12,28},{16,0},{20,4},{24,8},{28,12},{1,17},{... | collective-permute-start | bytes 3145736 | tf_op jit(solution)/shard_map/ppermute | solution.py:160
  745.4 111.4 %collective-permute-start.68 = (bf16[256,2048]{1,0:T(8,128)(2,1)}, bf16[256,2048]{1,0:T(8,128)(2,1)}, u32[]{:S(2)}, u32[]{:S(2)}) collective-permute-start(bf16[256,2048]{1,0:T(8,128)(2,1)} %get-tuple-element.170), channel_id=1, source_target_pairs={{0,24},{4,28},{8,0},{12,4},{16,8},{20,12},{24,16},{28,20},{1,25},{... | collective-permute-start | bytes 3145736 | tf_op jit(solution)/shard_map/ppermute | solution.py:160
  745.4 84.8 %collective-permute-start.44 = (bf16[256,2048]{1,0:T(8,128)(2,1)}, bf16[256,2048]{1,0:T(8,128)(2,1)}, u32[]{:S(2)}, u32[]{:S(2)}) collective-permute-start(bf16[256,2048]{1,0:T(8,128)(2,1)} %dynamic-slice_convert_fusion.1), channel_id=1, source_target_pairs={{0,2},{1,3},{2,0},{3,1},{4,6},{5,7},{6,4},{7,5},{8,10},{9,11},{10,... | collective-permute-start | bytes 3145736 | tf_op jit(solution)/shard_map/ppermute | solution.py:168
  762.3 94.5 %collective-permute-start.66 = (bf16[256,2048]{1,0:T(8,128)(2,1)}, bf16[256,2048]{1,0:T(8,128)(2,1)S(1)}, u32[]{:S(2)}, u32[]{:S(2)}) collective-permute-start(bf16[256,2048]{1,0:T(8,128)(2,1)} %get-tuple-element.168), channel_id=1, source_target_pairs={{0,8},{4,12},{8,16},{12,20},{16,24},{20,28},{24,0},{28,4},{1,9},{5... | collective-permute-start | bytes 3145736 | tf_op jit(solution)/shard_map/ppermute | solution.py:160
  (160 other events, 4009.5 us)

commit v3 on v2

--- a/solution.py
+++ b/solution.py
@@ -132,8 +132,8 @@
     return stacked.astype(jnp.bfloat16)
 
 
-def after(value, *earlier):
-    return lax.optimization_barrier((value,) + earlier)[0]
+def after(value, earlier):
+    return lax.optimization_barrier((value, *earlier))[0] if earlier else value
 
 
 class Links:
@@ -144,12 +144,21 @@
         self.group = mesh.shape["tensor"]
         self.cores = 2 if self.group % 2 == 0 else 1
         self.chips = self.group // self.cores
+        shifts = range(1, self.outer)
+        self.near = [k for k in shifts if min(k, self.outer - k) == 1]
+        self.far = [k for k in shifts if min(k, self.outer - k) > 1]
 
     def place(self):
         index = lax.axis_index("dp")
-        self.out_at, self.in_at = index // self.inner, index % self.inner
+        self.out_at, self.in_at = lax.div(index, self.inner), lax.rem(index, self.inner)
         index = lax.axis_index("tensor")
-        self.chip_at, self.core_at = index // self.cores, index % self.cores
+        self.chip_at, self.core_at = lax.div(index, self.cores), lax.rem(index, self.cores)
+        self.last = []
+
+    def owner(self, k, j):
+        over_outer = lax.rem(self.out_at + k % self.outer, self.outer)
+        over_inner = lax.rem(self.in_at + j % self.inner, self.inner)
+        return over_outer * self.inner + over_inner
 
     def shift(self, value, over_outer, over_inner):
         pairs = []
@@ -167,66 +176,39 @@
                 pairs.append((a * self.cores + b, to))
         return lax.ppermute(value, "tensor", pairs)
 
-    def outer_order(self):
-        return sorted(range(1, self.outer), key=lambda k: min(k, self.outer - k))
-
-    def gather(self, shard, gate):
-        rows = shard.shape[0]
-        full = jnp.zeros((rows * self.count,) + shard.shape[1:], shard.dtype)
-        arrived = {0: shard}
-        if gate:
-            shard = after(shard, *gate)
-        for k in self.outer_order():
-            arrived[k] = self.shift(shard, k, 0)
-        for k, piece in arrived.items():
-            for j in range(self.inner):
-                part = self.shift(piece, 0, j) if j else piece
-                owner = (self.out_at - k) % self.outer * self.inner + (self.in_at - j) % self.inner
-                full = lax.dynamic_update_slice_in_dim(full, part, owner * rows, 0)
-        return full, [arrived[k] for k in self.outer_order()]
-
-    def reduce(self, partial):
-        rows = partial.shape[0] // self.count
-
-        def block(k, j):
-            owner = (self.out_at + k) % self.outer * self.inner + (self.in_at + j) % self.inner
-            return lax.dynamic_slice_in_dim(partial, owner * rows, rows, 0)
-
-        total = None
-        for k in self.outer_order() + [0]:
-            sums = block(k, 0).astype(wide)
-            for j in range(1, self.inner):
-                sums = sums + self.shift(block(k, j), 0, j).astype(wide)
-            if k:
-                sums = self.shift(sums.astype(low_type), k, 0).astype(wide)
-            total = sums if total is None else total + sums
-        return total
-
-    def gather_small(self, shard):
-        columns = shard.shape[1]
-        full = jnp.zeros((shard.shape[0], self.count, columns), shard.dtype)
-        for k in range(self.outer):
-            for j in range(self.inner):
-                part = self.shift(shard, k, j) if k or j else shard
-                owner = (self.out_at - k) % self.outer * self.inner + (self.in_at - j) % self.inner
-                full = lax.dynamic_update_slice_in_dim(full, part[:, None], owner, 1)
-        return full.reshape(shard.shape[0], -1)
+    def round(self, *moves):
+        results = []
+        for value, k, j, kept, key in moves:
+            kept[key] = self.shift(after(value, self.last), k, j)
+            results.append(kept[key])
+        self.last = results
 
     def reduce_small(self, partial):
-        split = partial.reshape(partial.shape[0], self.count, -1)
-        total = None
-        for k in range(self.outer):
-            for j in range(self.inner):
-                owner = (self.out_at + k) % self.outer * self.inner + (self.in_at + j) % self.inner
-                part = lax.dynamic_index_in_dim(split, owner, 1, keepdims=False)
-                part = self.shift(part, k, j) if k or j else part
-                total = part if total is None else total + part
+        total = partial
         for parts, step in ((self.cores, (0, 1)), (self.chips, (1, 0))):
             moving = total
             for _ in range(parts - 1):
                 moving = self.turn(moving, *step)
                 total = total + moving
-        return total
+        columns = total.shape[1] // self.count
+        split = total.reshape(total.shape[0], self.outer, self.inner, columns)
+
+        def column(j):
+            at = lax.rem(self.in_at + j, self.inner)
+            return lax.dynamic_index_in_dim(split, at, 2, keepdims=False)
+
+        sums = column(0)
+        for j in range(1, self.inner):
+            sums = sums + self.shift(column(j), 0, j)
+
+        def block(k):
+            at = lax.rem(self.out_at + k, self.outer)
+            return lax.dynamic_index_in_dim(sums, at, 1, keepdims=False)
+
+        result = block(0)
+        for k in range(1, self.outer):
+            result = result + self.shift(block(k), k, 0)
+        return result
 
     def own_rows(self, value):
         rows = value.shape[0] // self.group
@@ -238,9 +220,8 @@
         rows = partial.shape[0] // self.cores
 
         def half(j):
-            return lax.dynamic_slice_in_dim(
-                partial, (self.core_at + j) % self.cores * rows, rows, 0
-            )
+            at = lax.rem(self.core_at + j, self.cores)
+            return lax.dynamic_slice_in_dim(partial, at * rows, rows, 0)
 
         sums = half(0).astype(wide)
         for j in range(1, self.cores):
@@ -248,9 +229,8 @@
         rows = rows // self.chips
 
         def quarter(values, j):
-            return lax.dynamic_slice_in_dim(
-                values, (self.chip_at + j) % self.chips * rows, rows, 0
-            )
+            at = lax.rem(self.chip_at + j, self.chips)
+            return lax.dynamic_slice_in_dim(values, at * rows, rows, 0)
 
         total = quarter(sums, 0)
         low_sums = sums.astype(low_type)
@@ -269,9 +249,79 @@
             moving = own
             for j in range(1, parts):
                 moving = self.turn(moving, *step)
-                full = lax.dynamic_update_slice_in_dim(full, moving, (at - j) % parts * rows, 0)
+                place = lax.rem(at + parts - j, parts) * rows
+                full = lax.dynamic_update_slice_in_dim(full, moving, place, 0)
             own = full
         return own
+
+
+class Gather:
+    def __init__(self, links, shard):
+        self.links = links
+        self.held = {(0, 0): shard}
+
+    def outward(self, steps):
+        return [(self.held[0, 0], k, 0, self.held, (k, 0)) for k in steps]
+
+    def across(self, steps):
+        inner = range(1, self.links.inner)
+        return [(self.held[k, 0], 0, j, self.held, (k, j)) for k in steps for j in inner]
+
+    def first(self):
+        return self.outward(self.links.near) + self.across([0])
+
+    def second(self):
+        return self.outward(self.links.far) + self.across(self.links.near)
+
+    def third(self):
+        return self.across(self.links.far)
+
+    def full(self, rows):
+        shape = (rows * self.links.count,) + self.held[0, 0].shape[1:]
+        result = jnp.zeros(shape, self.held[0, 0].dtype)
+        for (k, j), part in self.held.items():
+            place = self.links.owner(-k, -j) * rows
+            result = lax.dynamic_update_slice_in_dim(result, part[:rows], place, 0)
+        return result
+
+
+class Reduce:
+    def __init__(self, links, partial):
+        self.links, self.partial = links, partial
+        self.rows = partial.shape[0] // links.count
+        self.crossed, self.arrived = {}, {}
+
+    def block(self, k, j):
+        place = self.links.owner(k, j) * self.rows
+        return lax.dynamic_slice_in_dim(self.partial, place, self.rows, 0)
+
+    def across(self, steps):
+        inner = range(1, self.links.inner)
+        return [(self.block(k, j), 0, j, self.crossed, (k, j)) for k in steps for j in inner]
+
+    def sums(self, k):
+        total = self.block(k, 0).astype(wide)
+        for j in range(1, self.links.inner):
+            total = total + self.crossed[k, j].astype(wide)
+        return total
+
+    def outward(self, steps):
+        return [(self.sums(k).astype(low_type), k, 0, self.arrived, k) for k in steps]
+
+    def first(self):
+        return self.across(self.links.near)
+
+    def second(self):
+        return self.outward(self.links.near) + self.across(self.links.far + [0])
+
+    def third(self):
+        return self.outward(self.links.far)
+
+    def total(self):
+        result = self.sums(0)
+        for part in self.arrived.values():
+            result = result + part.astype(wide)
+        return result
 
 
 def adam_update(master, moment, square, gradient, rate_value, decay_value):
@@ -323,15 +373,35 @@
     shard_rows, kinds_count, local_width = attend_weights.shape
     head_count = local_width // HEAD_DIM
 
-    norm_values = links.gather_small(layernorm_params.astype(low_type)).astype(wide)
     attend_low = attend_weights.astype(low_type).reshape(shard_rows, kinds_count * local_width)
     combine_low = combine_weights.astype(low_type).T
     expand_low = expand_weights.astype(low_type)
     shrink_low = shrink_weights.astype(low_type).T
-    attend_full, gate = links.gather(attend_low, ())
-    combine_full, gate_two = links.gather(combine_low, gate[-1:])
-    expand_full, gate_three = links.gather(expand_low, gate_two[:1])
-    shrink_full, _ = links.gather(shrink_low, gate_three[-1:])
+    norm_low = layernorm_params.astype(low_type).reshape(1, -1)
+    spare = attend_low.shape[1] - norm_low.shape[1]
+    norm_low = jnp.pad(norm_low, ((0, 7), (0, spare)))
+    attend_move = Gather(links, jnp.concatenate([attend_low, norm_low], axis=0))
+    combine_move, expand_move, shrink_move = (
+        Gather(links, shard) for shard in (combine_low, expand_low, shrink_low)
+    )
+    links.round(*attend_move.first())
+    links.round(*attend_move.second())
+    links.round(*attend_move.third(), *combine_move.first())
+    links.round(*combine_move.second())
+    links.round(*combine_move.third(), *expand_move.first())
+    links.round(*expand_move.second())
+    links.round(*expand_move.third(), *shrink_move.first())
+    links.round(*shrink_move.second())
+
+    norm_rows = layernorm_params.shape[0]
+    norm_values = jnp.zeros((norm_rows, links.count, width // links.count), low_type)
+    for (k, j), part in attend_move.held.items():
+        part = part[shard_rows, : norm_rows * (width // links.count)].reshape(norm_rows, 1, -1)
+        norm_values = lax.dynamic_update_slice_in_dim(norm_values, part, links.owner(-k, -j), 1)
+    norm_values = norm_values.reshape(norm_rows, width).astype(wide)
+    attend_full = attend_move.full(shard_rows)
+    combine_full = combine_move.full(shard_rows)
+    expand_full = expand_move.full(shard_rows)
 
     hidden = hidden_in.astype(wide)
     scaled_one, _ = norm_parts(hidden)
@@ -360,26 +430,30 @@
     factor = loss_numerator.astype(wide) / (4.0 * (1.0 + self_generated.astype(wide)))
     branch_grad_low = (factor[:, None] * out_cotangent.astype(wide)).astype(low_type)
     out_grad_own = links.own_rows(factor)[:, None] * links.own_rows(out_cotangent).astype(wide)
-    shrink_grad = dot_low("nd,nf->df", branch_grad_low, activated_low)
-    shrink_sum = links.reduce(shrink_grad).T
+    shrink_back = Reduce(links, dot_low("nd,nf->df", branch_grad_low, activated_low))
+    links.round(*shrink_move.third(), *shrink_back.first())
+    shrink_full = shrink_move.full(shard_rows)
+    links.round(*shrink_back.second())
 
     activated_grad = jnp.einsum(
         "nd,df->nf", branch_grad_low, shrink_full, preferred_element_type=wide
     )
     expanded_grad_low = (activated_grad * slope).astype(low_type)
     normed_two_grad = links.reduce_tensor(dot_low("nf,df->nd", expanded_grad_low, expand_full))
-    expand_grad = dot_low("nd,nf->df", normed_two_low, expanded_grad_low)
-    expand_sum = links.reduce(expand_grad)
+    expand_back = Reduce(links, dot_low("nd,nf->df", normed_two_low, expanded_grad_low))
+    links.round(*shrink_back.third(), *expand_back.first())
+    shrink_sum = shrink_back.total().T
+    links.round(*expand_back.second())
     residual_from_norm, gain_two_grad, shift_two_grad = norm_back(
         normed_two_grad, scaled_two, inverse_two, norm_values[2]
     )
     residual_grad = out_grad_own + residual_from_norm
     attended_grad_low = links.gather_tensor(residual_grad.astype(low_type))
     mixed_grad = dot_low("nd,de->ne", attended_grad_low, combine_full)
-    combine_grad = dot_low("nd,ne->de", attended_grad_low, mixed_low)
-    combine_sum = links.reduce(combine_grad).T
-    branch = links.reduce_tensor(dot_low("nf,df->nd", activated_low, shrink_full))
-    layer_output = links.gather_tensor((residual + branch).astype(low_type))
+    combine_back = Reduce(links, dot_low("nd,ne->de", attended_grad_low, mixed_low))
+    links.round(*expand_back.third(), *combine_back.first())
+    expand_sum = expand_back.total()
+    links.round(*combine_back.second())
     mixed_grad_rows = mixed_grad.reshape(row_count, row_length, head_count, HEAD_DIM)
     projected_grad = jnp.concatenate(
         [
@@ -388,8 +462,12 @@
         ],
         axis=0,
     ).reshape(local_tokens, kinds_count * local_width)
-    attend_grad = dot_low("nd,ne->de", normed_low, projected_grad)
-    attend_sum = links.reduce(attend_grad).reshape(attend_weights.shape)
+    attend_back = Reduce(links, dot_low("nd,ne->de", normed_low, projected_grad))
+    links.round(*combine_back.third(), *attend_back.first())
+    combine_sum = combine_back.total().T
+    links.round(*attend_back.second())
+    links.round(*attend_back.third())
+    attend_sum = attend_back.total().reshape(attend_weights.shape)
     normed_one_grad = links.reduce_tensor(dot_low("ne,de->nd", projected_grad, attend_full))
     scaled_own, inverse_own = norm_parts(hidden_own)
     hidden_from_norm, gain_one_grad, shift_one_grad = norm_back(
@@ -401,6 +479,8 @@
     norm_sum = links.reduce_small(
         jnp.stack([gain_one_grad, shift_one_grad, gain_two_grad, shift_two_grad])
     )
+    branch = links.reduce_tensor(dot_low("nf,df->nd", activated_low, shrink_full))
+    layer_output = links.gather_tensor((residual + branch).astype(low_type))
     kinds = (
         (
             attend_weights,

time: 1160 us -> 950 us (0.82)
  starting transfers between devices: 265 us -> 89.2 us
  waiting for transfers between devices: 468 us -> 404 us
  local copies, waits for them, and re-layouts: 174 us -> 196 us
    ppermute x70 -> x60, starting transfers between devices: 254 us -> 75.6 us  [shift(): return lax.ppermute(value, 'dp', pairs)]
    ppermute x70 -> x60, waiting for transfers between devices: 433 us -> 399 us  [shift(): return lax.ppermute(value, 'dp', pairs)]
    ppermute x18, waiting for transfers between devices: 34.7 us -> 4.29 us  [turn(): return lax.ppermute(value, 'tensor', pairs)]
    slice x0 -> x22, local copies, waits for them, and re-layouts: none -> 17.6 us  [the longest x15 13.2 us: full(): result = lax.dynamic_update_slice_in_dim(result, part[:rows], place, 0)]
    unnamed x212 -> x241, local copies, waits for them, and re-layouts: 58.1 us -> 55.6 us
  transfers between devices with their start and end apart: 88 -> 78, of which waited for: 37 -> 33; matrix products, arithmetic and copies ran while one was open for 25% -> 34% of each run, Pallas kernels for 0% -> 0%
where the time goes in v3:
time: 950 us; the launch traced here: 941 us
  waiting for transfers between devices  404 us (43%)
  local copies, waits for them, and re-layouts  196 us (21%)
  matrix products  148 us (16%)
  other arithmetic  101 us (11%)
  starting transfers between devices  89.2 us (9%)
    ppermute x60, waiting for transfers between devices, shift(): return lax.ppermute(value, 'dp', pairs)  399 us
    dot_general x10, matrix products, dot_low(): jnp.einsum(spec, left, right, preferred_element_type=wide).astype(low_type)  86.5 us
    ppermute x60, starting transfers between devices, shift(): return lax.ppermute(value, 'dp', pairs)  75.6 us
    unnamed x241, local copies, waits for them, and re-layouts  55.6 us
    dynamic_update_slice x30, local copies, waits for them, and re-layouts, full(): result = lax.dynamic_update_slice_in_dim(result, part[:rows], place, 0)  38.3 us
    convert_element_type x5, other arithmetic, shards(): master_new.astype(jnp.bfloat16)  23.6 us
    dot_general x1, matrix products, shards(): jnp.einsum('nd,df->nf', branch_grad_low, shrink_full, preferred_element_t...  19.5 us
  transfers between devices with their start and end apart: 78, of which 33 were waited for; matrix products, arithmetic and copies ran while one was open for 34% of the time, Pallas kernels for 0%

profile of v3, /device:TPU:0, one launch (start us, length us, event | category | flops | bytes accessed | tf_op | source)
XLA Modules:
  0.0 940.5 jit_solution(8449584539615882667)
XLA Ops:
  30.5 14.5 %collective-permute-done.1 = bf16[264,1536]{1,0:T(8,128)(2,1)} collective-permute-done((bf16[264,1536]{1,0:T(8,128)(2,1)}, bf16[264,1536]{1,0:T(8,128)(2,1)}, u32[]{:S(2)}, u32[]{:S(2)}) %collective-permute-start.1) | collective-permute-done | bytes 811040 | tf_op jit(solution)/shard_map/ppermute | solution.py:169
  61.3 27.9 %collective-permute-done.3 = bf16[264,1536]{1,0:T(8,128)(2,1)} collective-permute-done((bf16[264,1536]{1,0:T(8,128)(2,1)}, bf16[264,1536]{1,0:T(8,128)(2,1)}, u32[]{:S(2)}, u32[]{:S(2)}) %collective-permute-start.3) | collective-permute-done | bytes 811040 | tf_op jit(solution)/shard_map/ppermute | solution.py:169
  121.5 12.4 %convolution_convert_fusion.4 = bf16[1024,1536]{1,0:T(8,128)(2,1)} fusion(bf16[2048,1536]{0,1:T(8,128)(2,1)} %constant_dynamic-update-slice_fusion.40, bf16[1024,2048]{1,0:T(8,128)(2,1)} %param.25, f32[2048]{0:T(1024)S(1)} %bitcast.175, f32[2048]{0:T(1024)S(1)} %bitcast.168, f32[1024]{0:T(1024)S(1)} %copy-done.97, f32[1024]{0:T(1024)S(1)} %copy-done.86), kind=kOutput, calls=%fused_computation.51 | convolution fusion | flops 6456606720 | bytes 13656064 | tf_op jit(solution)/shard_map/nd,de->ne/dot_general | solution.py:338
  203.9 19.8 %collective-permute-done.19 = bf16[256,2048]{1,0:T(8,128)(2,1)} collective-permute-done((bf16[256,2048]{1,0:T(8,128)(2,1)S(1)}, bf16[256,2048]{1,0:T(8,128)(2,1)}, u32[]{:S(2)}, u32[]{:S(2)}) %collective-permute-start.19) | collective-permute-done | bytes 1048608 | tf_op jit(solution)/shard_map/ppermute | solution.py:169
  251.3 20.4 %collective-permute-done.21 = bf16[256,2048]{1,0:T(8,128)(2,1)} collective-permute-done((bf16[256,2048]{1,0:T(8,128)(2,1)S(1)}, bf16[256,2048]{1,0:T(8,128)(2,1)}, u32[]{:S(2)}, u32[]{:S(2)}) %collective-permute-start.21) | collective-permute-done | bytes 1048608 | tf_op jit(solution)/shard_map/ppermute | solution.py:169
  300.5 18.1 %collective-permute-done.26 = bf16[256,2048]{0,1:T(8,128)(2,1)} collective-permute-done((bf16[256,2048]{0,1:T(8,128)(2,1)}, bf16[256,2048]{0,1:T(8,128)(2,1)}, u32[]{:S(2)}, u32[]{:S(2)}) %collective-permute-start.26) | collective-permute-done | bytes 1048608 | tf_op jit(solution)/shard_map/ppermute | solution.py:169
  334.4 33.6 %collective-permute-done.28 = bf16[256,2048]{0,1:T(8,128)(2,1)} collective-permute-done((bf16[256,2048]{0,1:T(8,128)(2,1)}, bf16[256,2048]{0,1:T(8,128)(2,1)}, u32[]{:S(2)}, u32[]{:S(2)}) %collective-permute-start.28) | collective-permute-done | bytes 1048608 | tf_op jit(solution)/shard_map/ppermute | solution.py:169
  379.8 13.1 %collective-permute-done.31 = bf16[256,2048]{0,1:T(8,128)(2,1)S(1)} collective-permute-done((bf16[256,2048]{0,1:T(8,128)(2,1)}, bf16[256,2048]{0,1:T(8,128)(2,1)S(1)}, u32[]{:S(2)}, u32[]{:S(2)}) %collective-permute-start.31) | collective-permute-done | bytes 1048608 | tf_op jit(solution)/shard_map/ppermute | solution.py:169
  394.2 11.3 %fusion.93 = f32[1024,2048]{1,0:T(8,128)S(1)} fusion(bf16[1024,2048]{1,0:T(8,128)(2,1)S(1)} %constant_dynamic-update-slice_fusion.28, bf16[2048,2048]{0,1:T(8,128)(2,1)} %constant_dynamic-update-slice_fusion.20), kind=kOutput, calls=%fused_computation.295 | convolution fusion | flops 8589934592 | bytes 20971520 | tf_op jit(solution)/shard_map/nd,df->nf/dot_general | solution.py:426
  408.8 13.6 %convolution_convert_fusion.6 = bf16[1024,2048]{1,0:T(8,128)(2,1)} fusion(bf16[2048,2048]{0,1:T(8,128)(2,1)} %constant_dynamic-update-slice_fusion.12, f32[1024,2048]{1,0:T(8,128)S(1)} %fusion.93), kind=kOutput, calls=%fused_computation.53 | convolution fusion | flops 8610906112 | bytes 20971520 | tf_op jit(solution)/shard_map/nf,df->nd/dot_general | solution.py:338
  422.4 19.5 %fusion.14 = bf16[1024,2048]{1,0:T(8,128)(2,1)} fusion(f32[1024,2048]{1,0:T(8,128)} %copy-done.102, bf16[2048,2048]{0,1:T(8,128)(2,1)} %constant_dynamic-update-slice_fusion.12, bf16[1024,2048]{1,0:T(8,128)(2,1)} %param.26, f32[1024]{0:T(1024)S(1)} %multiply_divide_fusion), kind=kOutput, calls=%fused_computation.18 | convolution fusion | flops 8633974784 | bytes 25169920 | tf_op jit(solution)/shard_map/nd,df->nf/dot_general | solution.py:438
  441.9 13.5 %convolution_convert_fusion.1 = bf16[2048,2048]{1,0:T(8,128)(2,1)S(1)} fusion(bf16[1024,2048]{1,0:T(8,128)(2,1)} %param.26, f32[1024]{0:T(1024)S(1)} %multiply_divide_fusion, f32[1024,2048]{1,0:T(8,128)} %copy-done.102), kind=kOutput, calls=%fused_computation.34 | convolution fusion | flops 8619294720 | bytes 20975616 | tf_op jit(solution)/shard_map/nd,nf->df/dot_general | solution.py:338
  462.0 11.6 %convolution_convert_fusion.5 = bf16[1024,2048]{1,0:T(8,128)(2,1)S(1)} fusion(bf16[1024,2048]{1,0:T(8,128)(2,1)S(1)} %copy-done.103, bf16[2048,2048]{0,1:T(8,128)(2,1)} %constant_dynamic-update-slice_fusion.20), kind=kOutput, calls=%fused_computation.52 | convolution fusion | flops 8592031744 | bytes 16777216 | tf_op jit(solution)/shard_map/nf,df->nd/dot_general | solution.py:338
  475.2 10.7 %collective-permute-done.45 = bf16[256,2048]{1,0:T(8,128)(2,1)S(1)} collective-permute-done((bf16[256,2048]{1,0:T(8,128)(2,1)S(1)}, bf16[256,2048]{1,0:T(8,128)(2,1)S(1)}, u32[]{:S(2)}, u32[]{:S(2)}) %collective-permute-start.45) | collective-permute-done | bytes 1048608 | tf_op jit(solution)/shard_map/ppermute | solution.py:169
  485.9 22.1 %collective-permute-done.44 = bf16[256,2048]{1,0:T(8,128)(2,1)S(1)} collective-permute-done((bf16[256,2048]{1,0:T(8,128)(2,1)S(1)}, bf16[256,2048]{1,0:T(8,128)(2,1)S(1)}, u32[]{:S(2)}, u32[]{:S(2)}) %collective-permute-start.44) | collective-permute-done | bytes 1048608 | tf_op jit(solution)/shard_map/ppermute | solution.py:169
  508.8 11.0 %convolution_convert_fusion.2 = bf16[2048,2048]{1,0:T(8,128)(2,1)S(1)} fusion(bf16[1024,2048]{1,0:T(8,128)(2,1)S(1)} %constant_dynamic-update-slice_fusion.28, bf16[1024,2048]{1,0:T(8,128)(2,1)} %fusion.14), kind=kOutput, calls=%fused_computation.35 | convolution fusion | flops 8594128896 | bytes 16777216 | tf_op jit(solution)/shard_map/nd,nf->df/dot_general | solution.py:338
  521.1 13.1 %collective-permute-done.46 = bf16[256,2048]{1,0:T(8,128)(2,1)} collective-permute-done((bf16[256,2048]{1,0:T(8,128)(2,1)S(1)}, bf16[256,2048]{1,0:T(8,128)(2,1)}, u32[]{:S(2)}, u32[]{:S(2)}) %collective-permute-start.46) | collective-permute-done | bytes 1048608 | tf_op jit(solution)/shard_map/ppermute | solution.py:169
  555.3 10.1 %collective-permute-done.47 = bf16[256,2048]{1,0:T(8,128)(2,1)} collective-permute-done((bf16[256,2048]{1,0:T(8,128)(2,1)S(1)}, bf16[256,2048]{1,0:T(8,128)(2,1)}, u32[]{:S(2)}, u32[]{:S(2)}) %collective-permute-start.47) | collective-permute-done | bytes 1048608 | tf_op jit(solution)/shard_map/ppermute | solution.py:169
  565.4 17.4 %collective-permute-done.48 = bf16[256,2048]{1,0:T(8,128)(2,1)} collective-permute-done((bf16[256,2048]{1,0:T(8,128)(2,1)S(1)}, bf16[256,2048]{1,0:T(8,128)(2,1)}, u32[]{:S(2)}, u32[]{:S(2)}) %collective-permute-start.48) | collective-permute-done | bytes 1048608 | tf_op jit(solution)/shard_map/ppermute | solution.py:169
  609.2 19.8 %collective-permute-done.51 = bf16[256,2048]{1,0:T(8,128)(2,1)S(1)} collective-permute-done((bf16[256,2048]{1,0:T(8,128)(2,1)}, bf16[256,2048]{1,0:T(8,128)(2,1)S(1)}, u32[]{:S(2)}, u32[]{:S(2)}) %collective-permute-start.51) | collective-permute-done | bytes 1048608 | tf_op jit(solution)/shard_map/ppermute | solution.py:169
  739.8 29.8 %collective-permute-done.57 = bf16[256,2048]{1,0:T(8,128)(2,1)S(1)} collective-permute-done((bf16[256,2048]{1,0:T(8,128)(2,1)S(1)}, bf16[256,2048]{1,0:T(8,128)(2,1)S(1)}, u32[]{:S(2)}, u32[]{:S(2)}) %collective-permute-start.57) | collective-permute-done | bytes 1048608 | tf_op jit(solution)/shard_map/ppermute | solution.py:169
  815.6 14.1 %collective-permute-done.65 = bf16[256,1536]{0,1:T(8,128)(2,1)S(1)} collective-permute-done((bf16[256,1536]{0,1:T(8,128)(2,1)S(1)}, bf16[256,1536]{0,1:T(8,128)(2,1)S(1)}, u32[]{:S(2)}, u32[]{:S(2)}) %collective-permute-start.65) | collective-permute-done | bytes 786464 | tf_op jit(solution)/shard_map/ppermute | solution.py:169
  837.2 12.9 %collective-permute-done.70 = bf16[256,1536]{0,1:T(8,128)(2,1)S(1)} collective-permute-done((bf16[256,1536]{0,1:T(8,128)(2,1)S(1)}, bf16[256,1536]{0,1:T(8,128)(2,1)S(1)}, u32[]{:S(2)}, u32[]{:S(2)}) %collective-permute-start.70) | collective-permute-done | bytes 786464 | tf_op jit(solution)/shard_map/ppermute | solution.py:169
  891.6 25.0 %collective-permute-done.71 = bf16[256,1536]{0,1:T(8,128)(2,1)S(1)} collective-permute-done((bf16[256,1536]{0,1:T(8,128)(2,1)}, bf16[256,1536]{0,1:T(8,128)(2,1)S(1)}, u32[]{:S(2)}, u32[]{:S(2)}) %collective-permute-start.71) | collective-permute-done | bytes 786464 | tf_op jit(solution)/shard_map/ppermute | solution.py:169
  (588 shorter events, 522.6 us)
Async XLA Ops:
  174.0 53.2 %collective-permute-start.14 = (bf16[512,2048]{1,0:T(8,128)(2,1)}, bf16[512,2048]{1,0:T(8,128)(2,1)}, u32[]{:S(2)}, u32[]{:S(2)}) collective-permute-start(bf16[512,2048]{1,0:T(8,128)(2,1)} %constant_dynamic-slice_fusion.25), channel_id=1, source_target_pairs={{0,1},{1,0},{2,3},{3,2},{4,5},{5,4},{6,7},{7,6},{8,9},{9,8},{10,11... | collective-permute-start | bytes 6291464 | tf_op jit(solution)/shard_map/ppermute | solution.py:177
  177.4 46.3 %collective-permute-start.19 = (bf16[256,2048]{1,0:T(8,128)(2,1)S(1)}, bf16[256,2048]{1,0:T(8,128)(2,1)}, u32[]{:S(2)}, u32[]{:S(2)}) collective-permute-start(bf16[256,2048]{1,0:T(8,128)(2,1)S(1)} %convert_element_type.375), channel_id=1, source_target_pairs={{0,24},{4,28},{8,0},{12,4},{16,8},{20,12},{24,16},{28,20},{1,25},{... | collective-permute-start | bytes 3145736 | tf_op jit(solution)/shard_map/ppermute | solution.py:169
  223.7 48.0 %collective-permute-start.21 = (bf16[256,2048]{1,0:T(8,128)(2,1)S(1)}, bf16[256,2048]{1,0:T(8,128)(2,1)}, u32[]{:S(2)}, u32[]{:S(2)}) collective-permute-start(bf16[256,2048]{1,0:T(8,128)(2,1)S(1)} %convert_element_type.375), channel_id=1, source_target_pairs={{0,16},{4,20},{8,24},{12,28},{16,0},{20,4},{24,8},{28,12},{1,17},{... | collective-permute-start | bytes 3145736 | tf_op jit(solution)/shard_map/ppermute | solution.py:169
  225.2 46.5 %collective-permute-start.22 = (bf16[256,2048]{1,0:T(8,128)(2,1)}, bf16[256,2048]{1,0:T(8,128)(2,1)}, u32[]{:S(2)}, u32[]{:S(2)}) collective-permute-start(bf16[256,2048]{1,0:T(8,128)(2,1)} %collective-permute-done.18), channel_id=1, source_target_pairs={{0,4},{4,0},{8,12},{12,8},{16,20},{20,16},{24,28},{28,24},{1,5},{5... | collective-permute-start | bytes 3145736 | tf_op jit(solution)/shard_map/ppermute | solution.py:169
  225.8 45.9 %collective-permute-start.23 = (bf16[256,2048]{1,0:T(8,128)(2,1)}, bf16[256,2048]{1,0:T(8,128)(2,1)}, u32[]{:S(2)}, u32[]{:S(2)}) collective-permute-start(bf16[256,2048]{1,0:T(8,128)(2,1)} %collective-permute-done.19), channel_id=1, source_target_pairs={{0,4},{4,0},{8,12},{12,8},{16,20},{20,16},{24,28},{28,24},{1,5},{5... | collective-permute-start | bytes 3145736 | tf_op jit(solution)/shard_map/ppermute | solution.py:169
  272.6 46.0 %collective-permute-start.26 = (bf16[256,2048]{0,1:T(8,128)(2,1)}, bf16[256,2048]{0,1:T(8,128)(2,1)}, u32[]{:S(2)}, u32[]{:S(2)}) collective-permute-start(bf16[256,2048]{0,1:T(8,128)(2,1)} %get-tuple-element.89), channel_id=1, source_target_pairs={{0,24},{4,28},{8,0},{12,4},{16,8},{20,12},{24,16},{28,20},{1,25},{... | collective-permute-start | bytes 3145736 | tf_op jit(solution)/shard_map/ppermute | solution.py:169
  276.3 45.5 %collective-permute-start.24 = (bf16[256,2048]{1,0:T(8,128)(2,1)}, bf16[256,2048]{1,0:T(8,128)(2,1)}, u32[]{:S(2)}, u32[]{:S(2)}) collective-permute-start(bf16[256,2048]{1,0:T(8,128)(2,1)} %collective-permute-done.21), channel_id=1, source_target_pairs={{0,4},{4,0},{8,12},{12,8},{16,20},{20,16},{24,28},{28,24},{1,5},{5... | collective-permute-start | bytes 3145736 | tf_op jit(solution)/shard_map/ppermute | solution.py:169
  321.8 46.2 %collective-permute-start.28 = (bf16[256,2048]{0,1:T(8,128)(2,1)}, bf16[256,2048]{0,1:T(8,128)(2,1)}, u32[]{:S(2)}, u32[]{:S(2)}) collective-permute-start(bf16[256,2048]{0,1:T(8,128)(2,1)} %get-tuple-element.89), channel_id=1, source_target_pairs={{0,16},{4,20},{8,24},{12,28},{16,0},{20,4},{24,8},{28,12},{1,17},{... | collective-permute-start | bytes 3145736 | tf_op jit(solution)/shard_map/ppermute | solution.py:169
  321.8 46.2 %collective-permute-start.29 = (bf16[256,2048]{0,1:T(8,128)(2,1)}, bf16[256,2048]{0,1:T(8,128)(2,1)}, u32[]{:S(2)}, u32[]{:S(2)}) collective-permute-start(bf16[256,2048]{0,1:T(8,128)(2,1)} %collective-permute-done.25), channel_id=1, source_target_pairs={{0,4},{4,0},{8,12},{12,8},{16,20},{20,16},{24,28},{28,24},{1,5},{5... | collective-permute-start | bytes 3145736 | tf_op jit(solution)/shard_map/ppermute | solution.py:169
  328.7 65.2 %collective-permute-start.17 = (bf16[512,2048]{1,0:T(8,128)(2,1)}, bf16[512,2048]{1,0:T(8,128)(2,1)S(1)}, u32[]{:S(2)}, u32[]{:S(2)}) collective-permute-start(bf16[512,2048]{1,0:T(8,128)(2,1)} %constant_dynamic-update-slice_fusion.30), channel_id=1, source_target_pairs={{0,1},{1,0},{2,3},{3,2},{4,5},{5,4},{6,7},{7,6},{8,9},{9,8},{10,11... | collective-permute-start | bytes 6291464 | tf_op jit(solution)/shard_map/ppermute | solution.py:177
  458.6 89.5 %collective-permute-start.32 = (bf16[512,2048]{1,0:T(8,128)(2,1)}, bf16[512,2048]{1,0:T(8,128)(2,1)}, u32[]{:S(2)}, u32[]{:S(2)}) collective-permute-start(bf16[512,2048]{1,0:T(8,128)(2,1)} %constant_dynamic-slice_fusion.24), channel_id=1, source_target_pairs={{0,1},{1,0},{2,3},{3,2},{4,5},{5,4},{6,7},{7,6},{8,9},{9,8},{10,11... | collective-permute-start | bytes 6291464 | tf_op jit(solution)/shard_map/ppermute | solution.py:177
  460.7 47.3 %collective-permute-start.44 = (bf16[256,2048]{1,0:T(8,128)(2,1)S(1)}, bf16[256,2048]{1,0:T(8,128)(2,1)S(1)}, u32[]{:S(2)}, u32[]{:S(2)}) collective-permute-start(bf16[256,2048]{1,0:T(8,128)(2,1)S(1)} %get-tuple-element.93), channel_id=1, source_target_pairs={{0,4},{4,0},{8,12},{12,8},{16,20},{20,16},{24,28},{28,24},{1,5},{5... | collective-permute-start | bytes 3145736 | tf_op jit(solution)/shard_map/ppermute | solution.py:169
  475.2 66.2 %collective-permute-start.36 = (bf16[512,2048]{1,0:T(8,128)(2,1)}, bf16[512,2048]{1,0:T(8,128)(2,1)}, u32[]{:S(2)}, u32[]{:S(2)}) collective-permute-start(bf16[512,2048]{1,0:T(8,128)(2,1)} %constant_dynamic-slice_fusion.23), channel_id=1, source_target_pairs={{0,1},{1,0},{2,3},{3,2},{4,5},{5,4},{6,7},{7,6},{8,9},{9,8},{10,11... | collective-permute-start | bytes 6291464 | tf_op jit(solution)/shard_map/ppermute | solution.py:177
  537.4 45.4 %collective-permute-start.48 = (bf16[256,2048]{1,0:T(8,128)(2,1)S(1)}, bf16[256,2048]{1,0:T(8,128)(2,1)}, u32[]{:S(2)}, u32[]{:S(2)}) collective-permute-start(bf16[256,2048]{1,0:T(8,128)(2,1)S(1)} %get-tuple-element.97), channel_id=1, source_target_pairs={{0,24},{4,28},{8,0},{12,4},{16,8},{20,12},{24,16},{28,20},{1,25},{... | collective-permute-start | bytes 3145736 | tf_op jit(solution)/shard_map/ppermute | solution.py:169
  550.6 47.0 %collective-permute-start.33 = (bf16[256,2048]{1,0:T(8,128)(2,1)S(1)}, bf16[256,2048]{1,0:T(8,128)(2,1)S(1)}, u32[]{:S(2)}, u32[]{:S(2)}) collective-permute-start(bf16[256,2048]{1,0:T(8,128)(2,1)S(1)} %dynamic-slice_convert_fusion.2), channel_id=1, source_target_pairs={{0,2},{1,3},{2,0},{3,1},{4,6},{5,7},{6,4},{7,5},{8,10},{9,11},{10,... | collective-permute-start | bytes 3145736 | tf_op jit(solution)/shard_map/ppermute | solution.py:177
  599.4 54.6 %collective-permute-start.34 = (bf16[256,2048]{1,0:T(8,128)(2,1)}, bf16[256,2048]{1,0:T(8,128)(2,1)}, u32[]{:S(2)}, u32[]{:S(2)}) collective-permute-start(bf16[256,2048]{1,0:T(8,128)(2,1)} %get-tuple-element.292), channel_id=1, source_target_pairs={{0,2},{1,3},{2,0},{3,1},{4,6},{5,7},{6,4},{7,5},{8,10},{9,11},{10,... | collective-permute-start | bytes 3145736 | tf_op jit(solution)/shard_map/ppermute | solution.py:177
  630.7 92.5 %collective-permute-start.56 = (bf16[256,2048]{1,0:T(8,128)(2,1)}, bf16[256,2048]{1,0:T(8,128)(2,1)}, u32[]{:S(2)}, u32[]{:S(2)}) collective-permute-start(bf16[256,2048]{1,0:T(8,128)(2,1)} %get-tuple-element.105), channel_id=1, source_target_pairs={{0,4},{4,0},{8,12},{12,8},{16,20},{20,16},{24,28},{28,24},{1,5},{5... | collective-permute-start | bytes 3145736 | tf_op jit(solution)/shard_map/ppermute | solution.py:169
  656.4 113.8 %collective-permute-start.35 = (bf16[512,2048]{1,0:T(8,128)(2,1)}, bf16[512,2048]{1,0:T(8,128)(2,1)}, u32[]{:S(2)}, u32[]{:S(2)}) collective-permute-start(bf16[512,2048]{1,0:T(8,128)(2,1)} %constant_dynamic-update-slice_fusion.10), channel_id=1, source_target_pairs={{0,1},{1,0},{2,3},{3,2},{4,5},{5,4},{6,7},{7,6},{8,9},{9,8},{10,11... | collective-permute-start | bytes 6291464 | tf_op jit(solution)/shard_map/ppermute | solution.py:177
  667.2 56.1 %collective-permute-start.54 = (bf16[256,2048]{1,0:T(8,128)(2,1)}, bf16[256,2048]{1,0:T(8,128)(2,1)}, u32[]{:S(2)}, u32[]{:S(2)}) collective-permute-start(bf16[256,2048]{1,0:T(8,128)(2,1)} %get-tuple-element.103), channel_id=1, source_target_pairs={{0,8},{4,12},{8,16},{12,20},{16,24},{20,28},{24,0},{28,4},{1,9},{5... | collective-permute-start | bytes 3145736 | tf_op jit(solution)/shard_map/ppermute | solution.py:169
  667.2 56.1 %collective-permute-start.55 = (bf16[256,2048]{1,0:T(8,128)(2,1)}, bf16[256,2048]{1,0:T(8,128)(2,1)}, u32[]{:S(2)}, u32[]{:S(2)}) collective-permute-start(bf16[256,2048]{1,0:T(8,128)(2,1)} %get-tuple-element.104), channel_id=1, source_target_pairs={{0,24},{4,28},{8,0},{12,4},{16,8},{20,12},{24,16},{28,20},{1,25},{... | collective-permute-start | bytes 3145736 | tf_op jit(solution)/shard_map/ppermute | solution.py:169
  713.5 70.3 %collective-permute-start.40 = (bf16[512,2048]{1,0:T(8,128)(2,1)S(1)}, bf16[512,2048]{1,0:T(8,128)(2,1)S(1)}, u32[]{:S(2)}, u32[]{:S(2)}) collective-permute-start(bf16[512,2048]{1,0:T(8,128)(2,1)S(1)} %constant_dynamic-slice_fusion.22), channel_id=1, source_target_pairs={{0,1},{1,0},{2,3},{3,2},{4,5},{5,4},{6,7},{7,6},{8,9},{9,8},{10,11... | collective-permute-start | bytes 6291464 | tf_op jit(solution)/shard_map/ppermute | solution.py:177
  723.3 46.3 %collective-permute-start.57 = (bf16[256,2048]{1,0:T(8,128)(2,1)S(1)}, bf16[256,2048]{1,0:T(8,128)(2,1)S(1)}, u32[]{:S(2)}, u32[]{:S(2)}) collective-permute-start(bf16[256,2048]{1,0:T(8,128)(2,1)S(1)} %copy-done.59), channel_id=1, source_target_pairs={{0,16},{4,20},{8,24},{12,28},{16,0},{20,4},{24,8},{28,12},{1,17},{... | collective-permute-start | bytes 3145736 | tf_op jit(solution)/shard_map/ppermute | solution.py:169
  784.8 46.9 %collective-permute-start.41 = (bf16[256,2048]{1,0:T(8,128)(2,1)S(1)}, bf16[256,2048]{1,0:T(8,128)(2,1)S(1)}, u32[]{:S(2)}, u32[]{:S(2)}) collective-permute-start(bf16[256,2048]{1,0:T(8,128)(2,1)S(1)} %dynamic-slice_convert_fusion), channel_id=1, source_target_pairs={{0,2},{1,3},{2,0},{3,1},{4,6},{5,7},{6,4},{7,5},{8,10},{9,11},{10,... | collective-permute-start | bytes 3145736 | tf_op jit(solution)/shard_map/ppermute | solution.py:177
  835.1 49.8 %collective-permute-start.42 = (bf16[256,2048]{1,0:T(8,128)(2,1)}, bf16[256,2048]{1,0:T(8,128)(2,1)}, u32[]{:S(2)}, u32[]{:S(2)}) collective-permute-start(bf16[256,2048]{1,0:T(8,128)(2,1)} %get-tuple-element.285), channel_id=1, source_target_pairs={{0,2},{1,3},{2,0},{3,1},{4,6},{5,7},{6,4},{7,5},{8,10},{9,11},{10,... | collective-permute-start | bytes 3145736 | tf_op jit(solution)/shard_map/ppermute | solution.py:177
  (163 other events, 2711.3 us)

commit v4 on v2

--- a/solution.py
+++ b/solution.py
@@ -4,6 +4,8 @@
 import jax
 import jax.numpy as jnp
 from jax import lax
+from jax.experimental import pallas as pl
+from jax.experimental.pallas import tpu as pltpu
 from jax.sharding import PartitionSpec as P
 
 HEAD_DIM = 128
@@ -55,11 +57,11 @@
 
 
 def allowed_mask(segment, first_row, block_rows):
-    row_length = segment.shape[0]
     query_places = first_row + jnp.arange(block_rows, dtype=jnp.int32)
-    key_places = jnp.arange(row_length, dtype=jnp.int32)
-    query_segment = segment[first_row : first_row + block_rows]
-    return (query_segment[:, None] == segment[None, :]) & (
+    last_row = first_row + block_rows
+    key_places = jnp.arange(last_row, dtype=jnp.int32)
+    query_segment = segment[first_row:last_row]
+    return (query_segment[:, None] == segment[None, :last_row]) & (
         key_places[None, :] <= query_places[:, None]
     )
 
@@ -73,9 +75,11 @@
     logsum_parts = []
     for first_row in range(0, row_length, block_rows):
         query_block = queries[first_row : first_row + block_rows]
+        keys_seen = keys_row[: first_row + block_rows]
+        values_seen = values_row[: first_row + block_rows]
         allowed = allowed_mask(segment, first_row, block_rows)
         scores = (
-            jnp.einsum("qhd,khd->hqk", query_block, keys_row, preferred_element_type=jnp.float32)
+            jnp.einsum("qhd,khd->hqk", query_block, keys_seen, preferred_element_type=jnp.float32)
             * score_scale
         )
         masked = jnp.where(allowed[None], scores, -1e30)
@@ -84,7 +88,7 @@
         row_total = jnp.sum(exponent, axis=-1, keepdims=True)
         softmax_low = (exponent / row_total).astype(jnp.bfloat16)
         out_parts.append(
-            jnp.einsum("hqk,khd->qhd", softmax_low, values_row, preferred_element_type=jnp.float32)
+            jnp.einsum("hqk,khd->qhd", softmax_low, values_seen, preferred_element_type=jnp.float32)
         )
         logsum_parts.append((row_top + jnp.log(row_total))[..., 0])
     return (jnp.concatenate(out_parts, axis=0), jnp.concatenate(logsum_parts, axis=1))
@@ -95,69 +99,148 @@
     row_length = queries.shape[0]
     block_rows = min(512, row_length)
     score_scale = HEAD_DIM ** (-0.5)
-    keys_grad = jnp.zeros(keys_row.shape, jnp.float32)
-    values_grad = jnp.zeros(values_row.shape, jnp.float32)
+    keys_grad = []
+    values_grad = []
     query_parts = []
     for first_row in range(0, row_length, block_rows):
-        query_block = queries[first_row : first_row + block_rows]
-        grad_block = grad_row[first_row : first_row + block_rows]
+        last_row = first_row + block_rows
+        query_block = queries[first_row:last_row]
+        grad_block = grad_row[first_row:last_row]
+        keys_seen, values_seen = keys_row[:last_row], values_row[:last_row]
         allowed = allowed_mask(segment, first_row, block_rows)
         scores = (
-            jnp.einsum("qhd,khd->hqk", query_block, keys_row, preferred_element_type=jnp.float32)
+            jnp.einsum("qhd,khd->hqk", query_block, keys_seen, preferred_element_type=jnp.float32)
             * score_scale
         )
         masked = jnp.where(allowed[None], scores, -1e30)
-        softmax_full = jnp.exp(masked - logsum[:, first_row : first_row + block_rows, None])
+        softmax_full = jnp.exp(masked - logsum[:, first_row:last_row, None])
         softmax_low = softmax_full.astype(jnp.bfloat16)
-        values_grad = values_grad + jnp.einsum(
-            "hqk,qhd->khd", softmax_low, grad_block, preferred_element_type=jnp.float32
+        values_grad.append(
+            jnp.einsum(
+                "hqk,qhd->khd", softmax_low, grad_block, preferred_element_type=jnp.float32
+            )
         )
         prob_grad = jnp.einsum(
-            "qhd,khd->hqk", grad_block, values_row, preferred_element_type=jnp.float32
+            "qhd,khd->hqk", grad_block, values_seen, preferred_element_type=jnp.float32
         )
         row_delta = jnp.sum(prob_grad * softmax_full, axis=-1, keepdims=True)
         score_grad = (softmax_full * (prob_grad - row_delta)).astype(jnp.bfloat16)
         query_parts.append(
-            jnp.einsum("hqk,khd->qhd", score_grad, keys_row, preferred_element_type=jnp.float32)
+            jnp.einsum("hqk,khd->qhd", score_grad, keys_seen, preferred_element_type=jnp.float32)
             * score_scale
         )
-        keys_grad = (
-            keys_grad
-            + jnp.einsum(
+        keys_grad.append(
+            jnp.einsum(
                 "hqk,qhd->khd", score_grad, query_block, preferred_element_type=jnp.float32
             )
             * score_scale
         )
-    stacked = jnp.stack([jnp.concatenate(query_parts, axis=0), keys_grad, values_grad], axis=1)
+
+    def added(parts):
+        total = parts[-1]
+        for part in parts[:-1]:
+            missing = row_length - part.shape[0]
+            total = total + jnp.pad(part, ((0, missing), (0, 0), (0, 0)))
+        return total
+
+    query_grad = jnp.concatenate(query_parts, axis=0)
+    stacked = jnp.stack([query_grad, added(keys_grad), added(values_grad)], axis=1)
     return stacked.astype(jnp.bfloat16)
 
 
 def after(value, *earlier):
-    return lax.optimization_barrier((value,) + earlier)[0]
+    return lax.optimization_barrier((value, *earlier))[0] if earlier else value
+
+
+def copy_block(order_ref, in_ref, out_ref):
+    out_ref[...] = in_ref[...]
+
+
+def reorder_columns(values, order):
+    rows, width = values.shape
+    count = order.shape[0]
+    columns = width // count
+    if columns % 128:
+        blocks = [
+            lax.dynamic_slice_in_dim(values, order[i] * columns, columns, 1) for i in range(count)
+        ]
+        return jnp.concatenate(blocks, axis=1)
+    return pl.pallas_call(
+        copy_block,
+        out_shape=jax.ShapeDtypeStruct(values.shape, values.dtype),
+        grid_spec=pltpu.PrefetchScalarGridSpec(
+            num_scalar_prefetch=1,
+            grid=(count,),
+            in_specs=[pl.BlockSpec((rows, columns), lambda i, order_ref: (0, order_ref[i]))],
+            out_specs=pl.BlockSpec((rows, columns), lambda i, order_ref: (0, i)),
+        ),
+        cost_estimate=pl.CostEstimate(
+            flops=0, bytes_accessed=2 * values.size * values.dtype.itemsize, transcendentals=0
+        ),
+    )(order, values)
+
+
+def turn_block(in_ref, out_ref):
+    out_ref[...] = in_ref[...].T
+
+
+def turned(values):
+    rows, width = values.shape
+    columns = min(512, width)
+    return pl.pallas_call(
+        turn_block,
+        out_shape=jax.ShapeDtypeStruct((width, rows), values.dtype),
+        grid=(width // columns,),
+        in_specs=[pl.BlockSpec((rows, columns), lambda i: (0, i))],
+        out_specs=pl.BlockSpec((columns, rows), lambda i: (i, 0)),
+        cost_estimate=pl.CostEstimate(
+            flops=0, bytes_accessed=2 * values.size * values.dtype.itemsize, transcendentals=0
+        ),
+    )(values)
 
 
 class Links:
+    outer_order = (0, 2, 1, 3)
+
     def __init__(self, mesh):
         self.count = mesh.shape["dp"]
-        self.outer = 4 if self.count % 4 == 0 else 1
+        self.outer = len(self.outer_order)
         self.inner = self.count // self.outer
         self.group = mesh.shape["tensor"]
-        self.cores = 2 if self.group % 2 == 0 else 1
+        self.cores = 2
         self.chips = self.group // self.cores
 
     def place(self):
         index = lax.axis_index("dp")
-        self.out_at, self.in_at = index // self.inner, index % self.inner
+        out_at, in_at = lax.div(index, self.inner), lax.rem(index, self.inner)
         index = lax.axis_index("tensor")
-        self.chip_at, self.core_at = index // self.cores, index % self.cores
-
-    def shift(self, value, over_outer, over_inner):
+        self.chip_at, self.core_at = lax.div(index, self.cores), lax.rem(index, self.cores)
+        order = jnp.asarray(self.outer_order, jnp.int32)
+        inner = jnp.arange(self.inner, dtype=jnp.int32)
+        self.to_own = (
+            (out_at ^ order)[None, :] * self.inner + (in_at ^ inner)[:, None]
+        ).reshape(-1)
+        outer = jnp.arange(self.outer, dtype=jnp.int32) ^ out_at
+        placed = (outer & 1) * 2 + (outer >> 1)
+        self.from_own = ((inner ^ in_at)[None, :] * self.outer + placed[:, None]).reshape(-1)
+        self.running = []
+
+    def flip(self, value, over_outer, over_inner):
         pairs = []
         for a in range(self.outer):
             for b in range(self.inner):
-                to = (a + over_outer) % self.outer * self.inner + (b + over_inner) % self.inner
+                to = (a ^ over_outer) * self.inner + (b ^ over_inner)
                 pairs.append((a * self.inner + b, to))
         return lax.ppermute(value, "dp", pairs)
+
+    def round(self, moves, carried=()):
+        before = self.running
+        held = [moved[0] for moved in moves] + [store[key] for store, key in before]
+        held = [*lax.optimization_barrier(tuple(held)), *carried]
+        for value, (_, over_outer, over_inner, store, key) in zip(held, moves):
+            store[key] = self.flip(value, over_outer, over_inner)
+        self.running = [moved[3:] for moved in moves]
+        return held[len(moves) + len(before) :]
 
     def turn(self, value, over_chips, over_cores):
         pairs = []
@@ -167,66 +250,19 @@
                 pairs.append((a * self.cores + b, to))
         return lax.ppermute(value, "tensor", pairs)
 
-    def outer_order(self):
-        return sorted(range(1, self.outer), key=lambda k: min(k, self.outer - k))
-
-    def gather(self, shard, gate):
-        rows = shard.shape[0]
-        full = jnp.zeros((rows * self.count,) + shard.shape[1:], shard.dtype)
-        arrived = {0: shard}
-        if gate:
-            shard = after(shard, *gate)
-        for k in self.outer_order():
-            arrived[k] = self.shift(shard, k, 0)
-        for k, piece in arrived.items():
-            for j in range(self.inner):
-                part = self.shift(piece, 0, j) if j else piece
-                owner = (self.out_at - k) % self.outer * self.inner + (self.in_at - j) % self.inner
-                full = lax.dynamic_update_slice_in_dim(full, part, owner * rows, 0)
-        return full, [arrived[k] for k in self.outer_order()]
-
-    def reduce(self, partial):
-        rows = partial.shape[0] // self.count
-
-        def block(k, j):
-            owner = (self.out_at + k) % self.outer * self.inner + (self.in_at + j) % self.inner
-            return lax.dynamic_slice_in_dim(partial, owner * rows, rows, 0)
-
-        total = None
-        for k in self.outer_order() + [0]:
-            sums = block(k, 0).astype(wide)
-            for j in range(1, self.inner):
-                sums = sums + self.shift(block(k, j), 0, j).astype(wide)
-            if k:
-                sums = self.shift(sums.astype(low_type), k, 0).astype(wide)
-            total = sums if total is None else total + sums
-        return total
-
-    def gather_small(self, shard):
-        columns = shard.shape[1]
-        full = jnp.zeros((shard.shape[0], self.count, columns), shard.dtype)
-        for k in range(self.outer):
-            for j in range(self.inner):
-                part = self.shift(shard, k, j) if k or j else shard
-                owner = (self.out_at - k) % self.outer * self.inner + (self.in_at - j) % self.inner
-                full = lax.dynamic_update_slice_in_dim(full, part[:, None], owner, 1)
-        return full.reshape(shard.shape[0], -1)
-
     def reduce_small(self, partial):
-        split = partial.reshape(partial.shape[0], self.count, -1)
-        total = None
-        for k in range(self.outer):
-            for j in range(self.inner):
-                owner = (self.out_at + k) % self.outer * self.inner + (self.in_at + j) % self.inner
-                part = lax.dynamic_index_in_dim(split, owner, 1, keepdims=False)
-                part = self.shift(part, k, j) if k or j else part
-                total = part if total is None else total + part
+        total = partial
         for parts, step in ((self.cores, (0, 1)), (self.chips, (1, 0))):
             moving = total
             for _ in range(parts - 1):
                 moving = self.turn(moving, *step)
                 total = total + moving
-        return total
+        split = total.reshape(total.shape[0], self.inner, self.outer, -1)
+        sums = split[:, 0]
+        for j in range(1, self.inner):
+            sums = sums + self.flip(split[:, j], 0, j)
+        half = sums[:, :2] + self.flip(sums[:, 2:], 1, 0)
+        return half[:, 0] + self.flip(half[:, 1], 2, 0)
 
     def own_rows(self, value):
         rows = value.shape[0] // self.group
@@ -238,9 +274,8 @@
         rows = partial.shape[0] // self.cores
 
         def half(j):
-            return lax.dynamic_slice_in_dim(
-                partial, (self.core_at + j) % self.cores * rows, rows, 0
-            )
+            at = lax.rem(self.core_at + j, self.cores)
+            return lax.dynamic_slice_in_dim(partial, at * rows, rows, 0)
 
         sums = half(0).astype(wide)
         for j in range(1, self.cores):
@@ -248,9 +283,8 @@
         rows = rows // self.chips
 
         def quarter(values, j):
-            return lax.dynamic_slice_in_dim(
-                values, (self.chip_at + j) % self.chips * rows, rows, 0
-            )
+            at = lax.rem(self.chip_at + j, self.chips)
+            return lax.dynamic_slice_in_dim(values, at * rows, rows, 0)
 
         total = quarter(sums, 0)
         low_sums = sums.astype(low_type)
@@ -269,9 +303,83 @@
             moving = own
             for j in range(1, parts):
                 moving = self.turn(moving, *step)
-                full = lax.dynamic_update_slice_in_dim(full, moving, (at - j) % parts * rows, 0)
+                place = lax.rem(at + parts - j, parts) * rows
+                full = lax.dynamic_update_slice_in_dim(full, moving, place, 0)
             own = full
         return own
+
+
+class Gather:
+    def __init__(self, links, shard):
+        self.links = links
+        self.held = {"own": shard}
+
+    def far(self):
+        return [(self.held["own"], 2, 0, self.held, "far")]
+
+    def near(self):
+        pair = jnp.concatenate([self.held["own"], self.held["far"]], axis=0)
+        return [(pair, 1, 0, self.held, "near")]
+
+    def across(self, name):
+        if name == "pair":
+            value = jnp.concatenate([self.held["own"], self.held["far"]], axis=0)
+        else:
+            value = self.held[name]
+        partners = range(1, self.links.inner)
+        return [(value, 0, j, self.held, (name, j)) for j in partners]
+
+    def parts(self):
+        rows = self.held["own"].shape[0]
+        names = [name for name in ("own", "far", "near")]
+        for j in range(1, self.links.inner):
+            names += [(name, j) for name in ("pair", "own", "far", "near") if (name, j) in self.held]
+        for name in names:
+            for first in range(0, self.held[name].shape[0], rows):
+                yield self.held[name], first
+
+    def full(self, rows):
+        return jnp.concatenate([part[first : first + rows] for part, first in self.parts()], axis=0)
+
+
+class Reduce:
+    def __init__(self, links, rows, make):
+        self.links, self.rows = links, rows
+        size = 2 * rows
+        starts = [j * 2 * size for j in range(links.inner)]
+        self.away = {j: make(starts[j] + size, starts[j] + 2 * size) for j in range(1, links.inner)}
+        self.close = {j: make(starts[j], starts[j] + size) for j in range(1, links.inner)}
+        self.mine = make(0, 2 * size)
+        self.size = size
+        self.held = {}
+
+    def terms(self):
+        return [*self.away.values(), *self.close.values(), self.mine]
+
+    def first(self):
+        return [(part, 0, j, self.held, ("away", j)) for j, part in self.away.items()]
+
+    def second(self):
+        return [(part, 0, j, self.held, ("close", j)) for j, part in self.close.items()]
+
+    def near(self):
+        sums = self.mine[self.size :].astype(wide)
+        for j in self.away:
+            sums = sums + self.held["away", j].astype(wide)
+        return [(sums.astype(low_type), 1, 0, self.held, "near")]
+
+    def sums(self, first, last):
+        sums = self.mine[first:last].astype(wide) + self.held["near"][first:last].astype(wide)
+        for j in self.close:
+            sums = sums + self.held["close", j][first:last].astype(wide)
+        return sums
+
+    def far(self):
+        sums = self.sums(self.rows, self.size)
+        return [(sums.astype(low_type), 2, 0, self.held, "far")]
+
+    def total(self):
+        return self.sums(0, self.rows) + self.held["far"].astype(wide)
 
 
 def adam_update(master, moment, square, gradient, rate_value, decay_value):
@@ -323,18 +431,35 @@
     shard_rows, kinds_count, local_width = attend_weights.shape
     head_count = local_width // HEAD_DIM
 
-    norm_values = links.gather_small(layernorm_params.astype(low_type)).astype(wide)
     attend_low = attend_weights.astype(low_type).reshape(shard_rows, kinds_count * local_width)
     combine_low = combine_weights.astype(low_type).T
     expand_low = expand_weights.astype(low_type)
     shrink_low = shrink_weights.astype(low_type).T
-    attend_full, gate = links.gather(attend_low, ())
-    combine_full, gate_two = links.gather(combine_low, gate[-1:])
-    expand_full, gate_three = links.gather(expand_low, gate_two[:1])
-    shrink_full, _ = links.gather(shrink_low, gate_three[-1:])
-
-    hidden = hidden_in.astype(wide)
-    scaled_one, _ = norm_parts(hidden)
+    norm_rows, norm_columns = layernorm_params.shape
+    norm_low = layernorm_params.astype(low_type).reshape(1, -1)
+    spare = attend_low.shape[1] - norm_low.shape[1]
+    norm_low = jnp.pad(norm_low, ((0, 7), (0, spare)))
+    attend_move = Gather(links, jnp.concatenate([attend_low, norm_low], axis=0))
+    combine_move, expand_move, shrink_move = (
+        Gather(links, shard) for shard in (combine_low, expand_low, shrink_low)
+    )
+    links.round(attend_move.far() + combine_move.far() + attend_move.across("own"))
+    links.round(attend_move.near() + attend_move.across("far") + combine_move.across("pair"))
+    links.round(combine_move.near() + expand_move.far() + attend_move.across("near"))
+    links.round(expand_move.near() + combine_move.across("near") + expand_move.across("pair"))
+
+    norm_values = jnp.concatenate(
+        [
+            part[first + shard_rows, : norm_rows * norm_columns].reshape(norm_rows, -1)
+            for part, first in attend_move.parts()
+        ],
+        axis=1,
+    ).astype(wide)
+    attend_full = attend_move.full(shard_rows)
+
+    hidden_low = reorder_columns(hidden_in, links.to_own)
+    cotangent_low = reorder_columns(out_cotangent, links.to_own)
+    scaled_one, _ = norm_parts(hidden_low.astype(wide))
     normed_low = (scaled_one * norm_values[0] + norm_values[1]).astype(low_type)
     projected = dot_low("nd,de->ne", normed_low, attend_full)
     shaped = projected.reshape(row_count, row_length, kinds_count, head_count, HEAD_DIM)
@@ -346,40 +471,55 @@
     mixed_low = jnp.concatenate(
         [mixed.reshape(row_length, local_width).astype(low_type) for mixed, _ in forward], axis=0
     )
+    (mixed_low,) = links.round(shrink_move.far() + expand_move.across("near"), [mixed_low])
+    combine_full = combine_move.full(shard_rows)
     attended = links.reduce_tensor(dot_low("ne,de->nd", mixed_low, combine_full))
-    hidden_own = links.own_rows(hidden_in).astype(wide)
+    hidden_own = links.own_rows(hidden_low).astype(wide)
     residual = hidden_own + attended
     scaled_two, inverse_two = norm_parts(residual)
     normed_two_low = links.gather_tensor(
         (scaled_two * norm_values[2] + norm_values[3]).astype(low_type)
     )
+    (normed_two_low,) = links.round(
+        shrink_move.near() + shrink_move.across("pair"), [normed_two_low]
+    )
+    expand_full = expand_move.full(shard_rows)
     expanded = jnp.einsum("nd,df->nf", normed_two_low, expand_full, preferred_element_type=wide)
-    activated, slope = gelu_parts(expanded)
-    activated_low = activated.astype(low_type)
+    activated_low = gelu_parts(expanded)[0].astype(low_type)
 
     factor = loss_numerator.astype(wide) / (4.0 * (1.0 + self_generated.astype(wide)))
-    branch_grad_low = (factor[:, None] * out_cotangent.astype(wide)).astype(low_type)
-    out_grad_own = links.own_rows(factor)[:, None] * links.own_rows(out_cotangent).astype(wide)
-    shrink_grad = dot_low("nd,nf->df", branch_grad_low, activated_low)
-    shrink_sum = links.reduce(shrink_grad).T
-
+    branch_grad_low = (factor[:, None] * cotangent_low.astype(wide)).astype(low_type)
+    out_grad_own = links.own_rows(factor)[:, None] * links.own_rows(cotangent_low).astype(wide)
+
+    def gradient_rows(left, right):
+        return lambda first, last: dot_low("nd,nf->df", left[:, first:last], right)
+
+    activated_low, expanded = links.round(shrink_move.across("near"), [activated_low, expanded])
+    slope = gelu_parts(expanded)[1]
+    shrink_back = Reduce(links, shard_rows, gradient_rows(branch_grad_low, activated_low))
+    links.round(shrink_back.first(), shrink_back.terms())
+
+    shrink_full = shrink_move.full(shard_rows)
     activated_grad = jnp.einsum(
         "nd,df->nf", branch_grad_low, shrink_full, preferred_element_type=wide
     )
     expanded_grad_low = (activated_grad * slope).astype(low_type)
-    normed_two_grad = links.reduce_tensor(dot_low("nf,df->nd", expanded_grad_low, expand_full))
-    expand_grad = dot_low("nd,nf->df", normed_two_low, expanded_grad_low)
-    expand_sum = links.reduce(expand_grad)
+    normed_two_partial = dot_low("nf,df->nd", expanded_grad_low, expand_full)
+    normed_two_partial, expanded_grad_low = links.round(
+        shrink_back.second() + shrink_back.near(), [normed_two_partial, expanded_grad_low]
+    )
+    normed_two_grad = links.reduce_tensor(normed_two_partial)
     residual_from_norm, gain_two_grad, shift_two_grad = norm_back(
         normed_two_grad, scaled_two, inverse_two, norm_values[2]
     )
     residual_grad = out_grad_own + residual_from_norm
     attended_grad_low = links.gather_tensor(residual_grad.astype(low_type))
+    expand_back = Reduce(links, shard_rows, gradient_rows(normed_two_low, expanded_grad_low))
+    attended_grad_low, *_ = links.round(
+        expand_back.first() + shrink_back.far(), [attended_grad_low, *expand_back.terms()]
+    )
     mixed_grad = dot_low("nd,de->ne", attended_grad_low, combine_full)
-    combine_grad = dot_low("nd,ne->de", attended_grad_low, mixed_low)
-    combine_sum = links.reduce(combine_grad).T
-    branch = links.reduce_tensor(dot_low("nf,df->nd", activated_low, shrink_full))
-    layer_output = links.gather_tensor((residual + branch).astype(low_type))
+    combine_back = Reduce(links, shard_rows, gradient_rows(attended_grad_low, mixed_low))
     mixed_grad_rows = mixed_grad.reshape(row_count, row_length, head_count, HEAD_DIM)
     projected_grad = jnp.concatenate(
         [
@@ -388,19 +528,36 @@
         ],
         axis=0,
     ).reshape(local_tokens, kinds_count * local_width)
-    attend_grad = dot_low("nd,ne->de", normed_low, projected_grad)
-    attend_sum = links.reduce(attend_grad).reshape(attend_weights.shape)
-    normed_one_grad = links.reduce_tensor(dot_low("ne,de->nd", projected_grad, attend_full))
+    projected_grad, activated_low, *_ = links.round(
+        expand_back.second() + expand_back.near(),
+        [projected_grad, activated_low, *combine_back.terms()],
+    )
+    shrink_sum = turned(shrink_back.total())
+    attend_back = Reduce(links, shard_rows, gradient_rows(normed_low, projected_grad))
+    normed_one_partial = dot_low("ne,de->nd", projected_grad, attend_full)
+    links.round(
+        combine_back.first() + combine_back.second() + expand_back.far(),
+        [normed_one_partial, *attend_back.terms()],
+    )
+    normed_one_grad = links.reduce_tensor(normed_one_partial)
     scaled_own, inverse_own = norm_parts(hidden_own)
     hidden_from_norm, gain_one_grad, shift_one_grad = norm_back(
         normed_one_grad, scaled_own, inverse_own, norm_values[0]
     )
-    input_gradient = links.gather_tensor((residual_grad + hidden_from_norm).astype(low_type)).astype(
-        wide
-    )
+    input_own = reorder_columns((residual_grad + hidden_from_norm).astype(low_type), links.from_own)
+    links.round(attend_back.first() + combine_back.near())
+    expand_sum = expand_back.total()
+    input_gradient = links.gather_tensor(input_own).astype(wide)
     norm_sum = links.reduce_small(
         jnp.stack([gain_one_grad, shift_one_grad, gain_two_grad, shift_two_grad])
     )
+    branch = links.reduce_tensor(dot_low("nf,df->nd", activated_low, shrink_full))
+    output_own = reorder_columns((residual + branch).astype(low_type), links.from_own)
+    layer_output = links.gather_tensor(output_own)
+    links.round(attend_back.second() + attend_back.near() + combine_back.far())
+    links.round(attend_back.far())
+    combine_sum = turned(combine_back.total())
+    attend_sum = attend_back.total().reshape(attend_weights.shape)
     kinds = (
         (
             attend_weights,

time: 1160 us -> 872 us (0.75)
  starting transfers between devices: 265 us -> 53.2 us
  waiting for transfers between devices: 468 us -> 373 us
  Pallas kernels: 0 us -> 33.4 us
  local copies, waits for them, and re-layouts: 174 us -> 153 us
  other arithmetic: 93.8 us -> 111 us
  matrix products: 150 us -> 135 us
    ppermute x70 -> x36, starting transfers between devices: 254 us -> 41.6 us  [flip(): return lax.ppermute(value, 'dp', pairs)]
    ppermute x70 -> x36, waiting for transfers between devices: 433 us -> 356 us  [flip(): return lax.ppermute(value, 'dp', pairs)]
    dynamic_update_slice x45 -> x8, local copies, waits for them, and re-layouts: 52.8 us -> 13.2 us  [gather_tensor(): full = lax.dynamic_update_slice_in_dim(full, moving, place, 0)]
    pallas_call x0 -> x6, Pallas kernels: none -> 33.4 us  [the longest x4 26.8 us: reorder_columns(): pl.pallas_call(copy_block, out_shape=jax.ShapeDtypeStruct(values.shape, v...]
    unnamed x212 -> x239, local copies, waits for them, and re-layouts: 58.1 us -> 79.5 us
    convert_element_type x6 -> x13, other arithmetic: 13.9 us -> 32.1 us  [the longest x4 9.94 us: near(): return [(sums.astype(low_type), 1, 0, self.held, 'near')]]
    ppermute x18, waiting for transfers between devices: 34.7 us -> 16.7 us  [turn(): return lax.ppermute(value, 'tensor', pairs)]
    ppermute x7 -> x0, local copies, waits for them, and re-layouts: 14.4 us -> none  [shift(): return lax.ppermute(value, 'dp', pairs)]
  transfers between devices with their start and end apart: 88 -> 54, of which waited for: 37 -> 27; matrix products, arithmetic and copies ran while one was open for 25% -> 36% of each run, Pallas kernels for 0% -> 4%
where the time goes in v4:
time: 872 us; the launch traced here: 860 us
  waiting for transfers between devices  373 us (43%)
  local copies, waits for them, and re-layouts  153 us (18%)
  matrix products  135 us (15%)
  other arithmetic  111 us (13%)
  starting transfers between devices  53.2 us (6%)
  Pallas kernels  33.4 us (4%)
    ppermute x36, waiting for transfers between devices, flip(): return lax.ppermute(value, 'dp', pairs)  356 us
    dot_general x18, matrix products, dot_low(): jnp.einsum(spec, left, right, preferred_element_type=wide).astype(low_type)  87 us
    unnamed x239, local copies, waits for them, and re-layouts  79.5 us
    ppermute x36, starting transfers between devices, flip(): return lax.ppermute(value, 'dp', pairs)  41.6 us
    pallas_call x4, Pallas kernels, reorder_columns(): pl.pallas_call(copy_block, out_shape=jax.ShapeDtypeStruct(values.shape, v...  26.8 us
    convert_element_type x5, other arithmetic, shards(): master_new.astype(jnp.bfloat16)  18.3 us
    dot_general x1, matrix products, shards(): jnp.einsum('nd,df->nf', branch_grad_low, shrink_full, preferred_element_t...  18.3 us
  transfers between devices with their start and end apart: 54, of which 27 were waited for; matrix products, arithmetic and copies ran while one was open for 36% of the time, Pallas kernels for 4%

profile of v4, /device:TPU:0, one launch (start us, length us, event | category | flops | bytes accessed | tf_op | source)
XLA Modules:
  0.0 860.5 jit_solution(10039567017908374896)
XLA Ops:
  30.1 27.1 %collective-permute-done.1 = bf16[256,512]{0,1:T(8,128)(2,1)S(1)} collective-permute-done((bf16[256,512]{0,1:T(8,128)(2,1)S(1)}, bf16[256,512]{0,1:T(8,128)(2,1)S(1)}, u32[]{:S(2)}, u32[]{:S(2)}) %collective-permute-start.1) | collective-permute-done | bytes 262176 | tf_op jit(solution)/shard_map/ppermute | solution.py:234
  72.6 11.1 %collective-permute-done.4 = bf16[264,1536]{1,0:T(8,128)(2,1)} collective-permute-done((bf16[264,1536]{1,0:T(8,128)(2,1)}, bf16[264,1536]{1,0:T(8,128)(2,1)}, u32[]{:S(2)}, u32[]{:S(2)}) %collective-permute-start.4) | collective-permute-done | bytes 811040 | tf_op jit(solution)/shard_map/ppermute | solution.py:234
  117.0 17.0 %collective-permute-done.7 = bf16[512,512]{0,1:T(8,128)(2,1)} collective-permute-done((bf16[512,512]{0,1:T(8,128)(2,1)}, bf16[512,512]{0,1:T(8,128)(2,1)}, u32[]{:S(2)}, u32[]{:S(2)}) %collective-permute-start.7) | collective-permute-done | bytes 524320 | tf_op jit(solution)/shard_map/ppermute | solution.py:234
  136.6 9.1 %collective-permute-done.8 = bf16[256,2048]{1,0:T(8,128)(2,1)S(1)} collective-permute-done((bf16[256,2048]{1,0:T(8,128)(2,1)S(1)}, bf16[256,2048]{1,0:T(8,128)(2,1)S(1)}, u32[]{:S(2)}, u32[]{:S(2)}) %collective-permute-start.8) | collective-permute-done | bytes 1048608 | tf_op jit(solution)/shard_map/ppermute | solution.py:234
  157.8 8.1 convolution_convert_fusion.1
  202.6 7.7 shard_map.459
  219.5 28.4 %collective-permute-done.14 = bf16[512,2048]{1,0:T(8,128)(2,1)} collective-permute-done((bf16[512,2048]{1,0:T(8,128)(2,1)S(1)}, bf16[512,2048]{1,0:T(8,128)(2,1)}, u32[]{:S(2)}, u32[]{:S(2)}) %collective-permute-start.14) | collective-permute-done | bytes 2097184 | tf_op jit(solution)/shard_map/ppermute | solution.py:234
  270.5 26.8 %collective-permute-done.17 = bf16[256,2048]{0,1:T(8,128)(2,1)} collective-permute-done((bf16[256,2048]{0,1:T(8,128)(2,1)}, bf16[256,2048]{0,1:T(8,128)(2,1)}, u32[]{:S(2)}, u32[]{:S(2)}) %collective-permute-start.17) | collective-permute-done | bytes 1048608 | tf_op jit(solution)/shard_map/ppermute | solution.py:234
  318.3 28.3 %collective-permute-done.18 = bf16[512,2048]{0,1:T(8,128)(2,1)S(1)} collective-permute-done((bf16[512,2048]{0,1:T(8,128)(2,1)S(1)}, bf16[512,2048]{0,1:T(8,128)(2,1)S(1)}, u32[]{:S(2)}, u32[]{:S(2)}) %collective-permute-start.18) | collective-permute-done | bytes 2097184 | tf_op jit(solution)/shard_map/ppermute | solution.py:234
  351.6 13.2 %multiply_convert_fusion.2 = (bf16[1024,2048]{1,0:T(8,128)(2,1)}, f32[1024,2048]{1,0:T(8,128)}) fusion(bf16[1024,2048]{1,0:T(8,128)(2,1)S(1)} %constant_dynamic-update-slice_fusion.43, bf16[2048,2048]{1,0:T(8,128)(2,1)S(1)} %bitcast.186), kind=kOutput, calls=%fused_computation.23 | convolution fusion | flops 8608808960 | bytes 25165824 | tf_op jit(solution)/shard_map/nd,df->nf/dot_general | solution.py:487
  375.9 17.3 %collective-permute-done.20 = bf16[512,2048]{0,1:T(8,128)(2,1)S(1)} collective-permute-done((bf16[512,2048]{0,1:T(8,128)(2,1)S(1)}, bf16[512,2048]{0,1:T(8,128)(2,1)S(1)}, u32[]{:S(2)}, u32[]{:S(2)}) %collective-permute-start.20) | collective-permute-done | bytes 2097184 | tf_op jit(solution)/shard_map/ppermute | solution.py:234
  394.8 11.3 %convolution_convert_fusion.3 = bf16[1024,2048]{1,0:T(8,128)(2,1)S(1)} fusion(bf16[1024,2048]{1,0:T(8,128)(2,1)S(1)} %copy-done.91, bf16[2048,2048]{0,1:T(8,128)(2,1)} %constant_dynamic-update-slice_fusion.26), kind=kOutput, calls=%fused_computation.47 | convolution fusion | flops 8592031744 | bytes 16777216 | tf_op jit(solution)/shard_map/nf,df->nd/dot_general | solution.py:396
  408.6 18.3 %fusion.14 = bf16[1024,2048]{1,0:T(8,128)(2,1)} fusion(f32[1024,2048]{1,0:T(8,128)} %get-tuple-element.273, bf16[1024,2048]{1,0:T(8,128)(2,1)S(1)} %copy-done.28, bf16[2048,2048]{0,1:T(8,128)(2,1)} %constant_dynamic-update-slice_fusion.26), kind=kOutput, calls=%fused_computation.18 | convolution fusion | flops 8627683328 | bytes 25165824 | tf_op jit(solution)/shard_map/nd,df->nf/dot_general | solution.py:503
  426.9 12.7 %convolution_convert_fusion.2 = bf16[1024,2048]{1,0:T(8,128)(2,1)S(1)} fusion(bf16[1024,2048]{1,0:T(8,128)(2,1)} %fusion.14, bf16[2048,2048]{1,0:T(8,128)(2,1)} %constant_dynamic-update-slice_fusion.21), kind=kOutput, calls=%fused_computation.46 | convolution fusion | flops 8592031744 | bytes 16777216 | tf_op jit(solution)/shard_map/nf,df->nd/dot_general | solution.py:396
  464.8 29.9 %collective-permute-done.33 = bf16[512,2048]{1,0:T(8,128)(2,1)S(1)} collective-permute-done((bf16[512,2048]{1,0:T(8,128)(2,1)}, bf16[512,2048]{1,0:T(8,128)(2,1)S(1)}, u32[]{:S(2)}, u32[]{:S(2)}) %collective-permute-start.33) | collective-permute-done | bytes 2097184 | tf_op jit(solution)/shard_map/ppermute | solution.py:234
  526.0 18.4 %collective-permute-done.34 = bf16[512,2048]{1,0:T(8,128)(2,1)} collective-permute-done((bf16[512,2048]{1,0:T(8,128)(2,1)}, bf16[512,2048]{1,0:T(8,128)(2,1)}, u32[]{:S(2)}, u32[]{:S(2)}) %collective-permute-start.34) | collective-permute-done | bytes 2097184 | tf_op jit(solution)/shard_map/ppermute | solution.py:234
  549.7 9.1 %collective-permute-done.23 = bf16[256,2048]{1,0:T(8,128)(2,1)S(1)} collective-permute-done((bf16[256,2048]{1,0:T(8,128)(2,1)}, bf16[256,2048]{1,0:T(8,128)(2,1)S(1)}, u32[]{:S(2)}, u32[]{:S(2)}) %collective-permute-start.23) | collective-permute-done | bytes 1048608 | tf_op jit(solution)/shard_map/ppermute | solution.py:251
  568.6 26.3 %collective-permute-done.37 = bf16[256,2048]{1,0:T(8,128)(2,1)S(1)} collective-permute-done((bf16[256,2048]{1,0:T(8,128)(2,1)S(1)}, bf16[256,2048]{1,0:T(8,128)(2,1)S(1)}, u32[]{:S(2)}, u32[]{:S(2)}) %collective-permute-start.37) | collective-permute-done | bytes 1048608 | tf_op jit(solution)/shard_map/ppermute | solution.py:234
  673.6 10.2 %collective-permute-done.40 = bf16[512,512]{1,0:T(8,128)(2,1)S(1)} collective-permute-done((bf16[512,512]{1,0:T(8,128)(2,1)S(1)}, bf16[512,512]{1,0:T(8,128)(2,1)S(1)}, u32[]{:S(2)}, u32[]{:S(2)}) %collective-permute-start.40) | collective-permute-done | bytes 524320 | tf_op jit(solution)/shard_map/ppermute | solution.py:234
  684.8 8.3 collective-permute-done.41
  693.0 22.7 %collective-permute-done.42 = bf16[256,2048]{1,0:T(8,128)(2,1)S(1)} collective-permute-done((bf16[256,2048]{1,0:T(8,128)(2,1)S(1)}, bf16[256,2048]{1,0:T(8,128)(2,1)S(1)}, u32[]{:S(2)}, u32[]{:S(2)}) %collective-permute-start.42) | collective-permute-done | bytes 1048608 | tf_op jit(solution)/shard_map/ppermute | solution.py:234
  739.1 12.5 %collective-permute-done.51 = f32[4,4,256]{2,0,1:T(4,128)S(1)} collective-permute-done((f32[4,4,256]{2,0,1:T(4,128)S(1)}, f32[4,4,256]{2,0,1:T(4,128)S(1)}, u32[]{:S(2)}, u32[]{:S(2)}) %collective-permute-start.51) | collective-permute-done | bytes 16416 | tf_op jit(solution)/shard_map/ppermute | solution.py:234
  762.7 27.0 %collective-permute-done.53 = f32[4,256]{1,0:T(4,128)S(1)} collective-permute-done((f32[4,256]{1,0:T(4,128)S(1)}, f32[4,256]{1,0:T(4,128)S(1)}, u32[]{:S(2)}, u32[]{:S(2)}) %collective-permute-start.53) | collective-permute-done | bytes 4128 | tf_op jit(solution)/shard_map/ppermute | solution.py:234
  822.0 19.1 %collective-permute-done.48 = bf16[256,1536]{1,0:T(8,128)(2,1)S(1)} collective-permute-done((bf16[256,1536]{1,0:T(8,128)(2,1)S(1)}, bf16[256,1536]{1,0:T(8,128)(2,1)S(1)}, u32[]{:S(2)}, u32[]{:S(2)}) %collective-permute-start.48) | collective-permute-done | bytes 786464 | tf_op jit(solution)/shard_map/ppermute | solution.py:234
  (517 shorter events, 438.4 us)
Async XLA Ops:
  6.3 51.8 %collective-permute-start = (bf16[264,1536]{1,0:T(8,128)(2,1)}, bf16[264,1536]{1,0:T(8,128)(2,1)}, u32[]{:S(2)}, u32[]{:S(2)}) collective-permute-start(bf16[264,1536]{1,0:T(8,128)(2,1)} %copy.178), channel_id=1, source_target_pairs={{0,16},{4,20},{8,24},{12,28},{16,0},{20,4},{24,8},{28,12},{1,17},{... | collective-permute-start | bytes 2433032 | tf_op jit(solution)/shard_map/ppermute | solution.py:234
  11.6 48.8 %collective-permute-start.2 = (bf16[264,1536]{1,0:T(8,128)(2,1)}, bf16[264,1536]{1,0:T(8,128)(2,1)}, u32[]{:S(2)}, u32[]{:S(2)}) collective-permute-start(bf16[264,1536]{1,0:T(8,128)(2,1)} %copy.181), channel_id=1, source_target_pairs={{0,4},{4,0},{8,12},{12,8},{16,20},{20,16},{24,28},{28,24},{1,5},{5... | collective-permute-start | bytes 2433032 | tf_op jit(solution)/shard_map/ppermute | solution.py:234
  97.4 48.4 %collective-permute-start.8 = (bf16[256,2048]{1,0:T(8,128)(2,1)S(1)}, bf16[256,2048]{1,0:T(8,128)(2,1)S(1)}, u32[]{:S(2)}, u32[]{:S(2)}) collective-permute-start(bf16[256,2048]{1,0:T(8,128)(2,1)S(1)} %get-tuple-element.68), channel_id=1, source_target_pairs={{0,16},{4,20},{8,24},{12,28},{16,0},{20,4},{24,8},{28,12},{1,17},{... | collective-permute-start | bytes 3145736 | tf_op jit(solution)/shard_map/ppermute | solution.py:234
  100.5 46.9 %collective-permute-start.6 = (bf16[528,1536]{1,0:T(8,128)(2,1)}, bf16[528,1536]{1,0:T(8,128)(2,1)}, u32[]{:S(2)}, u32[]{:S(2)}) collective-permute-start(bf16[528,1536]{1,0:T(8,128)(2,1)} %collective-permute-done.3), channel_id=1, source_target_pairs={{0,4},{4,0},{8,12},{12,8},{16,20},{20,16},{24,28},{28,24},{1,5},{5... | collective-permute-start | bytes 4866056 | tf_op jit(solution)/shard_map/ppermute | solution.py:234
  199.8 48.1 %collective-permute-start.14 = (bf16[512,2048]{1,0:T(8,128)(2,1)S(1)}, bf16[512,2048]{1,0:T(8,128)(2,1)}, u32[]{:S(2)}, u32[]{:S(2)}) collective-permute-start(bf16[512,2048]{1,0:T(8,128)(2,1)S(1)} %copy-done.54), channel_id=1, source_target_pairs={{0,8},{4,12},{8,0},{12,4},{16,24},{20,28},{24,16},{28,20},{1,9},{5... | collective-permute-start | bytes 6291464 | tf_op jit(solution)/shard_map/ppermute | solution.py:234
  200.5 47.9 %collective-permute-start.15 = (bf16[512,2048]{1,0:T(8,128)(2,1)S(1)}, bf16[512,2048]{1,0:T(8,128)(2,1)}, u32[]{:S(2)}, u32[]{:S(2)}) collective-permute-start(bf16[512,2048]{1,0:T(8,128)(2,1)S(1)} %copy-done.54), channel_id=1, source_target_pairs={{0,4},{4,0},{8,12},{12,8},{16,20},{20,16},{24,28},{28,24},{1,5},{5... | collective-permute-start | bytes 6291464 | tf_op jit(solution)/shard_map/ppermute | solution.py:234
  248.3 48.9 %collective-permute-start.17 = (bf16[256,2048]{0,1:T(8,128)(2,1)}, bf16[256,2048]{0,1:T(8,128)(2,1)}, u32[]{:S(2)}, u32[]{:S(2)}) collective-permute-start(bf16[256,2048]{0,1:T(8,128)(2,1)} %get-tuple-element.73), channel_id=1, source_target_pairs={{0,16},{4,20},{8,24},{12,28},{16,0},{20,4},{24,8},{28,12},{1,17},{... | collective-permute-start | bytes 3145736 | tf_op jit(solution)/shard_map/ppermute | solution.py:234
  251.7 47.2 %collective-permute-start.16 = (bf16[512,2048]{1,0:T(8,128)(2,1)}, bf16[512,2048]{1,0:T(8,128)(2,1)}, u32[]{:S(2)}, u32[]{:S(2)}) collective-permute-start(bf16[512,2048]{1,0:T(8,128)(2,1)} %collective-permute-done.14), channel_id=1, source_target_pairs={{0,4},{4,0},{8,12},{12,8},{16,20},{20,16},{24,28},{28,24},{1,5},{5... | collective-permute-start | bytes 6291464 | tf_op jit(solution)/shard_map/ppermute | solution.py:234
  299.0 47.6 %collective-permute-start.18 = (bf16[512,2048]{0,1:T(8,128)(2,1)S(1)}, bf16[512,2048]{0,1:T(8,128)(2,1)S(1)}, u32[]{:S(2)}, u32[]{:S(2)}) collective-permute-start(bf16[512,2048]{0,1:T(8,128)(2,1)S(1)} %pad_maximum_fusion.2), channel_id=1, source_target_pairs={{0,8},{4,12},{8,0},{12,4},{16,24},{20,28},{24,16},{28,20},{1,9},{5... | collective-permute-start | bytes 6291464 | tf_op jit(solution)/shard_map/ppermute | solution.py:234
  299.3 47.3 %collective-permute-start.19 = (bf16[512,2048]{0,1:T(8,128)(2,1)S(1)}, bf16[512,2048]{0,1:T(8,128)(2,1)S(1)}, u32[]{:S(2)}, u32[]{:S(2)}) collective-permute-start(bf16[512,2048]{0,1:T(8,128)(2,1)S(1)} %pad_maximum_fusion.2), channel_id=1, source_target_pairs={{0,4},{4,0},{8,12},{12,8},{16,20},{20,16},{24,28},{28,24},{1,5},{5... | collective-permute-start | bytes 6291464 | tf_op jit(solution)/shard_map/ppermute | solution.py:234
  446.4 48.2 %collective-permute-start.33 = (bf16[512,2048]{1,0:T(8,128)(2,1)}, bf16[512,2048]{1,0:T(8,128)(2,1)S(1)}, u32[]{:S(2)}, u32[]{:S(2)}) collective-permute-start(bf16[512,2048]{1,0:T(8,128)(2,1)} %convolution_convert_fusion.8), channel_id=1, source_target_pairs={{0,4},{4,0},{8,12},{12,8},{16,20},{20,16},{24,28},{28,24},{1,5},{5... | collective-permute-start | bytes 6291464 | tf_op jit(solution)/shard_map/ppermute | solution.py:234
  496.8 47.6 %collective-permute-start.34 = (bf16[512,2048]{1,0:T(8,128)(2,1)}, bf16[512,2048]{1,0:T(8,128)(2,1)}, u32[]{:S(2)}, u32[]{:S(2)}) collective-permute-start(bf16[512,2048]{1,0:T(8,128)(2,1)} %add_convert_fusion.1), channel_id=1, source_target_pairs={{0,8},{4,12},{8,0},{12,4},{16,24},{20,28},{24,16},{28,20},{1,9},{5... | collective-permute-start | bytes 6291464 | tf_op jit(solution)/shard_map/ppermute | solution.py:234
  498.2 47.3 %collective-permute-start.35 = (bf16[512,2048]{1,0:T(8,128)(2,1)}, bf16[512,2048]{1,0:T(8,128)(2,1)}, u32[]{:S(2)}, u32[]{:S(2)}) collective-permute-start(bf16[512,2048]{1,0:T(8,128)(2,1)} %convolution_convert_fusion.9), channel_id=1, source_target_pairs={{0,4},{4,0},{8,12},{12,8},{16,20},{20,16},{24,28},{28,24},{1,5},{5... | collective-permute-start | bytes 6291464 | tf_op jit(solution)/shard_map/ppermute | solution.py:234
  547.9 47.0 %collective-permute-start.37 = (bf16[256,2048]{1,0:T(8,128)(2,1)S(1)}, bf16[256,2048]{1,0:T(8,128)(2,1)S(1)}, u32[]{:S(2)}, u32[]{:S(2)}) collective-permute-start(bf16[256,2048]{1,0:T(8,128)(2,1)S(1)} %add_convert_fusion.4), channel_id=1, source_target_pairs={{0,16},{4,20},{8,24},{12,28},{16,0},{20,4},{24,8},{28,12},{1,17},{... | collective-permute-start | bytes 3145736 | tf_op jit(solution)/shard_map/ppermute | solution.py:234
  548.1 63.7 %collective-permute-start.36 = (bf16[512,2048]{1,0:T(8,128)(2,1)}, bf16[512,2048]{1,0:T(8,128)(2,1)}, u32[]{:S(2)}, u32[]{:S(2)}) collective-permute-start(bf16[512,2048]{1,0:T(8,128)(2,1)} %convolution_convert_fusion.10), channel_id=1, source_target_pairs={{0,4},{4,0},{8,12},{12,8},{16,20},{20,16},{24,28},{28,24},{1,5},{5... | collective-permute-start | bytes 6291464 | tf_op jit(solution)/shard_map/ppermute | solution.py:234
  549.7 68.2 %collective-permute-start.28 = (bf16[512,2048]{1,0:T(8,128)(2,1)}, bf16[512,2048]{1,0:T(8,128)(2,1)}, u32[]{:S(2)}, u32[]{:S(2)}) collective-permute-start(bf16[512,2048]{1,0:T(8,128)(2,1)} %constant_dynamic-update-slice_fusion.37), channel_id=1, source_target_pairs={{0,1},{1,0},{2,3},{3,2},{4,5},{5,4},{6,7},{7,6},{8,9},{9,8},{10,11... | collective-permute-start | bytes 6291464 | tf_op jit(solution)/shard_map/ppermute | solution.py:251
  559.8 90.5 %collective-permute-start.24 = (bf16[512,2048]{1,0:T(8,128)(2,1)}, bf16[512,2048]{1,0:T(8,128)(2,1)}, u32[]{:S(2)}, u32[]{:S(2)}) collective-permute-start(bf16[512,2048]{1,0:T(8,128)(2,1)} %constant_dynamic-update-slice_fusion.41), channel_id=1, source_target_pairs={{0,1},{1,0},{2,3},{3,2},{4,5},{5,4},{6,7},{7,6},{8,9},{9,8},{10,11... | collective-permute-start | bytes 6291464 | tf_op jit(solution)/shard_map/ppermute | solution.py:251
  617.4 48.0 %collective-permute-start.38 = (bf16[512,2048]{1,0:T(8,128)(2,1)}, bf16[512,2048]{1,0:T(8,128)(2,1)}, u32[]{:S(2)}, u32[]{:S(2)}) collective-permute-start(bf16[512,2048]{1,0:T(8,128)(2,1)} %add_convert_fusion), channel_id=1, source_target_pairs={{0,8},{4,12},{8,0},{12,4},{16,24},{20,28},{24,16},{28,20},{1,9},{5... | collective-permute-start | bytes 6291464 | tf_op jit(solution)/shard_map/ppermute | solution.py:234
  617.4 48.0 %collective-permute-start.39 = (bf16[512,2048]{1,0:T(8,128)(2,1)}, bf16[512,2048]{1,0:T(8,128)(2,1)}, u32[]{:S(2)}, u32[]{:S(2)}) collective-permute-start(bf16[512,2048]{1,0:T(8,128)(2,1)} %convolution_convert_fusion.11), channel_id=1, source_target_pairs={{0,4},{4,0},{8,12},{12,8},{16,20},{20,16},{24,28},{28,24},{1,5},{5... | collective-permute-start | bytes 6291464 | tf_op jit(solution)/shard_map/ppermute | solution.py:234
  667.5 48.2 %collective-permute-start.42 = (bf16[256,2048]{1,0:T(8,128)(2,1)S(1)}, bf16[256,2048]{1,0:T(8,128)(2,1)S(1)}, u32[]{:S(2)}, u32[]{:S(2)}) collective-permute-start(bf16[256,2048]{1,0:T(8,128)(2,1)S(1)} %add_convert_fusion.3), channel_id=1, source_target_pairs={{0,16},{4,20},{8,24},{12,28},{16,0},{20,4},{24,8},{28,12},{1,17},{... | collective-permute-start | bytes 3145736 | tf_op jit(solution)/shard_map/ppermute | solution.py:234
  672.0 52.0 %collective-permute-start.30 = (bf16[256,2048]{1,0:T(8,128)(2,1)S(1)}, bf16[256,2048]{1,0:T(8,128)(2,1)S(1)}, u32[]{:S(2)}, u32[]{:S(2)}) collective-permute-start(bf16[256,2048]{1,0:T(8,128)(2,1)S(1)} %dynamic-slice_convert_fusion), channel_id=1, source_target_pairs={{0,2},{1,3},{2,0},{3,1},{4,6},{5,7},{6,4},{7,5},{8,10},{9,11},{10,... | collective-permute-start | bytes 3145736 | tf_op jit(solution)/shard_map/ppermute | solution.py:251
  757.4 49.7 %collective-permute-start.45 = (bf16[512,1536]{1,0:T(8,128)(2,1)}, bf16[512,1536]{1,0:T(8,128)(2,1)}, u32[]{:S(2)}, u32[]{:S(2)}) collective-permute-start(bf16[512,1536]{1,0:T(8,128)(2,1)} %add_convert_fusion.2), channel_id=1, source_target_pairs={{0,8},{4,12},{8,0},{12,4},{16,24},{20,28},{24,16},{28,20},{1,9},{5... | collective-permute-start | bytes 4718600 | tf_op jit(solution)/shard_map/ppermute | solution.py:234
  757.7 49.3 %collective-permute-start.46 = (bf16[512,1536]{1,0:T(8,128)(2,1)}, bf16[512,1536]{1,0:T(8,128)(2,1)}, u32[]{:S(2)}, u32[]{:S(2)}) collective-permute-start(bf16[512,1536]{1,0:T(8,128)(2,1)} %convolution_convert_fusion.13), channel_id=1, source_target_pairs={{0,4},{4,0},{8,12},{12,8},{16,20},{20,16},{24,28},{28,24},{1,5},{5... | collective-permute-start | bytes 4718600 | tf_op jit(solution)/shard_map/ppermute | solution.py:234
  762.6 49.5 %collective-permute-start.32 = (bf16[512,2048]{1,0:T(8,128)(2,1)S(1)}, bf16[512,2048]{1,0:T(8,128)(2,1)}, u32[]{:S(2)}, u32[]{:S(2)}) collective-permute-start(bf16[512,2048]{1,0:T(8,128)(2,1)S(1)} %constant_dynamic-update-slice_fusion.33), channel_id=1, source_target_pairs={{0,1},{1,0},{2,3},{3,2},{4,5},{5,4},{6,7},{7,6},{8,9},{9,8},{10,11... | collective-permute-start | bytes 6291464 | tf_op jit(solution)/shard_map/ppermute | solution.py:251
  (129 other events, 1745.6 us)

commit v5 on v4

v5 whole, which is shorter than its diff:
```python
import functools
import math

import jax
import jax.numpy as jnp
from jax import lax
from jax.experimental import pallas as pl
from jax.experimental.pallas import tpu as pltpu
from jax.sharding import PartitionSpec as P

HEAD_DIM = 128
STEP = 10


beta_first = 0.5
beta_second = 0.5
average_decay = 0.5
adam_epsilon = 1e-08
weight_decay = 0.1
matrix_rate = 0.02
norm_rate = 0.2
norm_epsilon = 1e-05
low_type = jnp.bfloat16
wide = jnp.float32
work_share = 0.1
kernel_memory = 40 * 1024 * 1024


def norm_parts(values):
    center = values - jnp.mean(values, axis=-1, keepdims=True)
    spread = jnp.mean(center * center, axis=-1, keepdims=True)
    inverse = lax.rsqrt(spread + norm_epsilon)
    return center * inverse, inverse


def norm_back(grad, scaled, inverse, gain_row):
    inner = grad * gain_row
    mean_inner = jnp.mean(inner, axis=-1, keepdims=True)
    mean_scaled = jnp.mean(inner * scaled, axis=-1, keepdims=True)
    result = inverse * (inner - mean_inner - scaled * mean_scaled)
    return result, jnp.sum(grad * scaled, axis=0), jnp.sum(grad, axis=0)


def gelu_parts(v):
    scale = math.sqrt(2.0 / math.pi)
    bend = jnp.tanh(scale * (v + 0.044715 * (v * v * v)))
    slope = 0.5 * (1.0 + bend) + 0.5 * v * (1.0 - bend * bend) * scale * (
        1.0 + 3.0 * 0.044715 * (v * v)
    )
    return 0.5 * v * (1.0 + bend), slope


def segment_ids(lengths_row, row_length):
    order = jnp.arange(lengths_row.shape[0], dtype=jnp.int32)
    earlier = order[None, :] <= order[:, None]
    bounds = jnp.sum(jnp.where(earlier, lengths_row[None, :], 0), axis=1)
    places = jnp.arange(row_length, dtype=jnp.int32)
    return jnp.sum((places[:, None] >= bounds[None, :]).astype(jnp.int32), axis=1)


def work(flops, size, exponents=0):
    return pl.CostEstimate(
        flops=int(flops * work_share), bytes_accessed=int(size * work_share), transcendentals=exponents
    )


def tile(size, most):
    return math.gcd(size, most)


product_dims = {
    "nn": (((1,), (0,)), ((), ())),
    "nt": (((1,), (1,)), ((), ())),
    "tn": (((0,), (0,)), ((), ())),
}


def product(left, right, kind):
    return lax.dot_general(left, right, product_dims[kind], preferred_element_type=wide)


class Pieces:
    def __init__(self, parts, rows):
        self.rows = rows
        self.arrays, self.places = [], []
        for array, first in parts:
            if not self.arrays or self.arrays[-1] is not array:
                self.arrays.append(array)
            self.places.append((len(self.arrays) - 1, first))
        self.shape = (rows * len(self.places), self.arrays[0].shape[1])

    def read(self, refs):
        start = 0
        while start < len(self.places):
            which, first = self.places[start]
            last = start + 1
            while (
                last < len(self.places)
                and self.places[last] == (which, first + (last - start) * self.rows)
            ):
                last += 1
            count = (last - start) * self.rows
            yield start * self.rows, count, refs[which][first : first + count, :]
            start = last


def matmul(left, right, kind, body, kinds_out, beside=None, first=0, last=None, most=(512, 512)):
    depth = left.shape[0 if kind == "tn" else 1]
    rows = (last or left.shape[1 if kind == "tn" else 0]) - first
    columns = right.shape[0 if kind == "nt" else 1]
    pieces = right if isinstance(right, Pieces) else None
    rights = pieces.arrays if pieces else [right]
    down, along = tile(math.gcd(rows, first), most[0]), tile(columns, most[1])
    if pieces and kind == "nt":
        down, along = tile(rows, 256), columns
    skip = first // down
    if kind == "tn":
        left_spec = pl.BlockSpec((depth, down), lambda j, i: (0, i + skip))
    else:
        left_spec = pl.BlockSpec((down, depth), lambda j, i: (i + skip, 0))
    if kind == "nt":
        height = [x.shape[0] if pieces else along for x in rights]
        right_specs = [pl.BlockSpec((x, depth), lambda j, i: (j, 0)) for x in height]
    else:
        right_specs = [pl.BlockSpec((x.shape[0], along), lambda j, i: (0, j)) for x in rights]
    out_spec = pl.BlockSpec((down, along), lambda j, i: (i, j))
    more = [] if beside is None else [beside]

    def kernel(left_ref, *refs):
        rights_in, refs = refs[: len(rights)], refs[len(rights) :]
        values = [ref[...] for ref in refs[: len(more)]]
        outs = refs[len(more) :]
        if pieces and kind == "nt":
            for start, count, piece in pieces.read(rights_in):
                made = body(product(left_ref[...], piece, kind), *values)
                for ref, value in zip(outs, made):
                    ref[:, start : start + count] = value.astype(ref.dtype)
            return
        if pieces:
            total = sum(
                product(left_ref[:, start : start + count], piece, kind)
                for start, count, piece in pieces.read(rights_in)
            )
        else:
            total = product(left_ref[...], rights_in[0][...], kind)
        for ref, value in zip(outs, body(total, *values)):
            ref[...] = value.astype(ref.dtype)

    shapes = [jax.ShapeDtypeStruct((rows, columns), kind_out) for kind_out in kinds_out]
    size = sum(x.size * x.dtype.itemsize for x in (left, *rights, *more, *shapes))
    return pl.pallas_call(
        kernel,
        out_shape=shapes,
        grid=(columns // along, rows // down),
        in_specs=[left_spec] + right_specs + [out_spec] * len(more),
        out_specs=[out_spec] * len(shapes),
        compiler_params=pltpu.CompilerParams(vmem_limit_bytes=kernel_memory),
        cost_estimate=work(2 * rows * columns * depth, size),
    )(left, *rights, *more)


def dot_low(left, right, kind, first=0, last=None):
    return matmul(left, right, kind, lambda made: (made,), [low_type], first=first, last=last)[0]


def block_softmax(queries, keys_seen, segment_down, segment_along, first_row):
    scores = product(queries, keys_seen, "nt") * HEAD_DIM ** (-0.5)
    places = lax.broadcasted_iota(jnp.int32, scores.shape, 0) + first_row
    key_places = lax.broadcasted_iota(jnp.int32, scores.shape, 1)
    allowed = (segment_down == segment_along) & (key_places <= places)
    masked = jnp.where(allowed, scores, -1e30)
    exponent = jnp.exp(masked - jnp.max(masked, axis=-1, keepdims=True))
    return exponent * (1.0 / jnp.sum(exponent, axis=-1, keepdims=True))


def attend_kernel(query_ref, key_ref, value_ref, down_ref, along_ref, out_ref):
    row_length = query_ref.shape[0]
    block = tile(row_length, 256)
    for first in range(0, row_length, block):
        last = first + block
        soft = block_softmax(
            query_ref[first:last, :],
            key_ref[:last, :],
            down_ref[first:last, :],
            along_ref[:, :last],
            first,
        )
        made = product(soft.astype(low_type), value_ref[:last, :], "nn")
        out_ref[first:last, :] = made.astype(low_type)


def attend_back_kernel(
    query_ref, key_ref, value_ref, grad_ref, down_ref, along_ref, out_ref, key_sum, value_sum
):
    row_length = query_ref.shape[0]
    block = tile(row_length, 256)
    scale = HEAD_DIM ** (-0.5)
    kind = pl.program_id(2)

    @pl.when(kind == 0)
    def _():
        key_sum[...] = jnp.zeros_like(key_sum)
        value_sum[...] = jnp.zeros_like(value_sum)
        for first in range(0, row_length, block):
            last = first + block
            queries, grads = query_ref[first:last, :], grad_ref[first:last, :]
            soft = block_softmax(
                queries, key_ref[:last, :], down_ref[first:last, :], along_ref[:, :last], first
            )
            value_sum[:last, :] += product(soft.astype(low_type), grads, "tn")
            prob_grad = product(grads, value_ref[:last, :], "nt")
            row_delta = jnp.sum(prob_grad * soft, axis=-1, keepdims=True)
            score_grad = (soft * (prob_grad - row_delta)).astype(low_type)
            made = product(score_grad, key_ref[:last, :], "nn") * scale
            out_ref[first:last, :] = made.astype(low_type)
            key_sum[:last, :] += product(score_grad, queries, "tn")

    @pl.when(kind == 1)
    def _():
        out_ref[...] = (key_sum[...] * scale).astype(low_type)

    @pl.when(kind == 2)
    def _():
        out_ref[...] = value_sum[...].astype(low_type)


def attention(projected, segments, grads=None):
    row_count, row_length = segments.shape
    tokens, columns = projected.shape
    head_count = columns // (3 * HEAD_DIM)
    shape = (row_length, HEAD_DIM)
    down = segments.reshape(tokens, 1)
    along = segments.reshape(row_count, 1, row_length)

    def spec(kind):
        return pl.BlockSpec(shape, lambda r, h, *_: (r, kind * head_count + h))

    in_specs = [spec(0), spec(1), spec(2)] + ([] if grads is None else [spec(0)])
    in_specs += [
        pl.BlockSpec((row_length, 1), lambda r, h, *_: (r, 0)),
        pl.BlockSpec((None, 1, row_length), lambda r, h, *_: (r, 0, 0)),
    ]
    square = 2 * row_count * head_count * row_length * row_length * HEAD_DIM
    params = pltpu.CompilerParams(vmem_limit_bytes=kernel_memory)
    if grads is None:
        return pl.pallas_call(
            attend_kernel,
            out_shape=jax.ShapeDtypeStruct((tokens, head_count * HEAD_DIM), low_type),
            grid=(row_count, head_count),
            in_specs=in_specs,
            out_specs=spec(0),
            compiler_params=params,
            cost_estimate=work(2 * square, projected.size * 4),
        )(projected, projected, projected, down, along)
    return pl.pallas_call(
        attend_back_kernel,
        out_shape=jax.ShapeDtypeStruct(projected.shape, low_type),
        grid=(row_count, head_count, 3),
        in_specs=in_specs,
        out_specs=pl.BlockSpec(shape, lambda r, h, kind: (r, kind * head_count + h)),
        scratch_shapes=[pltpu.VMEM(shape, wide), pltpu.VMEM(shape, wide)],
        compiler_params=params,
        cost_estimate=work(5 * square, projected.size * 6),
    )(projected, projected, projected, grads, down, along)


def after(value, *earlier):
    return lax.optimization_barrier((value, *earlier))[0] if earlier else value


def copy_block(order_ref, in_ref, out_ref):
    out_ref[...] = in_ref[...]


def reorder_columns(values, order):
    rows, width = values.shape
    count = order.shape[0]
    columns = width // count
    if columns % 128:
        blocks = [
            lax.dynamic_slice_in_dim(values, order[i] * columns, columns, 1) for i in range(count)
        ]
        return jnp.concatenate(blocks, axis=1)
    return pl.pallas_call(
        copy_block,
        out_shape=jax.ShapeDtypeStruct(values.shape, values.dtype),
        grid_spec=pltpu.PrefetchScalarGridSpec(
            num_scalar_prefetch=1,
            grid=(count,),
            in_specs=[pl.BlockSpec((rows, columns), lambda i, order_ref: (0, order_ref[i]))],
            out_specs=pl.BlockSpec((rows, columns), lambda i, order_ref: (0, i)),
        ),
        cost_estimate=pl.CostEstimate(
            flops=0, bytes_accessed=2 * values.size * values.dtype.itemsize, transcendentals=0
        ),
    )(order, values)


def turn_block(in_ref, out_ref):
    out_ref[...] = in_ref[...].T


def turned(values):
    rows, width = values.shape
    columns = min(512, width)
    return pl.pallas_call(
        turn_block,
        out_shape=jax.ShapeDtypeStruct((width, rows), values.dtype),
        grid=(width // columns,),
        in_specs=[pl.BlockSpec((rows, columns), lambda i: (0, i))],
        out_specs=pl.BlockSpec((columns, rows), lambda i: (i, 0)),
        cost_estimate=pl.CostEstimate(
            flops=0, bytes_accessed=2 * values.size * values.dtype.itemsize, transcendentals=0
        ),
    )(values)


class Links:
    outer_order = (0, 2, 1, 3)

    def __init__(self, mesh):
        self.count = mesh.shape["dp"]
        self.outer = len(self.outer_order)
        self.inner = self.count // self.outer
        self.group = mesh.shape["tensor"]
        self.cores = 2
        self.chips = self.group // self.cores

    def place(self):
        index = lax.axis_index("dp")
        out_at, in_at = lax.div(index, self.inner), lax.rem(index, self.inner)
        index = lax.axis_index("tensor")
        self.chip_at, self.core_at = lax.div(index, self.cores), lax.rem(index, self.cores)
        order = jnp.asarray(self.outer_order, jnp.int32)
        inner = jnp.arange(self.inner, dtype=jnp.int32)
        self.to_own = (
            (out_at ^ order)[None, :] * self.inner + (in_at ^ inner)[:, None]
        ).reshape(-1)
        outer = jnp.arange(self.outer, dtype=jnp.int32) ^ out_at
        placed = (outer & 1) * 2 + (outer >> 1)
        self.from_own = ((inner ^ in_at)[None, :] * self.outer + placed[:, None]).reshape(-1)
        self.running = []

    def flip(self, value, over_outer, over_inner):
        pairs = []
        for a in range(self.outer):
            for b in range(self.inner):
                to = (a ^ over_outer) * self.inner + (b ^ over_inner)
                pairs.append((a * self.inner + b, to))
        return lax.ppermute(value, "dp", pairs)

    def across(self, over_outer, over_inner):
        return lambda value: self.flip(value, over_outer, over_inner)

    def round(self, make_moves, carried=()):
        held = [store[key] for store, key in self.running]
        held = lax.optimization_barrier((*held, *carried))
        for (store, key), value in zip(self.running, held):
            store[key] = value
        moves = make_moves()
        values = lax.optimization_barrier((*(value for value, *_ in moves), *held))
        for value, (_, send, store, key) in zip(values, moves):
            store[key] = send(value)
        count = len(self.running)
        self.running = [(store, key) for *_, store, key in moves]
        return held[count:]

    def turn(self, value, over_chips, over_cores):
        pairs = []
        for a in range(self.chips):
            for b in range(self.cores):
                to = (a + over_chips) % self.chips * self.cores + (b + over_cores) % self.cores
                pairs.append((a * self.cores + b, to))
        return lax.ppermute(value, "tensor", pairs)

    def sum_tensor(self, total):
        for parts, step in ((self.cores, (0, 1)), (self.chips, (1, 0))):
            moving = total
            for _ in range(parts - 1):
                moving = self.turn(moving, *step)
                total = total + moving
        return total

    def along(self, over_chips, over_cores):
        return lambda value: self.turn(value, over_chips, over_cores)

    def own_rows(self, value):
        rows = value.shape[0] // self.group
        return lax.dynamic_slice_in_dim(
            value, (self.core_at * self.chips + self.chip_at) * rows, rows, 0
        )


class Gather:
    here = ("own", "far", "far0", "far1", "near", "near_own", "near_far")
    there = ("pair", "own", "far", "near", "near0", "near1", "near_own", "near_far")

    def __init__(self, links, shard, step=None):
        self.links = links
        self.step = step or shard.shape[0]
        self.held = {"own": shard}

    def out(self, name, value, distance):
        return [(value, self.links.across(distance, 0), self.held, name)]

    def joined(self, *names):
        return jnp.concatenate([self.held[name] for name in names], axis=0)

    def far(self):
        return self.out("far", self.held["own"], 2)

    def near(self):
        return self.out("near", self.joined("own", "far"), 1)

    def across(self, name, value=None):
        if value is None:
            value = self.joined("own", "far") if name == "pair" else self.held[name]
        partners = range(1, self.links.inner)
        return [(value, self.links.across(0, j), self.held, (name, j)) for j in partners]

    def half(self, name, part):
        value = self.held[name]
        rows = value.shape[0] // 2
        return value[part * rows : (part + 1) * rows]

    def parts(self):
        names = [name for name in self.here if name in self.held]
        for j in range(1, self.links.inner):
            names += [(name, j) for name in self.there if (name, j) in self.held]
        for name in names:
            for first in range(0, self.held[name].shape[0], self.step):
                yield self.held[name], first

    def full(self, rows):
        return Pieces(self.parts(), rows)


class Reduce:
    def __init__(self, links, rows, make):
        self.links, self.rows = links, rows
        size = 2 * rows
        starts = [j * 2 * size for j in range(links.inner)]
        self.away = {j: make(starts[j] + size, starts[j] + 2 * size) for j in range(1, links.inner)}
        self.close = {j: make(starts[j], starts[j] + size) for j in range(1, links.inner)}
        self.mine = make(0, 2 * size)
        self.size = size
        self.held = {}

    def terms(self):
        return [*self.away.values(), *self.close.values(), self.mine]

    def span(self, part, size):
        return (0, size) if part is None else (part * size // 2, (part + 1) * size // 2)

    def move(self, name, j, part, value, send):
        key = (name, j) if part is None else (name, j, part)
        return (value, send, self.held, key)

    def got(self, name, j, first, last, size):
        if (name, j) in self.held:
            return self.held[name, j][first:last]
        if last - first > size // 2:
            halves = [self.held[name, j, 0], self.held[name, j, 1]]
            return jnp.concatenate(halves, axis=0)[first:last]
        part = first // (size // 2)
        skip = part * (size // 2)
        return self.held[name, j, part][first - skip : last - skip]

    def inward(self, name, terms, part):
        first, last = self.span(part, self.size)
        return [
            self.move(name, j, part, term[first:last], self.links.across(0, j))
            for j, term in terms.items()
        ]

    def first(self, part=None):
        return self.inward("away", self.away, part)

    def second(self, part=None):
        return self.inward("close", self.close, part)

    def both(self):
        return [
            (
                jnp.concatenate([self.close[j], self.away[j]], axis=0),
                self.links.across(0, j),
                self.held,
                ("both", j),
            )
            for j in self.away
        ]

    def split_both(self):
        for j in self.away:
            self.held["close", j] = self.held["both", j][: self.size]
            self.held["away", j] = self.held["both", j][self.size :]

    def near(self, part=None):
        first, last = self.span(part, self.size)
        sums = self.mine[self.size + first : self.size + last].astype(wide)
        for j in self.away:
            sums = sums + self.got("away", j, first, last, self.size).astype(wide)
        return [self.move("near", 0, part, sums.astype(low_type), self.links.across(1, 0))]

    def sums(self, first, last):
        sums = self.mine[first:last].astype(wide)
        sums = sums + self.got("near", 0, first, last, self.size).astype(wide)
        for j in self.close:
            sums = sums + self.got("close", j, first, last, self.size).astype(wide)
        return sums

    def far(self, part=None):
        first, last = self.span(part, self.rows)
        sums = self.sums(self.rows + first, self.rows + last).astype(low_type)
        return [self.move("far", 0, part, sums, self.links.across(2, 0))]

    def total(self):
        parts = [None] if ("far", 0) in self.held else [0, 1]
        spans = [self.span(part, self.rows) for part in parts]
        sums = [
            self.sums(*span) + self.got("far", 0, *span, self.rows).astype(wide) for span in spans
        ]
        return jnp.concatenate(sums, axis=0)


class ReduceTensor:
    def __init__(self, links, partial):
        self.links, self.partial = links, partial
        self.held = {}

    def half(self, j):
        rows = self.partial.shape[0] // self.links.cores
        at = lax.rem(self.links.core_at + j, self.links.cores)
        return lax.dynamic_slice_in_dim(self.partial, at * rows, rows, 0)

    def first(self):
        return [(self.half(1), self.links.along(0, 1), self.held, "half")]

    def quarter(self, j):
        links = self.links
        sums = self.half(0).astype(wide) + self.held["half"].astype(wide)
        rows = sums.shape[0] // links.chips
        at = lax.rem(links.chip_at + j, links.chips)
        return lax.dynamic_slice_in_dim(sums, at * rows, rows, 0)

    def second(self):
        return [
            (self.quarter(j).astype(low_type), self.links.along(j, 0), self.held, j)
            for j in range(1, self.links.chips)
        ]

    def second_now(self):
        for value, send, store, key in self.second():
            store[key] = send(value)

    def total(self):
        return self.quarter(0) + sum(
            self.held[j].astype(wide) for j in range(1, self.links.chips)
        )


class GatherTensor:
    def __init__(self, links, own):
        self.links, self.own = links, own
        self.held = {}

    def first(self):
        return [
            (self.own, self.links.along(j, 0), self.held, j) for j in range(1, self.links.chips)
        ]

    def first_now(self):
        for value, send, store, key in self.first():
            store[key] = send(value)

    def terms(self):
        return [self.half()]

    def carry(self, joined, *_):
        self.whole_half = joined

    @staticmethod
    def joined(parts, at):
        count, rows = len(parts), parts[0].shape[0]
        full = jnp.zeros((count * rows,) + parts[0].shape[1:], parts[0].dtype)
        for j, part in enumerate(parts):
            place = lax.rem(at + count - j, count) * rows
            full = lax.dynamic_update_slice_in_dim(full, part, place, 0)
        return full

    whole_half = None

    def half(self):
        links = self.links
        if self.whole_half is not None:
            return self.whole_half
        return self.joined([self.own, *(self.held[j] for j in range(1, links.chips))], links.chip_at)

    def second(self):
        return [(self.half(), self.links.along(0, 1), self.held, "other")]

    def second_now(self):
        for value, send, store, key in self.second():
            store[key] = send(value)

    def full(self):
        return self.joined([self.half(), self.held["other"]], self.links.core_at)


class ReduceSmall:
    def __init__(self, links, partial):
        self.links = links
        self.split = partial.reshape(partial.shape[0], links.inner, links.outer, -1)
        self.held = {}

    def first(self):
        return [
            (self.split[:, j], self.links.across(0, j), self.held, j + 2)
            for j in range(1, self.links.inner)
        ]

    def outward(self):
        self.sums = self.split[:, 0] + sum(
            self.held[j + 2] for j in range(1, self.links.inner)
        )
        order = self.links.outer_order
        return [
            (self.sums[:, i], self.links.across(order[i], 0), self.held, -i)
            for i in range(1, len(order))
        ]

    def total(self):
        return self.sums[:, 0] + sum(self.held[-i] for i in range(1, self.links.outer))


def adam_update(master, moment, square, gradient, rate_value, decay_value):
    moment_new = beta_first * moment + (1.0 - beta_first) * gradient
    square_new = beta_second * square + (1.0 - beta_second) * gradient * gradient
    fix_first = 1.0 - beta_first**STEP
    fix_second = 1.0 - beta_second**STEP
    direction = moment_new / fix_first / (jnp.sqrt(square_new / fix_second) + adam_epsilon)
    master_new = master - rate_value * (direction + decay_value * master)
    return (master_new, moment_new, square_new)


def shards(
    links,
    hidden_in,
    out_cotangent,
    episode_lengths,
    self_generated,
    loss_numerator,
    attend_weights,
    attend_first,
    attend_second,
    attend_average,
    combine_weights,
    combine_first,
    combine_second,
    combine_average,
    expand_weights,
    expand_first,
    expand_second,
    expand_average,
    shrink_weights,
    shrink_first,
    shrink_second,
    shrink_average,
    layernorm_params,
    layernorm_first,
    layernorm_second,
    layernorm_average,
):
    links.place()
    local_tokens, width = hidden_in.shape
    row_count = episode_lengths.shape[0]
    row_length = local_tokens // row_count
    shard_rows, kinds_count, local_width = attend_weights.shape

    attend_low = attend_weights.astype(low_type).reshape(shard_rows, kinds_count * local_width)
    combine_low = combine_weights.astype(low_type).T
    expand_low = expand_weights.astype(low_type)
    shrink_low = shrink_weights.astype(low_type).T
    norm_rows, norm_columns = layernorm_params.shape
    norm_low = layernorm_params.astype(low_type).reshape(1, -1)
    spare = attend_low.shape[1] - norm_low.shape[1]
    norm_low = jnp.pad(norm_low, ((0, 15), (0, spare)))
    attend_move = Gather(links, jnp.concatenate([attend_low, norm_low], axis=0))
    combine_move, expand_move = Gather(links, combine_low), Gather(links, expand_low)
    half_rows = shard_rows // 2
    shrink_move = Gather(links, shrink_low, half_rows)
    moves = (attend_move, combine_move, expand_move, shrink_move)
    hidden_in, out_cotangent, *shards_low = lax.optimization_barrier(
        (hidden_in, out_cotangent, *(move.held["own"] for move in moves))
    )
    for move, shard in zip(moves, shards_low):
        move.held["own"] = shard
    links.round(
        lambda: attend_move.far()
        + combine_move.far()
        + attend_move.across("own")
        + expand_move.across("own")
    )
    hidden_low = reorder_columns(hidden_in, links.to_own)
    cotangent_low = reorder_columns(out_cotangent, links.to_own)
    factor = loss_numerator.astype(wide) / (4.0 * (1.0 + self_generated.astype(wide)))
    branch_grad_low = (factor[:, None] * cotangent_low.astype(wide)).astype(low_type)
    out_grad_own = links.own_rows(factor)[:, None] * links.own_rows(cotangent_low).astype(wide)
    segments = jnp.stack([segment_ids(lengths, row_length) for lengths in episode_lengths])
    scaled_one, _ = norm_parts(hidden_low.astype(wide))
    scaled_one, branch_grad_low, segments = links.round(
        lambda: attend_move.near() + attend_move.across("far") + combine_move.across("pair"),
        [scaled_one, branch_grad_low, segments],
    )
    links.round(lambda: combine_move.near() + expand_move.far() + attend_move.across("near"))

    norm_values = jnp.concatenate(
        [
            part[first + shard_rows, : norm_rows * norm_columns].reshape(norm_rows, -1)
            for part, first in attend_move.parts()
        ],
        axis=1,
    ).astype(wide)
    normed_low = (scaled_one * norm_values[0] + norm_values[1]).astype(low_type)

    (normed_low,) = links.round(
        lambda: expand_move.near() + combine_move.across("near") + expand_move.across("far"),
        [normed_low],
    )
    attend_full = attend_move.full(shard_rows)
    projected = dot_low(normed_low, attend_full, "nn")
    mixed_low = attention(projected, segments)
    combine_full = combine_move.full(shard_rows)
    attended = ReduceTensor(links, dot_low(mixed_low, combine_full, "nt"))

    links.round(
        lambda: attended.first()
        + shrink_move.out("far0", shrink_move.half("own", 0), 2)
        + expand_move.across("near0", expand_move.half("near", 0)),
        [attended.partial],
    )
    hidden_own = links.own_rows(hidden_low).astype(wide)
    links.round(
        lambda: attended.second()
        + shrink_move.out("far1", shrink_move.half("own", 1), 2)
        + expand_move.across("near1", expand_move.half("near", 1))
    )
    residual = hidden_own + attended.total()
    scaled_two, inverse_two = norm_parts(residual)
    normed_two = GatherTensor(
        links, (scaled_two * norm_values[2] + norm_values[3]).astype(low_type)
    )
    (normed_two.own,) = links.round(
        lambda: normed_two.first()
        + shrink_move.out("near_own", shrink_move.held["own"], 1)
        + shrink_move.across("own"),
        [normed_two.own],
    )
    links.round(
        lambda: normed_two.second()
        + shrink_move.out("near_far", shrink_move.joined("far0", "far1"), 1)
        + shrink_move.across("far", shrink_move.joined("far0", "far1"))
    )
    links.round(lambda: shrink_move.across("near_own") + shrink_move.across("near_far"))
    normed_two_low = normed_two.full()
    expand_full = expand_move.full(shard_rows)
    expanded, activated_low = matmul(
        normed_two_low,
        expand_full,
        "nn",
        lambda made: (made, gelu_parts(made)[0]),
        [wide, low_type],
    )

    def gradient_rows(left, right):
        return lambda first, last: dot_low(left, right, "tn", first, last)

    shrink_back = Reduce(links, shard_rows, gradient_rows(branch_grad_low, activated_low))

    expanded, activated_low, *_ = links.round(
        shrink_back.first, [expanded, activated_low, *shrink_back.terms()]
    )
    shrink_full = shrink_move.full(half_rows)
    (expanded_grad_low,) = matmul(
        branch_grad_low,
        shrink_full,
        "nn",
        lambda made, before: (made * gelu_parts(before)[1],),
        [low_type],
        expanded,
    )
    normed_two_back = ReduceTensor(links, dot_low(expanded_grad_low, expand_full, "nt"))

    normed_two_back.partial, expanded_grad_low, activated_low = links.round(
        lambda: normed_two_back.first() + shrink_back.second(1) + shrink_back.near(1),
        [normed_two_back.partial, expanded_grad_low, activated_low],
    )
    expand_back = Reduce(links, shard_rows, gradient_rows(normed_two_low, expanded_grad_low))
    links.round(
        lambda: normed_two_back.second() + shrink_back.second(0) + shrink_back.near(0),
        [*expand_back.away.values()],
    )
    residual_from_norm, gain_two_grad, shift_two_grad = norm_back(
        normed_two_back.total(), scaled_two, inverse_two, norm_values[2]
    )
    residual_grad = out_grad_own + residual_from_norm
    attended_grad = GatherTensor(links, residual_grad.astype(low_type))

    attended_grad.own, activated_low = links.round(
        lambda: attended_grad.first() + expand_back.first(1) + shrink_back.far(1),
        [attended_grad.own, activated_low],
    )
    branch = ReduceTensor(links, dot_low(activated_low, shrink_full, "nt"))
    links.round(
        lambda: attended_grad.second()
        + branch.first()
        + expand_back.first(0)
        + shrink_back.far(0),
        [branch.partial],
    )
    links.round(
        lambda: branch.second() + expand_back.second() + expand_back.near(),
        expand_back.terms(),
    )
    attended_grad_low = attended_grad.full()
    mixed_grad = dot_low(attended_grad_low, combine_full, "nn")
    projected_grad = attention(projected, segments, mixed_grad)
    combine_back = Reduce(links, shard_rows, gradient_rows(attended_grad_low, mixed_low))
    attend_back = Reduce(links, shard_rows, gradient_rows(normed_low, projected_grad))
    normed_one_back = ReduceTensor(links, dot_low(projected_grad, attend_full, "nt"))

    shrink_back.mine, *_ = links.round(
        lambda: normed_one_back.first() + combine_back.both() + expand_back.far(1),
        [shrink_back.mine, normed_one_back.partial, *attend_back.terms(), *combine_back.terms()],
    )
    output = GatherTensor(
        links,
        reorder_columns((residual + branch.total()).astype(low_type), links.from_own),
    )
    combine_back.split_both()
    links.round(
        lambda: normed_one_back.second()
        + attend_back.first()
        + combine_back.near()
        + expand_back.far(0)
    )
    shrink_sum = turned(shrink_back.total())
    scaled_own, inverse_own = norm_parts(hidden_own)
    links.round(
        lambda: output.first() + attend_back.second() + attend_back.near() + combine_back.far(),
        [output.own],
    )
    hidden_from_norm, gain_one_grad, shift_one_grad = norm_back(
        normed_one_back.total(), scaled_own, inverse_own, norm_values[0]
    )
    input_own = reorder_columns((residual_grad + hidden_from_norm).astype(low_type), links.from_own)
    input_back = GatherTensor(links, input_own)
    input_back.first_now()
    norm_grads = ReduceSmall(
        links,
        links.sum_tensor(jnp.stack([gain_one_grad, shift_one_grad, gain_two_grad, shift_two_grad])),
    )
    for value, send, store, key in norm_grads.first():
        store[key] = send(value)
    input_half = input_back.terms()

    expand_back.mine, *input_half = links.round(
        lambda: input_back.second() + output.second() + attend_back.far(),
        [expand_back.mine, *input_half],
    )
    expand_sum = expand_back.total()
    combine_sum = turned(combine_back.total())
    input_back.carry(*input_half)
    layer_output = output.full()
    input_gradient = input_back.full().astype(wide)
    (input_gradient, layer_output) = links.round(norm_grads.outward, [input_gradient, layer_output])
    norm_sum = norm_grads.total()
    attend_sum = attend_back.total().reshape(attend_weights.shape)
    kinds = (
        (
            attend_weights,
            attend_first,
            attend_second,
            attend_average,
            attend_sum,
            matrix_rate,
            weight_decay,
        ),
        (
            combine_weights,
            combine_first,
            combine_second,
            combine_average,
            combine_sum,
            matrix_rate,
            weight_decay,
        ),
        (
            expand_weights,
            expand_first,
            expand_second,
            expand_average,
            expand_sum,
            matrix_rate,
            weight_decay,
        ),
        (
            shrink_weights,
            shrink_first,
            shrink_second,
            shrink_average,
            shrink_sum,
            matrix_rate,
            weight_decay,
        ),
        (
            layernorm_params,
            layernorm_first,
            layernorm_second,
            layernorm_average,
            norm_sum,
            norm_rate,
            0.0,
        ),
    )
    results = [layer_output, input_gradient]
    for master, moment, square, average, gradient, rate_value, decay_value in kinds:
        master_new, moment_new, square_new = adam_update(
            master, moment, square, gradient, rate_value, decay_value
        )
        smooth_new = average_decay * average + (1.0 - average_decay) * master_new
        results.extend(
            [master_new, moment_new, square_new, smooth_new, master_new.astype(jnp.bfloat16)]
        )
    return tuple(results)


def solution(mesh):
    placed = (
        P("dp", None),
        P("dp", None),
        P("dp", None),
        P("dp"),
        P("dp"),
        P("dp", None, "tensor"),
        P("dp", None, "tensor"),
        P("dp", None, "tensor"),
        P("dp", None, "tensor"),
        P("tensor", "dp"),
        P("tensor", "dp"),
        P("tensor", "dp"),
        P("tensor", "dp"),
        P("dp", "tensor"),
        P("dp", "tensor"),
        P("dp", "tensor"),
        P("dp", "tensor"),
        P("tensor", "dp"),
        P("tensor", "dp"),
        P("tensor", "dp"),
        P("tensor", "dp"),
        P(None, "dp"),
        P(None, "dp"),
        P(None, "dp"),
        P(None, "dp"),
    )
    return jax.shard_map(
        functools.partial(shards, Links(mesh)),
        mesh=mesh,
        in_specs=placed,
        out_specs=(
            P("dp", None),
            P("dp", None),
            P("dp", None, "tensor"),
            P("dp", None, "tensor"),
            P("dp", None, "tensor"),
            P("dp", None, "tensor"),
            P("dp", None, "tensor"),
            P("tensor", "dp"),
            P("tensor", "dp"),
            P("tensor", "dp"),
            P("tensor", "dp"),
            P("tensor", "dp"),
            P("dp", "tensor"),
            P("dp", "tensor"),
            P("dp", "tensor"),
            P("dp", "tensor"),
            P("dp", "tensor"),
            P("tensor", "dp"),
            P("tensor", "dp"),
            P("tensor", "dp"),
            P("tensor", "dp"),
            P("tensor", "dp"),
            P(None, "dp"),
            P(None, "dp"),
            P(None, "dp"),
            P(None, "dp"),
            P(None, "dp"),
        ),
        check_vma=False,
    )
```

time: 872 us -> 836 us (0.959)
  Pallas kernels: 33.4 us -> 197 us
  matrix products: 135 us -> 0 us
  waiting for transfers between devices: 373 us -> 326 us
  local copies, waits for them, and re-layouts: 153 us -> 108 us
  starting transfers between devices: 53.2 us -> 67.6 us
  other arithmetic: 111 us -> 124 us
    pallas_call x0 -> x22, Pallas kernels: none -> 164 us  [the longest x20 135 us: matmul(): pl.pallas_call(kernel, out_shape=shapes, grid=(columns // along, rows //...]
    dot_general x32 -> x0, matrix products: 135 us -> none  [the longest x18 87 us: dot_low(): jnp.einsum(spec, left, right, preferred_element_type=wide).astype(low_type)]
    ppermute x36 -> x47, waiting for transfers between devices: 356 us -> 244 us  [flip(): return lax.ppermute(value, 'dp', pairs)]
    ppermute x18, waiting for transfers between devices: 16.7 us -> 82.7 us  [turn(): return lax.ppermute(value, 'tensor', pairs)]
    unnamed x239 -> x230, local copies, waits for them, and re-layouts: 79.5 us -> 51.4 us
    ppermute x36 -> x47, starting transfers between devices: 41.6 us -> 56.3 us  [flip(): return lax.ppermute(value, 'dp', pairs)]
    convert_element_type x11 -> x13, other arithmetic: 27.5 us -> 37.7 us  [the longest x4 12.8 us: near(): sums.astype(low_type)]
    add x13 -> x11, other arithmetic: 17.8 us -> 22.6 us  [the longest x4 11.5 us: total(): self.sums(*span) + self.got('far', 0, *span, self.rows).astype(wide)]
  transfers between devices with their start and end apart: 54 -> 65, of which waited for: 27 -> 28; matrix products, arithmetic and copies ran while one was open for 36% -> 17% of each run, Pallas kernels for 4% -> 24%
where the time goes in v5:
time: 836 us; the launch traced here: 825 us
  waiting for transfers between devices  326 us (39%)
  Pallas kernels  197 us (24%)
  other arithmetic  124 us (15%)
  local copies, waits for them, and re-layouts  108 us (13%)
  starting transfers between devices  67.6 us (8%)
    ppermute x47, waiting for transfers between devices, flip(): return lax.ppermute(value, 'dp', pairs)  244 us
    pallas_call x20, Pallas kernels, matmul(): pl.pallas_call(kernel, out_shape=shapes, grid=(columns // along, rows //...  135 us
    ppermute x18, waiting for transfers between devices, turn(): return lax.ppermute(value, 'tensor', pairs)  82.7 us
    ppermute x47, starting transfers between devices, flip(): return lax.ppermute(value, 'dp', pairs)  56.3 us
    unnamed x230, local copies, waits for them, and re-layouts  51.4 us
    pallas_call x4, Pallas kernels, reorder_columns(): pl.pallas_call(copy_block, out_shape=jax.ShapeDtypeStruct(values.shape, v...  26.6 us
    dynamic_update_slice x16, local copies, waits for them, and re-layouts, joined(): full = lax.dynamic_update_slice_in_dim(full, part, place, 0)  23.7 us
    pallas_call x1, Pallas kernels, attention(): pl.pallas_call(attend_back_kernel, out_shape=jax.ShapeDtypeStruct(project...  19.2 us
  transfers between devices with their start and end apart: 65, of which 28 were waited for; matrix products, arithmetic and copies ran while one was open for 17% of the time, Pallas kernels for 24%

profile of v5, /device:TPU:0, one launch (start us, length us, event | category | flops | bytes accessed | tf_op | source)
XLA Modules:
  0.0 825.1 jit_solution(3313757721315693726)
XLA Ops:
  44.2 17.5 %collective-permute-done.1.refs_1_ = bf16[256,512]{1,0:T(8,128)(2,1)S(1)} collective-permute-done((bf16[256,512]{1,0:T(8,128)(2,1)S(1)}, bf16[256,512]{1,0:T(8,128)(2,1)S(1)}, u32[]{:S(2)}, u32[]{:S(2)}) %collective-permute-start.1) | collective-permute-done | bytes 262176 | tf_op jit(solution)/shard_map/ppermute | solution.py:350
  64.7 29.4 %collective-permute-done.6.refs_3_ = bf16[512,512]{1,0:T(8,128)(2,1)S(1)} collective-permute-done((bf16[512,512]{1,0:T(8,128)(2,1)S(1)}, bf16[512,512]{1,0:T(8,128)(2,1)S(1)}, u32[]{:S(2)}, u32[]{:S(2)}) %collective-permute-start.6) | collective-permute-done | bytes 524320 | tf_op jit(solution)/shard_map/ppermute | solution.py:350
  107.6 28.9 %collective-permute-done.9.refs_5_ = bf16[544,1536]{1,0:T(8,128)(2,1)} collective-permute-done((bf16[544,1536]{1,0:T(8,128)(2,1)}, bf16[544,1536]{1,0:T(8,128)(2,1)}, u32[]{:S(2)}, u32[]{:S(2)}) %collective-permute-start.9) | collective-permute-done | bytes 1671200 | tf_op jit(solution)/shard_map/ppermute | solution.py:350
  165.2 9.3 %shard_map.459.query_ref.key_ref.value_ref = bf16[1024,1536]{1,0:T(8,128)(2,1)S(1)} custom-call(bf16[1024,2048]{1,0:T(8,128)(2,1)S(1)} %copy-done, bf16[272,1536]{1,0:T(8,128)(2,1)S(1)} %copy-done.22, bf16[272,1536]{1,0:T(8,128)(2,1)S(1)} %copy-done.25, bf16[544,1536]{1,0:T(8,128)(2,1)} %collective-permute-done.4.refs_2_, ...), custom_call_target="tpu_custom_call" | custom-call | flops 644245120 | bytes 1402470 | tf_op jit(solution)/shard_map/pallas_call | solution.py:151
  174.6 10.0 %shard_map.460.left_ref.refs_0_ = bf16[1024,512]{1,0:T(8,128)(2,1)S(1)} custom-call(bf16[1024,1536]{1,0:T(8,128)(2,1)S(1)} %shard_map.459.query_ref.key_ref.value_ref, bf16[1024,1536]{1,0:T(8,128)(2,1)S(1)} %shard_map.459.query_ref.key_ref.value_ref, bf16[1024,1536]{1,0:T(8,128)(2,1)S(1)} %shard_map.459.query_ref.key_ref.value_ref, ...), custom_call_target="tpu_custom_call" | custom-call | flops 214748368 | bytes 629145 | tf_op jit(solution)/shard_map/pallas_call | solution.py:246
  208.4 23.9 %collective-permute-done.14.refs_1_ = bf16[128,2048]{1,0:T(8,128)(2,1)} collective-permute-done((bf16[128,2048]{1,0:T(8,128)(2,1)}, bf16[128,2048]{1,0:T(8,128)(2,1)}, u32[]{:S(2)}, u32[]{:S(2)}) %collective-permute-start.14) | collective-permute-done | bytes 524320 | tf_op jit(solution)/shard_map/ppermute | solution.py:350
  243.5 20.0 %collective-permute-done.16 = bf16[256,2048]{1,0:T(8,128)(2,1)} collective-permute-done((bf16[256,2048]{1,0:T(8,128)(2,1)}, bf16[256,2048]{1,0:T(8,128)(2,1)}, u32[]{:S(2)}, u32[]{:S(2)}) %collective-permute-start.16) | collective-permute-done | bytes 1048608 | tf_op jit(solution)/shard_map/ppermute | solution.py:374
  275.2 18.3 %collective-permute-done.19 = bf16[256,2048]{1,0:T(8,128)(2,1)} collective-permute-done((bf16[256,2048]{1,0:T(8,128)(2,1)}, bf16[256,2048]{1,0:T(8,128)(2,1)}, u32[]{:S(2)}, u32[]{:S(2)}) %collective-permute-start.19) | collective-permute-done | bytes 1048608 | tf_op jit(solution)/shard_map/ppermute | solution.py:374
  298.5 24.5 %collective-permute-done.23.refs_4_ = bf16[256,2048]{1,0:T(8,128)(2,1)} collective-permute-done((bf16[256,2048]{1,0:T(8,128)(2,1)S(1)}, bf16[256,2048]{1,0:T(8,128)(2,1)}, u32[]{:S(2)}, u32[]{:S(2)}) %collective-permute-start.23) | collective-permute-done | bytes 1048608 | tf_op jit(solution)/shard_map/ppermute | solution.py:350
  333.0 17.2 %shard_map.462 = (f32[1024,2048]{1,0:T(8,128)}, bf16[1024,2048]{1,0:T(8,128)(2,1)S(1)}) custom-call(bf16[1024,2048]{1,0:T(8,128)(2,1)} %copy-done.2, bf16[256,2048]{1,0:T(8,128)(2,1)S(1)} %copy-done.15, bf16[256,2048]{1,0:T(8,128)(2,1)} %collective-permute-done.8.refs_1_, bf16[512,2048]{1,0:T(8,128)(2,1)} %collective-permute-done.11.refs_2_, ...), custom_call_target="tpu_custom_call" | custom-call | flops 858993472 | bytes 2516582 | tf_op jit(solution)/shard_map/pallas_call | solution.py:151
  374.8 19.1 %shard_map.466.left_ref.refs_0_ = bf16[1024,2048]{1,0:T(8,128)(2,1)S(1)} custom-call(bf16[1024,2048]{1,0:T(8,128)(2,1)} %multiply_convert_fusion.left_ref, bf16[256,2048]{1,0:T(8,128)(2,1)} %bitcast.39.refs_0_, bf16[128,2048]{1,0:T(8,128)(2,1)} %collective-permute-done.14.refs_1_, bf16[128,2048]{1,0:T(8,128)(2,1)} %collective-permute-done.17.refs_2_, ...), custom_call_target="tpu_custom_call" | custom-call | flops 858993472 | bytes 2516582 | tf_op jit(solution)/shard_map/pallas_call | solution.py:151
  397.2 13.1 %shard_map.467 = bf16[1024,2048]{1,0:T(8,128)(2,1)S(1)} custom-call(bf16[1024,2048]{1,0:T(8,128)(2,1)} %copy-done.5, bf16[256,2048]{1,0:T(8,128)(2,1)S(1)} %copy-done.16, bf16[256,2048]{1,0:T(8,128)(2,1)} %collective-permute-done.8.refs_1_, bf16[512,2048]{1,0:T(8,128)(2,1)} %collective-permute-done.11.refs_2_, ...), custom_call_target="tpu_custom_call" | custom-call | flops 858993472 | bytes 1677721 | tf_op jit(solution)/shard_map/pallas_call | solution.py:151
  410.6 8.5 %collective-permute-done.27 = bf16[512,2048]{1,0:T(8,128)(2,1)} collective-permute-done((bf16[512,2048]{1,0:T(8,128)(2,1)}, bf16[512,2048]{1,0:T(8,128)(2,1)}, u32[]{:S(2)}, u32[]{:S(2)}) %collective-permute-start.27) | collective-permute-done | bytes 2097184 | tf_op jit(solution)/shard_map/ppermute | solution.py:350
  428.1 20.6 %collective-permute-done.29 = bf16[256,2048]{1,0:T(8,128)(2,1)} collective-permute-done((bf16[256,2048]{1,0:T(8,128)(2,1)}, bf16[256,2048]{1,0:T(8,128)(2,1)}, u32[]{:S(2)}, u32[]{:S(2)}) %collective-permute-start.29) | collective-permute-done | bytes 1048608 | tf_op jit(solution)/shard_map/ppermute | solution.py:350
  459.6 16.6 %collective-permute-done.31 = bf16[256,2048]{1,0:T(8,128)(2,1)S(1)} collective-permute-done((bf16[256,2048]{1,0:T(8,128)(2,1)S(1)}, bf16[256,2048]{1,0:T(8,128)(2,1)S(1)}, u32[]{:S(2)}, u32[]{:S(2)}) %collective-permute-start.31) | collective-permute-done | bytes 1048608 | tf_op jit(solution)/shard_map/ppermute | solution.py:374
  486.8 14.0 %shard_map.469 = bf16[1024,2048]{1,0:T(8,128)(2,1)S(1)} custom-call(bf16[1024,2048]{1,0:T(8,128)(2,1)} %copy-done.7, bf16[256,2048]{1,0:T(8,128)(2,1)} %bitcast.39.refs_0_, bf16[128,2048]{1,0:T(8,128)(2,1)} %collective-permute-done.14.refs_1_, bf16[128,2048]{1,0:T(8,128)(2,1)} %collective-permute-done.17.refs_2_, ...), custom_call_target="tpu_custom_call" | custom-call | flops 858993472 | bytes 1677721 | tf_op jit(solution)/shard_map/pallas_call | solution.py:151
  515.9 7.4 shard_map.471
  523.3 14.5 %collective-permute-done.40 = bf16[128,2048]{1,0:T(8,128)(2,1)} collective-permute-done((bf16[128,2048]{1,0:T(8,128)(2,1)}, bf16[128,2048]{1,0:T(8,128)(2,1)}, u32[]{:S(2)}, u32[]{:S(2)}) %collective-permute-start.40) | collective-permute-done | bytes 524320 | tf_op jit(solution)/shard_map/ppermute | solution.py:350
  558.4 19.2 %shard_map.473.left_ref.refs_0_ = bf16[1024,1536]{1,0:T(8,128)(2,1)S(1)} custom-call(bf16[1024,1536]{1,0:T(8,128)(2,1)S(1)} %shard_map.459.query_ref.key_ref.value_ref, bf16[1024,1536]{1,0:T(8,128)(2,1)S(1)} %shard_map.459.query_ref.key_ref.value_ref, bf16[1024,1536]{1,0:T(8,128)(2,1)S(1)} %shard_map.459.query_ref.key_ref.value_ref, ...), custom_call_target="tpu_custom_call" | custom-call | flops 536870912 | bytes 943718 | tf_op jit(solution)/shard_map/pallas_call | solution.py:255
  589.7 9.8 %shard_map.474 = bf16[1024,2048]{1,0:T(8,128)(2,1)S(1)} custom-call(bf16[1024,1536]{1,0:T(8,128)(2,1)S(1)} %shard_map.473.left_ref.refs_0_, bf16[272,1536]{1,0:T(8,128)(2,1)S(1)} %copy-done.23, bf16[272,1536]{1,0:T(8,128)(2,1)S(1)} %copy-done.26, bf16[544,1536]{1,0:T(8,128)(2,1)} %collective-permute-done.4.refs_2_, ...), custom_call_target="tpu_custom_call" | custom-call | flops 644245120 | bytes 1402470 | tf_op jit(solution)/shard_map/pallas_call | solution.py:151
  627.9 14.1 %collective-permute-done.45 = bf16[1024,512]{1,0:T(8,128)(2,1)} collective-permute-done((bf16[1024,512]{1,0:T(8,128)(2,1)}, bf16[1024,512]{1,0:T(8,128)(2,1)}, u32[]{:S(2)}, u32[]{:S(2)}) %collective-permute-start.45) | collective-permute-done | bytes 1048608 | tf_op jit(solution)/shard_map/ppermute | solution.py:350
  674.0 18.1 %collective-permute-done.49 = bf16[512,512]{1,0:T(8,128)(2,1)S(1)} collective-permute-done((bf16[512,512]{1,0:T(8,128)(2,1)}, bf16[512,512]{1,0:T(8,128)(2,1)S(1)}, u32[]{:S(2)}, u32[]{:S(2)}) %collective-permute-start.49) | collective-permute-done | bytes 524320 | tf_op jit(solution)/shard_map/ppermute | solution.py:350
  714.9 15.6 %collective-permute-done.60 = f32[4,2048]{1,0:T(4,128)S(1)} collective-permute-done((f32[4,2048]{1,0:T(4,128)S(1)}, f32[4,2048]{1,0:T(4,128)S(1)}, u32[]{:S(2)}, u32[]{:S(2)}) %collective-permute-start.60) | collective-permute-done | bytes 32800 | tf_op jit(solution)/shard_map/ppermute | solution.py:374
  740.1 12.1 %collective-permute-done.51 = bf16[256,2048]{1,0:T(8,128)(2,1)S(1)} collective-permute-done((bf16[256,2048]{1,0:T(8,128)(2,1)}, bf16[256,2048]{1,0:T(8,128)(2,1)S(1)}, u32[]{:S(2)}, u32[]{:S(2)}) %collective-permute-start.51) | collective-permute-done | bytes 1048608 | tf_op jit(solution)/shard_map/ppermute | solution.py:374
  (496 shorter events, 421.1 us)
Async XLA Ops:
  8.6 53.1 %collective-permute-start.3 = (bf16[256,2048]{1,0:T(8,128)(2,1)S(1)}, bf16[256,2048]{1,0:T(8,128)(2,1)}, u32[]{:S(2)}, u32[]{:S(2)}) collective-permute-start(bf16[256,2048]{1,0:T(8,128)(2,1)S(1)} %convert_element_type.327.refs_0_), channel_id=1, source_target_pairs={{0,4},{4,0},{8,12},{12,8},{16,20},{20,16},{24,28},{28,24},{1,5},{5... | collective-permute-start | bytes 3145736 | tf_op jit(solution)/shard_map/ppermute | solution.py:350
  11.6 50.1 %collective-permute-start = (bf16[272,1536]{1,0:T(8,128)(2,1)S(1)}, bf16[272,1536]{1,0:T(8,128)(2,1)S(1)}, u32[]{:S(2)}, u32[]{:S(2)}) collective-permute-start(bf16[272,1536]{1,0:T(8,128)(2,1)S(1)} %fusion.19.refs_0_), channel_id=1, source_target_pairs={{0,16},{4,20},{8,24},{12,28},{16,0},{20,4},{24,8},{28,12},{1,17},{... | collective-permute-start | bytes 2506760 | tf_op jit(solution)/shard_map/ppermute | solution.py:350
  14.2 47.5 %collective-permute-start.2 = (bf16[272,1536]{1,0:T(8,128)(2,1)S(1)}, bf16[272,1536]{1,0:T(8,128)(2,1)}, u32[]{:S(2)}, u32[]{:S(2)}) collective-permute-start(bf16[272,1536]{1,0:T(8,128)(2,1)S(1)} %fusion.19.refs_0_), channel_id=1, source_target_pairs={{0,4},{4,0},{8,12},{12,8},{16,20},{20,16},{24,28},{28,24},{1,5},{5... | collective-permute-start | bytes 2506760 | tf_op jit(solution)/shard_map/ppermute | solution.py:350
  14.7 47.0 %collective-permute-start.1 = (bf16[256,512]{1,0:T(8,128)(2,1)S(1)}, bf16[256,512]{1,0:T(8,128)(2,1)S(1)}, u32[]{:S(2)}, u32[]{:S(2)}) collective-permute-start(bf16[256,512]{1,0:T(8,128)(2,1)S(1)} %bitcast.41), channel_id=1, source_target_pairs={{0,16},{4,20},{8,24},{12,28},{16,0},{20,4},{24,8},{28,12},{1,17},{... | collective-permute-start | bytes 786440 | tf_op jit(solution)/shard_map/ppermute | solution.py:350
  61.9 37.5 %collective-permute-start.4 = (bf16[544,1536]{1,0:T(8,128)(2,1)S(1)}, bf16[544,1536]{1,0:T(8,128)(2,1)}, u32[]{:S(2)}, u32[]{:S(2)}) collective-permute-start(bf16[544,1536]{1,0:T(8,128)(2,1)S(1)} %pad_maximum_fusion.3), channel_id=1, source_target_pairs={{0,8},{4,12},{8,0},{12,4},{16,24},{20,28},{24,16},{28,20},{1,9},{5... | collective-permute-start | bytes 5013512 | tf_op jit(solution)/shard_map/ppermute | solution.py:350
  99.4 37.0 %collective-permute-start.9 = (bf16[544,1536]{1,0:T(8,128)(2,1)}, bf16[544,1536]{1,0:T(8,128)(2,1)}, u32[]{:S(2)}, u32[]{:S(2)}) collective-permute-start(bf16[544,1536]{1,0:T(8,128)(2,1)} %collective-permute-done.4.refs_2_), channel_id=1, source_target_pairs={{0,4},{4,0},{8,12},{12,8},{16,20},{20,16},{24,28},{28,24},{1,5},{5... | collective-permute-start | bytes 5013512 | tf_op jit(solution)/shard_map/ppermute | solution.py:350
  102.4 48.6 %collective-permute-start.8 = (bf16[256,2048]{1,0:T(8,128)(2,1)S(1)}, bf16[256,2048]{1,0:T(8,128)(2,1)}, u32[]{:S(2)}, u32[]{:S(2)}) collective-permute-start(bf16[256,2048]{1,0:T(8,128)(2,1)S(1)} %convert_element_type.327.refs_0_), channel_id=1, source_target_pairs={{0,16},{4,20},{8,24},{12,28},{16,0},{20,4},{24,8},{28,12},{1,17},{... | collective-permute-start | bytes 3145736 | tf_op jit(solution)/shard_map/ppermute | solution.py:350
  105.8 38.1 %collective-permute-start.7 = (bf16[512,512]{1,0:T(8,128)(2,1)}, bf16[512,512]{1,0:T(8,128)(2,1)}, u32[]{:S(2)}, u32[]{:S(2)}) collective-permute-start(bf16[512,512]{1,0:T(8,128)(2,1)} %copy-done.94), channel_id=1, source_target_pairs={{0,8},{4,12},{8,0},{12,4},{16,24},{20,28},{24,16},{28,20},{1,9},{5... | collective-permute-start | bytes 1572872 | tf_op jit(solution)/shard_map/ppermute | solution.py:350
  153.7 46.9 %collective-permute-start.11 = (bf16[512,2048]{1,0:T(8,128)(2,1)}, bf16[512,2048]{1,0:T(8,128)(2,1)}, u32[]{:S(2)}, u32[]{:S(2)}) collective-permute-start(bf16[512,2048]{1,0:T(8,128)(2,1)} %pad_maximum_fusion), channel_id=1, source_target_pairs={{0,8},{4,12},{8,0},{12,4},{16,24},{20,28},{24,16},{28,20},{1,9},{5... | collective-permute-start | bytes 6291464 | tf_op jit(solution)/shard_map/ppermute | solution.py:350
  154.2 43.4 %collective-permute-start.12 = (bf16[256,2048]{1,0:T(8,128)(2,1)}, bf16[256,2048]{1,0:T(8,128)(2,1)}, u32[]{:S(2)}, u32[]{:S(2)}) collective-permute-start(bf16[256,2048]{1,0:T(8,128)(2,1)} %collective-permute-done.8.refs_1_), channel_id=1, source_target_pairs={{0,4},{4,0},{8,12},{12,8},{16,20},{20,16},{24,28},{28,24},{1,5},{5... | collective-permute-start | bytes 3145736 | tf_op jit(solution)/shard_map/ppermute | solution.py:350
  325.4 43.9 %collective-permute-start.25 = (bf16[256,2048]{1,0:T(8,128)(2,1)}, bf16[256,2048]{1,0:T(8,128)(2,1)}, u32[]{:S(2)}, u32[]{:S(2)}) collective-permute-start(bf16[256,2048]{1,0:T(8,128)(2,1)} %collective-permute-done.20.refs_3_), channel_id=1, source_target_pairs={{0,4},{4,0},{8,12},{12,8},{16,20},{20,16},{24,28},{28,24},{1,5},{5... | collective-permute-start | bytes 3145736 | tf_op jit(solution)/shard_map/ppermute | solution.py:350
  326.0 46.8 %collective-permute-start.26 = (bf16[256,2048]{1,0:T(8,128)(2,1)}, bf16[256,2048]{1,0:T(8,128)(2,1)}, u32[]{:S(2)}, u32[]{:S(2)}) collective-permute-start(bf16[256,2048]{1,0:T(8,128)(2,1)} %collective-permute-done.23.refs_4_), channel_id=1, source_target_pairs={{0,4},{4,0},{8,12},{12,8},{16,20},{20,16},{24,28},{28,24},{1,5},{5... | collective-permute-start | bytes 3145736 | tf_op jit(solution)/shard_map/ppermute | solution.py:350
  372.7 46.4 %collective-permute-start.27 = (bf16[512,2048]{1,0:T(8,128)(2,1)}, bf16[512,2048]{1,0:T(8,128)(2,1)}, u32[]{:S(2)}, u32[]{:S(2)}) collective-permute-start(bf16[512,2048]{1,0:T(8,128)(2,1)} %shard_map.463), channel_id=1, source_target_pairs={{0,4},{4,0},{8,12},{12,8},{16,20},{20,16},{24,28},{28,24},{1,5},{5... | collective-permute-start | bytes 6291464 | tf_op jit(solution)/shard_map/ppermute | solution.py:350
  545.3 57.2 %collective-permute-start.42 = (bf16[512,2048]{1,0:T(8,128)(2,1)S(1)}, bf16[512,2048]{1,0:T(8,128)(2,1)S(1)}, u32[]{:S(2)}, u32[]{:S(2)}) collective-permute-start(bf16[512,2048]{1,0:T(8,128)(2,1)S(1)} %shard_map.470), channel_id=1, source_target_pairs={{0,4},{4,0},{8,12},{12,8},{16,20},{20,16},{24,28},{28,24},{1,5},{5... | collective-permute-start | bytes 6291464 | tf_op jit(solution)/shard_map/ppermute | solution.py:350
  546.0 56.5 %collective-permute-start.43 = (bf16[512,2048]{1,0:T(8,128)(2,1)}, bf16[512,2048]{1,0:T(8,128)(2,1)}, u32[]{:S(2)}, u32[]{:S(2)}) collective-permute-start(bf16[512,2048]{1,0:T(8,128)(2,1)} %add_convert_fusion.1), channel_id=1, source_target_pairs={{0,8},{4,12},{8,0},{12,4},{16,24},{20,28},{24,16},{28,20},{1,9},{5... | collective-permute-start | bytes 6291464 | tf_op jit(solution)/shard_map/ppermute | solution.py:350
  546.0 56.5 %collective-permute-start.41 = (bf16[256,2048]{1,0:T(8,128)(2,1)}, bf16[256,2048]{1,0:T(8,128)(2,1)}, u32[]{:S(2)}, u32[]{:S(2)}) collective-permute-start(bf16[256,2048]{1,0:T(8,128)(2,1)} %dynamic-slice_convert_fusion.1), channel_id=1, source_target_pairs={{0,2},{1,3},{2,0},{3,1},{4,6},{5,7},{6,4},{7,5},{8,10},{9,11},{10,... | collective-permute-start | bytes 3145736 | tf_op jit(solution)/shard_map/ppermute | solution.py:374
  606.3 37.8 %collective-permute-start.44 = (bf16[512,2048]{1,0:T(8,128)(2,1)}, bf16[512,2048]{1,0:T(8,128)(2,1)}, u32[]{:S(2)}, u32[]{:S(2)}) collective-permute-start(bf16[512,2048]{1,0:T(8,128)(2,1)} %constant_dynamic-slice_fusion), channel_id=1, source_target_pairs={{0,1},{1,0},{2,3},{3,2},{4,5},{5,4},{6,7},{7,6},{8,9},{9,8},{10,11... | collective-permute-start | bytes 6291464 | tf_op jit(solution)/shard_map/ppermute | solution.py:374
  649.8 45.7 %collective-permute-start.48 = (bf16[512,1536]{1,0:T(8,128)(2,1)}, bf16[512,1536]{1,0:T(8,128)(2,1)}, u32[]{:S(2)}, u32[]{:S(2)}) collective-permute-start(bf16[512,1536]{1,0:T(8,128)(2,1)} %shard_map.477), channel_id=1, source_target_pairs={{0,4},{4,0},{8,12},{12,8},{16,20},{20,16},{24,28},{28,24},{1,5},{5... | collective-permute-start | bytes 4718600 | tf_op jit(solution)/shard_map/ppermute | solution.py:350
  654.8 40.7 %collective-permute-start.47 = (bf16[256,2048]{1,0:T(8,128)(2,1)}, bf16[256,2048]{1,0:T(8,128)(2,1)}, u32[]{:S(2)}, u32[]{:S(2)}) collective-permute-start(bf16[256,2048]{1,0:T(8,128)(2,1)} %dynamic-slice_convert_fusion), channel_id=1, source_target_pairs={{0,2},{1,3},{2,0},{3,1},{4,6},{5,7},{6,4},{7,5},{8,10},{9,11},{10,... | collective-permute-start | bytes 3145736 | tf_op jit(solution)/shard_map/ppermute | solution.py:374
  702.5 50.7 %collective-permute-start.53 = (bf16[512,1536]{1,0:T(8,128)(2,1)}, bf16[512,1536]{1,0:T(8,128)(2,1)}, u32[]{:S(2)}, u32[]{:S(2)}) collective-permute-start(bf16[512,1536]{1,0:T(8,128)(2,1)} %shard_map.478), channel_id=1, source_target_pairs={{0,4},{4,0},{8,12},{12,8},{16,20},{20,16},{24,28},{28,24},{1,5},{5... | collective-permute-start | bytes 4718600 | tf_op jit(solution)/shard_map/ppermute | solution.py:350
  703.6 49.6 %collective-permute-start.54 = (bf16[512,1536]{1,0:T(8,128)(2,1)}, bf16[512,1536]{1,0:T(8,128)(2,1)}, u32[]{:S(2)}, u32[]{:S(2)}) collective-permute-start(bf16[512,1536]{1,0:T(8,128)(2,1)} %add_convert_fusion.2), channel_id=1, source_target_pairs={{0,8},{4,12},{8,0},{12,4},{16,24},{20,28},{24,16},{28,20},{1,9},{5... | collective-permute-start | bytes 4718600 | tf_op jit(solution)/shard_map/ppermute | solution.py:350
  703.6 49.6 %collective-permute-start.52 = (bf16[256,2048]{1,0:T(8,128)(2,1)}, bf16[256,2048]{1,0:T(8,128)(2,1)}, u32[]{:S(2)}, u32[]{:S(2)}) collective-permute-start(bf16[256,2048]{1,0:T(8,128)(2,1)} %shard_map.481), channel_id=1, source_target_pairs={{0,2},{1,3},{2,0},{3,1},{4,6},{5,7},{6,4},{7,5},{8,10},{9,11},{10,... | collective-permute-start | bytes 3145736 | tf_op jit(solution)/shard_map/ppermute | solution.py:374
  713.7 38.5 %collective-permute-start.51 = (bf16[256,2048]{1,0:T(8,128)(2,1)}, bf16[256,2048]{1,0:T(8,128)(2,1)S(1)}, u32[]{:S(2)}, u32[]{:S(2)}) collective-permute-start(bf16[256,2048]{1,0:T(8,128)(2,1)} %shard_map.482), channel_id=1, source_target_pairs={{0,2},{1,3},{2,0},{3,1},{4,6},{5,7},{6,4},{7,5},{8,10},{9,11},{10,... | collective-permute-start | bytes 3145736 | tf_op jit(solution)/shard_map/ppermute | solution.py:374
  762.3 37.5 %collective-permute-start.58 = (bf16[256,1536]{1,0:T(8,128)(2,1)}, bf16[256,1536]{1,0:T(8,128)(2,1)}, u32[]{:S(2)}, u32[]{:S(2)}) collective-permute-start(bf16[256,1536]{1,0:T(8,128)(2,1)} %add_convert_fusion.7), channel_id=1, source_target_pairs={{0,16},{4,20},{8,24},{12,28},{16,0},{20,4},{24,8},{28,12},{1,17},{... | collective-permute-start | bytes 2359304 | tf_op jit(solution)/shard_map/ppermute | solution.py:350
  (146 other events, 2160.4 us)

commit v6 on v5

--- a/solution.py
+++ b/solution.py
@@ -315,6 +315,42 @@
     )(values)
 
 
+def adam_kernel(rate_value, decay_value, terms, *refs):
+    gradient = sum(ref[...].astype(wide) for ref in refs[:terms])
+    states, outs = refs[terms : terms + 4], refs[terms + 4 :]
+    width = states[0].shape[2]
+    for j in range(states[0].shape[1]):
+        master, moment, square, average = (ref[:, j, :] for ref in states)
+        made = adam_update(
+            master,
+            moment,
+            square,
+            gradient[:, j * width : (j + 1) * width],
+            rate_value,
+            decay_value,
+        )
+        smooth = average_decay * average + (1.0 - average_decay) * made[0]
+        for ref, value in zip(outs, (*made, smooth)):
+            ref[:, j, :] = value
+
+
+def adam_planes(terms, states, rate_value, decay_value):
+    rows, planes, width = states[0].shape
+    block = tile(rows, 32)
+    flat = pl.BlockSpec((block, planes * width), lambda i: (i, 0))
+    deep = pl.BlockSpec((block, planes, width), lambda i: (i, 0, 0))
+    size = sum(x.size * x.dtype.itemsize for x in terms) + 32 * states[0].size
+    return pl.pallas_call(
+        functools.partial(adam_kernel, rate_value, decay_value, len(terms)),
+        out_shape=[jax.ShapeDtypeStruct(states[0].shape, wide)] * 4,
+        grid=(rows // block,),
+        in_specs=[flat] * len(terms) + [deep] * 4,
+        out_specs=[deep] * 4,
+        compiler_params=pltpu.CompilerParams(vmem_limit_bytes=kernel_memory),
+        cost_estimate=pl.CostEstimate(flops=0, bytes_accessed=size, transcendentals=0),
+    )(*terms, *states)
+
+
 class Links:
     outer_order = (0, 2, 1, 3)
 
@@ -358,9 +394,8 @@
         for (store, key), value in zip(self.running, held):
             store[key] = value
         moves = make_moves()
-        values = lax.optimization_barrier((*(value for value, *_ in moves), *held))
-        for value, (_, send, store, key) in zip(values, moves):
-            store[key] = send(value)
+        for value, send, store, key in moves:
+            store[key] = send(after(value, *held))
         count = len(self.running)
         self.running = [(store, key) for *_, store, key in moves]
         return held[count:]
@@ -436,17 +471,26 @@
 
 
 class Reduce:
-    def __init__(self, links, rows, make):
+    def __init__(self, links, rows, make, joint=False):
         self.links, self.rows = links, rows
         size = 2 * rows
         starts = [j * 2 * size for j in range(links.inner)]
-        self.away = {j: make(starts[j] + size, starts[j] + 2 * size) for j in range(1, links.inner)}
-        self.close = {j: make(starts[j], starts[j] + size) for j in range(1, links.inner)}
+        self.whole = {}
+        if joint:
+            self.whole = {j: make(starts[j], starts[j] + 2 * size) for j in range(1, links.inner)}
+            self.away = {j: made[size:] for j, made in self.whole.items()}
+            self.close = {j: made[:size] for j, made in self.whole.items()}
+        else:
+            ends = [start + 2 * size for start in starts]
+            self.away = {j: make(starts[j] + size, ends[j]) for j in range(1, links.inner)}
+            self.close = {j: make(starts[j], starts[j] + size) for j in range(1, links.inner)}
         self.mine = make(0, 2 * size)
         self.size = size
         self.held = {}
 
     def terms(self):
+        if self.whole:
+            return [*self.whole.values(), self.mine]
         return [*self.away.values(), *self.close.values(), self.mine]
 
     def span(self, part, size):
@@ -481,13 +525,8 @@
 
     def both(self):
         return [
-            (
-                jnp.concatenate([self.close[j], self.away[j]], axis=0),
-                self.links.across(0, j),
-                self.held,
-                ("both", j),
-            )
-            for j in self.away
+            (made, self.links.across(0, j), self.held, ("both", j))
+            for j, made in self.whole.items()
         ]
 
     def split_both(self):
@@ -513,6 +552,10 @@
         first, last = self.span(part, self.rows)
         sums = self.sums(self.rows + first, self.rows + last).astype(low_type)
         return [self.move("far", 0, part, sums, self.links.across(2, 0))]
+
+    def last_terms(self):
+        near = self.held["near", 0]
+        return [self.mine, near, *(self.held["close", j] for j in self.close), self.held["far", 0]]
 
     def total(self):
         parts = [None] if ("far", 0) in self.held else [0, 1]
@@ -528,33 +571,30 @@
         self.links, self.partial = links, partial
         self.held = {}
 
-    def half(self, j):
-        rows = self.partial.shape[0] // self.links.cores
-        at = lax.rem(self.links.core_at + j, self.links.cores)
-        return lax.dynamic_slice_in_dim(self.partial, at * rows, rows, 0)
+    def part(self, over_chips, over_cores):
+        links = self.links
+        rows = self.partial.shape[0] // links.group
+        chip = lax.rem(links.chip_at + over_chips, links.chips)
+        core = lax.rem(links.core_at + over_cores, links.cores)
+        return lax.dynamic_slice_in_dim(self.partial, (core * links.chips + chip) * rows, rows, 0)
 
     def first(self):
-        return [(self.half(1), self.links.along(0, 1), self.held, "half")]
-
-    def quarter(self, j):
-        links = self.links
-        sums = self.half(0).astype(wide) + self.held["half"].astype(wide)
-        rows = sums.shape[0] // links.chips
-        at = lax.rem(links.chip_at + j, links.chips)
-        return lax.dynamic_slice_in_dim(sums, at * rows, rows, 0)
+        return [
+            (self.part(j, 1), self.links.along(0, 1), self.held, ("half", j))
+            for j in reversed(range(self.links.chips))
+        ]
+
+    def sums(self, j):
+        return self.part(j, 0).astype(wide) + self.held["half", j].astype(wide)
 
     def second(self):
         return [
-            (self.quarter(j).astype(low_type), self.links.along(j, 0), self.held, j)
+            (self.sums(j).astype(low_type), self.links.along(j, 0), self.held, j)
             for j in range(1, self.links.chips)
         ]
 
-    def second_now(self):
-        for value, send, store, key in self.second():
-            store[key] = send(value)
-
     def total(self):
-        return self.quarter(0) + sum(
+        return self.sums(0) + sum(
             self.held[j].astype(wide) for j in range(1, self.links.chips)
         )
 
@@ -565,46 +605,32 @@
         self.held = {}
 
     def first(self):
+        chips = range(1, self.links.chips)
+        return [(self.own, self.links.along(j, 0), self.held, (j, 0)) for j in chips] + [
+            (self.own, self.links.along(0, 1), self.held, (0, 1))
+        ]
+
+    def second(self):
+        chips = range(1, self.links.chips)
         return [
-            (self.own, self.links.along(j, 0), self.held, j) for j in range(1, self.links.chips)
+            (self.held[j, 0], self.links.along(0, 1), self.held, (j, 1)) for j in chips
         ]
 
-    def first_now(self):
-        for value, send, store, key in self.first():
+    def now(self, moves):
+        for value, send, store, key in moves:
             store[key] = send(value)
 
-    def terms(self):
-        return [self.half()]
-
-    def carry(self, joined, *_):
-        self.whole_half = joined
-
-    @staticmethod
-    def joined(parts, at):
-        count, rows = len(parts), parts[0].shape[0]
-        full = jnp.zeros((count * rows,) + parts[0].shape[1:], parts[0].dtype)
-        for j, part in enumerate(parts):
-            place = lax.rem(at + count - j, count) * rows
-            full = lax.dynamic_update_slice_in_dim(full, part, place, 0)
+    def full(self):
+        links = self.links
+        rows = self.own.shape[0]
+        full = jnp.zeros((links.group * rows,) + self.own.shape[1:], self.own.dtype)
+        for (j, k), part in {(0, 0): self.own, **self.held}.items():
+            chip = lax.rem(links.chip_at + links.chips - j, links.chips)
+            core = lax.rem(links.core_at + k, links.cores)
+            full = lax.dynamic_update_slice_in_dim(
+                full, part, (core * links.chips + chip) * rows, 0
+            )
         return full
-
-    whole_half = None
-
-    def half(self):
-        links = self.links
-        if self.whole_half is not None:
-            return self.whole_half
-        return self.joined([self.own, *(self.held[j] for j in range(1, links.chips))], links.chip_at)
-
-    def second(self):
-        return [(self.half(), self.links.along(0, 1), self.held, "other")]
-
-    def second_now(self):
-        for value, send, store, key in self.second():
-            store[key] = send(value)
-
-    def full(self):
-        return self.joined([self.half(), self.held["other"]], self.links.core_at)
 
 
 class ReduceSmall:
@@ -689,18 +715,8 @@
     combine_move, expand_move = Gather(links, combine_low), Gather(links, expand_low)
     half_rows = shard_rows // 2
     shrink_move = Gather(links, shrink_low, half_rows)
-    moves = (attend_move, combine_move, expand_move, shrink_move)
-    hidden_in, out_cotangent, *shards_low = lax.optimization_barrier(
-        (hidden_in, out_cotangent, *(move.held["own"] for move in moves))
-    )
-    for move, shard in zip(moves, shards_low):
-        move.held["own"] = shard
-    links.round(
-        lambda: attend_move.far()
-        + combine_move.far()
-        + attend_move.across("own")
-        + expand_move.across("own")
-    )
+    later = (combine_move, shrink_move)
+    links.round(lambda: attend_move.far() + attend_move.across("own"))
     hidden_low = reorder_columns(hidden_in, links.to_own)
     cotangent_low = reorder_columns(out_cotangent, links.to_own)
     factor = loss_numerator.astype(wide) / (4.0 * (1.0 + self_generated.astype(wide)))
@@ -708,11 +724,21 @@
     out_grad_own = links.own_rows(factor)[:, None] * links.own_rows(cotangent_low).astype(wide)
     segments = jnp.stack([segment_ids(lengths, row_length) for lengths in episode_lengths])
     scaled_one, _ = norm_parts(hidden_low.astype(wide))
-    scaled_one, branch_grad_low, segments = links.round(
-        lambda: attend_move.near() + attend_move.across("far") + combine_move.across("pair"),
-        [scaled_one, branch_grad_low, segments],
-    )
-    links.round(lambda: combine_move.near() + expand_move.far() + attend_move.across("near"))
+    scaled_one, branch_grad_low, segments, *own = links.round(
+        lambda: attend_move.near()
+        + combine_move.far()
+        + attend_move.across("far")
+        + expand_move.across("own"),
+        [scaled_one, branch_grad_low, segments, *(move.held["own"] for move in later)],
+    )
+    for move, shard in zip(later, own):
+        move.held["own"] = shard
+    links.round(
+        lambda: combine_move.near()
+        + expand_move.far()
+        + attend_move.across("near")
+        + combine_move.across("pair")
+    )
 
     norm_values = jnp.concatenate(
         [
@@ -798,7 +824,7 @@
     expand_back = Reduce(links, shard_rows, gradient_rows(normed_two_low, expanded_grad_low))
     links.round(
         lambda: normed_two_back.second() + shrink_back.second(0) + shrink_back.near(0),
-        [*expand_back.away.values()],
+        expand_back.terms(),
     )
     residual_from_norm, gain_two_grad, shift_two_grad = norm_back(
         normed_two_back.total(), scaled_two, inverse_two, norm_values[2]
@@ -818,14 +844,13 @@
         + shrink_back.far(0),
         [branch.partial],
     )
-    links.round(
-        lambda: branch.second() + expand_back.second() + expand_back.near(),
-        expand_back.terms(),
-    )
     attended_grad_low = attended_grad.full()
     mixed_grad = dot_low(attended_grad_low, combine_full, "nn")
     projected_grad = attention(projected, segments, mixed_grad)
-    combine_back = Reduce(links, shard_rows, gradient_rows(attended_grad_low, mixed_low))
+    (projected_grad,) = links.round(
+        lambda: branch.second() + expand_back.second() + expand_back.near(), [projected_grad]
+    )
+    combine_back = Reduce(links, shard_rows, gradient_rows(attended_grad_low, mixed_low), True)
     attend_back = Reduce(links, shard_rows, gradient_rows(normed_low, projected_grad))
     normed_one_back = ReduceTensor(links, dot_low(projected_grad, attend_full, "nt"))
 
@@ -846,46 +871,45 @@
     )
     shrink_sum = turned(shrink_back.total())
     scaled_own, inverse_own = norm_parts(hidden_own)
-    links.round(
-        lambda: output.first() + attend_back.second() + attend_back.near() + combine_back.far(),
-        [output.own],
-    )
     hidden_from_norm, gain_one_grad, shift_one_grad = norm_back(
         normed_one_back.total(), scaled_own, inverse_own, norm_values[0]
     )
     input_own = reorder_columns((residual_grad + hidden_from_norm).astype(low_type), links.from_own)
     input_back = GatherTensor(links, input_own)
-    input_back.first_now()
-    norm_grads = ReduceSmall(
-        links,
-        links.sum_tensor(jnp.stack([gain_one_grad, shift_one_grad, gain_two_grad, shift_two_grad])),
-    )
+    input_back.own, output.own = links.round(
+        lambda: attend_back.second()
+        + attend_back.near()
+        + input_back.first()[:-1]
+        + combine_back.far(),
+        [input_own, output.own],
+    )
+    output.now(output.first()[:-1])
+    norm_terms = jnp.stack([gain_one_grad, shift_one_grad, gain_two_grad, shift_two_grad])
+
+    (expand_back.mine, norm_terms) = links.round(
+        lambda: input_back.first()[-1:] + attend_back.far(), [expand_back.mine, norm_terms]
+    )
+    input_back.now(input_back.second())
+    output.now(output.first()[-1:])
+    output.now(output.second())
+    norm_grads = ReduceSmall(links, links.sum_tensor(norm_terms))
     for value, send, store, key in norm_grads.first():
         store[key] = send(value)
-    input_half = input_back.terms()
-
-    expand_back.mine, *input_half = links.round(
-        lambda: input_back.second() + output.second() + attend_back.far(),
-        [expand_back.mine, *input_half],
-    )
     expand_sum = expand_back.total()
     combine_sum = turned(combine_back.total())
-    input_back.carry(*input_half)
     layer_output = output.full()
     input_gradient = input_back.full().astype(wide)
-    (input_gradient, layer_output) = links.round(norm_grads.outward, [input_gradient, layer_output])
+    (input_gradient, layer_output, norm_grads.split) = links.round(
+        norm_grads.outward, [input_gradient, layer_output, norm_grads.split]
+    )
     norm_sum = norm_grads.total()
-    attend_sum = attend_back.total().reshape(attend_weights.shape)
+    attend_new = adam_planes(
+        attend_back.last_terms(),
+        (attend_weights, attend_first, attend_second, attend_average),
+        matrix_rate,
+        weight_decay,
+    )
     kinds = (
-        (
-            attend_weights,
-            attend_first,
-            attend_second,
-            attend_average,
-            attend_sum,
-            matrix_rate,
-            weight_decay,
-        ),
         (
             combine_weights,
             combine_first,
@@ -923,7 +947,7 @@
             0.0,
         ),
     )
-    results = [layer_output, input_gradient]
+    results = [layer_output, input_gradient, *attend_new, attend_new[0].astype(low_type)]
     for master, moment, square, average, gradient, rate_value, decay_value in kinds:
         master_new, moment_new, square_new = adam_update(
             master, moment, square, gradient, rate_value, decay_value

time: 836 us -> 775 us (0.927)
  waiting for transfers between devices: 326 us -> 271 us
  local copies, waits for them, and re-layouts: 108 us -> 97.4 us
    ppermute x47, waiting for transfers between devices: 244 us -> 206 us  [flip(): return lax.ppermute(value, 'dp', pairs)]
    ppermute x18 -> x26, waiting for transfers between devices: 82.7 us -> 64.9 us  [turn(): return lax.ppermute(value, 'tensor', pairs)]
    add x4 -> x1, other arithmetic: 11 us -> 0.52 us  [place(): placed = (outer & 1) * 2 + (outer >> 1)]
    convert_element_type x1 -> x5, other arithmetic: 0.08 us -> 9.73 us  [the longest x4 9.37 us: second(): self.sums(j).astype(low_type)]
    unnamed x230 -> x295, local copies, waits for them, and re-layouts: 51.4 us -> 56.8 us
    pallas_call x20 -> x19, Pallas kernels: 135 us -> 135 us  [matmul(): pl.pallas_call(kernel, out_shape=shapes, grid=(columns // along, rows //...]
  transfers between devices with their start and end apart: 65 -> 73, of which waited for: 28 -> 28; matrix products, arithmetic and copies ran while one was open for 17% -> 21% of each run, Pallas kernels for 24% -> 27%
where the time goes in v6:
time: 775 us; the launch traced here: 764 us
  waiting for transfers between devices  271 us (35%)
  Pallas kernels  205 us (26%)
  other arithmetic  117 us (15%)
  local copies, waits for them, and re-layouts  97.4 us (13%)
  starting transfers between devices  70.8 us (9%)
    ppermute x47, waiting for transfers between devices, flip(): return lax.ppermute(value, 'dp', pairs)  206 us
    pallas_call x19, Pallas kernels, matmul(): pl.pallas_call(kernel, out_shape=shapes, grid=(columns // along, rows //...  135 us
    ppermute x26, waiting for transfers between devices, turn(): return lax.ppermute(value, 'tensor', pairs)  64.9 us
    ppermute x47, starting transfers between devices, flip(): return lax.ppermute(value, 'dp', pairs)  57.2 us
    unnamed x295, local copies, waits for them, and re-layouts  56.8 us
    pallas_call x4, Pallas kernels, reorder_columns(): pl.pallas_call(copy_block, out_shape=jax.ShapeDtypeStruct(values.shape, v...  26.6 us
    pallas_call x1, Pallas kernels, attention(): pl.pallas_call(attend_back_kernel, out_shape=jax.ShapeDtypeStruct(project...  19.4 us
    dynamic_update_slice x16, local copies, waits for them, and re-layouts, full(): lax.dynamic_update_slice_in_dim(full, part, (core * links.chips + chip) *...  15.8 us
  transfers between devices with their start and end apart: 73, of which 28 were waited for; matrix products, arithmetic and copies ran while one was open for 21% of the time, Pallas kernels for 27%

profile of v6, /device:TPU:0, one launch (start us, length us, event | category | flops | bytes accessed | tf_op | source)
XLA Modules:
  0.0 763.6 jit_solution(1808791161719285408)
XLA Ops:
  10.1 7.3 shard_map.458
  22.0 7.4 shard_map.457
  50.9 36.9 %collective-permute-done.3.refs_1_ = bf16[256,512]{1,0:T(8,128)(2,1)S(1)} collective-permute-done((bf16[256,512]{1,0:T(8,128)(2,1)S(1)}, bf16[256,512]{1,0:T(8,128)(2,1)S(1)}, u32[]{:S(2)}, u32[]{:S(2)}) %collective-permute-start.3) | collective-permute-done | bytes 262176 | tf_op jit(solution)/shard_map/ppermute | solution.py:386
  103.5 26.5 %collective-permute-done.8.refs_5_ = bf16[544,1536]{1,0:T(8,128)(2,1)} collective-permute-done((bf16[544,1536]{1,0:T(8,128)(2,1)S(1)}, bf16[544,1536]{1,0:T(8,128)(2,1)}, u32[]{:S(2)}, u32[]{:S(2)}) %collective-permute-start.8) | collective-permute-done | bytes 1671200 | tf_op jit(solution)/shard_map/ppermute | solution.py:386
  161.8 9.3 %shard_map.459.query_ref.key_ref.value_ref = bf16[1024,1536]{1,0:T(8,128)(2,1)S(1)} custom-call(bf16[1024,2048]{1,0:T(8,128)(2,1)S(1)} %copy-done, bf16[272,1536]{1,0:T(8,128)(2,1)S(1)} %copy-done.35, bf16[272,1536]{1,0:T(8,128)(2,1)S(1)} %copy-done.32, bf16[544,1536]{1,0:T(8,128)(2,1)S(1)} %copy-done.38, bf16[272,1536]{1,0:T(8,128)(2,1)S(1)} %copy-done.66, ...), custom_call_target="tpu_custom_call" | custom-call | flops 644245120 | bytes 1402470 | tf_op jit(solution)/shard_map/pallas_call | solution.py:151
  171.1 9.9 %shard_map.460.left_ref.refs_0_ = bf16[1024,512]{1,0:T(8,128)(2,1)S(1)} custom-call(bf16[1024,1536]{1,0:T(8,128)(2,1)S(1)} %shard_map.459.query_ref.key_ref.value_ref, bf16[1024,1536]{1,0:T(8,128)(2,1)S(1)} %shard_map.459.query_ref.key_ref.value_ref, bf16[1024,1536]{1,0:T(8,128)(2,1)S(1)} %shard_map.459.query_ref.key_ref.value_ref, ...), custom_call_target="tpu_custom_call" | custom-call | flops 214748368 | bytes 629145 | tf_op jit(solution)/shard_map/pallas_call | solution.py:246
  202.0 26.0 %collective-permute-done.15.refs_1_ = bf16[128,2048]{1,0:T(8,128)(2,1)} collective-permute-done((bf16[128,2048]{1,0:T(8,128)(2,1)}, bf16[128,2048]{1,0:T(8,128)(2,1)}, u32[]{:S(2)}, u32[]{:S(2)}) %collective-permute-start.15) | collective-permute-done | bytes 524320 | tf_op jit(solution)/shard_map/ppermute | solution.py:386
  234.9 21.4 %collective-permute-done.17 = bf16[256,2048]{1,0:T(8,128)(2,1)} collective-permute-done((bf16[256,2048]{1,0:T(8,128)(2,1)}, bf16[256,2048]{1,0:T(8,128)(2,1)}, u32[]{:S(2)}, u32[]{:S(2)}) %collective-permute-start.17) | collective-permute-done | bytes 1048608 | tf_op jit(solution)/shard_map/ppermute | solution.py:409
  266.2 19.7 %collective-permute-done.22.refs_3_ = bf16[256,2048]{1,0:T(8,128)(2,1)S(1)} collective-permute-done((bf16[256,2048]{1,0:T(8,128)(2,1)S(1)}, bf16[256,2048]{1,0:T(8,128)(2,1)S(1)}, u32[]{:S(2)}, u32[]{:S(2)}) %collective-permute-start.22) | collective-permute-done | bytes 1048608 | tf_op jit(solution)/shard_map/ppermute | solution.py:386
  289.6 21.4 %collective-permute-done.25.refs_4_ = bf16[256,2048]{1,0:T(8,128)(2,1)} collective-permute-done((bf16[256,2048]{1,0:T(8,128)(2,1)}, bf16[256,2048]{1,0:T(8,128)(2,1)}, u32[]{:S(2)}, u32[]{:S(2)}) %collective-permute-start.25) | collective-permute-done | bytes 1048608 | tf_op jit(solution)/shard_map/ppermute | solution.py:386
  319.9 16.9 %shard_map.462 = (f32[1024,2048]{1,0:T(8,128)}, bf16[1024,2048]{1,0:T(8,128)(2,1)S(1)}) custom-call(bf16[1024,2048]{1,0:T(8,128)(2,1)} %copy-done.2, bf16[256,2048]{1,0:T(8,128)(2,1)S(1)} %copy-done.23, bf16[256,2048]{1,0:T(8,128)(2,1)} %collective-permute-done.7.refs_1_, bf16[512,2048]{1,0:T(8,128)(2,1)} %collective-permute-done.11.refs_2_, ...), custom_call_target="tpu_custom_call" | custom-call | flops 858993472 | bytes 2516582 | tf_op jit(solution)/shard_map/pallas_call | solution.py:151
  360.4 18.3 %shard_map.466.left_ref.refs_0_ = bf16[1024,2048]{1,0:T(8,128)(2,1)S(1)} custom-call(bf16[1024,2048]{1,0:T(8,128)(2,1)} %multiply_convert_fusion.left_ref, bf16[256,2048]{1,0:T(8,128)(2,1)S(1)} %bitcast.43, bf16[128,2048]{1,0:T(8,128)(2,1)} %collective-permute-done.15.refs_1_, bf16[128,2048]{1,0:T(8,128)(2,1)S(1)} %copy-done.41, ...), custom_call_target="tpu_custom_call" | custom-call | flops 858993472 | bytes 2516582 | tf_op jit(solution)/shard_map/pallas_call | solution.py:151
  380.7 12.8 %shard_map.467 = bf16[1024,2048]{1,0:T(8,128)(2,1)S(1)} custom-call(bf16[1024,2048]{1,0:T(8,128)(2,1)} %copy-done.5, bf16[256,2048]{1,0:T(8,128)(2,1)S(1)} %copy-done.24, bf16[256,2048]{1,0:T(8,128)(2,1)} %collective-permute-done.7.refs_1_, bf16[512,2048]{1,0:T(8,128)(2,1)} %collective-permute-done.11.refs_2_, bf16[256,2048]{1,0:T(8,128)(2,1)S(1)} %copy-done.46, ...), custom_call_target="tpu_custom_call" | custom-call | flops 858993472 | bytes 1677721 | tf_op jit(solution)/shard_map/pallas_call | solution.py:151
  434.6 16.9 %collective-permute-done.34 = bf16[256,2048]{1,0:T(8,128)(2,1)S(1)} collective-permute-done((bf16[256,2048]{1,0:T(8,128)(2,1)S(1)}, bf16[256,2048]{1,0:T(8,128)(2,1)S(1)}, u32[]{:S(2)}, u32[]{:S(2)}) %collective-permute-start.34) | collective-permute-done | bytes 1048608 | tf_op jit(solution)/shard_map/ppermute | solution.py:409
  463.4 13.2 %shard_map.471 = bf16[1024,2048]{1,0:T(8,128)(2,1)S(1)} custom-call(bf16[1024,2048]{1,0:T(8,128)(2,1)} %copy-done.11, bf16[256,2048]{1,0:T(8,128)(2,1)S(1)} %bitcast.44, bf16[128,2048]{1,0:T(8,128)(2,1)} %collective-permute-done.15.refs_1_, bf16[128,2048]{1,0:T(8,128)(2,1)S(1)} %copy-done.41, bf16[256,2048]{1,0:T(8,128)(2,1)S(1)} %copy-done.49, ...), custom_call_target="tpu_custom_call" | custom-call | flops 858993472 | bytes 1677721 | tf_op jit(solution)/shard_map/pallas_call | solution.py:151
  476.6 13.2 %collective-permute-done.40 = bf16[128,2048]{1,0:T(8,128)(2,1)S(1)} collective-permute-done((bf16[128,2048]{1,0:T(8,128)(2,1)S(1)}, bf16[128,2048]{1,0:T(8,128)(2,1)S(1)}, u32[]{:S(2)}, u32[]{:S(2)}) %collective-permute-start.40) | collective-permute-done | bytes 524320 | tf_op jit(solution)/shard_map/ppermute | solution.py:386
  498.3 19.4 %shard_map.473.left_ref.refs_0_ = bf16[1024,1536]{1,0:T(8,128)(2,1)S(1)} custom-call(bf16[1024,1536]{1,0:T(8,128)(2,1)S(1)} %shard_map.459.query_ref.key_ref.value_ref, bf16[1024,1536]{1,0:T(8,128)(2,1)S(1)} %shard_map.459.query_ref.key_ref.value_ref, bf16[1024,1536]{1,0:T(8,128)(2,1)S(1)} %shard_map.459.query_ref.key_ref.value_ref, ...), custom_call_target="tpu_custom_call" | custom-call | flops 536870912 | bytes 943718 | tf_op jit(solution)/shard_map/pallas_call | solution.py:255
  556.0 9.9 %shard_map.474 = bf16[1024,2048]{1,0:T(8,128)(2,1)S(1)} custom-call(bf16[1024,1536]{1,0:T(8,128)(2,1)S(1)} %copy-done.8, bf16[272,1536]{1,0:T(8,128)(2,1)S(1)} %copy-done.36, bf16[272,1536]{1,0:T(8,128)(2,1)S(1)} %copy-done.33, bf16[544,1536]{1,0:T(8,128)(2,1)S(1)} %copy-done.39, bf16[272,1536]{1,0:T(8,128)(2,1)S(1)} %copy-done.67, ...), custom_call_target="tpu_custom_call" | custom-call | flops 644245120 | bytes 1402470 | tf_op jit(solution)/shard_map/pallas_call | solution.py:151
  595.6 8.8 %collective-permute-done.52 = bf16[128,2048]{1,0:T(8,128)(2,1)} collective-permute-done((bf16[128,2048]{1,0:T(8,128)(2,1)}, bf16[128,2048]{1,0:T(8,128)(2,1)}, u32[]{:S(2)}, u32[]{:S(2)}) %collective-permute-start.52) | collective-permute-done | bytes 524320 | tf_op jit(solution)/shard_map/ppermute | solution.py:386
  620.4 10.7 %collective-permute-done.53 = bf16[256,2048]{1,0:T(8,128)(2,1)S(1)} collective-permute-done((bf16[256,2048]{1,0:T(8,128)(2,1)S(1)}, bf16[256,2048]{1,0:T(8,128)(2,1)S(1)}, u32[]{:S(2)}, u32[]{:S(2)}) %collective-permute-start.53) | collective-permute-done | bytes 1048608 | tf_op jit(solution)/shard_map/ppermute | solution.py:409
  642.5 7.5 collective-permute-done.54
  665.6 12.5 %collective-permute-done.64 = bf16[256,2048]{1,0:T(8,128)(2,1)} collective-permute-done((bf16[256,2048]{1,0:T(8,128)(2,1)S(1)}, bf16[256,2048]{1,0:T(8,128)(2,1)}, u32[]{:S(2)}, u32[]{:S(2)}) %collective-permute-start.64) | collective-permute-done | bytes 1048608 | tf_op jit(solution)/shard_map/ppermute | solution.py:409
  682.3 12.3 %collective-permute-done.60 = bf16[256,512]{1,0:T(8,128)(2,1)S(1)} collective-permute-done((bf16[256,512]{1,0:T(8,128)(2,1)S(1)}, bf16[256,512]{1,0:T(8,128)(2,1)S(1)}, u32[]{:S(2)}, u32[]{:S(2)}) %collective-permute-start.60) | collective-permute-done | bytes 262176 | tf_op jit(solution)/shard_map/ppermute | solution.py:386
  746.4 7.6 %shard_map.482 = (f32[256,3,512]{2,1,0:T(4,128)S(1)}, f32[256,3,512]{2,1,0:T(4,128)S(1)}, f32[256,3,512]{2,1,0:T(4,128)S(1)}, f32[256,3,512]{2,1,0:T(4,128)S(1)}) custom-call(bf16[1024,1536]{1,0:T(8,128)(2,1)} %copy-done.14, bf16[512,1536]{1,0:T(8,128)(2,1)S(1)} %copy-done.62, bf16[512,1536]{1,0:T(8,128)(2,1)S(1)} %copy-done.64, ...), custom_call_target="tpu_custom_call" | custom-call | bytes 19660800 | tf_op jit(solution)/shard_map/pallas_call | solution.py:343
  (564 shorter events, 395.2 us)
Async XLA Ops:
  2.8 41.5 %collective-permute-start = (bf16[272,1536]{1,0:T(8,128)(2,1)S(1)}, bf16[272,1536]{1,0:T(8,128)(2,1)S(1)}, u32[]{:S(2)}, u32[]{:S(2)}) collective-permute-start(bf16[272,1536]{1,0:T(8,128)(2,1)S(1)} %pad_maximum_fusion.5.refs_0_), channel_id=1, source_target_pairs={{0,16},{4,20},{8,24},{12,28},{16,0},{20,4},{24,8},{28,12},{1,17},{... | collective-permute-start | bytes 2506760 | tf_op jit(solution)/shard_map/ppermute | solution.py:386
  6.9 37.4 %collective-permute-start.1 = (bf16[272,1536]{1,0:T(8,128)(2,1)S(1)}, bf16[272,1536]{1,0:T(8,128)(2,1)S(1)}, u32[]{:S(2)}, u32[]{:S(2)}) collective-permute-start(bf16[272,1536]{1,0:T(8,128)(2,1)S(1)} %pad_maximum_fusion.5.refs_0_), channel_id=1, source_target_pairs={{0,4},{4,0},{8,12},{12,8},{16,20},{20,16},{24,28},{28,24},{1,5},{5... | collective-permute-start | bytes 2506760 | tf_op jit(solution)/shard_map/ppermute | solution.py:386
  45.3 44.8 %collective-permute-start.2 = (bf16[544,1536]{1,0:T(8,128)(2,1)S(1)}, bf16[544,1536]{1,0:T(8,128)(2,1)S(1)}, u32[]{:S(2)}, u32[]{:S(2)}) collective-permute-start(bf16[544,1536]{1,0:T(8,128)(2,1)S(1)} %pad_maximum_fusion.3), channel_id=1, source_target_pairs={{0,8},{4,12},{8,0},{12,4},{16,24},{20,28},{24,16},{28,20},{1,9},{5... | collective-permute-start | bytes 5013512 | tf_op jit(solution)/shard_map/ppermute | solution.py:386
  47.1 42.0 %collective-permute-start.5 = (bf16[256,2048]{1,0:T(8,128)(2,1)S(1)}, bf16[256,2048]{1,0:T(8,128)(2,1)S(1)}, u32[]{:S(2)}, u32[]{:S(2)}) collective-permute-start(bf16[256,2048]{1,0:T(8,128)(2,1)S(1)} %convert_element_type.338.refs_0_), channel_id=1, source_target_pairs={{0,4},{4,0},{8,12},{12,8},{16,20},{20,16},{24,28},{28,24},{1,5},{5... | collective-permute-start | bytes 3145736 | tf_op jit(solution)/shard_map/ppermute | solution.py:386
  47.7 41.4 %collective-permute-start.4 = (bf16[272,1536]{1,0:T(8,128)(2,1)S(1)}, bf16[272,1536]{1,0:T(8,128)(2,1)S(1)}, u32[]{:S(2)}, u32[]{:S(2)}) collective-permute-start(bf16[272,1536]{1,0:T(8,128)(2,1)S(1)} %collective-permute-done.refs_1_), channel_id=1, source_target_pairs={{0,4},{4,0},{8,12},{12,8},{16,20},{20,16},{24,28},{28,24},{1,5},{5... | collective-permute-start | bytes 2506760 | tf_op jit(solution)/shard_map/ppermute | solution.py:386
  49.2 38.6 %collective-permute-start.3 = (bf16[256,512]{1,0:T(8,128)(2,1)S(1)}, bf16[256,512]{1,0:T(8,128)(2,1)S(1)}, u32[]{:S(2)}, u32[]{:S(2)}) collective-permute-start(bf16[256,512]{1,0:T(8,128)(2,1)S(1)} %bitcast.46), channel_id=1, source_target_pairs={{0,16},{4,20},{8,24},{12,28},{16,0},{20,4},{24,8},{28,12},{1,17},{... | collective-permute-start | bytes 786440 | tf_op jit(solution)/shard_map/ppermute | solution.py:386
  90.4 39.5 %collective-permute-start.8 = (bf16[544,1536]{1,0:T(8,128)(2,1)S(1)}, bf16[544,1536]{1,0:T(8,128)(2,1)}, u32[]{:S(2)}, u32[]{:S(2)}) collective-permute-start(bf16[544,1536]{1,0:T(8,128)(2,1)S(1)} %collective-permute-done.2.refs_2_), channel_id=1, source_target_pairs={{0,4},{4,0},{8,12},{12,8},{16,20},{20,16},{24,28},{28,24},{1,5},{5... | collective-permute-start | bytes 5013512 | tf_op jit(solution)/shard_map/ppermute | solution.py:386
  96.0 44.6 %collective-permute-start.6 = (bf16[512,512]{1,0:T(8,128)(2,1)}, bf16[512,512]{1,0:T(8,128)(2,1)}, u32[]{:S(2)}, u32[]{:S(2)}) collective-permute-start(bf16[512,512]{1,0:T(8,128)(2,1)} %pad_maximum_fusion.6), channel_id=1, source_target_pairs={{0,8},{4,12},{8,0},{12,4},{16,24},{20,28},{24,16},{28,20},{1,9},{5... | collective-permute-start | bytes 1572872 | tf_op jit(solution)/shard_map/ppermute | solution.py:386
  98.9 41.8 %collective-permute-start.9 = (bf16[512,512]{1,0:T(8,128)(2,1)}, bf16[512,512]{1,0:T(8,128)(2,1)S(1)}, u32[]{:S(2)}, u32[]{:S(2)}) collective-permute-start(bf16[512,512]{1,0:T(8,128)(2,1)} %pad_maximum_fusion.6), channel_id=1, source_target_pairs={{0,4},{4,0},{8,12},{12,8},{16,20},{20,16},{24,28},{28,24},{1,5},{5... | collective-permute-start | bytes 1572872 | tf_op jit(solution)/shard_map/ppermute | solution.py:386
  100.2 47.5 %collective-permute-start.7 = (bf16[256,2048]{1,0:T(8,128)(2,1)S(1)}, bf16[256,2048]{1,0:T(8,128)(2,1)}, u32[]{:S(2)}, u32[]{:S(2)}) collective-permute-start(bf16[256,2048]{1,0:T(8,128)(2,1)S(1)} %convert_element_type.338.refs_0_), channel_id=1, source_target_pairs={{0,16},{4,20},{8,24},{12,28},{16,0},{20,4},{24,8},{28,12},{1,17},{... | collective-permute-start | bytes 3145736 | tf_op jit(solution)/shard_map/ppermute | solution.py:386
  150.5 45.8 %collective-permute-start.11 = (bf16[512,2048]{1,0:T(8,128)(2,1)}, bf16[512,2048]{1,0:T(8,128)(2,1)}, u32[]{:S(2)}, u32[]{:S(2)}) collective-permute-start(bf16[512,2048]{1,0:T(8,128)(2,1)} %pad_maximum_fusion), channel_id=1, source_target_pairs={{0,8},{4,12},{8,0},{12,4},{16,24},{20,28},{24,16},{28,20},{1,9},{5... | collective-permute-start | bytes 6291464 | tf_op jit(solution)/shard_map/ppermute | solution.py:386
  150.5 41.7 %collective-permute-start.12 = (bf16[256,2048]{1,0:T(8,128)(2,1)}, bf16[256,2048]{1,0:T(8,128)(2,1)}, u32[]{:S(2)}, u32[]{:S(2)}) collective-permute-start(bf16[256,2048]{1,0:T(8,128)(2,1)} %collective-permute-done.7.refs_1_), channel_id=1, source_target_pairs={{0,4},{4,0},{8,12},{12,8},{16,20},{20,16},{24,28},{28,24},{1,5},{5... | collective-permute-start | bytes 3145736 | tf_op jit(solution)/shard_map/ppermute | solution.py:386
  312.0 43.9 %collective-permute-start.28 = (bf16[256,2048]{1,0:T(8,128)(2,1)}, bf16[256,2048]{1,0:T(8,128)(2,1)}, u32[]{:S(2)}, u32[]{:S(2)}) collective-permute-start(bf16[256,2048]{1,0:T(8,128)(2,1)} %collective-permute-done.25.refs_4_), channel_id=1, source_target_pairs={{0,4},{4,0},{8,12},{12,8},{16,20},{20,16},{24,28},{28,24},{1,5},{5... | collective-permute-start | bytes 3145736 | tf_op jit(solution)/shard_map/ppermute | solution.py:386
  313.0 44.8 %collective-permute-start.27 = (bf16[256,2048]{1,0:T(8,128)(2,1)}, bf16[256,2048]{1,0:T(8,128)(2,1)}, u32[]{:S(2)}, u32[]{:S(2)}) collective-permute-start(bf16[256,2048]{1,0:T(8,128)(2,1)} %copy-done.47), channel_id=1, source_target_pairs={{0,4},{4,0},{8,12},{12,8},{16,20},{20,16},{24,28},{28,24},{1,5},{5... | collective-permute-start | bytes 3145736 | tf_op jit(solution)/shard_map/ppermute | solution.py:386
  357.7 44.0 %collective-permute-start.29 = (bf16[512,2048]{1,0:T(8,128)(2,1)}, bf16[512,2048]{1,0:T(8,128)(2,1)}, u32[]{:S(2)}, u32[]{:S(2)}) collective-permute-start(bf16[512,2048]{1,0:T(8,128)(2,1)} %shard_map.463), channel_id=1, source_target_pairs={{0,4},{4,0},{8,12},{12,8},{16,20},{20,16},{24,28},{28,24},{1,5},{5... | collective-permute-start | bytes 6291464 | tf_op jit(solution)/shard_map/ppermute | solution.py:386
  522.1 48.1 %collective-permute-start.48 = (bf16[512,2048]{1,0:T(8,128)(2,1)}, bf16[512,2048]{1,0:T(8,128)(2,1)}, u32[]{:S(2)}, u32[]{:S(2)}) collective-permute-start(bf16[512,2048]{1,0:T(8,128)(2,1)} %add_convert_fusion.1), channel_id=1, source_target_pairs={{0,8},{4,12},{8,0},{12,4},{16,24},{20,28},{24,16},{28,20},{1,9},{5... | collective-permute-start | bytes 6291464 | tf_op jit(solution)/shard_map/ppermute | solution.py:386
  523.5 47.5 %collective-permute-start.47 = (bf16[512,2048]{1,0:T(8,128)(2,1)}, bf16[512,2048]{1,0:T(8,128)(2,1)}, u32[]{:S(2)}, u32[]{:S(2)}) collective-permute-start(bf16[512,2048]{1,0:T(8,128)(2,1)} %shard_map.469), channel_id=1, source_target_pairs={{0,4},{4,0},{8,12},{12,8},{16,20},{20,16},{24,28},{28,24},{1,5},{5... | collective-permute-start | bytes 6291464 | tf_op jit(solution)/shard_map/ppermute | solution.py:386
  527.1 41.7 %collective-permute-start.46 = (bf16[256,2048]{1,0:T(8,128)(2,1)}, bf16[256,2048]{1,0:T(8,128)(2,1)}, u32[]{:S(2)}, u32[]{:S(2)}) collective-permute-start(bf16[256,2048]{1,0:T(8,128)(2,1)} %add_convert_fusion.5), channel_id=1, source_target_pairs={{0,2},{1,3},{2,0},{3,1},{4,6},{5,7},{6,4},{7,5},{8,10},{9,11},{10,... | collective-permute-start | bytes 3145736 | tf_op jit(solution)/shard_map/ppermute | solution.py:409
  614.1 35.9 %collective-permute-start.54 = (bf16[512,1536]{1,0:T(8,128)(2,1)}, bf16[512,1536]{1,0:T(8,128)(2,1)}, u32[]{:S(2)}, u32[]{:S(2)}) collective-permute-start(bf16[512,1536]{1,0:T(8,128)(2,1)} %shard_map.475), channel_id=1, source_target_pairs={{0,4},{4,0},{8,12},{12,8},{16,20},{20,16},{24,28},{28,24},{1,5},{5... | collective-permute-start | bytes 4718600 | tf_op jit(solution)/shard_map/ppermute | solution.py:386
  653.4 44.6 %collective-permute-start.58 = (bf16[512,1536]{1,0:T(8,128)(2,1)S(1)}, bf16[512,1536]{1,0:T(8,128)(2,1)S(1)}, u32[]{:S(2)}, u32[]{:S(2)}) collective-permute-start(bf16[512,1536]{1,0:T(8,128)(2,1)S(1)} %add_convert_fusion.2), channel_id=1, source_target_pairs={{0,8},{4,12},{8,0},{12,4},{16,24},{20,28},{24,16},{28,20},{1,9},{5... | collective-permute-start | bytes 4718600 | tf_op jit(solution)/shard_map/ppermute | solution.py:386
  656.9 41.0 %collective-permute-start.57 = (bf16[512,1536]{1,0:T(8,128)(2,1)S(1)}, bf16[512,1536]{1,0:T(8,128)(2,1)S(1)}, u32[]{:S(2)}, u32[]{:S(2)}) collective-permute-start(bf16[512,1536]{1,0:T(8,128)(2,1)S(1)} %copy-done.78), channel_id=1, source_target_pairs={{0,4},{4,0},{8,12},{12,8},{16,20},{20,16},{24,28},{28,24},{1,5},{5... | collective-permute-start | bytes 4718600 | tf_op jit(solution)/shard_map/ppermute | solution.py:386
  661.4 36.6 %collective-permute-start.59 = (bf16[256,2048]{1,0:T(8,128)(2,1)}, bf16[256,2048]{1,0:T(8,128)(2,1)}, u32[]{:S(2)}, u32[]{:S(2)}) collective-permute-start(bf16[256,2048]{1,0:T(8,128)(2,1)} %shard_map.480), channel_id=1, source_target_pairs={{0,2},{1,3},{2,0},{3,1},{4,6},{5,7},{6,4},{7,5},{8,10},{9,11},{10,... | collective-permute-start | bytes 3145736 | tf_op jit(solution)/shard_map/ppermute | solution.py:409
  682.1 41.2 %collective-permute-start.66 = (bf16[256,2048]{1,0:T(8,128)(2,1)}, bf16[256,2048]{1,0:T(8,128)(2,1)}, u32[]{:S(2)}, u32[]{:S(2)}) collective-permute-start(bf16[256,2048]{1,0:T(8,128)(2,1)} %collective-permute-done.64), channel_id=1, source_target_pairs={{0,1},{1,0},{2,3},{3,2},{4,5},{5,4},{6,7},{7,6},{8,9},{9,8},{10,11... | collective-permute-start | bytes 3145736 | tf_op jit(solution)/shard_map/ppermute | solution.py:409
  703.2 37.9 %collective-permute-start.62 = (bf16[256,1536]{1,0:T(8,128)(2,1)}, bf16[256,1536]{1,0:T(8,128)(2,1)S(1)}, u32[]{:S(2)}, u32[]{:S(2)}) collective-permute-start(bf16[256,1536]{1,0:T(8,128)(2,1)} %add_convert_fusion.11), channel_id=1, source_target_pairs={{0,16},{4,20},{8,24},{12,28},{16,0},{20,4},{24,8},{28,12},{1,17},{... | collective-permute-start | bytes 2359304 | tf_op jit(solution)/shard_map/ppermute | solution.py:386
  (187 other events, 2635.3 us)

commit v7 on v6

--- a/solution.py
+++ b/solution.py
@@ -23,7 +23,7 @@
 low_type = jnp.bfloat16
 wide = jnp.float32
 work_share = 0.1
-kernel_memory = 40 * 1024 * 1024
+kernel_memory = 23 * 1024 * 1024
 
 
 def norm_parts(values):
@@ -318,34 +318,26 @@
 def adam_kernel(rate_value, decay_value, terms, *refs):
     gradient = sum(ref[...].astype(wide) for ref in refs[:terms])
     states, outs = refs[terms : terms + 4], refs[terms + 4 :]
-    width = states[0].shape[2]
-    for j in range(states[0].shape[1]):
-        master, moment, square, average = (ref[:, j, :] for ref in states)
-        made = adam_update(
-            master,
-            moment,
-            square,
-            gradient[:, j * width : (j + 1) * width],
-            rate_value,
-            decay_value,
-        )
-        smooth = average_decay * average + (1.0 - average_decay) * made[0]
-        for ref, value in zip(outs, (*made, smooth)):
-            ref[:, j, :] = value
+    master, moment, square, average = (ref[...] for ref in states)
+    made = adam_update(master, moment, square, gradient, rate_value, decay_value)
+    smooth = average_decay * average + (1.0 - average_decay) * made[0]
+    for ref, value in zip(outs, (*made, smooth, made[0])):
+        ref[...] = value.astype(ref.dtype)
 
 
 def adam_planes(terms, states, rate_value, decay_value):
-    rows, planes, width = states[0].shape
-    block = tile(rows, 32)
-    flat = pl.BlockSpec((block, planes * width), lambda i: (i, 0))
-    deep = pl.BlockSpec((block, planes, width), lambda i: (i, 0, 0))
-    size = sum(x.size * x.dtype.itemsize for x in terms) + 32 * states[0].size
+    planes, rows, width = states[0].shape
+    block = tile(rows, 128)
+    flat = pl.BlockSpec((block, width), lambda j, i: (i, j))
+    deep = pl.BlockSpec((None, block, width), lambda j, i: (j, i, 0))
+    size = sum(x.size * x.dtype.itemsize for x in terms) + 34 * states[0].size
+    kinds = [wide] * 4 + [low_type]
     return pl.pallas_call(
         functools.partial(adam_kernel, rate_value, decay_value, len(terms)),
-        out_shape=[jax.ShapeDtypeStruct(states[0].shape, wide)] * 4,
-        grid=(rows // block,),
+        out_shape=[jax.ShapeDtypeStruct(states[0].shape, kind) for kind in kinds],
+        grid=(planes, rows // block),
         in_specs=[flat] * len(terms) + [deep] * 4,
-        out_specs=[deep] * 4,
+        out_specs=[deep] * 5,
         compiler_params=pltpu.CompilerParams(vmem_limit_bytes=kernel_memory),
         cost_estimate=pl.CostEstimate(flops=0, bytes_accessed=size, transcendentals=0),
     )(*terms, *states)
@@ -452,6 +444,11 @@
             value = self.joined("own", "far") if name == "pair" else self.held[name]
         partners = range(1, self.links.inner)
         return [(value, self.links.across(0, j), self.held, (name, j)) for j in partners]
+
+    def beside(self, name, result):
+        send = self.links.across(1, 0)
+        partners = range(1, self.links.inner)
+        return [(self.held[name, j], send, self.held, (result, j)) for j in partners]
 
     def half(self, name, part):
         value = self.held[name]
@@ -703,6 +700,10 @@
     row_length = local_tokens // row_count
     shard_rows, kinds_count, local_width = attend_weights.shape
 
+    attend_states = [
+        state.transpose(1, 0, 2)
+        for state in (attend_weights, attend_first, attend_second, attend_average)
+    ]
     attend_low = attend_weights.astype(low_type).reshape(shard_rows, kinds_count * local_width)
     combine_low = combine_weights.astype(low_type).T
     expand_low = expand_weights.astype(low_type)
@@ -733,11 +734,12 @@
     )
     for move, shard in zip(later, own):
         move.held["own"] = shard
-    links.round(
+    attend_states = links.round(
         lambda: combine_move.near()
         + expand_move.far()
         + attend_move.across("near")
-        + combine_move.across("pair")
+        + combine_move.across("pair"),
+        attend_states,
     )
 
     norm_values = jnp.concatenate(
@@ -787,15 +789,15 @@
         + shrink_move.out("near_far", shrink_move.joined("far0", "far1"), 1)
         + shrink_move.across("far", shrink_move.joined("far0", "far1"))
     )
-    links.round(lambda: shrink_move.across("near_own") + shrink_move.across("near_far"))
+    links.round(lambda: shrink_move.across("near_far") + shrink_move.beside("own", "near_own"))
     normed_two_low = normed_two.full()
     expand_full = expand_move.full(shard_rows)
-    expanded, activated_low = matmul(
+    activated_low, slope = matmul(
         normed_two_low,
         expand_full,
         "nn",
-        lambda made: (made, gelu_parts(made)[0]),
-        [wide, low_type],
+        gelu_parts,
+        [low_type, wide],
     )
 
     def gradient_rows(left, right):
@@ -803,17 +805,17 @@
 
     shrink_back = Reduce(links, shard_rows, gradient_rows(branch_grad_low, activated_low))
 
-    expanded, activated_low, *_ = links.round(
-        shrink_back.first, [expanded, activated_low, *shrink_back.terms()]
+    slope, activated_low, *_ = links.round(
+        shrink_back.first, [slope, activated_low, *shrink_back.away.values()]
     )
     shrink_full = shrink_move.full(half_rows)
     (expanded_grad_low,) = matmul(
         branch_grad_low,
         shrink_full,
         "nn",
-        lambda made, before: (made * gelu_parts(before)[1],),
+        lambda made, before: (made * before,),
         [low_type],
-        expanded,
+        slope,
     )
     normed_two_back = ReduceTensor(links, dot_low(expanded_grad_low, expand_full, "nt"))
 
@@ -905,7 +907,7 @@
     norm_sum = norm_grads.total()
     attend_new = adam_planes(
         attend_back.last_terms(),
-        (attend_weights, attend_first, attend_second, attend_average),
+        attend_states,
         matrix_rate,
         weight_decay,
     )
@@ -947,7 +949,7 @@
             0.0,
         ),
     )
-    results = [layer_output, input_gradient, *attend_new, attend_new[0].astype(low_type)]
+    results = [layer_output, input_gradient, *(made.transpose(1, 0, 2) for made in attend_new)]
     for master, moment, square, average, gradient, rate_value, decay_value in kinds:
         master_new, moment_new, square_new = adam_update(
             master, moment, square, gradient, rate_value, decay_value

time: 775 us -> 747 us (0.964)
  local copies, waits for them, and re-layouts: 97.4 us -> 82.3 us
  other arithmetic: 117 us -> 107 us
  Pallas kernels: 205 us -> 196 us
    unnamed x295 -> x278, local copies, waits for them, and re-layouts: 56.8 us -> 45.7 us
  transfers between devices with their start and end apart: 73 -> 73, of which waited for: 28 -> 27; matrix products, arithmetic and copies ran while one was open for 21% -> 18% of each run, Pallas kernels for 27% -> 27%
where the time goes in v7:
time: 747 us; the launch traced here: 736 us
  waiting for transfers between devices  278 us (37%)
  Pallas kernels  196 us (26%)
  other arithmetic  107 us (14%)
  local copies, waits for them, and re-layouts  82.3 us (11%)
  starting transfers between devices  69.9 us (9%)
    ppermute x47, waiting for transfers between devices, flip(): return lax.ppermute(value, 'dp', pairs)  212 us
    pallas_call x19, Pallas kernels, matmul(): pl.pallas_call(kernel, out_shape=shapes, grid=(columns // along, rows //...  128 us
    ppermute x26, waiting for transfers between devices, turn(): return lax.ppermute(value, 'tensor', pairs)  66.2 us
    ppermute x47, starting transfers between devices, flip(): return lax.ppermute(value, 'dp', pairs)  56.2 us
    unnamed x278, local copies, waits for them, and re-layouts  45.7 us
    pallas_call x4, Pallas kernels, reorder_columns(): pl.pallas_call(copy_block, out_shape=jax.ShapeDtypeStruct(values.shape, v...  26.4 us
    pallas_call x1, Pallas kernels, attention(): pl.pallas_call(attend_back_kernel, out_shape=jax.ShapeDtypeStruct(project...  19.4 us
    dynamic_update_slice x16, local copies, waits for them, and re-layouts, full(): lax.dynamic_update_slice_in_dim(full, part, (core * links.chips + chip) *...  15.8 us
  transfers between devices with their start and end apart: 73, of which 27 were waited for; matrix products, arithmetic and copies ran while one was open for 18% of the time, Pallas kernels for 27%

profile of v7, /device:TPU:0, one launch (start us, length us, event | category | flops | bytes accessed | tf_op | source)
XLA Modules:
  0.0 735.6 jit_solution(9078306517220666671)
XLA Ops:
  10.1 7.3 shard_map.458
  22.0 7.4 %shard_map.457 = bf16[1024,2048]{1,0:T(8,128)(2,1)} custom-call(s32[8]{0:T(128)} %add.488.order_ref, bf16[1024,2048]{1,0:T(8,128)(2,1)} %in_ref.2), custom_call_target="tpu_custom_call" | custom-call | bytes 8388608 | tf_op jit(solution)/shard_map/pallas_call | solution.py:284
  50.9 36.9 %collective-permute-done.3.refs_1_ = bf16[256,512]{1,0:T(8,128)(2,1)S(1)} collective-permute-done((bf16[256,512]{1,0:T(8,128)(2,1)S(1)}, bf16[256,512]{1,0:T(8,128)(2,1)S(1)}, u32[]{:S(2)}, u32[]{:S(2)}) %collective-permute-start.3) | collective-permute-done | bytes 262176 | tf_op jit(solution)/shard_map/ppermute | solution.py:378
  103.5 26.5 %collective-permute-done.8.refs_5_ = bf16[544,1536]{1,0:T(8,128)(2,1)} collective-permute-done((bf16[544,1536]{1,0:T(8,128)(2,1)S(1)}, bf16[544,1536]{1,0:T(8,128)(2,1)}, u32[]{:S(2)}, u32[]{:S(2)}) %collective-permute-start.8) | collective-permute-done | bytes 1671200 | tf_op jit(solution)/shard_map/ppermute | solution.py:378
  161.8 9.3 %shard_map.459.query_ref.key_ref.value_ref = bf16[1024,1536]{1,0:T(8,128)(2,1)S(1)} custom-call(bf16[1024,2048]{1,0:T(8,128)(2,1)S(1)} %copy-done, bf16[272,1536]{1,0:T(8,128)(2,1)S(1)} %copy-done.26, bf16[272,1536]{1,0:T(8,128)(2,1)S(1)} %copy-done.23, bf16[544,1536]{1,0:T(8,128)(2,1)S(1)} %copy-done.29, bf16[272,1536]{1,0:T(8,128)(2,1)S(1)} %copy-done.62, ...), custom_call_target="tpu_custom_call" | custom-call | flops 644245120 | bytes 1402470 | tf_op jit(solution)/shard_map/pallas_call | solution.py:151
  171.1 9.9 %shard_map.460.left_ref.refs_0_ = bf16[1024,512]{1,0:T(8,128)(2,1)S(1)} custom-call(bf16[1024,1536]{1,0:T(8,128)(2,1)S(1)} %shard_map.459.query_ref.key_ref.value_ref, bf16[1024,1536]{1,0:T(8,128)(2,1)S(1)} %shard_map.459.query_ref.key_ref.value_ref, bf16[1024,1536]{1,0:T(8,128)(2,1)S(1)} %shard_map.459.query_ref.key_ref.value_ref, ...), custom_call_target="tpu_custom_call" | custom-call | flops 214748368 | bytes 629145 | tf_op jit(solution)/shard_map/pallas_call | solution.py:246
  202.1 26.0 %collective-permute-done.15.refs_1_ = bf16[128,2048]{1,0:T(8,128)(2,1)} collective-permute-done((bf16[128,2048]{1,0:T(8,128)(2,1)}, bf16[128,2048]{1,0:T(8,128)(2,1)}, u32[]{:S(2)}, u32[]{:S(2)}) %collective-permute-start.15) | collective-permute-done | bytes 524320 | tf_op jit(solution)/shard_map/ppermute | solution.py:378
  235.0 21.4 %collective-permute-done.17 = bf16[256,2048]{1,0:T(8,128)(2,1)} collective-permute-done((bf16[256,2048]{1,0:T(8,128)(2,1)}, bf16[256,2048]{1,0:T(8,128)(2,1)}, u32[]{:S(2)}, u32[]{:S(2)}) %collective-permute-start.17) | collective-permute-done | bytes 1048608 | tf_op jit(solution)/shard_map/ppermute | solution.py:401
  266.2 19.7 %collective-permute-done.22.refs_3_ = bf16[256,2048]{1,0:T(8,128)(2,1)S(1)} collective-permute-done((bf16[256,2048]{1,0:T(8,128)(2,1)S(1)}, bf16[256,2048]{1,0:T(8,128)(2,1)S(1)}, u32[]{:S(2)}, u32[]{:S(2)}) %collective-permute-start.22) | collective-permute-done | bytes 1048608 | tf_op jit(solution)/shard_map/ppermute | solution.py:378
  289.6 22.0 %collective-permute-done.25.refs_4_ = bf16[256,2048]{1,0:T(8,128)(2,1)} collective-permute-done((bf16[256,2048]{1,0:T(8,128)(2,1)}, bf16[256,2048]{1,0:T(8,128)(2,1)}, u32[]{:S(2)}, u32[]{:S(2)}) %collective-permute-start.25) | collective-permute-done | bytes 1048608 | tf_op jit(solution)/shard_map/ppermute | solution.py:378
  318.6 16.7 %shard_map.462 = (bf16[1024,2048]{1,0:T(8,128)(2,1)S(1)}, f32[1024,2048]{1,0:T(8,128)S(1)}) custom-call(bf16[1024,2048]{1,0:T(8,128)(2,1)S(1)} %constant_dynamic-update-slice_fusion.20.left_ref, bf16[256,2048]{1,0:T(8,128)(2,1)S(1)} %copy-done.16, bf16[256,2048]{1,0:T(8,128)(2,1)} %collective-permute-done.7.refs_1_, ...), custom_call_target="tpu_custom_call" | custom-call | flops 858993472 | bytes 2516582 | tf_op jit(solution)/shard_map/pallas_call | solution.py:151
  363.8 13.4 %shard_map.464.left_ref.refs_0_ = bf16[1024,2048]{1,0:T(8,128)(2,1)S(1)} custom-call(bf16[1024,2048]{1,0:T(8,128)(2,1)S(1)} %copy-done.2, bf16[256,2048]{1,0:T(8,128)(2,1)S(1)} %bitcast.52, bf16[128,2048]{1,0:T(8,128)(2,1)} %collective-permute-done.15.refs_1_, bf16[128,2048]{1,0:T(8,128)(2,1)S(1)} %copy-done.33, bf16[256,2048]{1,0:T(8,128)(2,1)S(1)} %copy-done.39, ...), custom_call_target="tpu_custom_call" | custom-call | flops 858993472 | bytes 2516582 | tf_op jit(solution)/shard_map/pallas_call | solution.py:151
  377.2 12.4 %shard_map.465 = bf16[1024,2048]{1,0:T(8,128)(2,1)S(1)} custom-call(bf16[1024,2048]{1,0:T(8,128)(2,1)S(1)} %shard_map.464.left_ref.refs_0_, bf16[256,2048]{1,0:T(8,128)(2,1)S(1)} %copy-done.16, bf16[256,2048]{1,0:T(8,128)(2,1)} %collective-permute-done.7.refs_1_, bf16[512,2048]{1,0:T(8,128)(2,1)} %collective-permute-done.11.refs_2_, ...), custom_call_target="tpu_custom_call" | custom-call | flops 858993472 | bytes 1677721 | tf_op jit(solution)/shard_map/pallas_call | solution.py:151
  419.7 15.4 %collective-permute-done.34 = bf16[256,2048]{1,0:T(8,128)(2,1)S(1)} collective-permute-done((bf16[256,2048]{1,0:T(8,128)(2,1)S(1)}, bf16[256,2048]{1,0:T(8,128)(2,1)S(1)}, u32[]{:S(2)}, u32[]{:S(2)}) %collective-permute-start.34) | collective-permute-done | bytes 1048608 | tf_op jit(solution)/shard_map/ppermute | solution.py:401
  443.4 12.2 %shard_map.471 = bf16[1024,2048]{1,0:T(8,128)(2,1)S(1)} custom-call(bf16[1024,2048]{1,0:T(8,128)(2,1)S(1)} %copy-done.8, bf16[256,2048]{1,0:T(8,128)(2,1)S(1)} %bitcast.53, bf16[128,2048]{1,0:T(8,128)(2,1)} %collective-permute-done.15.refs_1_, bf16[128,2048]{1,0:T(8,128)(2,1)S(1)} %copy-done.33, bf16[256,2048]{1,0:T(8,128)(2,1)S(1)} %copy-done.39, ...), custom_call_target="tpu_custom_call" | custom-call | flops 858993472 | bytes 1677721 | tf_op jit(solution)/shard_map/pallas_call | solution.py:151
  455.6 14.2 %collective-permute-done.40 = bf16[128,2048]{1,0:T(8,128)(2,1)S(1)} collective-permute-done((bf16[128,2048]{1,0:T(8,128)(2,1)S(1)}, bf16[128,2048]{1,0:T(8,128)(2,1)S(1)}, u32[]{:S(2)}, u32[]{:S(2)}) %collective-permute-start.40) | collective-permute-done | bytes 524320 | tf_op jit(solution)/shard_map/ppermute | solution.py:378
  479.0 19.4 %shard_map.473.left_ref.refs_0_ = bf16[1024,1536]{1,0:T(8,128)(2,1)S(1)} custom-call(bf16[1024,1536]{1,0:T(8,128)(2,1)S(1)} %shard_map.459.query_ref.key_ref.value_ref, bf16[1024,1536]{1,0:T(8,128)(2,1)S(1)} %shard_map.459.query_ref.key_ref.value_ref, bf16[1024,1536]{1,0:T(8,128)(2,1)S(1)} %shard_map.459.query_ref.key_ref.value_ref, ...), custom_call_target="tpu_custom_call" | custom-call | flops 536870912 | bytes 943718 | tf_op jit(solution)/shard_map/pallas_call | solution.py:255
  527.8 8.8 %shard_map.474 = bf16[1024,2048]{1,0:T(8,128)(2,1)S(1)} custom-call(bf16[1024,1536]{1,0:T(8,128)(2,1)S(1)} %copy-done.4, bf16[272,1536]{1,0:T(8,128)(2,1)S(1)} %copy-done.27, bf16[272,1536]{1,0:T(8,128)(2,1)S(1)} %copy-done.24, bf16[544,1536]{1,0:T(8,128)(2,1)S(1)} %copy-done.30, bf16[272,1536]{1,0:T(8,128)(2,1)S(1)} %copy-done.63, ...), custom_call_target="tpu_custom_call" | custom-call | flops 644245120 | bytes 1402470 | tf_op jit(solution)/shard_map/pallas_call | solution.py:151
  539.7 10.8 %collective-permute-done.48 = bf16[512,2048]{1,0:T(8,128)(2,1)} collective-permute-done((bf16[512,2048]{1,0:T(8,128)(2,1)}, bf16[512,2048]{1,0:T(8,128)(2,1)}, u32[]{:S(2)}, u32[]{:S(2)}) %collective-permute-start.48) | collective-permute-done | bytes 2097184 | tf_op jit(solution)/shard_map/ppermute | solution.py:378
  575.9 9.0 %collective-permute-done.52 = bf16[128,2048]{1,0:T(8,128)(2,1)} collective-permute-done((bf16[128,2048]{1,0:T(8,128)(2,1)}, bf16[128,2048]{1,0:T(8,128)(2,1)}, u32[]{:S(2)}, u32[]{:S(2)}) %collective-permute-start.52) | collective-permute-done | bytes 524320 | tf_op jit(solution)/shard_map/ppermute | solution.py:378
  600.5 11.5 %collective-permute-done.53 = bf16[256,2048]{1,0:T(8,128)(2,1)S(1)} collective-permute-done((bf16[256,2048]{1,0:T(8,128)(2,1)S(1)}, bf16[256,2048]{1,0:T(8,128)(2,1)S(1)}, u32[]{:S(2)}, u32[]{:S(2)}) %collective-permute-start.53) | collective-permute-done | bytes 1048608 | tf_op jit(solution)/shard_map/ppermute | solution.py:401
  623.2 7.7 %collective-permute-done.54 = bf16[512,1536]{1,0:T(8,128)(2,1)} collective-permute-done((bf16[512,1536]{1,0:T(8,128)(2,1)}, bf16[512,1536]{1,0:T(8,128)(2,1)}, u32[]{:S(2)}, u32[]{:S(2)}) %collective-permute-start.54) | collective-permute-done | bytes 1572896 | tf_op jit(solution)/shard_map/ppermute | solution.py:378
  645.7 13.3 %collective-permute-done.64 = bf16[256,2048]{1,0:T(8,128)(2,1)} collective-permute-done((bf16[256,2048]{1,0:T(8,128)(2,1)S(1)}, bf16[256,2048]{1,0:T(8,128)(2,1)}, u32[]{:S(2)}, u32[]{:S(2)}) %collective-permute-start.64) | collective-permute-done | bytes 1048608 | tf_op jit(solution)/shard_map/ppermute | solution.py:401
  663.2 11.5 %collective-permute-done.60 = bf16[256,512]{1,0:T(8,128)(2,1)S(1)} collective-permute-done((bf16[256,512]{1,0:T(8,128)(2,1)S(1)}, bf16[256,512]{1,0:T(8,128)(2,1)S(1)}, u32[]{:S(2)}, u32[]{:S(2)}) %collective-permute-start.60) | collective-permute-done | bytes 262176 | tf_op jit(solution)/shard_map/ppermute | solution.py:378
  (547 shorter events, 370.3 us)
Async XLA Ops:
  2.8 41.5 %collective-permute-start = (bf16[272,1536]{1,0:T(8,128)(2,1)S(1)}, bf16[272,1536]{1,0:T(8,128)(2,1)S(1)}, u32[]{:S(2)}, u32[]{:S(2)}) collective-permute-start(bf16[272,1536]{1,0:T(8,128)(2,1)S(1)} %pad_maximum_fusion.5.refs_0_), channel_id=1, source_target_pairs={{0,16},{4,20},{8,24},{12,28},{16,0},{20,4},{24,8},{28,12},{1,17},{... | collective-permute-start | bytes 2506760 | tf_op jit(solution)/shard_map/ppermute | solution.py:378
  6.9 37.4 %collective-permute-start.1 = (bf16[272,1536]{1,0:T(8,128)(2,1)S(1)}, bf16[272,1536]{1,0:T(8,128)(2,1)S(1)}, u32[]{:S(2)}, u32[]{:S(2)}) collective-permute-start(bf16[272,1536]{1,0:T(8,128)(2,1)S(1)} %pad_maximum_fusion.5.refs_0_), channel_id=1, source_target_pairs={{0,4},{4,0},{8,12},{12,8},{16,20},{20,16},{24,28},{28,24},{1,5},{5... | collective-permute-start | bytes 2506760 | tf_op jit(solution)/shard_map/ppermute | solution.py:378
  45.3 45.1 %collective-permute-start.2 = (bf16[544,1536]{1,0:T(8,128)(2,1)S(1)}, bf16[544,1536]{1,0:T(8,128)(2,1)S(1)}, u32[]{:S(2)}, u32[]{:S(2)}) collective-permute-start(bf16[544,1536]{1,0:T(8,128)(2,1)S(1)} %pad_maximum_fusion.3), channel_id=1, source_target_pairs={{0,8},{4,12},{8,0},{12,4},{16,24},{20,28},{24,16},{28,20},{1,9},{5... | collective-permute-start | bytes 5013512 | tf_op jit(solution)/shard_map/ppermute | solution.py:378
  47.1 42.0 %collective-permute-start.5 = (bf16[256,2048]{1,0:T(8,128)(2,1)S(1)}, bf16[256,2048]{1,0:T(8,128)(2,1)S(1)}, u32[]{:S(2)}, u32[]{:S(2)}) collective-permute-start(bf16[256,2048]{1,0:T(8,128)(2,1)S(1)} %convert_element_type.335.refs_0_), channel_id=1, source_target_pairs={{0,4},{4,0},{8,12},{12,8},{16,20},{20,16},{24,28},{28,24},{1,5},{5... | collective-permute-start | bytes 3145736 | tf_op jit(solution)/shard_map/ppermute | solution.py:378
  47.7 41.4 %collective-permute-start.4 = (bf16[272,1536]{1,0:T(8,128)(2,1)S(1)}, bf16[272,1536]{1,0:T(8,128)(2,1)S(1)}, u32[]{:S(2)}, u32[]{:S(2)}) collective-permute-start(bf16[272,1536]{1,0:T(8,128)(2,1)S(1)} %collective-permute-done.refs_1_), channel_id=1, source_target_pairs={{0,4},{4,0},{8,12},{12,8},{16,20},{20,16},{24,28},{28,24},{1,5},{5... | collective-permute-start | bytes 2506760 | tf_op jit(solution)/shard_map/ppermute | solution.py:378
  49.2 38.6 %collective-permute-start.3 = (bf16[256,512]{1,0:T(8,128)(2,1)S(1)}, bf16[256,512]{1,0:T(8,128)(2,1)S(1)}, u32[]{:S(2)}, u32[]{:S(2)}) collective-permute-start(bf16[256,512]{1,0:T(8,128)(2,1)S(1)} %bitcast.58), channel_id=1, source_target_pairs={{0,16},{4,20},{8,24},{12,28},{16,0},{20,4},{24,8},{28,12},{1,17},{... | collective-permute-start | bytes 786440 | tf_op jit(solution)/shard_map/ppermute | solution.py:378
  90.4 39.6 %collective-permute-start.8 = (bf16[544,1536]{1,0:T(8,128)(2,1)S(1)}, bf16[544,1536]{1,0:T(8,128)(2,1)}, u32[]{:S(2)}, u32[]{:S(2)}) collective-permute-start(bf16[544,1536]{1,0:T(8,128)(2,1)S(1)} %collective-permute-done.2.refs_2_), channel_id=1, source_target_pairs={{0,4},{4,0},{8,12},{12,8},{16,20},{20,16},{24,28},{28,24},{1,5},{5... | collective-permute-start | bytes 5013512 | tf_op jit(solution)/shard_map/ppermute | solution.py:378
  96.1 44.6 %collective-permute-start.6 = (bf16[512,512]{1,0:T(8,128)(2,1)}, bf16[512,512]{1,0:T(8,128)(2,1)}, u32[]{:S(2)}, u32[]{:S(2)}) collective-permute-start(bf16[512,512]{1,0:T(8,128)(2,1)} %pad_maximum_fusion.6), channel_id=1, source_target_pairs={{0,8},{4,12},{8,0},{12,4},{16,24},{20,28},{24,16},{28,20},{1,9},{5... | collective-permute-start | bytes 1572872 | tf_op jit(solution)/shard_map/ppermute | solution.py:378
  98.8 41.8 %collective-permute-start.9 = (bf16[512,512]{1,0:T(8,128)(2,1)}, bf16[512,512]{1,0:T(8,128)(2,1)S(1)}, u32[]{:S(2)}, u32[]{:S(2)}) collective-permute-start(bf16[512,512]{1,0:T(8,128)(2,1)} %pad_maximum_fusion.6), channel_id=1, source_target_pairs={{0,4},{4,0},{8,12},{12,8},{16,20},{20,16},{24,28},{28,24},{1,5},{5... | collective-permute-start | bytes 1572872 | tf_op jit(solution)/shard_map/ppermute | solution.py:378
  100.2 47.5 %collective-permute-start.7 = (bf16[256,2048]{1,0:T(8,128)(2,1)S(1)}, bf16[256,2048]{1,0:T(8,128)(2,1)}, u32[]{:S(2)}, u32[]{:S(2)}) collective-permute-start(bf16[256,2048]{1,0:T(8,128)(2,1)S(1)} %convert_element_type.335.refs_0_), channel_id=1, source_target_pairs={{0,16},{4,20},{8,24},{12,28},{16,0},{20,4},{24,8},{28,12},{1,17},{... | collective-permute-start | bytes 3145736 | tf_op jit(solution)/shard_map/ppermute | solution.py:378
  150.5 45.8 %collective-permute-start.11 = (bf16[512,2048]{1,0:T(8,128)(2,1)}, bf16[512,2048]{1,0:T(8,128)(2,1)}, u32[]{:S(2)}, u32[]{:S(2)}) collective-permute-start(bf16[512,2048]{1,0:T(8,128)(2,1)} %pad_maximum_fusion), channel_id=1, source_target_pairs={{0,8},{4,12},{8,0},{12,4},{16,24},{20,28},{24,16},{28,20},{1,9},{5... | collective-permute-start | bytes 6291464 | tf_op jit(solution)/shard_map/ppermute | solution.py:378
  150.5 41.7 %collective-permute-start.12 = (bf16[256,2048]{1,0:T(8,128)(2,1)}, bf16[256,2048]{1,0:T(8,128)(2,1)}, u32[]{:S(2)}, u32[]{:S(2)}) collective-permute-start(bf16[256,2048]{1,0:T(8,128)(2,1)} %collective-permute-done.7.refs_1_), channel_id=1, source_target_pairs={{0,4},{4,0},{8,12},{12,8},{16,20},{20,16},{24,28},{28,24},{1,5},{5... | collective-permute-start | bytes 3145736 | tf_op jit(solution)/shard_map/ppermute | solution.py:378
  151.8 33.3 %collective-permute-start.10 = (bf16[512,512]{1,0:T(8,128)(2,1)}, bf16[512,512]{1,0:T(8,128)(2,1)}, u32[]{:S(2)}, u32[]{:S(2)}) collective-permute-start(bf16[512,512]{1,0:T(8,128)(2,1)} %collective-permute-done.6.refs_2_), channel_id=1, source_target_pairs={{0,4},{4,0},{8,12},{12,8},{16,20},{20,16},{24,28},{28,24},{1,5},{5... | collective-permute-start | bytes 1572872 | tf_op jit(solution)/shard_map/ppermute | solution.py:378
  311.9 31.4 %collective-permute-start.28 = (bf16[256,2048]{1,0:T(8,128)(2,1)}, bf16[256,2048]{1,0:T(8,128)(2,1)S(1)}, u32[]{:S(2)}, u32[]{:S(2)}) collective-permute-start(bf16[256,2048]{1,0:T(8,128)(2,1)} %copy-done.40), channel_id=1, source_target_pairs={{0,8},{4,12},{8,0},{12,4},{16,24},{20,28},{24,16},{28,20},{1,9},{5... | collective-permute-start | bytes 3145736 | tf_op jit(solution)/shard_map/ppermute | solution.py:378
  345.3 44.6 %collective-permute-start.29 = (bf16[512,2048]{1,0:T(8,128)(2,1)}, bf16[512,2048]{1,0:T(8,128)(2,1)}, u32[]{:S(2)}, u32[]{:S(2)}) collective-permute-start(bf16[512,2048]{1,0:T(8,128)(2,1)} %shard_map.463), channel_id=1, source_target_pairs={{0,4},{4,0},{8,12},{12,8},{16,20},{20,16},{24,28},{28,24},{1,5},{5... | collective-permute-start | bytes 6291464 | tf_op jit(solution)/shard_map/ppermute | solution.py:378
  502.4 48.1 %collective-permute-start.48 = (bf16[512,2048]{1,0:T(8,128)(2,1)}, bf16[512,2048]{1,0:T(8,128)(2,1)}, u32[]{:S(2)}, u32[]{:S(2)}) collective-permute-start(bf16[512,2048]{1,0:T(8,128)(2,1)} %add_convert_fusion.1), channel_id=1, source_target_pairs={{0,8},{4,12},{8,0},{12,4},{16,24},{20,28},{24,16},{28,20},{1,9},{5... | collective-permute-start | bytes 6291464 | tf_op jit(solution)/shard_map/ppermute | solution.py:378
  504.3 47.4 %collective-permute-start.47 = (bf16[512,2048]{1,0:T(8,128)(2,1)}, bf16[512,2048]{1,0:T(8,128)(2,1)}, u32[]{:S(2)}, u32[]{:S(2)}) collective-permute-start(bf16[512,2048]{1,0:T(8,128)(2,1)} %shard_map.469), channel_id=1, source_target_pairs={{0,4},{4,0},{8,12},{12,8},{16,20},{20,16},{24,28},{28,24},{1,5},{5... | collective-permute-start | bytes 6291464 | tf_op jit(solution)/shard_map/ppermute | solution.py:378
  506.6 33.1 %collective-permute-start.46 = (bf16[256,2048]{1,0:T(8,128)(2,1)}, bf16[256,2048]{1,0:T(8,128)(2,1)}, u32[]{:S(2)}, u32[]{:S(2)}) collective-permute-start(bf16[256,2048]{1,0:T(8,128)(2,1)} %add_convert_fusion.5), channel_id=1, source_target_pairs={{0,2},{1,3},{2,0},{3,1},{4,6},{5,7},{6,4},{7,5},{8,10},{9,11},{10,... | collective-permute-start | bytes 3145736 | tf_op jit(solution)/shard_map/ppermute | solution.py:401
  594.6 36.4 %collective-permute-start.54 = (bf16[512,1536]{1,0:T(8,128)(2,1)}, bf16[512,1536]{1,0:T(8,128)(2,1)}, u32[]{:S(2)}, u32[]{:S(2)}) collective-permute-start(bf16[512,1536]{1,0:T(8,128)(2,1)} %shard_map.475), channel_id=1, source_target_pairs={{0,4},{4,0},{8,12},{12,8},{16,20},{20,16},{24,28},{28,24},{1,5},{5... | collective-permute-start | bytes 4718600 | tf_op jit(solution)/shard_map/ppermute | solution.py:378
  634.3 45.0 %collective-permute-start.58 = (bf16[512,1536]{1,0:T(8,128)(2,1)S(1)}, bf16[512,1536]{1,0:T(8,128)(2,1)S(1)}, u32[]{:S(2)}, u32[]{:S(2)}) collective-permute-start(bf16[512,1536]{1,0:T(8,128)(2,1)S(1)} %add_convert_fusion.2), channel_id=1, source_target_pairs={{0,8},{4,12},{8,0},{12,4},{16,24},{20,28},{24,16},{28,20},{1,9},{5... | collective-permute-start | bytes 4718600 | tf_op jit(solution)/shard_map/ppermute | solution.py:378
  637.1 42.3 %collective-permute-start.57 = (bf16[512,1536]{1,0:T(8,128)(2,1)S(1)}, bf16[512,1536]{1,0:T(8,128)(2,1)S(1)}, u32[]{:S(2)}, u32[]{:S(2)}) collective-permute-start(bf16[512,1536]{1,0:T(8,128)(2,1)S(1)} %copy-done.77), channel_id=1, source_target_pairs={{0,4},{4,0},{8,12},{12,8},{16,20},{20,16},{24,28},{28,24},{1,5},{5... | collective-permute-start | bytes 4718600 | tf_op jit(solution)/shard_map/ppermute | solution.py:378
  641.5 37.9 %collective-permute-start.59 = (bf16[256,2048]{1,0:T(8,128)(2,1)}, bf16[256,2048]{1,0:T(8,128)(2,1)}, u32[]{:S(2)}, u32[]{:S(2)}) collective-permute-start(bf16[256,2048]{1,0:T(8,128)(2,1)} %shard_map.480), channel_id=1, source_target_pairs={{0,2},{1,3},{2,0},{3,1},{4,6},{5,7},{6,4},{7,5},{8,10},{9,11},{10,... | collective-permute-start | bytes 3145736 | tf_op jit(solution)/shard_map/ppermute | solution.py:401
  663.0 41.7 %collective-permute-start.66 = (bf16[256,2048]{1,0:T(8,128)(2,1)}, bf16[256,2048]{1,0:T(8,128)(2,1)}, u32[]{:S(2)}, u32[]{:S(2)}) collective-permute-start(bf16[256,2048]{1,0:T(8,128)(2,1)} %collective-permute-done.64), channel_id=1, source_target_pairs={{0,1},{1,0},{2,3},{3,2},{4,5},{5,4},{6,7},{7,6},{8,9},{9,8},{10,11... | collective-permute-start | bytes 3145736 | tf_op jit(solution)/shard_map/ppermute | solution.py:401
  684.5 38.0 %collective-permute-start.62 = (bf16[256,1536]{1,0:T(8,128)(2,1)}, bf16[256,1536]{1,0:T(8,128)(2,1)}, u32[]{:S(2)}, u32[]{:S(2)}) collective-permute-start(bf16[256,1536]{1,0:T(8,128)(2,1)} %add_convert_fusion.11), channel_id=1, source_target_pairs={{0,16},{4,20},{8,24},{12,28},{16,0},{20,4},{24,8},{28,12},{1,17},{... | collective-permute-start | bytes 2359304 | tf_op jit(solution)/shard_map/ppermute | solution.py:378
  (183 other events, 2531.4 us)

commit v8 on v7

--- a/solution.py
+++ b/solution.py
@@ -23,7 +23,7 @@
 low_type = jnp.bfloat16
 wide = jnp.float32
 work_share = 0.1
-kernel_memory = 23 * 1024 * 1024
+kernel_memory = 25 * 1024 * 1024
 
 
 def norm_parts(values):
@@ -104,7 +104,7 @@
             start = last
 
 
-def matmul(left, right, kind, body, kinds_out, beside=None, first=0, last=None, most=(512, 512)):
+def matmul(left, right, kind, body, kinds_out, beside=None, first=0, last=None, most=(512, 1024)):
     depth = left.shape[0 if kind == "tn" else 1]
     rows = (last or left.shape[1 if kind == "tn" else 0]) - first
     columns = right.shape[0 if kind == "nt" else 1]
@@ -865,11 +865,12 @@
         reorder_columns((residual + branch.total()).astype(low_type), links.from_own),
     )
     combine_back.split_both()
-    links.round(
+    (shrink_back.mine,) = links.round(
         lambda: normed_one_back.second()
         + attend_back.first()
         + combine_back.near()
-        + expand_back.far(0)
+        + expand_back.far(0),
+        [shrink_back.mine],
     )
     shrink_sum = turned(shrink_back.total())
     scaled_own, inverse_own = norm_parts(hidden_own)

time: 747 us -> 737 us (0.987)
    ppermute x47, waiting for transfers between devices: 212 us -> 220 us  [flip(): return lax.ppermute(value, 'dp', pairs)]
    unnamed x278 -> x274, local copies, waits for them, and re-layouts: 45.7 us -> 41.5 us
  transfers between devices with their start and end apart: 73 -> 73, of which waited for: 27 -> 28; matrix products, arithmetic and copies ran while one was open for 18% -> 18% of each run, Pallas kernels for 27% -> 26%
where the time goes in v8:
time: 737 us; the launch traced here: 726 us
  waiting for transfers between devices  284 us (39%)
  Pallas kernels  190 us (26%)
  other arithmetic  108 us (15%)
  local copies, waits for them, and re-layouts  78.3 us (11%)
  starting transfers between devices  63.1 us (9%)
    ppermute x47, waiting for transfers between devices, flip(): return lax.ppermute(value, 'dp', pairs)  220 us
    pallas_call x19, Pallas kernels, matmul(): pl.pallas_call(kernel, out_shape=shapes, grid=(columns // along, rows //...  122 us
    ppermute x26, waiting for transfers between devices, turn(): return lax.ppermute(value, 'tensor', pairs)  63.7 us
    ppermute x47, starting transfers between devices, flip(): return lax.ppermute(value, 'dp', pairs)  50.2 us
    unnamed x274, local copies, waits for them, and re-layouts  41.5 us
    pallas_call x4, Pallas kernels, reorder_columns(): pl.pallas_call(copy_block, out_shape=jax.ShapeDtypeStruct(values.shape, v...  26.4 us
    pallas_call x1, Pallas kernels, attention(): pl.pallas_call(attend_back_kernel, out_shape=jax.ShapeDtypeStruct(project...  19.4 us
    dynamic_update_slice x16, local copies, waits for them, and re-layouts, full(): lax.dynamic_update_slice_in_dim(full, part, (core * links.chips + chip) *...  15.9 us
  transfers between devices with their start and end apart: 73, of which 28 were waited for; matrix products, arithmetic and copies ran while one was open for 18% of the time, Pallas kernels for 26%

profile of v8, /device:TPU:0, one launch (start us, length us, event | category | flops | bytes accessed | tf_op | source)
XLA Modules:
  0.0 726.3 jit_solution(2543100557045646280)
XLA Ops:
  10.1 7.3 %shard_map.458 = bf16[1024,2048]{1,0:T(8,128)(2,1)} custom-call(s32[8]{0:T(128)} %add.488.order_ref, bf16[1024,2048]{1,0:T(8,128)(2,1)} %in_ref.3), custom_call_target="tpu_custom_call" | custom-call | bytes 8388608 | tf_op jit(solution)/shard_map/pallas_call | solution.py:284
  22.0 7.4 %shard_map.457 = bf16[1024,2048]{1,0:T(8,128)(2,1)} custom-call(s32[8]{0:T(128)} %add.488.order_ref, bf16[1024,2048]{1,0:T(8,128)(2,1)} %in_ref.2), custom_call_target="tpu_custom_call" | custom-call | bytes 8388608 | tf_op jit(solution)/shard_map/pallas_call | solution.py:284
  50.9 36.8 %collective-permute-done.3.refs_1_ = bf16[256,512]{1,0:T(8,128)(2,1)S(1)} collective-permute-done((bf16[256,512]{1,0:T(8,128)(2,1)S(1)}, bf16[256,512]{1,0:T(8,128)(2,1)S(1)}, u32[]{:S(2)}, u32[]{:S(2)}) %collective-permute-start.3) | collective-permute-done | bytes 262176 | tf_op jit(solution)/shard_map/ppermute | solution.py:378
  103.5 26.4 %collective-permute-done.8.refs_5_ = bf16[544,1536]{1,0:T(8,128)(2,1)} collective-permute-done((bf16[544,1536]{1,0:T(8,128)(2,1)S(1)}, bf16[544,1536]{1,0:T(8,128)(2,1)}, u32[]{:S(2)}, u32[]{:S(2)}) %collective-permute-start.8) | collective-permute-done | bytes 1671200 | tf_op jit(solution)/shard_map/ppermute | solution.py:378
  161.8 9.3 %shard_map.459.query_ref.key_ref.value_ref = bf16[1024,1536]{1,0:T(8,128)(2,1)S(1)} custom-call(bf16[1024,2048]{1,0:T(8,128)(2,1)S(1)} %copy-done, bf16[272,1536]{1,0:T(8,128)(2,1)S(1)} %copy-done.25, bf16[272,1536]{1,0:T(8,128)(2,1)S(1)} %copy-done.22, bf16[544,1536]{1,0:T(8,128)(2,1)S(1)} %copy-done.28, bf16[272,1536]{1,0:T(8,128)(2,1)S(1)} %copy-done.61, ...), custom_call_target="tpu_custom_call" | custom-call | flops 644245120 | bytes 1402470 | tf_op jit(solution)/shard_map/pallas_call | solution.py:151
  171.1 9.9 %shard_map.460.left_ref.refs_0_ = bf16[1024,512]{1,0:T(8,128)(2,1)S(1)} custom-call(bf16[1024,1536]{1,0:T(8,128)(2,1)S(1)} %shard_map.459.query_ref.key_ref.value_ref, bf16[1024,1536]{1,0:T(8,128)(2,1)S(1)} %shard_map.459.query_ref.key_ref.value_ref, bf16[1024,1536]{1,0:T(8,128)(2,1)S(1)} %shard_map.459.query_ref.key_ref.value_ref, ...), custom_call_target="tpu_custom_call" | custom-call | flops 214748368 | bytes 629145 | tf_op jit(solution)/shard_map/pallas_call | solution.py:246
  202.1 26.0 %collective-permute-done.15.refs_1_ = bf16[128,2048]{1,0:T(8,128)(2,1)} collective-permute-done((bf16[128,2048]{1,0:T(8,128)(2,1)}, bf16[128,2048]{1,0:T(8,128)(2,1)}, u32[]{:S(2)}, u32[]{:S(2)}) %collective-permute-start.15) | collective-permute-done | bytes 524320 | tf_op jit(solution)/shard_map/ppermute | solution.py:378
  235.0 21.4 %collective-permute-done.17 = bf16[256,2048]{1,0:T(8,128)(2,1)} collective-permute-done((bf16[256,2048]{1,0:T(8,128)(2,1)}, bf16[256,2048]{1,0:T(8,128)(2,1)}, u32[]{:S(2)}, u32[]{:S(2)}) %collective-permute-start.17) | collective-permute-done | bytes 1048608 | tf_op jit(solution)/shard_map/ppermute | solution.py:401
  266.2 19.7 %collective-permute-done.22.refs_3_ = bf16[256,2048]{1,0:T(8,128)(2,1)S(1)} collective-permute-done((bf16[256,2048]{1,0:T(8,128)(2,1)S(1)}, bf16[256,2048]{1,0:T(8,128)(2,1)S(1)}, u32[]{:S(2)}, u32[]{:S(2)}) %collective-permute-start.22) | collective-permute-done | bytes 1048608 | tf_op jit(solution)/shard_map/ppermute | solution.py:378
  289.6 22.0 %collective-permute-done.25.refs_4_ = bf16[256,2048]{1,0:T(8,128)(2,1)} collective-permute-done((bf16[256,2048]{1,0:T(8,128)(2,1)}, bf16[256,2048]{1,0:T(8,128)(2,1)}, u32[]{:S(2)}, u32[]{:S(2)}) %collective-permute-start.25) | collective-permute-done | bytes 1048608 | tf_op jit(solution)/shard_map/ppermute | solution.py:378
  318.6 16.4 %shard_map.462 = (bf16[1024,2048]{1,0:T(8,128)(2,1)S(1)}, f32[1024,2048]{1,0:T(8,128)S(1)}) custom-call(bf16[1024,2048]{1,0:T(8,128)(2,1)S(1)} %constant_dynamic-update-slice_fusion.20.left_ref, bf16[256,2048]{1,0:T(8,128)(2,1)S(1)} %copy-done.16, bf16[256,2048]{1,0:T(8,128)(2,1)} %collective-permute-done.7.refs_1_, ...), custom_call_target="tpu_custom_call" | custom-call | flops 858993472 | bytes 2516582 | tf_op jit(solution)/shard_map/pallas_call | solution.py:151
  356.0 12.9 %shard_map.464.left_ref.refs_0_ = bf16[1024,2048]{1,0:T(8,128)(2,1)S(1)} custom-call(bf16[1024,2048]{1,0:T(8,128)(2,1)S(1)} %copy-done.2, bf16[256,2048]{1,0:T(8,128)(2,1)S(1)} %bitcast.52, bf16[128,2048]{1,0:T(8,128)(2,1)} %collective-permute-done.15.refs_1_, bf16[128,2048]{1,0:T(8,128)(2,1)S(1)} %copy-done.32, bf16[256,2048]{1,0:T(8,128)(2,1)S(1)} %copy-done.38, ...), custom_call_target="tpu_custom_call" | custom-call | flops 858993472 | bytes 2516582 | tf_op jit(solution)/shard_map/pallas_call | solution.py:151
  370.1 12.0 %shard_map.465 = bf16[1024,2048]{1,0:T(8,128)(2,1)S(1)} custom-call(bf16[1024,2048]{1,0:T(8,128)(2,1)S(1)} %shard_map.464.left_ref.refs_0_, bf16[256,2048]{1,0:T(8,128)(2,1)S(1)} %copy-done.16, bf16[256,2048]{1,0:T(8,128)(2,1)} %collective-permute-done.7.refs_1_, bf16[512,2048]{1,0:T(8,128)(2,1)} %collective-permute-done.11.refs_2_, ...), custom_call_target="tpu_custom_call" | custom-call | flops 858993472 | bytes 1677721 | tf_op jit(solution)/shard_map/pallas_call | solution.py:151
  412.8 14.3 %collective-permute-done.34 = bf16[256,2048]{1,0:T(8,128)(2,1)S(1)} collective-permute-done((bf16[256,2048]{1,0:T(8,128)(2,1)S(1)}, bf16[256,2048]{1,0:T(8,128)(2,1)S(1)}, u32[]{:S(2)}, u32[]{:S(2)}) %collective-permute-start.34) | collective-permute-done | bytes 1048608 | tf_op jit(solution)/shard_map/ppermute | solution.py:401
  435.4 12.2 %shard_map.471 = bf16[1024,2048]{1,0:T(8,128)(2,1)S(1)} custom-call(bf16[1024,2048]{1,0:T(8,128)(2,1)S(1)} %copy-done.8, bf16[256,2048]{1,0:T(8,128)(2,1)S(1)} %bitcast.53, bf16[128,2048]{1,0:T(8,128)(2,1)} %collective-permute-done.15.refs_1_, bf16[128,2048]{1,0:T(8,128)(2,1)S(1)} %copy-done.32, bf16[256,2048]{1,0:T(8,128)(2,1)S(1)} %copy-done.38, ...), custom_call_target="tpu_custom_call" | custom-call | flops 858993472 | bytes 1677721 | tf_op jit(solution)/shard_map/pallas_call | solution.py:151
  447.6 14.1 %collective-permute-done.40 = bf16[128,2048]{1,0:T(8,128)(2,1)S(1)} collective-permute-done((bf16[128,2048]{1,0:T(8,128)(2,1)S(1)}, bf16[128,2048]{1,0:T(8,128)(2,1)S(1)}, u32[]{:S(2)}, u32[]{:S(2)}) %collective-permute-start.40) | collective-permute-done | bytes 524320 | tf_op jit(solution)/shard_map/ppermute | solution.py:378
  471.0 19.4 %shard_map.473.left_ref.refs_0_ = bf16[1024,1536]{1,0:T(8,128)(2,1)S(1)} custom-call(bf16[1024,1536]{1,0:T(8,128)(2,1)S(1)} %shard_map.459.query_ref.key_ref.value_ref, bf16[1024,1536]{1,0:T(8,128)(2,1)S(1)} %shard_map.459.query_ref.key_ref.value_ref, bf16[1024,1536]{1,0:T(8,128)(2,1)S(1)} %shard_map.459.query_ref.key_ref.value_ref, ...), custom_call_target="tpu_custom_call" | custom-call | flops 536870912 | bytes 943718 | tf_op jit(solution)/shard_map/pallas_call | solution.py:255
  520.0 8.8 %shard_map.474 = bf16[1024,2048]{1,0:T(8,128)(2,1)S(1)} custom-call(bf16[1024,1536]{1,0:T(8,128)(2,1)S(1)} %copy-done.4, bf16[272,1536]{1,0:T(8,128)(2,1)S(1)} %copy-done.26, bf16[272,1536]{1,0:T(8,128)(2,1)S(1)} %copy-done.23, bf16[544,1536]{1,0:T(8,128)(2,1)S(1)} %copy-done.29, bf16[272,1536]{1,0:T(8,128)(2,1)S(1)} %copy-done.62, ...), custom_call_target="tpu_custom_call" | custom-call | flops 644245120 | bytes 1402470 | tf_op jit(solution)/shard_map/pallas_call | solution.py:151
  531.6 11.1 %collective-permute-done.48 = bf16[512,2048]{1,0:T(8,128)(2,1)} collective-permute-done((bf16[512,2048]{1,0:T(8,128)(2,1)}, bf16[512,2048]{1,0:T(8,128)(2,1)}, u32[]{:S(2)}, u32[]{:S(2)}) %collective-permute-start.48) | collective-permute-done | bytes 2097184 | tf_op jit(solution)/shard_map/ppermute | solution.py:378
  559.5 15.6 %collective-permute-done.52 = bf16[128,2048]{1,0:T(8,128)(2,1)} collective-permute-done((bf16[128,2048]{1,0:T(8,128)(2,1)}, bf16[128,2048]{1,0:T(8,128)(2,1)}, u32[]{:S(2)}, u32[]{:S(2)}) %collective-permute-start.52) | collective-permute-done | bytes 524320 | tf_op jit(solution)/shard_map/ppermute | solution.py:378
  593.2 7.7 %fusion.23 = (bf16[2048,256]{1,0:T(8,128)(2,1)}, f32[2048,256]{1,0:T(8,128)}, f32[2048,256]{1,0:T(8,128)}, f32[2048,256]{1,0:T(8,128)}) fusion(f32[2048,256]{1,0:T(8,128)} %param.43, f32[2048,256]{1,0:T(8,128)} %shard_map.484, f32[2048,256]{1,0:T(8,128)} %param.44, f32[2048,256]{1,0:T(8,128)} %param.45), kind=kLoop, calls=%fused_computation.153 | loop fusion | flops 7864320 | bytes 15728640 | tf_op jit(solution)/shard_map/convert_element_type | solution.py:960
  634.5 15.8 %collective-permute-done.64 = bf16[256,2048]{1,0:T(8,128)(2,1)} collective-permute-done((bf16[256,2048]{1,0:T(8,128)(2,1)S(1)}, bf16[256,2048]{1,0:T(8,128)(2,1)}, u32[]{:S(2)}, u32[]{:S(2)}) %collective-permute-start.64) | collective-permute-done | bytes 1048608 | tf_op jit(solution)/shard_map/ppermute | solution.py:401
  652.1 10.6 %collective-permute-done.60 = bf16[256,512]{1,0:T(8,128)(2,1)S(1)} collective-permute-done((bf16[256,512]{1,0:T(8,128)(2,1)S(1)}, bf16[256,512]{1,0:T(8,128)(2,1)S(1)}, u32[]{:S(2)}, u32[]{:S(2)}) %collective-permute-start.60) | collective-permute-done | bytes 262176 | tf_op jit(solution)/shard_map/ppermute | solution.py:378
  662.7 7.3 collective-permute-done.59
  (542 shorter events, 359.3 us)
Async XLA Ops:
  2.8 41.4 %collective-permute-start = (bf16[272,1536]{1,0:T(8,128)(2,1)S(1)}, bf16[272,1536]{1,0:T(8,128)(2,1)S(1)}, u32[]{:S(2)}, u32[]{:S(2)}) collective-permute-start(bf16[272,1536]{1,0:T(8,128)(2,1)S(1)} %pad_maximum_fusion.5.refs_0_), channel_id=1, source_target_pairs={{0,16},{4,20},{8,24},{12,28},{16,0},{20,4},{24,8},{28,12},{1,17},{... | collective-permute-start | bytes 2506760 | tf_op jit(solution)/shard_map/ppermute | solution.py:378
  6.9 37.3 %collective-permute-start.1 = (bf16[272,1536]{1,0:T(8,128)(2,1)S(1)}, bf16[272,1536]{1,0:T(8,128)(2,1)S(1)}, u32[]{:S(2)}, u32[]{:S(2)}) collective-permute-start(bf16[272,1536]{1,0:T(8,128)(2,1)S(1)} %pad_maximum_fusion.5.refs_0_), channel_id=1, source_target_pairs={{0,4},{4,0},{8,12},{12,8},{16,20},{20,16},{24,28},{28,24},{1,5},{5... | collective-permute-start | bytes 2506760 | tf_op jit(solution)/shard_map/ppermute | solution.py:378
  45.2 45.1 %collective-permute-start.2 = (bf16[544,1536]{1,0:T(8,128)(2,1)S(1)}, bf16[544,1536]{1,0:T(8,128)(2,1)S(1)}, u32[]{:S(2)}, u32[]{:S(2)}) collective-permute-start(bf16[544,1536]{1,0:T(8,128)(2,1)S(1)} %pad_maximum_fusion.3), channel_id=1, source_target_pairs={{0,8},{4,12},{8,0},{12,4},{16,24},{20,28},{24,16},{28,20},{1,9},{5... | collective-permute-start | bytes 5013512 | tf_op jit(solution)/shard_map/ppermute | solution.py:378
  47.0 42.0 %collective-permute-start.5 = (bf16[256,2048]{1,0:T(8,128)(2,1)S(1)}, bf16[256,2048]{1,0:T(8,128)(2,1)S(1)}, u32[]{:S(2)}, u32[]{:S(2)}) collective-permute-start(bf16[256,2048]{1,0:T(8,128)(2,1)S(1)} %convert_element_type.335.refs_0_), channel_id=1, source_target_pairs={{0,4},{4,0},{8,12},{12,8},{16,20},{20,16},{24,28},{28,24},{1,5},{5... | collective-permute-start | bytes 3145736 | tf_op jit(solution)/shard_map/ppermute | solution.py:378
  47.6 41.4 %collective-permute-start.4 = (bf16[272,1536]{1,0:T(8,128)(2,1)S(1)}, bf16[272,1536]{1,0:T(8,128)(2,1)S(1)}, u32[]{:S(2)}, u32[]{:S(2)}) collective-permute-start(bf16[272,1536]{1,0:T(8,128)(2,1)S(1)} %collective-permute-done.refs_1_), channel_id=1, source_target_pairs={{0,4},{4,0},{8,12},{12,8},{16,20},{20,16},{24,28},{28,24},{1,5},{5... | collective-permute-start | bytes 2506760 | tf_op jit(solution)/shard_map/ppermute | solution.py:378
  49.1 38.6 %collective-permute-start.3 = (bf16[256,512]{1,0:T(8,128)(2,1)S(1)}, bf16[256,512]{1,0:T(8,128)(2,1)S(1)}, u32[]{:S(2)}, u32[]{:S(2)}) collective-permute-start(bf16[256,512]{1,0:T(8,128)(2,1)S(1)} %bitcast.56), channel_id=1, source_target_pairs={{0,16},{4,20},{8,24},{12,28},{16,0},{20,4},{24,8},{28,12},{1,17},{... | collective-permute-start | bytes 786440 | tf_op jit(solution)/shard_map/ppermute | solution.py:378
  90.3 39.6 %collective-permute-start.8 = (bf16[544,1536]{1,0:T(8,128)(2,1)S(1)}, bf16[544,1536]{1,0:T(8,128)(2,1)}, u32[]{:S(2)}, u32[]{:S(2)}) collective-permute-start(bf16[544,1536]{1,0:T(8,128)(2,1)S(1)} %collective-permute-done.2.refs_2_), channel_id=1, source_target_pairs={{0,4},{4,0},{8,12},{12,8},{16,20},{20,16},{24,28},{28,24},{1,5},{5... | collective-permute-start | bytes 5013512 | tf_op jit(solution)/shard_map/ppermute | solution.py:378
  96.0 44.6 %collective-permute-start.6 = (bf16[512,512]{1,0:T(8,128)(2,1)}, bf16[512,512]{1,0:T(8,128)(2,1)}, u32[]{:S(2)}, u32[]{:S(2)}) collective-permute-start(bf16[512,512]{1,0:T(8,128)(2,1)} %pad_maximum_fusion.6), channel_id=1, source_target_pairs={{0,8},{4,12},{8,0},{12,4},{16,24},{20,28},{24,16},{28,20},{1,9},{5... | collective-permute-start | bytes 1572872 | tf_op jit(solution)/shard_map/ppermute | solution.py:378
  98.8 41.8 %collective-permute-start.9 = (bf16[512,512]{1,0:T(8,128)(2,1)}, bf16[512,512]{1,0:T(8,128)(2,1)S(1)}, u32[]{:S(2)}, u32[]{:S(2)}) collective-permute-start(bf16[512,512]{1,0:T(8,128)(2,1)} %pad_maximum_fusion.6), channel_id=1, source_target_pairs={{0,4},{4,0},{8,12},{12,8},{16,20},{20,16},{24,28},{28,24},{1,5},{5... | collective-permute-start | bytes 1572872 | tf_op jit(solution)/shard_map/ppermute | solution.py:378
  100.2 47.5 %collective-permute-start.7 = (bf16[256,2048]{1,0:T(8,128)(2,1)S(1)}, bf16[256,2048]{1,0:T(8,128)(2,1)}, u32[]{:S(2)}, u32[]{:S(2)}) collective-permute-start(bf16[256,2048]{1,0:T(8,128)(2,1)S(1)} %convert_element_type.335.refs_0_), channel_id=1, source_target_pairs={{0,16},{4,20},{8,24},{12,28},{16,0},{20,4},{24,8},{28,12},{1,17},{... | collective-permute-start | bytes 3145736 | tf_op jit(solution)/shard_map/ppermute | solution.py:378
  150.5 45.8 %collective-permute-start.11 = (bf16[512,2048]{1,0:T(8,128)(2,1)}, bf16[512,2048]{1,0:T(8,128)(2,1)}, u32[]{:S(2)}, u32[]{:S(2)}) collective-permute-start(bf16[512,2048]{1,0:T(8,128)(2,1)} %pad_maximum_fusion), channel_id=1, source_target_pairs={{0,8},{4,12},{8,0},{12,4},{16,24},{20,28},{24,16},{28,20},{1,9},{5... | collective-permute-start | bytes 6291464 | tf_op jit(solution)/shard_map/ppermute | solution.py:378
  150.5 41.7 %collective-permute-start.12 = (bf16[256,2048]{1,0:T(8,128)(2,1)}, bf16[256,2048]{1,0:T(8,128)(2,1)}, u32[]{:S(2)}, u32[]{:S(2)}) collective-permute-start(bf16[256,2048]{1,0:T(8,128)(2,1)} %collective-permute-done.7.refs_1_), channel_id=1, source_target_pairs={{0,4},{4,0},{8,12},{12,8},{16,20},{20,16},{24,28},{28,24},{1,5},{5... | collective-permute-start | bytes 3145736 | tf_op jit(solution)/shard_map/ppermute | solution.py:378
  151.8 33.3 %collective-permute-start.10 = (bf16[512,512]{1,0:T(8,128)(2,1)}, bf16[512,512]{1,0:T(8,128)(2,1)}, u32[]{:S(2)}, u32[]{:S(2)}) collective-permute-start(bf16[512,512]{1,0:T(8,128)(2,1)} %collective-permute-done.6.refs_2_), channel_id=1, source_target_pairs={{0,4},{4,0},{8,12},{12,8},{16,20},{20,16},{24,28},{28,24},{1,5},{5... | collective-permute-start | bytes 1572872 | tf_op jit(solution)/shard_map/ppermute | solution.py:378
  339.0 44.5 %collective-permute-start.29 = (bf16[512,2048]{1,0:T(8,128)(2,1)}, bf16[512,2048]{1,0:T(8,128)(2,1)}, u32[]{:S(2)}, u32[]{:S(2)}) collective-permute-start(bf16[512,2048]{1,0:T(8,128)(2,1)} %shard_map.463), channel_id=1, source_target_pairs={{0,4},{4,0},{8,12},{12,8},{16,20},{20,16},{24,28},{28,24},{1,5},{5... | collective-permute-start | bytes 6291464 | tf_op jit(solution)/shard_map/ppermute | solution.py:378
  494.5 48.2 %collective-permute-start.48 = (bf16[512,2048]{1,0:T(8,128)(2,1)}, bf16[512,2048]{1,0:T(8,128)(2,1)}, u32[]{:S(2)}, u32[]{:S(2)}) collective-permute-start(bf16[512,2048]{1,0:T(8,128)(2,1)} %add_convert_fusion.1), channel_id=1, source_target_pairs={{0,8},{4,12},{8,0},{12,4},{16,24},{20,28},{24,16},{28,20},{1,9},{5... | collective-permute-start | bytes 6291464 | tf_op jit(solution)/shard_map/ppermute | solution.py:378
  496.2 47.5 %collective-permute-start.47 = (bf16[512,2048]{1,0:T(8,128)(2,1)}, bf16[512,2048]{1,0:T(8,128)(2,1)}, u32[]{:S(2)}, u32[]{:S(2)}) collective-permute-start(bf16[512,2048]{1,0:T(8,128)(2,1)} %shard_map.469), channel_id=1, source_target_pairs={{0,4},{4,0},{8,12},{12,8},{16,20},{20,16},{24,28},{28,24},{1,5},{5... | collective-permute-start | bytes 6291464 | tf_op jit(solution)/shard_map/ppermute | solution.py:378
  580.9 35.4 %collective-permute-start.56 = (bf16[128,2048]{1,0:T(8,128)(2,1)}, bf16[128,2048]{1,0:T(8,128)(2,1)}, u32[]{:S(2)}, u32[]{:S(2)}) collective-permute-start(bf16[128,2048]{1,0:T(8,128)(2,1)} %get-tuple-element.331), channel_id=1, source_target_pairs={{0,16},{4,20},{8,24},{12,28},{16,0},{20,4},{24,8},{28,12},{1,17},{... | collective-permute-start | bytes 1572872 | tf_op jit(solution)/shard_map/ppermute | solution.py:378
  582.9 33.5 %collective-permute-start.55 = (bf16[512,512]{1,0:T(8,128)(2,1)}, bf16[512,512]{1,0:T(8,128)(2,1)}, u32[]{:S(2)}, u32[]{:S(2)}) collective-permute-start(bf16[512,512]{1,0:T(8,128)(2,1)} %add_convert_fusion.13), channel_id=1, source_target_pairs={{0,8},{4,12},{8,0},{12,4},{16,24},{20,28},{24,16},{28,20},{1,9},{5... | collective-permute-start | bytes 1572872 | tf_op jit(solution)/shard_map/ppermute | solution.py:378
  586.4 35.8 %collective-permute-start.54 = (bf16[512,1536]{1,0:T(8,128)(2,1)}, bf16[512,1536]{1,0:T(8,128)(2,1)}, u32[]{:S(2)}, u32[]{:S(2)}) collective-permute-start(bf16[512,1536]{1,0:T(8,128)(2,1)} %shard_map.475), channel_id=1, source_target_pairs={{0,4},{4,0},{8,12},{12,8},{16,20},{20,16},{24,28},{28,24},{1,5},{5... | collective-permute-start | bytes 4718600 | tf_op jit(solution)/shard_map/ppermute | solution.py:378
  624.8 45.2 %collective-permute-start.58 = (bf16[512,1536]{1,0:T(8,128)(2,1)S(1)}, bf16[512,1536]{1,0:T(8,128)(2,1)S(1)}, u32[]{:S(2)}, u32[]{:S(2)}) collective-permute-start(bf16[512,1536]{1,0:T(8,128)(2,1)S(1)} %add_convert_fusion.2), channel_id=1, source_target_pairs={{0,8},{4,12},{8,0},{12,4},{16,24},{20,28},{24,16},{28,20},{1,9},{5... | collective-permute-start | bytes 4718600 | tf_op jit(solution)/shard_map/ppermute | solution.py:378
  625.0 45.0 %collective-permute-start.57 = (bf16[512,1536]{1,0:T(8,128)(2,1)S(1)}, bf16[512,1536]{1,0:T(8,128)(2,1)S(1)}, u32[]{:S(2)}, u32[]{:S(2)}) collective-permute-start(bf16[512,1536]{1,0:T(8,128)(2,1)S(1)} %copy-done.76), channel_id=1, source_target_pairs={{0,4},{4,0},{8,12},{12,8},{16,20},{20,16},{24,28},{28,24},{1,5},{5... | collective-permute-start | bytes 4718600 | tf_op jit(solution)/shard_map/ppermute | solution.py:378
  629.5 40.5 %collective-permute-start.59 = (bf16[256,2048]{1,0:T(8,128)(2,1)}, bf16[256,2048]{1,0:T(8,128)(2,1)}, u32[]{:S(2)}, u32[]{:S(2)}) collective-permute-start(bf16[256,2048]{1,0:T(8,128)(2,1)} %shard_map.480), channel_id=1, source_target_pairs={{0,2},{1,3},{2,0},{3,1},{4,6},{5,7},{6,4},{7,5},{8,10},{9,11},{10,... | collective-permute-start | bytes 3145736 | tf_op jit(solution)/shard_map/ppermute | solution.py:401
  651.9 41.6 %collective-permute-start.66 = (bf16[256,2048]{1,0:T(8,128)(2,1)}, bf16[256,2048]{1,0:T(8,128)(2,1)}, u32[]{:S(2)}, u32[]{:S(2)}) collective-permute-start(bf16[256,2048]{1,0:T(8,128)(2,1)} %collective-permute-done.64), channel_id=1, source_target_pairs={{0,1},{1,0},{2,3},{3,2},{4,5},{5,4},{6,7},{7,6},{8,9},{9,8},{10,11... | collective-permute-start | bytes 3145736 | tf_op jit(solution)/shard_map/ppermute | solution.py:401
  675.2 38.0 %collective-permute-start.62 = (bf16[256,1536]{1,0:T(8,128)(2,1)}, bf16[256,1536]{1,0:T(8,128)(2,1)}, u32[]{:S(2)}, u32[]{:S(2)}) collective-permute-start(bf16[256,1536]{1,0:T(8,128)(2,1)} %add_convert_fusion.11), channel_id=1, source_target_pairs={{0,16},{4,20},{8,24},{12,28},{16,0},{20,4},{24,8},{28,12},{1,17},{... | collective-permute-start | bytes 2359304 | tf_op jit(solution)/shard_map/ppermute | solution.py:378
  (181 other events, 2451.7 us)

commit v9 on v8

--- a/solution.py
+++ b/solution.py
@@ -23,7 +23,7 @@
 low_type = jnp.bfloat16
 wide = jnp.float32
 work_share = 0.1
-kernel_memory = 25 * 1024 * 1024
+kernel_memory = 21 * 1024 * 1024
 
 
 def norm_parts(values):
@@ -120,7 +120,10 @@
         left_spec = pl.BlockSpec((down, depth), lambda j, i: (i + skip, 0))
     if kind == "nt":
         height = [x.shape[0] if pieces else along for x in rights]
-        right_specs = [pl.BlockSpec((x, depth), lambda j, i: (j, 0)) for x in height]
+        held = pl.Buffered(1) if pieces else None
+        right_specs = [
+            pl.BlockSpec((x, depth), lambda j, i: (j, 0), pipeline_mode=held) for x in height
+        ]
     else:
         right_specs = [pl.BlockSpec((x.shape[0], along), lambda j, i: (0, j)) for x in rights]
     out_spec = pl.BlockSpec((down, along), lambda j, i: (i, j))

time: 737 us -> 743 us (level)
  no operation moved by 1% of the time
where the time goes in v9:
time: 743 us; the launch traced here: 732 us
  waiting for transfers between devices  287 us (39%)
  Pallas kernels  190 us (26%)
  other arithmetic  108 us (15%)
  local copies, waits for them, and re-layouts  80 us (11%)
  starting transfers between devices  63.2 us (9%)
    ppermute x47, waiting for transfers between devices, flip(): return lax.ppermute(value, 'dp', pairs)  224 us
    pallas_call x19, Pallas kernels, matmul(): pl.pallas_call(kernel, out_shape=shapes, grid=(columns // along, rows //...  122 us
    ppermute x26, waiting for transfers between devices, turn(): return lax.ppermute(value, 'tensor', pairs)  63.4 us
    ppermute x47, starting transfers between devices, flip(): return lax.ppermute(value, 'dp', pairs)  50.4 us
    unnamed x274, local copies, waits for them, and re-layouts  43.2 us
    pallas_call x4, Pallas kernels, reorder_columns(): pl.pallas_call(copy_block, out_shape=jax.ShapeDtypeStruct(values.shape, v...  26.4 us
    pallas_call x1, Pallas kernels, attention(): pl.pallas_call(attend_back_kernel, out_shape=jax.ShapeDtypeStruct(project...  19.4 us
    dynamic_update_slice x16, local copies, waits for them, and re-layouts, full(): lax.dynamic_update_slice_in_dim(full, part, (core * links.chips + chip) *...  15.9 us
  transfers between devices with their start and end apart: 73, of which 28 were waited for; matrix products, arithmetic and copies ran while one was open for 18% of the time, Pallas kernels for 26%

profile of v9, /device:TPU:0, one launch (start us, length us, event | category | flops | bytes accessed | tf_op | source)
XLA Modules:
  0.0 731.6 jit_solution(17233916088670801228)
XLA Ops:
  10.1 7.3 shard_map.458
  22.0 7.4 %shard_map.457 = bf16[1024,2048]{1,0:T(8,128)(2,1)} custom-call(s32[8]{0:T(128)} %add.488.order_ref, bf16[1024,2048]{1,0:T(8,128)(2,1)} %in_ref.2), custom_call_target="tpu_custom_call" | custom-call | bytes 8388608 | tf_op jit(solution)/shard_map/pallas_call | solution.py:287
  50.9 36.8 %collective-permute-done.3.refs_1_ = bf16[256,512]{1,0:T(8,128)(2,1)S(1)} collective-permute-done((bf16[256,512]{1,0:T(8,128)(2,1)S(1)}, bf16[256,512]{1,0:T(8,128)(2,1)S(1)}, u32[]{:S(2)}, u32[]{:S(2)}) %collective-permute-start.3) | collective-permute-done | bytes 262176 | tf_op jit(solution)/shard_map/ppermute | solution.py:381
  103.5 26.5 %collective-permute-done.8.refs_5_ = bf16[544,1536]{1,0:T(8,128)(2,1)} collective-permute-done((bf16[544,1536]{1,0:T(8,128)(2,1)S(1)}, bf16[544,1536]{1,0:T(8,128)(2,1)}, u32[]{:S(2)}, u32[]{:S(2)}) %collective-permute-start.8) | collective-permute-done | bytes 1671200 | tf_op jit(solution)/shard_map/ppermute | solution.py:381
  161.8 9.3 %shard_map.459.query_ref.key_ref.value_ref = bf16[1024,1536]{1,0:T(8,128)(2,1)S(1)} custom-call(bf16[1024,2048]{1,0:T(8,128)(2,1)S(1)} %copy-done, bf16[272,1536]{1,0:T(8,128)(2,1)S(1)} %copy-done.26, bf16[272,1536]{1,0:T(8,128)(2,1)S(1)} %copy-done.23, bf16[544,1536]{1,0:T(8,128)(2,1)S(1)} %copy-done.29, bf16[272,1536]{1,0:T(8,128)(2,1)S(1)} %copy-done.62, ...), custom_call_target="tpu_custom_call" | custom-call | flops 644245120 | bytes 1402470 | tf_op jit(solution)/shard_map/pallas_call | solution.py:154
  171.1 9.9 %shard_map.460.left_ref.refs_0_ = bf16[1024,512]{1,0:T(8,128)(2,1)S(1)} custom-call(bf16[1024,1536]{1,0:T(8,128)(2,1)S(1)} %shard_map.459.query_ref.key_ref.value_ref, bf16[1024,1536]{1,0:T(8,128)(2,1)S(1)} %shard_map.459.query_ref.key_ref.value_ref, bf16[1024,1536]{1,0:T(8,128)(2,1)S(1)} %shard_map.459.query_ref.key_ref.value_ref, ...), custom_call_target="tpu_custom_call" | custom-call | flops 214748368 | bytes 629145 | tf_op jit(solution)/shard_map/pallas_call | solution.py:249
  202.1 26.0 %collective-permute-done.15.refs_1_ = bf16[128,2048]{1,0:T(8,128)(2,1)} collective-permute-done((bf16[128,2048]{1,0:T(8,128)(2,1)}, bf16[128,2048]{1,0:T(8,128)(2,1)}, u32[]{:S(2)}, u32[]{:S(2)}) %collective-permute-start.15) | collective-permute-done | bytes 524320 | tf_op jit(solution)/shard_map/ppermute | solution.py:381
  235.0 21.4 %collective-permute-done.17 = bf16[256,2048]{1,0:T(8,128)(2,1)} collective-permute-done((bf16[256,2048]{1,0:T(8,128)(2,1)}, bf16[256,2048]{1,0:T(8,128)(2,1)}, u32[]{:S(2)}, u32[]{:S(2)}) %collective-permute-start.17) | collective-permute-done | bytes 1048608 | tf_op jit(solution)/shard_map/ppermute | solution.py:404
  266.2 19.7 %collective-permute-done.22.refs_3_ = bf16[256,2048]{1,0:T(8,128)(2,1)S(1)} collective-permute-done((bf16[256,2048]{1,0:T(8,128)(2,1)S(1)}, bf16[256,2048]{1,0:T(8,128)(2,1)S(1)}, u32[]{:S(2)}, u32[]{:S(2)}) %collective-permute-start.22) | collective-permute-done | bytes 1048608 | tf_op jit(solution)/shard_map/ppermute | solution.py:381
  289.7 22.0 %collective-permute-done.25.refs_4_ = bf16[256,2048]{1,0:T(8,128)(2,1)} collective-permute-done((bf16[256,2048]{1,0:T(8,128)(2,1)}, bf16[256,2048]{1,0:T(8,128)(2,1)}, u32[]{:S(2)}, u32[]{:S(2)}) %collective-permute-start.25) | collective-permute-done | bytes 1048608 | tf_op jit(solution)/shard_map/ppermute | solution.py:381
  318.7 16.4 %shard_map.462 = (bf16[1024,2048]{1,0:T(8,128)(2,1)S(1)}, f32[1024,2048]{1,0:T(8,128)S(1)}) custom-call(bf16[1024,2048]{1,0:T(8,128)(2,1)S(1)} %constant_dynamic-update-slice_fusion.20.left_ref, bf16[256,2048]{1,0:T(8,128)(2,1)S(1)} %copy-done.16, bf16[256,2048]{1,0:T(8,128)(2,1)} %collective-permute-done.7.refs_1_, ...), custom_call_target="tpu_custom_call" | custom-call | flops 858993472 | bytes 2516582 | tf_op jit(solution)/shard_map/pallas_call | solution.py:154
  358.8 12.9 %shard_map.464.left_ref.refs_0_ = bf16[1024,2048]{1,0:T(8,128)(2,1)S(1)} custom-call(bf16[1024,2048]{1,0:T(8,128)(2,1)S(1)} %copy-done.2, bf16[256,2048]{1,0:T(8,128)(2,1)S(1)} %bitcast.52, bf16[128,2048]{1,0:T(8,128)(2,1)} %collective-permute-done.15.refs_1_, bf16[128,2048]{1,0:T(8,128)(2,1)S(1)} %copy-done.33, bf16[256,2048]{1,0:T(8,128)(2,1)S(1)} %copy-done.39, ...), custom_call_target="tpu_custom_call" | custom-call | flops 858993472 | bytes 2516582 | tf_op jit(solution)/shard_map/pallas_call | solution.py:154
  371.7 12.0 %shard_map.465 = bf16[1024,2048]{1,0:T(8,128)(2,1)S(1)} custom-call(bf16[1024,2048]{1,0:T(8,128)(2,1)S(1)} %shard_map.464.left_ref.refs_0_, bf16[256,2048]{1,0:T(8,128)(2,1)S(1)} %copy-done.16, bf16[256,2048]{1,0:T(8,128)(2,1)} %collective-permute-done.7.refs_1_, bf16[512,2048]{1,0:T(8,128)(2,1)} %collective-permute-done.11.refs_2_, ...), custom_call_target="tpu_custom_call" | custom-call | flops 858993472 | bytes 1677721 | tf_op jit(solution)/shard_map/pallas_call | solution.py:154
  418.2 14.2 %collective-permute-done.34 = bf16[256,2048]{1,0:T(8,128)(2,1)S(1)} collective-permute-done((bf16[256,2048]{1,0:T(8,128)(2,1)S(1)}, bf16[256,2048]{1,0:T(8,128)(2,1)S(1)}, u32[]{:S(2)}, u32[]{:S(2)}) %collective-permute-start.34) | collective-permute-done | bytes 1048608 | tf_op jit(solution)/shard_map/ppermute | solution.py:404
  441.0 12.2 %shard_map.471 = bf16[1024,2048]{1,0:T(8,128)(2,1)S(1)} custom-call(bf16[1024,2048]{1,0:T(8,128)(2,1)S(1)} %copy-done.8, bf16[256,2048]{1,0:T(8,128)(2,1)S(1)} %bitcast.53, bf16[128,2048]{1,0:T(8,128)(2,1)} %collective-permute-done.15.refs_1_, bf16[128,2048]{1,0:T(8,128)(2,1)S(1)} %copy-done.33, bf16[256,2048]{1,0:T(8,128)(2,1)S(1)} %copy-done.39, ...), custom_call_target="tpu_custom_call" | custom-call | flops 858993472 | bytes 1677721 | tf_op jit(solution)/shard_map/pallas_call | solution.py:154
  453.2 14.0 %collective-permute-done.40 = bf16[128,2048]{1,0:T(8,128)(2,1)S(1)} collective-permute-done((bf16[128,2048]{1,0:T(8,128)(2,1)S(1)}, bf16[128,2048]{1,0:T(8,128)(2,1)S(1)}, u32[]{:S(2)}, u32[]{:S(2)}) %collective-permute-start.40) | collective-permute-done | bytes 524320 | tf_op jit(solution)/shard_map/ppermute | solution.py:381
  475.6 19.4 %shard_map.473.left_ref.refs_0_ = bf16[1024,1536]{1,0:T(8,128)(2,1)S(1)} custom-call(bf16[1024,1536]{1,0:T(8,128)(2,1)S(1)} %shard_map.459.query_ref.key_ref.value_ref, bf16[1024,1536]{1,0:T(8,128)(2,1)S(1)} %shard_map.459.query_ref.key_ref.value_ref, bf16[1024,1536]{1,0:T(8,128)(2,1)S(1)} %shard_map.459.query_ref.key_ref.value_ref, ...), custom_call_target="tpu_custom_call" | custom-call | flops 536870912 | bytes 943718 | tf_op jit(solution)/shard_map/pallas_call | solution.py:258
  525.4 8.8 %shard_map.474 = bf16[1024,2048]{1,0:T(8,128)(2,1)S(1)} custom-call(bf16[1024,1536]{1,0:T(8,128)(2,1)S(1)} %copy-done.4, bf16[272,1536]{1,0:T(8,128)(2,1)S(1)} %copy-done.27, bf16[272,1536]{1,0:T(8,128)(2,1)S(1)} %copy-done.24, bf16[544,1536]{1,0:T(8,128)(2,1)S(1)} %copy-done.30, bf16[272,1536]{1,0:T(8,128)(2,1)S(1)} %copy-done.63, ...), custom_call_target="tpu_custom_call" | custom-call | flops 644245120 | bytes 1402470 | tf_op jit(solution)/shard_map/pallas_call | solution.py:154
  536.9 11.0 %collective-permute-done.48 = bf16[512,2048]{1,0:T(8,128)(2,1)} collective-permute-done((bf16[512,2048]{1,0:T(8,128)(2,1)}, bf16[512,2048]{1,0:T(8,128)(2,1)}, u32[]{:S(2)}, u32[]{:S(2)}) %collective-permute-start.48) | collective-permute-done | bytes 2097184 | tf_op jit(solution)/shard_map/ppermute | solution.py:381
  565.1 15.4 %collective-permute-done.52 = bf16[128,2048]{1,0:T(8,128)(2,1)} collective-permute-done((bf16[128,2048]{1,0:T(8,128)(2,1)}, bf16[128,2048]{1,0:T(8,128)(2,1)}, u32[]{:S(2)}, u32[]{:S(2)}) %collective-permute-start.52) | collective-permute-done | bytes 524320 | tf_op jit(solution)/shard_map/ppermute | solution.py:381
  598.6 7.7 %fusion.23 = (bf16[2048,256]{1,0:T(8,128)(2,1)}, f32[2048,256]{1,0:T(8,128)}, f32[2048,256]{1,0:T(8,128)}, f32[2048,256]{1,0:T(8,128)}) fusion(f32[2048,256]{1,0:T(8,128)} %param.43, f32[2048,256]{1,0:T(8,128)} %shard_map.484, f32[2048,256]{1,0:T(8,128)} %param.44, f32[2048,256]{1,0:T(8,128)} %param.45), kind=kLoop, calls=%fused_computation.153 | loop fusion | flops 7864320 | bytes 15728640 | tf_op jit(solution)/shard_map/convert_element_type | solution.py:963
  639.9 15.7 %collective-permute-done.64 = bf16[256,2048]{1,0:T(8,128)(2,1)} collective-permute-done((bf16[256,2048]{1,0:T(8,128)(2,1)S(1)}, bf16[256,2048]{1,0:T(8,128)(2,1)}, u32[]{:S(2)}, u32[]{:S(2)}) %collective-permute-start.64) | collective-permute-done | bytes 1048608 | tf_op jit(solution)/shard_map/ppermute | solution.py:404
  657.4 10.6 %collective-permute-done.60 = bf16[256,512]{1,0:T(8,128)(2,1)S(1)} collective-permute-done((bf16[256,512]{1,0:T(8,128)(2,1)S(1)}, bf16[256,512]{1,0:T(8,128)(2,1)S(1)}, u32[]{:S(2)}, u32[]{:S(2)}) %collective-permute-start.60) | collective-permute-done | bytes 262176 | tf_op jit(solution)/shard_map/ppermute | solution.py:381
  668.0 7.3 collective-permute-done.59
  (543 shorter events, 365.2 us)
Async XLA Ops:
  2.8 41.4 %collective-permute-start = (bf16[272,1536]{1,0:T(8,128)(2,1)S(1)}, bf16[272,1536]{1,0:T(8,128)(2,1)S(1)}, u32[]{:S(2)}, u32[]{:S(2)}) collective-permute-start(bf16[272,1536]{1,0:T(8,128)(2,1)S(1)} %pad_maximum_fusion.5.refs_0_), channel_id=1, source_target_pairs={{0,16},{4,20},{8,24},{12,28},{16,0},{20,4},{24,8},{28,12},{1,17},{... | collective-permute-start | bytes 2506760 | tf_op jit(solution)/shard_map/ppermute | solution.py:381
  6.9 37.3 %collective-permute-start.1 = (bf16[272,1536]{1,0:T(8,128)(2,1)S(1)}, bf16[272,1536]{1,0:T(8,128)(2,1)S(1)}, u32[]{:S(2)}, u32[]{:S(2)}) collective-permute-start(bf16[272,1536]{1,0:T(8,128)(2,1)S(1)} %pad_maximum_fusion.5.refs_0_), channel_id=1, source_target_pairs={{0,4},{4,0},{8,12},{12,8},{16,20},{20,16},{24,28},{28,24},{1,5},{5... | collective-permute-start | bytes 2506760 | tf_op jit(solution)/shard_map/ppermute | solution.py:381
  45.2 45.1 %collective-permute-start.2 = (bf16[544,1536]{1,0:T(8,128)(2,1)S(1)}, bf16[544,1536]{1,0:T(8,128)(2,1)S(1)}, u32[]{:S(2)}, u32[]{:S(2)}) collective-permute-start(bf16[544,1536]{1,0:T(8,128)(2,1)S(1)} %pad_maximum_fusion.3), channel_id=1, source_target_pairs={{0,8},{4,12},{8,0},{12,4},{16,24},{20,28},{24,16},{28,20},{1,9},{5... | collective-permute-start | bytes 5013512 | tf_op jit(solution)/shard_map/ppermute | solution.py:381
  47.0 42.0 %collective-permute-start.5 = (bf16[256,2048]{1,0:T(8,128)(2,1)S(1)}, bf16[256,2048]{1,0:T(8,128)(2,1)S(1)}, u32[]{:S(2)}, u32[]{:S(2)}) collective-permute-start(bf16[256,2048]{1,0:T(8,128)(2,1)S(1)} %convert_element_type.335.refs_0_), channel_id=1, source_target_pairs={{0,4},{4,0},{8,12},{12,8},{16,20},{20,16},{24,28},{28,24},{1,5},{5... | collective-permute-start | bytes 3145736 | tf_op jit(solution)/shard_map/ppermute | solution.py:381
  47.6 41.4 %collective-permute-start.4 = (bf16[272,1536]{1,0:T(8,128)(2,1)S(1)}, bf16[272,1536]{1,0:T(8,128)(2,1)S(1)}, u32[]{:S(2)}, u32[]{:S(2)}) collective-permute-start(bf16[272,1536]{1,0:T(8,128)(2,1)S(1)} %collective-permute-done.refs_1_), channel_id=1, source_target_pairs={{0,4},{4,0},{8,12},{12,8},{16,20},{20,16},{24,28},{28,24},{1,5},{5... | collective-permute-start | bytes 2506760 | tf_op jit(solution)/shard_map/ppermute | solution.py:381
  49.1 38.6 %collective-permute-start.3 = (bf16[256,512]{1,0:T(8,128)(2,1)S(1)}, bf16[256,512]{1,0:T(8,128)(2,1)S(1)}, u32[]{:S(2)}, u32[]{:S(2)}) collective-permute-start(bf16[256,512]{1,0:T(8,128)(2,1)S(1)} %bitcast.58), channel_id=1, source_target_pairs={{0,16},{4,20},{8,24},{12,28},{16,0},{20,4},{24,8},{28,12},{1,17},{... | collective-permute-start | bytes 786440 | tf_op jit(solution)/shard_map/ppermute | solution.py:381
  90.3 39.6 %collective-permute-start.8 = (bf16[544,1536]{1,0:T(8,128)(2,1)S(1)}, bf16[544,1536]{1,0:T(8,128)(2,1)}, u32[]{:S(2)}, u32[]{:S(2)}) collective-permute-start(bf16[544,1536]{1,0:T(8,128)(2,1)S(1)} %collective-permute-done.2.refs_2_), channel_id=1, source_target_pairs={{0,4},{4,0},{8,12},{12,8},{16,20},{20,16},{24,28},{28,24},{1,5},{5... | collective-permute-start | bytes 5013512 | tf_op jit(solution)/shard_map/ppermute | solution.py:381
  96.0 44.6 %collective-permute-start.6 = (bf16[512,512]{1,0:T(8,128)(2,1)}, bf16[512,512]{1,0:T(8,128)(2,1)}, u32[]{:S(2)}, u32[]{:S(2)}) collective-permute-start(bf16[512,512]{1,0:T(8,128)(2,1)} %pad_maximum_fusion.6), channel_id=1, source_target_pairs={{0,8},{4,12},{8,0},{12,4},{16,24},{20,28},{24,16},{28,20},{1,9},{5... | collective-permute-start | bytes 1572872 | tf_op jit(solution)/shard_map/ppermute | solution.py:381
  98.9 41.8 %collective-permute-start.9 = (bf16[512,512]{1,0:T(8,128)(2,1)}, bf16[512,512]{1,0:T(8,128)(2,1)S(1)}, u32[]{:S(2)}, u32[]{:S(2)}) collective-permute-start(bf16[512,512]{1,0:T(8,128)(2,1)} %pad_maximum_fusion.6), channel_id=1, source_target_pairs={{0,4},{4,0},{8,12},{12,8},{16,20},{20,16},{24,28},{28,24},{1,5},{5... | collective-permute-start | bytes 1572872 | tf_op jit(solution)/shard_map/ppermute | solution.py:381
  100.2 47.5 %collective-permute-start.7 = (bf16[256,2048]{1,0:T(8,128)(2,1)S(1)}, bf16[256,2048]{1,0:T(8,128)(2,1)}, u32[]{:S(2)}, u32[]{:S(2)}) collective-permute-start(bf16[256,2048]{1,0:T(8,128)(2,1)S(1)} %convert_element_type.335.refs_0_), channel_id=1, source_target_pairs={{0,16},{4,20},{8,24},{12,28},{16,0},{20,4},{24,8},{28,12},{1,17},{... | collective-permute-start | bytes 3145736 | tf_op jit(solution)/shard_map/ppermute | solution.py:381
  150.5 45.8 %collective-permute-start.11 = (bf16[512,2048]{1,0:T(8,128)(2,1)}, bf16[512,2048]{1,0:T(8,128)(2,1)}, u32[]{:S(2)}, u32[]{:S(2)}) collective-permute-start(bf16[512,2048]{1,0:T(8,128)(2,1)} %pad_maximum_fusion), channel_id=1, source_target_pairs={{0,8},{4,12},{8,0},{12,4},{16,24},{20,28},{24,16},{28,20},{1,9},{5... | collective-permute-start | bytes 6291464 | tf_op jit(solution)/shard_map/ppermute | solution.py:381
  150.5 41.7 %collective-permute-start.12 = (bf16[256,2048]{1,0:T(8,128)(2,1)}, bf16[256,2048]{1,0:T(8,128)(2,1)}, u32[]{:S(2)}, u32[]{:S(2)}) collective-permute-start(bf16[256,2048]{1,0:T(8,128)(2,1)} %collective-permute-done.7.refs_1_), channel_id=1, source_target_pairs={{0,4},{4,0},{8,12},{12,8},{16,20},{20,16},{24,28},{28,24},{1,5},{5... | collective-permute-start | bytes 3145736 | tf_op jit(solution)/shard_map/ppermute | solution.py:381
  151.8 33.3 %collective-permute-start.10 = (bf16[512,512]{1,0:T(8,128)(2,1)}, bf16[512,512]{1,0:T(8,128)(2,1)}, u32[]{:S(2)}, u32[]{:S(2)}) collective-permute-start(bf16[512,512]{1,0:T(8,128)(2,1)} %collective-permute-done.6.refs_2_), channel_id=1, source_target_pairs={{0,4},{4,0},{8,12},{12,8},{16,20},{20,16},{24,28},{28,24},{1,5},{5... | collective-permute-start | bytes 1572872 | tf_op jit(solution)/shard_map/ppermute | solution.py:381
  344.3 44.4 %collective-permute-start.29 = (bf16[512,2048]{1,0:T(8,128)(2,1)}, bf16[512,2048]{1,0:T(8,128)(2,1)}, u32[]{:S(2)}, u32[]{:S(2)}) collective-permute-start(bf16[512,2048]{1,0:T(8,128)(2,1)} %shard_map.463), channel_id=1, source_target_pairs={{0,4},{4,0},{8,12},{12,8},{16,20},{20,16},{24,28},{28,24},{1,5},{5... | collective-permute-start | bytes 6291464 | tf_op jit(solution)/shard_map/ppermute | solution.py:381
  499.8 48.1 %collective-permute-start.48 = (bf16[512,2048]{1,0:T(8,128)(2,1)}, bf16[512,2048]{1,0:T(8,128)(2,1)}, u32[]{:S(2)}, u32[]{:S(2)}) collective-permute-start(bf16[512,2048]{1,0:T(8,128)(2,1)} %add_convert_fusion.1), channel_id=1, source_target_pairs={{0,8},{4,12},{8,0},{12,4},{16,24},{20,28},{24,16},{28,20},{1,9},{5... | collective-permute-start | bytes 6291464 | tf_op jit(solution)/shard_map/ppermute | solution.py:381
  501.6 47.4 %collective-permute-start.47 = (bf16[512,2048]{1,0:T(8,128)(2,1)}, bf16[512,2048]{1,0:T(8,128)(2,1)}, u32[]{:S(2)}, u32[]{:S(2)}) collective-permute-start(bf16[512,2048]{1,0:T(8,128)(2,1)} %shard_map.469), channel_id=1, source_target_pairs={{0,4},{4,0},{8,12},{12,8},{16,20},{20,16},{24,28},{28,24},{1,5},{5... | collective-permute-start | bytes 6291464 | tf_op jit(solution)/shard_map/ppermute | solution.py:381
  586.2 35.4 %collective-permute-start.56 = (bf16[128,2048]{1,0:T(8,128)(2,1)}, bf16[128,2048]{1,0:T(8,128)(2,1)}, u32[]{:S(2)}, u32[]{:S(2)}) collective-permute-start(bf16[128,2048]{1,0:T(8,128)(2,1)} %get-tuple-element.331), channel_id=1, source_target_pairs={{0,16},{4,20},{8,24},{12,28},{16,0},{20,4},{24,8},{28,12},{1,17},{... | collective-permute-start | bytes 1572872 | tf_op jit(solution)/shard_map/ppermute | solution.py:381
  588.2 33.5 %collective-permute-start.55 = (bf16[512,512]{1,0:T(8,128)(2,1)}, bf16[512,512]{1,0:T(8,128)(2,1)}, u32[]{:S(2)}, u32[]{:S(2)}) collective-permute-start(bf16[512,512]{1,0:T(8,128)(2,1)} %add_convert_fusion.13), channel_id=1, source_target_pairs={{0,8},{4,12},{8,0},{12,4},{16,24},{20,28},{24,16},{28,20},{1,9},{5... | collective-permute-start | bytes 1572872 | tf_op jit(solution)/shard_map/ppermute | solution.py:381
  591.7 35.8 %collective-permute-start.54 = (bf16[512,1536]{1,0:T(8,128)(2,1)}, bf16[512,1536]{1,0:T(8,128)(2,1)}, u32[]{:S(2)}, u32[]{:S(2)}) collective-permute-start(bf16[512,1536]{1,0:T(8,128)(2,1)} %shard_map.475), channel_id=1, source_target_pairs={{0,4},{4,0},{8,12},{12,8},{16,20},{20,16},{24,28},{28,24},{1,5},{5... | collective-permute-start | bytes 4718600 | tf_op jit(solution)/shard_map/ppermute | solution.py:381
  630.1 45.2 %collective-permute-start.58 = (bf16[512,1536]{1,0:T(8,128)(2,1)S(1)}, bf16[512,1536]{1,0:T(8,128)(2,1)S(1)}, u32[]{:S(2)}, u32[]{:S(2)}) collective-permute-start(bf16[512,1536]{1,0:T(8,128)(2,1)S(1)} %add_convert_fusion.2), channel_id=1, source_target_pairs={{0,8},{4,12},{8,0},{12,4},{16,24},{20,28},{24,16},{28,20},{1,9},{5... | collective-permute-start | bytes 4718600 | tf_op jit(solution)/shard_map/ppermute | solution.py:381
  630.3 45.0 %collective-permute-start.57 = (bf16[512,1536]{1,0:T(8,128)(2,1)S(1)}, bf16[512,1536]{1,0:T(8,128)(2,1)S(1)}, u32[]{:S(2)}, u32[]{:S(2)}) collective-permute-start(bf16[512,1536]{1,0:T(8,128)(2,1)S(1)} %copy-done.77), channel_id=1, source_target_pairs={{0,4},{4,0},{8,12},{12,8},{16,20},{20,16},{24,28},{28,24},{1,5},{5... | collective-permute-start | bytes 4718600 | tf_op jit(solution)/shard_map/ppermute | solution.py:381
  634.8 40.5 %collective-permute-start.59 = (bf16[256,2048]{1,0:T(8,128)(2,1)}, bf16[256,2048]{1,0:T(8,128)(2,1)}, u32[]{:S(2)}, u32[]{:S(2)}) collective-permute-start(bf16[256,2048]{1,0:T(8,128)(2,1)} %shard_map.480), channel_id=1, source_target_pairs={{0,2},{1,3},{2,0},{3,1},{4,6},{5,7},{6,4},{7,5},{8,10},{9,11},{10,... | collective-permute-start | bytes 3145736 | tf_op jit(solution)/shard_map/ppermute | solution.py:404
  657.2 41.6 %collective-permute-start.66 = (bf16[256,2048]{1,0:T(8,128)(2,1)}, bf16[256,2048]{1,0:T(8,128)(2,1)}, u32[]{:S(2)}, u32[]{:S(2)}) collective-permute-start(bf16[256,2048]{1,0:T(8,128)(2,1)} %collective-permute-done.64), channel_id=1, source_target_pairs={{0,1},{1,0},{2,3},{3,2},{4,5},{5,4},{6,7},{7,6},{8,9},{9,8},{10,11... | collective-permute-start | bytes 3145736 | tf_op jit(solution)/shard_map/ppermute | solution.py:404
  680.5 38.0 %collective-permute-start.62 = (bf16[256,1536]{1,0:T(8,128)(2,1)}, bf16[256,1536]{1,0:T(8,128)(2,1)}, u32[]{:S(2)}, u32[]{:S(2)}) collective-permute-start(bf16[256,1536]{1,0:T(8,128)(2,1)} %add_convert_fusion.11), channel_id=1, source_target_pairs={{0,16},{4,20},{8,24},{12,28},{16,0},{20,4},{24,8},{28,12},{1,17},{... | collective-permute-start | bytes 2359304 | tf_op jit(solution)/shard_map/ppermute | solution.py:381
  (181 other events, 2492.5 us)
